TPU v7x, 32 devices: a whole 2x2x4 slice. The times are simulated.
32 devices in a mesh: grp: 8 (over z, x), fsdp: 4 (over y, core).
Axes of the slice: x: 2, y: 2, z: 4, core: 2. Of those that a mesh axis runs over, the one named last changes fastest.
Arguments:
- inputs: bfloat16 [96, 160, 768], P(('grp', 'fsdp')), may hold values from -6 to 6
- lengths: int32 [96], P(('grp', 'fsdp')), may hold values from 95 to 160, as said below
- cotangent: bfloat16 [96, 160, 768], P(('grp', 'fsdp')), may hold values from -6 to 6
- masters: float32 [2, 48, 384, 384], P(None, 'grp', 'fsdp')
- small_params: float32 [2, 9216], replicated
- small_moments: float32 [2, 9216], replicated, may hold values from 3840 to 15360
- left_stats: float32 [2, 48, 384, 384], P(None, 'grp', 'fsdp')
- right_stats: float32 [2, 48, 384, 384], P(None, 'grp', 'fsdp')
- left_roots: float32 [2, 48, 384, 384], P(None, 'grp', 'fsdp')
- right_roots: float32 [2, 48, 384, 384], P(None, 'grp', 'fsdp'), as said below
Outputs:
- activations: bfloat16 [96, 160, 768], P(('grp', 'fsdp'))
- input_grad: float32 [96, 160, 768], P(('grp', 'fsdp'))
- blocked_weight_gradients: float32 [2, 48, 384, 384], P(None, 'grp', 'fsdp')
- small_grads: float32 [2, 9216], replicated
- new_moments: float32 [2, 9216], replicated
- new_small: float32 [2, 9216], replicated
- new_left: float32 [2, 48, 384, 384], P(None, 'grp', 'fsdp')
- new_right: float32 [2, 48, 384, 384], P(None, 'grp', 'fsdp')
- new_masters: float32 [2, 48, 384, 384], P(None, 'grp', 'fsdp')
- new_copies: bfloat16 [2, 48, 384, 384], P(None, 'grp', 'fsdp')
Inputs may be any that keep to these rules, and one draw needn't show every extreme that they name: `lengths`: in every draw some chain has exactly 160 live residues and some exactly 95. `right_roots`: every block is symmetric.
All inputs are finite; a program needn't handle non-finite values.
Results may differ from a plain program's by a relative error of at most 0.02.
Values may be sent and summed in bfloat16 or wider, within the bound.
No kernel may reach another device: no remote copies, remote signals or barrier semaphores. Data moves between devices by JAX's collectives and lax.ppermute only.
A program may use at most 256 MiB of HBM per device.

v0:
```python
import jax
import jax.numpy as jnp
from jax import lax
from jax.sharding import PartitionSpec as P

HEADS = 12
ENCODER_LAYERS = 2


norm_epsilon = 1e-05
matrix_rate = 1.0
small_rate = 0.3
decay_rate = 0.5
moment_epsilon = 1e-08


def matmul(left, right):
    return jnp.dot(left, right, preferred_element_type=jnp.float32)


def matmul_t(left, right):
    return lax.dot_general(
        left, right, (((1,), (1,)), ((), ())), preferred_element_type=jnp.float32
    )


def outer_sum(left, right):
    return lax.dot_general(
        left, right, (((0,), (0,)), ((), ())), preferred_element_type=jnp.float32
    )


def activation(values):
    return jax.nn.gelu(values, approximate=False)


def total_rows(array):
    return jnp.sum(array.astype(jnp.float32), axis=0)


def norm_forward(values, gain, shift):
    center = values - jnp.mean(values, axis=-1, keepdims=True)
    spread = jnp.mean(center * center, axis=-1, keepdims=True)
    inverse = lax.rsqrt(spread + norm_epsilon)
    normalized = center * inverse
    return (normalized * gain + shift, normalized, inverse)


def norm_backward(gradient, normalized, inverse, gain):
    scaled = gradient * gain
    inner = (
        scaled
        - jnp.mean(scaled, axis=-1, keepdims=True)
        - normalized * jnp.mean(scaled * normalized, axis=-1, keepdims=True)
    )
    return (inverse * inner, jnp.sum(gradient * normalized, axis=0), jnp.sum(gradient, axis=0))


def split_small(vector, model_width):
    return [vector[segment * model_width : (segment + 1) * model_width] for segment in range(8)] + [
        vector[8 * model_width :]
    ]


def unblock(weight_blocks, model_width, ffn_width, block_border):
    model_count = model_width // block_border
    ffn_count = ffn_width // block_border
    layout = [(model_count, model_count)] * 4 + [(model_count, ffn_count), (ffn_count, model_count)]
    weight_matrices = []
    offset = 0
    for row_count, col_count in layout:
        selected = weight_blocks[offset : offset + row_count * col_count]
        weight_matrices.append(
            selected.reshape(row_count, col_count, block_border, block_border)
            .transpose(0, 2, 1, 3)
            .reshape(row_count * block_border, col_count * block_border)
        )
        offset += row_count * col_count
    return weight_matrices


def split_into_blocks(weight_matrices, block_border):
    pieces = []
    for matrix in weight_matrices:
        row_count = matrix.shape[0] // block_border
        col_count = matrix.shape[1] // block_border
        pieces.append(
            matrix.reshape(row_count, block_border, col_count, block_border)
            .transpose(0, 2, 1, 3)
            .reshape(row_count * col_count, block_border, block_border)
        )
    return jnp.concatenate(pieces, axis=0)


def local(
    inputs,
    lengths,
    cotangent,
    masters,
    small_params,
    small_moments,
    left_stats,
    right_stats,
    left_roots,
    right_roots,
):
    chains, seq_len, model_width = inputs.shape
    rows_count = chains * seq_len
    group_count = lax.axis_size("grp")
    shard_count = lax.axis_size("fsdp")
    own_blocks = masters.shape[1]
    own_rows = masters.shape[2]
    block_border = masters.shape[3]
    small_width = small_params.shape[1]
    ffn_width = small_width - 8 * model_width
    head_dim = model_width // HEADS
    score_scale = head_dim ** (-0.5)
    shape_heads = (chains, seq_len, HEADS, head_dim)
    key_valid = jnp.arange(seq_len)[None, :] < lengths[:, None]
    row_valid = key_valid.reshape(rows_count, 1).astype(jnp.float32)
    copies = masters.astype(jnp.bfloat16)

    def arrange(gathered):
        ordered = gathered.reshape(
            group_count, shard_count, own_blocks, own_rows, block_border
        ).transpose(0, 2, 1, 3, 4)
        return unblock(
            ordered.reshape(group_count * own_blocks, block_border, block_border),
            model_width,
            ffn_width,
            block_border,
        )

    def scores_of(query_heads, key_heads):
        raw = (
            jnp.einsum(
                "cqhd,ckhd->chqk", query_heads, key_heads, preferred_element_type=jnp.float32
            )
            * score_scale
        )
        return jnp.where(key_valid[:, None, None, :], raw, -1000000000.0)

    states = inputs.astype(jnp.float32).reshape(rows_count, model_width)
    stored_layers = []
    for layer_position in range(ENCODER_LAYERS):
        weight_matrices = arrange(
            lax.all_gather(
                copies[layer_position].reshape(1, -1), ("grp", "fsdp"), axis=0, tiled=True
            )
        )
        (
            forward_w_query,
            forward_w_key,
            forward_w_value,
            forward_w_out,
            forward_w_up,
            forward_w_down,
        ) = weight_matrices
        (
            bias_query,
            bias_value,
            bias_out,
            bias_down,
            forward_gain_one,
            shift_one,
            forward_gain_two,
            shift_two,
            bias_up,
        ) = split_small(small_params[layer_position], model_width)
        forward_states_low = states.astype(jnp.bfloat16)
        forward_queries = (matmul(forward_states_low, forward_w_query) + bias_query).astype(
            jnp.bfloat16
        )
        forward_key_rows = matmul(forward_states_low, forward_w_key).astype(jnp.bfloat16)
        forward_values = (matmul(forward_states_low, forward_w_value) + bias_value).astype(
            jnp.bfloat16
        )
        scores = scores_of(
            forward_queries.reshape(shape_heads), forward_key_rows.reshape(shape_heads)
        )
        forward_log_total = jax.nn.logsumexp(scores, axis=-1, keepdims=True)
        forward_attention = jnp.exp(scores - forward_log_total).astype(jnp.bfloat16)
        forward_context = jnp.einsum(
            "chqk,ckhd->cqhd",
            forward_attention,
            forward_values.reshape(shape_heads),
            preferred_element_type=jnp.float32,
        )
        forward_context = forward_context.reshape(rows_count, model_width).astype(jnp.bfloat16)
        attended = matmul(forward_context, forward_w_out) + bias_out
        normed_one, forward_unit_one, forward_inverse_one = norm_forward(
            states + attended, forward_gain_one, shift_one
        )
        forward_normed_low = normed_one.astype(jnp.bfloat16)
        forward_hidden = matmul(forward_normed_low, forward_w_up) + bias_up
        forward_active = activation(forward_hidden).astype(jnp.bfloat16)
        outputs, forward_unit_two, forward_inverse_two = norm_forward(
            normed_one + (matmul(forward_active, forward_w_down) + bias_down),
            forward_gain_two,
            shift_two,
        )
        forward_stored = (
            forward_states_low,
            forward_queries,
            forward_key_rows,
            forward_values,
            forward_log_total,
            forward_context,
            forward_unit_one,
            forward_inverse_one,
            forward_normed_low,
            forward_hidden,
            forward_active,
            forward_unit_two,
            forward_inverse_two,
        )
        states = outputs
        stored_layers.append(forward_stored)
    activations = states.astype(jnp.bfloat16).reshape(chains, seq_len, model_width)
    grad_states = cotangent.astype(jnp.float32).reshape(rows_count, model_width) * row_valid
    owned = [None] * ENCODER_LAYERS
    small_parts = [None] * ENCODER_LAYERS
    for layer_position in reversed(range(ENCODER_LAYERS)):
        weight_matrices = arrange(
            lax.all_gather(
                copies[layer_position].reshape(1, -1), ("grp", "fsdp"), axis=0, tiled=True
            )
        )
        grad_out = grad_states
        w_query, w_key, w_value, w_out, w_up, w_down = weight_matrices
        segments = split_small(small_params[layer_position], model_width)
        gain_one = segments[4]
        gain_two = segments[6]
        (
            states_low,
            queries,
            key_rows,
            values,
            log_total,
            context,
            unit_one,
            inverse_one,
            normed_low,
            hidden,
            active,
            unit_two,
            inverse_two,
        ) = stored_layers[layer_position]
        grad_two, grad_gain_two, grad_shift_two = norm_backward(
            grad_out, unit_two, inverse_two, gain_two
        )
        grad_ffn = grad_two.astype(jnp.bfloat16)
        grad_active = matmul_t(grad_ffn, w_down)
        unused_value, gelu_pull = jax.vjp(activation, hidden)
        grad_hidden = gelu_pull(grad_active)[0].astype(jnp.bfloat16)
        grad_normed = grad_two + matmul_t(grad_hidden, w_up)
        grad_one, grad_gain_one, grad_shift_one = norm_backward(
            grad_normed, unit_one, inverse_one, gain_one
        )
        grad_attended = grad_one.astype(jnp.bfloat16)
        grad_context = matmul_t(grad_attended, w_out).astype(jnp.bfloat16).reshape(shape_heads)
        backward_query_heads = queries.reshape(shape_heads)
        backward_key_heads = key_rows.reshape(shape_heads)
        value_heads = values.reshape(shape_heads)
        attention = jnp.exp(scores_of(backward_query_heads, backward_key_heads) - log_total)
        grad_attention = jnp.einsum(
            "cqhd,ckhd->chqk", grad_context, value_heads, preferred_element_type=jnp.float32
        )
        grad_values = jnp.einsum(
            "chqk,cqhd->ckhd",
            attention.astype(jnp.bfloat16),
            grad_context,
            preferred_element_type=jnp.float32,
        )
        grad_values = grad_values.reshape(rows_count, model_width).astype(jnp.bfloat16)
        grad_scores = (
            attention
            * (grad_attention - jnp.sum(attention * grad_attention, axis=-1, keepdims=True))
        ).astype(jnp.bfloat16)
        grad_queries = (
            jnp.einsum(
                "chqk,ckhd->cqhd",
                grad_scores,
                backward_key_heads,
                preferred_element_type=jnp.float32,
            )
            * score_scale
        )
        grad_queries = grad_queries.reshape(rows_count, model_width).astype(jnp.bfloat16)
        grad_keys = (
            jnp.einsum(
                "chqk,cqhd->ckhd",
                grad_scores,
                backward_query_heads,
                preferred_element_type=jnp.float32,
            )
            * score_scale
        )
        grad_keys = grad_keys.reshape(rows_count, model_width).astype(jnp.bfloat16)
        backward_grad_states = (
            grad_one
            + matmul_t(grad_queries, w_query)
            + matmul_t(grad_keys, w_key)
            + matmul_t(grad_values, w_value)
        )
        weight_factors = [
            outer_sum(states_low, grad_queries),
            outer_sum(states_low, grad_keys),
            outer_sum(states_low, grad_values),
            outer_sum(context, grad_attended),
            outer_sum(normed_low, grad_hidden),
            outer_sum(active, grad_ffn),
        ]
        small_terms = jnp.concatenate(
            [
                total_rows(grad_queries),
                total_rows(grad_values),
                total_rows(grad_attended),
                total_rows(grad_ffn),
                grad_gain_one,
                grad_shift_one,
                grad_gain_two,
                grad_shift_two,
                total_rows(grad_hidden),
            ]
        )
        grad_states, weight_factors, small_terms = (
            backward_grad_states,
            weight_factors,
            small_terms,
        )
        weight_blocks = split_into_blocks(weight_factors, block_border)
        group_blocks, group_small = (
            lax.psum_scatter(
                weight_blocks.astype(jnp.bfloat16), "fsdp", scatter_dimension=1, tiled=True
            ).astype(jnp.float32),
            lax.psum_scatter(
                small_terms.astype(jnp.bfloat16), "fsdp", scatter_dimension=0, tiled=True
            ).astype(jnp.float32),
        )
        summed_blocks, summed_small = (
            lax.psum(group_blocks.astype(jnp.bfloat16), "grp").astype(jnp.float32),
            lax.psum(group_small.astype(jnp.bfloat16), "grp").astype(jnp.float32),
        )
        owned[layer_position] = lax.dynamic_slice_in_dim(
            summed_blocks, lax.axis_index("grp") * own_blocks, own_blocks, 0
        )
        small_parts[layer_position] = summed_small
    input_grad = grad_states.reshape(chains, seq_len, model_width)
    blocked_weight_gradients = jnp.stack(owned)
    small_stack = jnp.stack(small_parts)
    whole_grads, small_grads = (
        lax.all_gather(
            blocked_weight_gradients.astype(jnp.bfloat16), "fsdp", axis=2, tiled=True
        ).astype(blocked_weight_gradients.dtype),
        lax.all_gather(small_stack.astype(jnp.bfloat16), "fsdp", axis=1, tiled=True).astype(
            small_stack.dtype
        ),
    )
    first_row = lax.axis_index("fsdp") * own_rows
    highest = lax.Precision.HIGHEST
    columns = lax.dynamic_slice_in_dim(whole_grads, first_row, own_rows, 3)
    new_left = decay_rate * left_stats + (1.0 - decay_rate) * jnp.einsum(
        "lbrk,lbck->lbrc", blocked_weight_gradients, whole_grads, precision=highest
    )
    new_right = decay_rate * right_stats + (1.0 - decay_rate) * jnp.einsum(
        "lbkr,lbkc->lbrc", columns, whole_grads, precision=highest
    )
    mixed_cols = jnp.einsum("lbrk,lbck->lbrc", whole_grads, right_roots, precision=highest)
    mixed = lax.all_gather(mixed_cols.astype(jnp.bfloat16), "fsdp", axis=3, tiled=True).astype(
        mixed_cols.dtype
    )
    update = jnp.einsum("lbrk,lbkc->lbrc", left_roots, mixed, precision=highest)
    new_masters = masters - matrix_rate * update
    new_copies = new_masters.astype(jnp.bfloat16)
    new_moments = decay_rate * small_moments + (1.0 - decay_rate) * small_grads * small_grads
    new_small = small_params - small_rate * small_grads / (jnp.sqrt(new_moments) + moment_epsilon)
    return (
        activations,
        input_grad,
        blocked_weight_gradients,
        small_grads,
        new_moments,
        new_small,
        new_left,
        new_right,
        new_masters,
        new_copies,
    )


def solution(mesh):
    return jax.shard_map(
        local,
        mesh=mesh,
        in_specs=(
            P(("grp", "fsdp"), None, None),
            P(("grp", "fsdp")),
            P(("grp", "fsdp"), None, None),
            P(None, "grp", "fsdp", None),
            P(),
            P(),
            P(None, "grp", "fsdp", None),
            P(None, "grp", "fsdp", None),
            P(None, "grp", "fsdp", None),
            P(None, "grp", "fsdp", None),
        ),
        out_specs=(
            P(("grp", "fsdp"), None, None),
            P(("grp", "fsdp"), None, None),
            P(None, "grp", "fsdp", None),
            P(),
            P(),
            P(),
            P(None, "grp", "fsdp", None),
            P(None, "grp", "fsdp", None),
            P(None, "grp", "fsdp", None),
            P(None, "grp", "fsdp", None),
        ),
        check_vma=False,
    )
```

profile of v0, /device:TPU:0, one launch (start us, length us, event | category | flops | bytes accessed | tf_op | source)
XLA Modules:
  0.0 1430.3 jit_solution(3990143595703663156)
XLA Ops:
  15.8 168.1 %all-gather.11.cloned.1.call-done = bf16[32,1,221184]{2,1,0:T(2,128)(2,1)} async-done(((bf16[1,1,221184]{2,1,0:T(2,128)(2,1)}), bf16[32,1,221184]{2,1,0:T(2,128)(2,1)}) %all-gather.11.cloned.1.call-update) | async-done | bytes 14155792 | tf_op jit(solution)/shard_map/all_gather | solution.py:147
  184.0 84.2 %reduce.16 = bf16[32,221184]{1,0:T(8,128)(2,1)} reduce(bf16[32,1,221184]{2,1,0:T(2,128)(2,1)} %all-gather.11.cloned.1.call-done, bf16[]{:T(256)} %constant.143), dimensions={1}, to_apply=%all-gather.reduce_sub_computation | reduce | bytes 28311554 | tf_op jit(solution)/shard_map/all_gather | solution.py:147
  268.2 9.8 copy.258
  282.3 5.0 copy-done.3
  289.2 8.9 fusion.76
  298.1 57.3 %all-gather.13.cloned.1.call-done = bf16[32,1,221184]{2,1,0:T(2,128)(2,1)} async-done(((bf16[1,1,221184]{2,1,0:T(2,128)(2,1)}), bf16[32,1,221184]{2,1,0:T(2,128)(2,1)}) %all-gather.13.cloned.1.call-update) | async-done | bytes 14155792 | tf_op jit(solution)/shard_map/all_gather | solution.py:147
  355.4 84.0 %reduce.25 = bf16[32,221184]{1,0:T(8,128)(2,1)} reduce(bf16[32,1,221184]{2,1,0:T(2,128)(2,1)} %all-gather.13.cloned.1.call-done, bf16[]{:T(256)} %constant.143), dimensions={1}, to_apply=%all-gather.1.reduce_sub_computation | reduce | bytes 28311554 | tf_op jit(solution)/shard_map/all_gather | solution.py:147
  439.4 8.1 copy.265
  452.0 5.0 copy-done.4
  459.3 9.0 fusion.74
  524.6 7.0 copy.143
  535.7 18.0 %multiply_convert_fusion.3 = (bf16[480,3072]{1,0:T(8,128)(2,1)S(1)}, f32[480,3072]{1,0:T(8,128)}, f32[480,3072]{1,0:T(8,128)}) fusion(f32[3072]{0:T(1024)S(1)} %bitcast.434, bf16[768,3072]{1,0:T(8,128)(2,1)S(1)} %bitcast.374, f32[480,768]{1,0:T(8,128)S(1)} %copy-done.22, f32[768]{0:T(1024)S(1)} %get-tuple-element.36, f32[768]{0:T(1024)S(1)} %get-tuple-element.37, ...), kind=kOutput, calls=%fused_computation.26 | convolution fusion | flops 2364088320 | bytes 20961024 | tf_op jit(solution)/shard_map/dot_general | solution.py:18
  622.0 7.1 copy.158
  633.2 16.9 %multiply_convert_fusion.2 = (bf16[480,3072]{1,0:T(8,128)(2,1)S(1)}, f32[480,3072]{1,0:T(8,128)S(1)}, f32[480,3072]{1,0:T(8,128)}) fusion(f32[3072]{0:T(1024)S(1)} %bitcast.436, bf16[768,3072]{1,0:T(8,128)(2,1)S(1)} %bitcast.387, f32[480,768]{1,0:T(8,128)S(1)} %copy-done.19, f32[768]{0:T(1024)S(1)} %copy-done.101, f32[768]{0:T(1024)S(1)} %copy-done.87, ...), kind=kOutput, calls=%fused_computation.10 | convolution fusion | flops 2364088320 | bytes 20961024 | tf_op jit(solution)/shard_map/dot_general | solution.py:18
  659.1 7.5 fusion.86
  680.4 6.0 multiply_reduce_fusion.1
  714.7 5.1 multiply_reduce_fusion.4
  720.9 8.5 fusion.89
  748.0 6.0 multiply_reduce_fusion
  809.8 10.1 reshape.562
  834.3 7.4 convolution_convert_fusion
  841.8 10.8 reshape.570
  852.6 5.6 copy.204
  881.9 58.9 %reduce-scatter.3.cloned.1.call-done = bf16[48,96,384]{2,1,0:T(8,128)(2,1)} async-done(((bf16[48,384,384]{2,1,0:T(8,128)(2,1)}), bf16[48,96,384]{2,1,0:T(8,128)(2,1)}) %reduce-scatter.3.cloned.1.call-update) | async-done | bytes 3538960 | tf_op jit(solution)/shard_map/reduce_scatter | solution.py:334
  940.8 111.9 %reduce-scatter.5.cloned.1.call-done = bf16[48,96,384]{2,1,0:T(8,128)(2,1)} async-done(((bf16[48,384,384]{2,1,0:T(8,128)(2,1)}), bf16[48,96,384]{2,1,0:T(8,128)(2,1)}) %reduce-scatter.5.cloned.1.call-update) | async-done | bytes 3538960 | tf_op jit(solution)/shard_map/reduce_scatter | solution.py:334
  1052.8 238.4 %all-reduce.7.cloned.1.call-done = (bf16[48,96,384]{2,1,0:T(8,128)(2,1)}, bf16[48,96,384]{2,1,0:T(8,128)(2,1)}) async-done(((bf16[48,96,384]{2,1,0:T(8,128)(2,1)}, bf16[48,96,384]{2,1,0:T(8,128)(2,1)}), (bf16[48,96,384]{2,1,0:T(8,128)(2,1)}, bf16[48,96,384]{2,1,0:T(8,128)(2,1)})) %all-reduce.7.cloned.1.call-update) | async-done | bytes 7077904 | tf_op jit(solution)/shard_map/psum | solution.py:342
  1295.4 29.7 %all-gather.7.cloned.1.call-done = bf16[2,6,384,384]{3,2,1,0:T(8,128)(2,1)} async-done(((bf16[2,6,96,384]{3,2,1,0:T(8,128)(2,1)}), bf16[2,6,384,384]{3,2,1,0:T(8,128)(2,1)}) %all-gather.7.cloned.1.call-update) | async-done | bytes 3538960 | tf_op jit(solution)/shard_map/all_gather | solution.py:353
  1325.1 6.3 convolution_convert_fusion.16
  1346.0 12.3 all-reduce.4
  1358.5 37.2 %all-reduce.2 = (bf16[1,2304]{1,0:T(2,128)(2,1)S(1)}, bf16[1,2304]{1,0:T(2,128)(2,1)S(1)}) all-reduce(bf16[1,2304]{1,0:T(2,128)(2,1)S(1)} %stack.25, bf16[1,2304]{1,0:T(2,128)(2,1)S(1)} %stack.24), channel_id=1, replica_groups=mesh['grp'=8,'fsdp'=4] {'grp'}, use_global_device_ids=true, to_apply=%region_47.48 | all-reduce | flops 4608 | bytes 18432 | tf_op jit(solution)/shard_map/psum | solution.py:343
  1395.8 5.6 all_gather.19
  1416.3 6.9 fusion.90
  (514 shorter events, 350.7 us)
Async XLA Ops:
  7.2 1409.1 %copy-start = (f32[2,6,96,384]{3,2,1,0:T(8,128)S(1)}, f32[2,6,96,384]{3,2,1,0:T(8,128)}, u32[]{:S(2)}) copy-start(f32[2,6,96,384]{3,2,1,0:T(8,128)} %param.18) | copy-start | bytes 5308420
  7.2 176.8 %all-gather.11.cloned.1.call-start = ((), (), s32[]{:S(2)}) async-start(), calls=%async_computation.6 | async-start | bytes 29196288 | tf_op jit(solution)/shard_map/all_gather | solution.py:147
  10.2 345.2 %all-gather.13.cloned.1.call-start = ((), (), s32[]{:S(2)}) async-start(), calls=%async_computation.7 | async-start | bytes 29196288 | tf_op jit(solution)/shard_map/all_gather | solution.py:147
  11.3 929.5 %reduce-scatter.3.cloned.1.call-start = ((), (), s32[]{:S(2)}) async-start(), calls=%async_computation.2 | async-start | bytes 17694720 | tf_op jit(solution)/shard_map/reduce_scatter | solution.py:334
  11.5 256.6 %copy-start.85 = (f32[480]{0:T(512)}, f32[480]{0:T(512)S(1)}, u32[]{:S(2)}) copy-start(f32[480]{0:T(512)S(1)} %reshape.572) | copy-start | bytes 5764
  12.3 255.9 %copy-start.81 = (f32[768]{0:T(1024)}, f32[768]{0:T(1024)S(1)}, u32[]{:S(2)}) copy-start(f32[768]{0:T(1024)S(1)} %get-tuple-element.26) | copy-start | bytes 9220
  12.3 541.5 %copy-start.88 = (f32[768]{0:T(1024)}, f32[768]{0:T(1024)S(1)}, u32[]{:S(2)}) copy-start(f32[768]{0:T(1024)S(1)} %get-tuple-element.37) | copy-start | bytes 9220
  12.3 541.5 %copy-start.103 = (f32[768]{0:T(1024)}, f32[768]{0:T(1024)S(1)}, u32[]{:S(2)}) copy-start(f32[768]{0:T(1024)S(1)} %get-tuple-element.36) | copy-start | bytes 9220
  15.8 519.5 %copy-start.91 = (f32[1,3072]{1,0:T(1,128)}, f32[1,3072]{1,0:T(1,128)S(1)}, u32[]{:S(2)}) copy-start(f32[1,3072]{1,0:T(1,128)S(1)} %get-tuple-element.83) | copy-start | bytes 36868
  459.3 9.0 copy-start.34
  517.0 36.8 %copy-start.98 = (f32[480]{0:T(512)}, f32[480]{0:T(512)S(1)}, u32[]{:S(2)}) copy-start(f32[480]{0:T(512)S(1)} %add_rsqrt_fusion.3) | copy-start | bytes 5764
  524.6 10.7 slice-start.14
  535.3 18.4 %copy-start.35 = (bf16[96,8,8,384]{3,1,2,0:T(8,128)(2,1)}, bf16[96,8,8,384]{3,1,2,0:T(8,128)(2,1)S(1)}, u32[]{:S(2)}) copy-start(bf16[96,8,8,384]{3,1,2,0:T(8,128)(2,1)S(1)} %copy.264) | copy-start | bytes 14155780
  556.5 56.4 %copy-start.5 = (f32[480,768]{1,0:T(8,128)}, f32[480,768]{1,0:T(8,128)S(1)}, u32[]{:S(2)}) copy-start(f32[480,768]{1,0:T(8,128)S(1)} %get-tuple-element.92) | copy-start | bytes 4423684
  614.3 55.7 %copy-start.96 = (f32[480]{0:T(512)}, f32[480]{0:T(512)S(1)}, u32[]{:S(2)}) copy-start(f32[480]{0:T(512)S(1)} %add_rsqrt_fusion.1) | copy-start | bytes 5764
  622.0 10.8 slice-start.22
  633.2 18.5 %copy-start.105 = (f32[768]{0:T(1024)S(1)}, f32[768]{0:T(1024)}, u32[]{:S(2)}) copy-start(f32[768]{0:T(1024)} %get-tuple-element.27) | copy-start | bytes 9220
  676.0 10.4 slice-start.2
  714.7 19.6 %slice-start.16 = ((s8[4718592]{0:T(1024)(128)(4,1)}), s8[4194304]{0:T(1024)(128)(4,1)S(1)}, s32[]{:S(2)}) async-start(s8[4718592]{0:T(1024)(128)(4,1)} %bitcast.375), calls=%async_computation.25 | async-start | bytes 8388608
  720.8 13.4 copy-start.48
  720.8 8.5 copy-start.23
  720.8 8.5 copy-start.89
  720.9 13.4 slice-start.17
  743.7 10.2 slice-start
  833.0 219.8 %reduce-scatter.5.cloned.1.call-start = ((), (), s32[]{:S(2)}) async-start(), calls=%async_computation.3 | async-start | bytes 17694720 | tf_op jit(solution)/shard_map/reduce_scatter | solution.py:334
  881.9 409.3 %all-reduce.7.cloned.1.call-start = ((), (), s32[]{:S(2)}) async-start(), calls=%async_computation.8 | async-start | bytes 14155776 | tf_op jit(solution)/shard_map/psum | solution.py:342
  1052.8 272.4 %all-gather.7.cloned.1.call-start = ((), (), s32[]{:S(2)}) async-start(), calls=%async_computation.4 | async-start | bytes 4423680 | tf_op jit(solution)/shard_map/all_gather | solution.py:353
  1293.3 31.8 %copy-start.44 = (f32[2,6,96,384]{3,2,1,0:T(8,128)S(1)}, f32[2,6,96,384]{3,2,1,0:T(8,128)}, u32[]{:S(2)}) copy-start(f32[2,6,96,384]{3,2,1,0:T(8,128)} %param.19) | copy-start | bytes 5308420
  1295.1 43.3 %copy-start.95 = (bf16[768]{0:T(1024)(128)(2,1)S(1)}, bf16[768]{0:T(1024)(128)(2,1)}, u32[]{:S(2)}) copy-start(bf16[768]{0:T(1024)(128)(2,1)} %get-tuple-element.58) | copy-start | bytes 4612
  1295.2 49.2 %copy-start.100 = (bf16[768]{0:T(1024)(128)(2,1)S(1)}, bf16[768]{0:T(1024)(128)(2,1)}, u32[]{:S(2)}) copy-start(bf16[768]{0:T(1024)(128)(2,1)} %get-tuple-element.24) | copy-start | bytes 4612
  1295.2 121.1 %all-gather.9.cloned.1.call-start = ((), (), s32[]{:S(2)}) async-start(), calls=%async_computation.5 | async-start | bytes 4423680 | tf_op jit(solution)/shard_map/all_gather | solution.py:370
  1331.5 72.3 %copy-start.52 = (bf16[96,8,2,384]{3,1,2,0:T(8,128)(2,1)S(1)}, bf16[96,8,2,384]{3,1,2,0:T(8,128)(2,1)}, u32[]{:S(2)}) copy-start(bf16[96,8,2,384]{3,1,2,0:T(8,128)(2,1)} %copy-done.51) | copy-start | bytes 3538948
  (118 other events, 389.7 us)
Sparse Core Ops, SparseCore 0:
  11.5 172.3 all-gather.10
  187.5 167.8 all-gather.12
  833.1 107.6 reduce-scatter.2
  943.3 109.4 reduce-scatter.4
  1056.6 234.5 all-reduce.6
  1295.3 29.8 all-gather.6
  1331.6 31.5 all-gather.8
where the time goes:
time: 1440 us; the launch traced here: 1430 us
  waiting for transfers between devices  664 us (46%)
  local copies, waits for them, and re-layouts  312 us (22%)
  other arithmetic  195 us (14%)
  matrix products  186 us (13%)
  blocking collectives  55.1 us (4%)
  between operations  16.8 us (1%)
    psum x1, waiting for transfers between devices, local(): lax.psum(group_blocks.astype(jnp.bfloat16), 'grp').astype(jnp.float32)  238 us
    all_gather x2, waiting for transfers between devices, local(): lax.all_gather(copies[layer_position].reshape(1, -1), ('grp', 'fsdp'), ax...  225 us
    reduce_scatter x2, waiting for transfers between devices, local(): lax.psum_scatter(weight_blocks.astype(jnp.bfloat16), 'fsdp', scatter_dime...  171 us
    all_gather x2, other arithmetic, local(): lax.all_gather(copies[layer_position].reshape(1, -1), ('grp', 'fsdp'), ax...  168 us
    unnamed x333, local copies, waits for them, and re-layouts  95.6 us
    reshape x12, local copies, waits for them, and re-layouts, split_into_blocks(): matrix.reshape(row_count, block_border, col_count, block_border)  53 us
    dot_general x12, matrix products, matmul(): return jnp.dot(left, right, preferred_element_type=jnp.float32)  50.1 us
    dot_general x12, matrix products, matmul_t(): lax.dot_general(left, right, (((1,), (1,)), ((), ())), preferred_element_...  41.7 us
  transfers between devices with their start and end apart: 7, of which 6 were waited for; matrix products, arithmetic and copies ran while one was open for 13% of the time, Pallas kernels for 0%

commit v1 on v0

v1 whole, which is shorter than its diff:
```python
import functools

import jax
import jax.numpy as jnp
from jax import lax
from jax.experimental import pallas as pl
from jax.experimental.pallas import tpu as pltpu
from jax.sharding import PartitionSpec as P

HEADS = 12
LAYERS = 2
Z_SLABS = 4
BF = jnp.bfloat16
F32 = jnp.float32

norm_epsilon = 1e-05
matrix_rate = 1.0
small_rate = 0.3
decay_rate = 0.5
moment_epsilon = 1e-08

VMEM = pl.BlockSpec(memory_space=pltpu.VMEM)
SMEM = pl.BlockSpec(memory_space=pltpu.SMEM)
HBM = pl.BlockSpec(memory_space=pl.ANY)
VMEM_LIMIT = 56 * 1024 * 1024


def shape(dims, dtype):
    return jax.ShapeDtypeStruct(tuple(dims), dtype)


def mm(a, b):
    return jnp.dot(a, b, preferred_element_type=F32)


def mm_bt(a, b):
    return lax.dot_general(a, b, (((1,), (1,)), ((), ())), preferred_element_type=F32)


def mm_at(a, b):
    return lax.dot_general(a, b, (((0,), (0,)), ((), ())), preferred_element_type=F32)


class Part:
    def __init__(self, zs, js, last, arrays):
        self.zs, self.js, self.last, self.arrays = tuple(zs), tuple(js), last, arrays

    def flat(self):
        return [a for row in self.arrays for a in row]


class Dims:
    def __init__(self, model, ffn, block, blocks, rows):
        self.model, self.ffn, self.block, self.blocks, self.rows = model, ffn, block, blocks, rows
        self.own = blocks // (2 * Z_SLABS)
        self.piece = block // 4
        wide, tall = model // block, ffn // block
        self.places = {}
        at = 0
        for name, rows_, cols_ in (
            ("q", wide, wide),
            ("k", wide, wide),
            ("v", wide, wide),
            ("o", wide, wide),
            ("up", wide, tall),
            ("down", tall, wide),
        ):
            self.places[name] = [
                (at + r * cols_ + c, r * block, c * block) for r in range(rows_) for c in range(cols_)
            ]
            at += rows_ * cols_

    def where(self, b):
        return b // (2 * self.own), (b // self.own) % 2, b % self.own


def find_part(parts, z, j):
    for number, part in enumerate(parts):
        if z in part.zs and j in part.js:
            return number, part.zs.index(z), part.js.index(j)
    raise ValueError("no part")


def needed_parts(dims, parts, names):
    used = set()
    for name in names:
        for b, _, _ in dims.places[name]:
            z, _, j = dims.where(b)
            used.add(find_part(parts, z, j)[0])
    return [parts[n] for n in sorted(used)]


def start_loads(dims, parts, refs, pos, name, dst, row0, col0, sem):
    x, y, c = pos
    piece = dims.piece

    def rows_at(base, quarter):
        return pl.ds(pl.multiple_of(base + piece * quarter, 16), piece)

    later = []
    for b, r, col in dims.places[name]:
        z, xq, j = dims.where(b)
        number, zi, ji = find_part(parts, z, j)
        cols = pl.ds(col0 + col, dims.block)
        if parts[number].last == "y":
            for dc in range(2):
                for dy in range(2):
                    src = refs[number][dc][dy].at[x ^ xq, zi, ji]
                    rows = rows_at(row0 + r, 2 * (y ^ dy) + (c ^ dc))
                    pltpu.make_async_copy(src, dst.at[rows, cols], sem).start()
        else:
            later.append((number, zi, ji, xq, r, cols))
    if later:
        for own_x in range(2):

            @pl.when(x == own_x)
            def _(own_x=own_x):
                for number, zi, ji, xq, r, cols in later:
                    for dc in range(2):
                        for yq in range(2):
                            src = refs[number][dc][own_x ^ xq].at[y ^ yq, zi, ji]
                            rows = rows_at(row0 + r, 2 * yq + (c ^ dc))
                            pltpu.make_async_copy(src, dst.at[rows, cols], sem).start()


def wait_for(ref, sem):
    pltpu.make_async_copy(ref, ref, sem).wait()


def start_stores(dims, parts, outs, pos, places, src, sem):
    x, y, c = pos
    piece = dims.piece
    for b, r, col in places:
        z, xq, j = dims.where(b)
        number, zi, ji = find_part(parts, z, j)
        for dc in range(2):
            for yq in range(2):
                rows = pl.ds(pl.multiple_of(r + piece * (2 * yq + (c ^ dc)), 16), piece)
                first, second = y ^ yq, x ^ xq
                if parts[number].last == "x":
                    first, second = second, first
                dst = outs[number][dc].at[first, second, zi, ji]
                pltpu.make_async_copy(src.at[rows, pl.ds(col, dims.block)], dst, sem).start()


def norm_forward(values):
    center = values - jnp.mean(values, axis=-1, keepdims=True)
    spread = jnp.mean(center * center, axis=-1, keepdims=True)
    inverse = lax.rsqrt(spread + norm_epsilon)
    return center * inverse, inverse


def norm_backward(gradient, unit, inverse, gain):
    scaled = gradient * gain
    inner = (
        scaled
        - jnp.mean(scaled, axis=-1, keepdims=True)
        - unit * jnp.mean(scaled * unit, axis=-1, keepdims=True)
    )
    return inverse * inner


def col_sum(values):
    return jnp.sum(values.astype(F32), axis=0, keepdims=True)


def segment(small_ref, number, width):
    return small_ref[0:1, number * width : (number + 1) * width]


def unflatten(refs, parts):
    out, at = [], 0
    for part in parts:
        rows = []
        for row in part.arrays:
            rows.append(refs[at : at + len(row)])
            at += len(row)
        out.append(rows)
    return out, refs[at:]


def half_masks(head):
    lane = lax.broadcasted_iota(jnp.int32, (1, 2 * head), 1)
    low = lane < head
    ones = jnp.where(low, 1.0, 0.0).astype(F32)
    return low, (ones.astype(BF), (1.0 - ones).astype(BF))


def attention_forward_kernel(dims, parts, chains, pos_ref, len_ref, x_ref, small_ref, *rest):
    refs, rest = unflatten(rest, parts)
    qkv_ref, lse_ref, ctx_ref, unit_ref, inv_ref, w, sems = rest
    width, seq = dims.model, dims.rows // chains
    head = width // HEADS
    pos = (pos_ref[1], pos_ref[2], pos_ref[3])
    for n, name in enumerate(("q", "k", "v", "o")):
        start_loads(dims, parts, refs, pos, name, w, 0, n * width, sems.at[n])
    xb = x_ref[...].astype(BF)
    for n, bias in ((0, 0), (1, None), (2, 1)):
        cols = slice(n * width, (n + 1) * width)
        wait_for(w.at[:, cols], sems.at[n])
        out = mm(xb, w[:, cols])
        if bias is not None:
            out = out + segment(small_ref, bias, width)
        qkv_ref[:, cols] = out.astype(BF)
    low, masks = half_masks(head)
    scale = head**-0.5

    def chain(i, carry):
        rows = pl.ds(pl.multiple_of(i * seq, 16), seq)
        valid = lax.broadcasted_iota(jnp.int32, (seq, seq), 0) < len_ref[i]
        for pair in range(HEADS // 2):
            at = pair * 2 * head
            q = qkv_ref[rows, at : at + 2 * head]
            k = qkv_ref[rows, width + at : width + at + 2 * head]
            v = qkv_ref[rows, 2 * width + at : 2 * width + at + 2 * head]
            outs = []
            for h in range(2):
                s = jnp.where(valid, mm_bt(k, q * masks[h]) * scale, -1000000000.0)
                top = jnp.max(s, axis=0, keepdims=True)
                e = jnp.exp(s - top)
                total = jnp.sum(e, axis=0, keepdims=True)
                lse_ref[i, 2 * pair + h : 2 * pair + h + 1, :] = top + jnp.log(total)
                outs.append(mm_at((e * (1.0 / total)).astype(BF), v))
            ctx_ref[rows, at : at + 2 * head] = jnp.where(low, outs[0], outs[1]).astype(BF)
        return carry

    lax.fori_loop(0, chains, chain, 0)
    wait_for(w.at[:, 3 * width :], sems.at[3])
    attended = mm(ctx_ref[...], w[:, 3 * width :]) + segment(small_ref, 2, width)
    unit, inverse = norm_forward(x_ref[...].astype(F32) + attended)
    unit_ref[...] = unit
    inv_ref[...] = inverse


def attention_forward(dims, parts, pos, lengths, x, small):
    parts = needed_parts(dims, parts, ("q", "k", "v", "o"))
    chains = lengths.shape[0]
    seq, width = dims.rows // chains, dims.model
    flat = [a for p in parts for a in p.flat()]
    return pl.pallas_call(
        functools.partial(attention_forward_kernel, dims, parts, chains),
        in_specs=[SMEM, SMEM, VMEM, VMEM] + [HBM] * len(flat),
        out_specs=[VMEM] * 5,
        out_shape=[
            shape((dims.rows, 3 * width), BF),
            shape((chains, HEADS, seq), F32),
            shape((dims.rows, width), BF),
            shape((dims.rows, width), F32),
            shape((dims.rows, 1), F32),
        ],
        scratch_shapes=[pltpu.VMEM((width, 4 * width), BF), pltpu.SemaphoreType.DMA((4,))],
        compiler_params=pltpu.CompilerParams(vmem_limit_bytes=VMEM_LIMIT),
        cost_estimate=pl.CostEstimate(
            flops=12 * dims.rows * width * width, bytes_accessed=16 << 20, transcendentals=1 << 20
        ),
        name="attention_forward",
    )(pos, lengths, x, small, *flat)


def ffn_forward_body(dims, small_ref, unit_ref, up, down, sems, act_ref, slope_ref):
    width = dims.model
    h1 = unit_ref[...] * segment(small_ref, 4, width) + segment(small_ref, 5, width)
    hb = h1.astype(BF)
    total = h1 + segment(small_ref, 3, width)
    wait_for(up, sems.at[0])
    for n in range(dims.ffn // width):
        cols = slice(n * width, (n + 1) * width)
        u = mm(hb, up[:, cols]) + segment(small_ref, 8 + n, width)
        cdf = 0.5 * (1.0 + lax.erf(u * 0.7071067811865476))
        act = (u * cdf).astype(BF)
        act_ref[:, cols] = act
        slope_ref[:, cols] = (cdf + u * (0.3989422804014327 * jnp.exp(-0.5 * u * u))).astype(BF)
        if n == 0:
            wait_for(down, sems.at[1])
        total = total + mm(act, down[cols, :])
    return total


def ffn_forward_kernel(dims, parts, pos_ref, unit_ref, small_ref, *rest):
    refs, rest = unflatten(rest, parts)
    act_ref, slope_ref, unit2_ref, inv2_ref, y_ref, up, down, sems = rest
    pos = (pos_ref[1], pos_ref[2], pos_ref[3])
    start_loads(dims, parts, refs, pos, "up", up, 0, 0, sems.at[0])
    start_loads(dims, parts, refs, pos, "down", down, 0, 0, sems.at[1])
    width = dims.model
    total = ffn_forward_body(dims, small_ref, unit_ref, up, down, sems, act_ref, slope_ref)
    unit, inverse = norm_forward(total)
    unit2_ref[...] = unit
    inv2_ref[...] = inverse
    y_ref[...] = unit * segment(small_ref, 6, width) + segment(small_ref, 7, width)


def ffn_forward(dims, parts, pos, unit, small):
    parts = needed_parts(dims, parts, ("up", "down"))
    flat = [a for p in parts for a in p.flat()]
    rows, width, ffn = dims.rows, dims.model, dims.ffn
    return pl.pallas_call(
        functools.partial(ffn_forward_kernel, dims, parts),
        in_specs=[SMEM, VMEM, VMEM] + [HBM] * len(flat),
        out_specs=[VMEM] * 5,
        out_shape=[
            shape((rows, ffn), BF),
            shape((rows, ffn), BF),
            shape((rows, width), F32),
            shape((rows, 1), F32),
            shape((rows, width), F32),
        ],
        scratch_shapes=[
            pltpu.VMEM((width, ffn), BF),
            pltpu.VMEM((ffn, width), BF),
            pltpu.SemaphoreType.DMA((2,)),
        ],
        compiler_params=pltpu.CompilerParams(vmem_limit_bytes=VMEM_LIMIT),
        cost_estimate=pl.CostEstimate(
            flops=4 * rows * width * ffn, bytes_accessed=24 << 20, transcendentals=3 << 20
        ),
        name="ffn_forward",
    )(pos, unit, small, *flat)


def ffn_backward_body(
    dims, outs_parts, outs, pos, gy, small_ref, unit_ref, inv_ref, ctx_ref, unit2, inv2, act_ref, slope_ref,
    up, down, wo, grad_up, grad_down, grad_o, sem_out, gz1_ref, gctx_ref, sums_ref, wait_o,
):
    width = dims.model
    gain1, gain2 = segment(small_ref, 4, width), segment(small_ref, 6, width)

    def put(number, values):
        sums_ref[0:1, number * width : (number + 1) * width] = values

    put(6, col_sum(gy * unit2))
    put(7, col_sum(gy))
    gz2 = norm_backward(gy, unit2, inv2, gain2)
    gf = gz2.astype(BF)
    put(3, col_sum(gf))
    hb = (unit_ref[...] * gain1 + segment(small_ref, 5, width)).astype(BF)
    gh1 = gz2
    block = dims.block
    for n in range(dims.ffn // width):
        cols = slice(n * width, (n + 1) * width)
        gu = (slope_ref[:, cols].astype(F32) * mm_bt(gf, down[cols, :])).astype(BF)
        put(8 + n, col_sum(gu))
        grad_up[:, cols] = mm_at(hb, gu).astype(BF)
        grad_down[cols, :] = mm_at(act_ref[:, cols], gf).astype(BF)
        low, high = n * width, (n + 1) * width
        start_stores(
            dims, outs_parts, outs, pos,
            [p for p in dims.places["up"] if low <= p[2] < high], grad_up, sem_out.at[0],
        )
        start_stores(
            dims, outs_parts, outs, pos,
            [p for p in dims.places["down"] if low <= p[1] < high], grad_down, sem_out.at[1],
        )
        gh1 = gh1 + mm_bt(gu, up[:, cols])
    unit = unit_ref[...]
    put(4, col_sum(gh1 * unit))
    put(5, col_sum(gh1))
    gz1 = norm_backward(gh1, unit, inv_ref[...], gain1)
    gz1_ref[...] = gz1
    ga = gz1.astype(BF)
    put(2, col_sum(ga))
    grad_o[...] = mm_at(ctx_ref[...], ga).astype(BF)
    start_stores(dims, outs_parts, outs, pos, dims.places["o"], grad_o, sem_out.at[2])
    wait_o()
    gctx_ref[...] = mm_bt(ga, wo[...]).astype(BF)
    put(0, jnp.zeros((1, width), F32))
    put(1, jnp.zeros((1, width), F32))
    wait_for(grad_up, sem_out.at[0])
    wait_for(grad_down, sem_out.at[1])
    wait_for(grad_o, sem_out.at[2])


def grad_shapes(dims, parts):
    return [
        shape((2, 2, len(p.zs), len(p.js), dims.piece, dims.block), BF) for p in parts for _ in range(2)
    ]


def pair_up(arrays, parts):
    return [Part(p.zs, p.js, p.last, list(arrays[2 * n : 2 * n + 2])) for n, p in enumerate(parts)]


def ffn_backward_kernel(dims, parts, outs_parts, pos_ref, gy_ref, small_ref, unit_ref, inv_ref, ctx_ref, unit2_ref, inv2_ref, act_ref, slope_ref, *rest):
    refs, rest = unflatten(rest, parts)
    gz1_ref, gctx_ref, sums_ref, *rest = rest
    count = 2 * len(outs_parts)
    outs = [rest[2 * n : 2 * n + 2] for n in range(len(outs_parts))]
    up, down, wo, grad_up, grad_down, grad_o, sems, sem_out = rest[count:]
    pos = (pos_ref[1], pos_ref[2], pos_ref[3])
    start_loads(dims, parts, refs, pos, "down", down, 0, 0, sems.at[1])
    start_loads(dims, parts, refs, pos, "up", up, 0, 0, sems.at[0])
    start_loads(dims, parts, refs, pos, "o", wo, 0, 0, sems.at[2])
    wait_for(down, sems.at[1])
    wait_for(up, sems.at[0])
    ffn_backward_body(
        dims, outs_parts, outs, pos, gy_ref[...], small_ref, unit_ref, inv_ref, ctx_ref,
        unit2_ref[...], inv2_ref[...], act_ref, slope_ref, up, down, wo, grad_up, grad_down, grad_o,
        sem_out, gz1_ref, gctx_ref, sums_ref, lambda: wait_for(wo, sems.at[2]),
    )


def ffn_backward(dims, parts, outs_parts, pos, gy, small, unit, inv, ctx, unit2, inv2, act, slope):
    parts = needed_parts(dims, parts, ("up", "down", "o"))
    flat = [a for p in parts for a in p.flat()]
    rows, width, ffn = dims.rows, dims.model, dims.ffn
    grads = grad_shapes(dims, outs_parts)
    out = pl.pallas_call(
        functools.partial(ffn_backward_kernel, dims, parts, outs_parts),
        in_specs=[SMEM] + [VMEM] * 9 + [HBM] * len(flat),
        out_specs=[VMEM] * 3 + [HBM] * len(grads),
        out_shape=[
            shape((rows, width), F32),
            shape((rows, width), BF),
            shape((1, small.shape[1]), F32),
        ]
        + grads,
        scratch_shapes=[
            pltpu.VMEM((width, ffn), BF),
            pltpu.VMEM((ffn, width), BF),
            pltpu.VMEM((width, width), BF),
            pltpu.VMEM((width, ffn), BF),
            pltpu.VMEM((ffn, width), BF),
            pltpu.VMEM((width, width), BF),
            pltpu.SemaphoreType.DMA((3,)),
            pltpu.SemaphoreType.DMA((3,)),
        ],
        compiler_params=pltpu.CompilerParams(vmem_limit_bytes=VMEM_LIMIT),
        cost_estimate=pl.CostEstimate(
            flops=8 * rows * width * ffn + 4 * rows * width * width, bytes_accessed=40 << 20, transcendentals=0
        ),
        name="ffn_backward",
    )(pos, gy, small, unit, inv, ctx, unit2, inv2, act, slope, *flat)
    return out[0], out[1], out[2], pair_up(out[3:], outs_parts)


def ffn_both_kernel(dims, parts, outs_parts, chains, pos_ref, len_ref, cot_ref, small_ref, unit_ref, inv_ref, ctx_ref, *rest):
    refs, rest = unflatten(rest, parts)
    y_ref, gz1_ref, gctx_ref, sums_ref, *rest = rest
    count = 2 * len(outs_parts)
    outs = [rest[2 * n : 2 * n + 2] for n in range(len(outs_parts))]
    up, down, wo, act_ref, slope_ref, grad_up, grad_down, grad_o, sems, sem_out = rest[count:]
    pos = (pos_ref[1], pos_ref[2], pos_ref[3])
    start_loads(dims, parts, refs, pos, "up", up, 0, 0, sems.at[0])
    start_loads(dims, parts, refs, pos, "down", down, 0, 0, sems.at[1])
    start_loads(dims, parts, refs, pos, "o", wo, 0, 0, sems.at[2])
    width, seq = dims.model, dims.rows // chains
    total = ffn_forward_body(dims, small_ref, unit_ref, up, down, sems, act_ref, slope_ref)
    unit2, inv2 = norm_forward(total)
    y_ref[...] = (unit2 * segment(small_ref, 6, width) + segment(small_ref, 7, width)).astype(BF)
    place = lax.broadcasted_iota(jnp.int32, (seq, width), 0)
    gy = jnp.concatenate(
        [
            jnp.where(place < len_ref[i], cot_ref[i * seq : (i + 1) * seq, :].astype(F32), 0.0)
            for i in range(chains)
        ],
        axis=0,
    )
    ffn_backward_body(
        dims, outs_parts, outs, pos, gy, small_ref, unit_ref, inv_ref, ctx_ref,
        unit2, inv2, act_ref, slope_ref, up, down, wo, grad_up, grad_down, grad_o,
        sem_out, gz1_ref, gctx_ref, sums_ref, lambda: wait_for(wo, sems.at[2]),
    )


def ffn_both(dims, parts, outs_parts, pos, lengths, cot, small, unit, inv, ctx):
    parts = needed_parts(dims, parts, ("up", "down", "o"))
    flat = [a for p in parts for a in p.flat()]
    rows, width, ffn = dims.rows, dims.model, dims.ffn
    grads = grad_shapes(dims, outs_parts)
    out = pl.pallas_call(
        functools.partial(ffn_both_kernel, dims, parts, outs_parts, lengths.shape[0]),
        in_specs=[SMEM, SMEM] + [VMEM] * 5 + [HBM] * len(flat),
        out_specs=[VMEM] * 4 + [HBM] * len(grads),
        out_shape=[
            shape((rows, width), BF),
            shape((rows, width), F32),
            shape((rows, width), BF),
            shape((1, small.shape[1]), F32),
        ]
        + grads,
        scratch_shapes=[
            pltpu.VMEM((width, ffn), BF),
            pltpu.VMEM((ffn, width), BF),
            pltpu.VMEM((width, width), BF),
            pltpu.VMEM((rows, ffn), BF),
            pltpu.VMEM((rows, ffn), BF),
            pltpu.VMEM((width, ffn), BF),
            pltpu.VMEM((ffn, width), BF),
            pltpu.VMEM((width, width), BF),
            pltpu.SemaphoreType.DMA((3,)),
            pltpu.SemaphoreType.DMA((3,)),
        ],
        compiler_params=pltpu.CompilerParams(vmem_limit_bytes=VMEM_LIMIT),
        cost_estimate=pl.CostEstimate(
            flops=12 * rows * width * ffn + 4 * rows * width * width,
            bytes_accessed=40 << 20,
            transcendentals=3 << 20,
        ),
        name="ffn_both",
    )(pos, lengths, cot, small, unit, inv, ctx, *flat)
    return out[0], out[1], out[2], out[3], pair_up(out[4:], outs_parts)


def attention_backward_kernel(dims, parts, outs_parts, chains, pos_ref, len_ref, gz1_ref, gctx_ref, qkv_ref, lse_ref, x_ref, *rest):
    refs, rest = unflatten(rest, parts)
    gx_ref, sums_ref, *rest = rest
    count = 2 * len(outs_parts)
    outs = [rest[2 * n : 2 * n + 2] for n in range(len(outs_parts))]
    w, grads_ref, grad_w, sems, sem_out = rest[count:]
    pos = (pos_ref[1], pos_ref[2], pos_ref[3])
    width, seq = dims.model, dims.rows // chains
    head = width // HEADS
    names = ("q", "k", "v")
    for n, name in enumerate(names):
        start_loads(dims, parts, refs, pos, name, w, 0, n * width, sems.at[n])
    low, masks = half_masks(head)
    scale = head**-0.5

    def chain(i, carry):
        rows = pl.ds(pl.multiple_of(i * seq, 16), seq)
        valid = lax.broadcasted_iota(jnp.int32, (seq, seq), 0) < len_ref[i]
        for pair in range(HEADS // 2):
            at = pair * 2 * head
            q = qkv_ref[rows, at : at + 2 * head]
            k = qkv_ref[rows, width + at : width + at + 2 * head]
            v = qkv_ref[rows, 2 * width + at : 2 * width + at + 2 * head]
            g = gctx_ref[rows, at : at + 2 * head]
            gq, gk, gv = [], [], []
            for h in range(2):
                s = jnp.where(valid, mm_bt(k, q * masks[h]) * scale, -1000000000.0)
                p = jnp.exp(s - lse_ref[i, 2 * pair + h : 2 * pair + h + 1, :])
                gp = mm_bt(v, g * masks[h])
                inner = jnp.sum(p * gp, axis=0, keepdims=True)
                gs = (p * (gp - inner)).astype(BF)
                gv.append(mm(p.astype(BF), g))
                gk.append(mm(gs, q))
                gq.append(mm_at(gs, k))
            grads_ref[rows, at : at + 2 * head] = (jnp.where(low, gq[0], gq[1]) * scale).astype(BF)
            grads_ref[rows, width + at : width + at + 2 * head] = (
                jnp.where(low, gk[0], gk[1]) * scale
            ).astype(BF)
            grads_ref[rows, 2 * width + at : 2 * width + at + 2 * head] = jnp.where(
                low, gv[0], gv[1]
            ).astype(BF)
        return carry

    lax.fori_loop(0, chains, chain, 0)
    xb = x_ref[...].astype(BF)
    for n, name in enumerate(names):
        cols = slice(n * width, (n + 1) * width)
        grad_w[:, cols] = mm_at(xb, grads_ref[:, cols]).astype(BF)
        places = [(b, r, c + n * width) for b, r, c in dims.places[name]]
        start_stores(dims, outs_parts, outs, pos, places, grad_w, sem_out)
    sums_ref[0:1, :width] = col_sum(grads_ref[:, :width])
    sums_ref[0:1, width:] = col_sum(grads_ref[:, 2 * width :])
    gx = gz1_ref[...]
    for n in range(3):
        cols = slice(n * width, (n + 1) * width)
        wait_for(w.at[:, cols], sems.at[n])
        gx = gx + mm_bt(grads_ref[:, cols], w[:, cols])
    gx_ref[...] = gx
    wait_for(grad_w, sem_out)


def attention_backward(dims, parts, outs_parts, pos, lengths, gz1, gctx, qkv, lse, x):
    parts = needed_parts(dims, parts, ("q", "k", "v"))
    flat = [a for p in parts for a in p.flat()]
    rows, width = dims.rows, dims.model
    grads = grad_shapes(dims, outs_parts)
    out = pl.pallas_call(
        functools.partial(attention_backward_kernel, dims, parts, outs_parts, lengths.shape[0]),
        in_specs=[SMEM, SMEM] + [VMEM] * 5 + [HBM] * len(flat),
        out_specs=[VMEM] * 2 + [HBM] * len(grads),
        out_shape=[shape((rows, width), F32), shape((1, 2 * width), F32)] + grads,
        scratch_shapes=[
            pltpu.VMEM((width, 3 * width), BF),
            pltpu.VMEM((rows, 3 * width), BF),
            pltpu.VMEM((width, 3 * width), BF),
            pltpu.SemaphoreType.DMA((3,)),
            pltpu.SemaphoreType.DMA,
        ],
        compiler_params=pltpu.CompilerParams(vmem_limit_bytes=VMEM_LIMIT),
        cost_estimate=pl.CostEstimate(
            flops=24 * rows * width * width, bytes_accessed=24 << 20, transcendentals=1 << 20
        ),
        name="attention_backward",
    )(pos, lengths, gz1, gctx, qkv, lse, x, *flat)
    return out[0], out[1], pair_up(out[2:], outs_parts)


class AnySlice:
    def __init__(self, dims):
        self.dims = dims
        own = range(dims.own)
        self.early = [Part((1, 2, 3), own, "y", None)]
        self.late = [Part((0,), own, "y", None)]

    def position(self):
        return jnp.zeros((4,), jnp.int32)

    def gather(self, low, layer):
        dims = self.dims
        whole = lax.all_gather(low, "fsdp", axis=1, tiled=True)
        whole = lax.all_gather(whole, "grp", axis=0, tiled=True)
        split = whole.reshape(Z_SLABS, 2, dims.own, 2, 2, dims.piece, dims.block)
        arrays = [[split[:, :, :, dy, dc].transpose(1, 0, 2, 3, 4) for dy in range(2)] for dc in range(2)]
        return [Part(range(Z_SLABS), range(dims.own), "y", arrays)]

    def reduce(self, early, late, layer):
        dims = self.dims
        pieces = []
        for part in (late[0], early[0]):
            stacked = jnp.stack(part.arrays)
            pieces.append(stacked.transpose(3, 2, 4, 1, 0, 5, 6))
        whole = jnp.concatenate(pieces, axis=0).reshape(dims.blocks, dims.block, dims.block)
        rows = lax.psum_scatter(whole, "fsdp", scatter_dimension=1, tiled=True)
        return lax.psum_scatter(rows, "grp", scatter_dimension=0, tiled=True).astype(F32)

    def small_sum(self, values):
        return lax.psum(values, ("grp", "fsdp"))

    def group(self, owned):
        return lax.all_gather(owned, "fsdp", axis=1, tiled=True)


def local(
    inputs,
    lengths,
    cotangent,
    masters,
    small_params,
    small_moments,
    left_stats,
    right_stats,
    left_roots,
    right_roots,
):
    chains, seq, width = inputs.shape
    rows = chains * seq
    groups, shards = lax.axis_size("grp"), lax.axis_size("fsdp")
    block = masters.shape[3]
    own_rows = masters.shape[2]
    ffn = small_params.shape[1] - 8 * width
    dims = Dims(width, ffn, block, groups * masters.shape[1], rows)
    net = AnySlice(dims)
    pos = net.position()
    low = [masters[n].astype(BF) for n in range(LAYERS)]
    weights = [net.gather(low[n], n) for n in range(LAYERS)]
    small = [small_params[n : n + 1] for n in range(LAYERS)]
    last = LAYERS - 1

    x = inputs.reshape(rows, width)
    saved = []
    for n in range(LAYERS):
        qkv, lse, ctx, unit, inv = attention_forward(dims, weights[n], pos, lengths, x, small[n])
        if n < last:
            act, slope, unit2, inv2, y = ffn_forward(dims, weights[n], pos, unit, small[n])
            saved.append((x, qkv, lse, ctx, unit, inv, act, slope, unit2, inv2))
            x = y
        else:
            saved.append((x, qkv, lse, ctx, unit, inv))

    owned = [None] * LAYERS
    sums = [None] * LAYERS
    gy = None
    for n in reversed(range(LAYERS)):
        if n == last:
            x, qkv, lse, ctx, unit, inv = saved[n]
            cot = cotangent.reshape(rows, width)
            y, gz1, gctx, sums_a, early = ffn_both(
                dims, weights[n], net.early, pos, lengths, cot, small[n], unit, inv, ctx
            )
            activations = y.reshape(chains, seq, width)
        else:
            x, qkv, lse, ctx, unit, inv, act, slope, unit2, inv2 = saved[n]
            gz1, gctx, sums_a, early = ffn_backward(
                dims, weights[n], net.early, pos, gy, small[n], unit, inv, ctx, unit2, inv2, act, slope
            )
        gy, sums_b, late = attention_backward(
            dims, weights[n], net.late, pos, lengths, gz1, gctx, qkv, lse, x
        )
        owned[n] = net.reduce(early, late, n)
        sums[n] = jnp.concatenate([sums_b[0], sums_a[0, 2 * width :]])
    input_grad = gy.reshape(chains, seq, width)

    small_grads = net.small_sum(jnp.stack(sums))
    blocked_weight_gradients = jnp.stack(owned)
    new_left, new_right, new_masters = [], [], []
    first_row = lax.axis_index("fsdp") * own_rows
    highest = lax.Precision.HIGHEST
    for n in range(LAYERS):
        whole = net.group(owned[n].astype(BF)).astype(F32)
        roots = net.group(right_roots[n].astype(BF)).astype(F32)
        columns = lax.dynamic_slice_in_dim(whole, first_row, own_rows, 2)
        new_left.append(
            decay_rate * left_stats[n]
            + (1.0 - decay_rate) * jnp.einsum("brk,bck->brc", owned[n], whole, precision=highest)
        )
        new_right.append(
            decay_rate * right_stats[n]
            + (1.0 - decay_rate) * jnp.einsum("bkr,bkc->brc", columns, whole, precision=highest)
        )
        mixed = jnp.einsum("brk,bkc->brc", whole, roots, precision=highest)
        update = jnp.einsum("brk,bkc->brc", left_roots[n], mixed, precision=highest)
        new_masters.append(masters[n] - matrix_rate * update)
    new_masters = jnp.stack(new_masters)
    new_moments = decay_rate * small_moments + (1.0 - decay_rate) * small_grads * small_grads
    new_small = small_params - small_rate * small_grads / (jnp.sqrt(new_moments) + moment_epsilon)
    return (
        activations,
        input_grad,
        blocked_weight_gradients,
        small_grads,
        new_moments,
        new_small,
        jnp.stack(new_left),
        jnp.stack(new_right),
        new_masters,
        new_masters.astype(BF),
    )


def solution(mesh):
    tokens, blocks = P(("grp", "fsdp"), None, None), P(None, "grp", "fsdp", None)
    return jax.shard_map(
        local,
        mesh=mesh,
        in_specs=(tokens, P(("grp", "fsdp")), tokens, blocks, P(), P(), blocks, blocks, blocks, blocks),
        out_specs=(tokens, tokens, blocks, P(), P(), P(), blocks, blocks, blocks, blocks),
        check_vma=False,
    )
```

time: 1440 us -> 1210 us (0.84)
  waiting for transfers between devices: 664 us -> 968 us
  local copies, waits for them, and re-layouts: 312 us -> 50.4 us
  other arithmetic: 195 us -> 24.8 us
  matrix products: 186 us -> 16.1 us
  Pallas kernels: 0 us -> 126 us
  blocking collectives: 55.1 us -> 0 us
    all_gather x4 -> x8, waiting for transfers between devices: 255 us -> 480 us  [the longest x2 353 us: gather(): whole = lax.all_gather(whole, 'grp', axis=0, tiled=True)]
    reduce_scatter x2 -> x4, waiting for transfers between devices: 171 us -> 362 us  [the longest x2 200 us: reduce(): rows = lax.psum_scatter(whole, 'fsdp', scatter_dimension=1, tiled=True)]
    dot_general x52 -> x8, matrix products: 186 us -> 16.1 us  [the longest x2 6.61 us: local(): mixed = jnp.einsum('brk,bkc->brc', whole, roots, precision=highest)]
    all_gather x2 -> x0, other arithmetic: 168 us -> none  [local(): lax.all_gather(copies[layer_position].reshape(1, -1), ('grp', 'fsdp'), ax...]
    reshape x40 -> x0, local copies, waits for them, and re-layouts: 139 us -> none  [the longest x12 53 us: split_into_blocks(): matrix.reshape(row_count, block_border, col_count, block_border)]
    pallas_call x0 -> x7, Pallas kernels: none -> 126 us  [the longest x2 40.3 us: attention_backward(): pl.pallas_call(functools.partial(attention_backward_kernel, dims, parts,...]
    psum x1, waiting for transfers between devices: 238 us -> 124 us  [small_sum(): return lax.psum(values, ('grp', 'fsdp'))]
    unnamed x333 -> x43, local copies, waits for them, and re-layouts: 95.6 us -> 4.01 us
  transfers between devices with their start and end apart: 7 -> 13, of which waited for: 6 -> 13; matrix products, arithmetic and copies ran while one was open for 13% -> 4% of each run, Pallas kernels for 0% -> 2%
where the time goes in v1:
time: 1210 us; the launch traced here: 1200 us
  waiting for transfers between devices  968 us (80%)
  Pallas kernels  126 us (10%)
  local copies, waits for them, and re-layouts  50.4 us (4%)
  other arithmetic  24.8 us (2%)
  matrix products  16.1 us (1%)
  between operations  14.5 us (1%)
    all_gather x2, waiting for transfers between devices, gather(): whole = lax.all_gather(whole, 'grp', axis=0, tiled=True)  353 us
    reduce_scatter x2, waiting for transfers between devices, reduce(): rows = lax.psum_scatter(whole, 'fsdp', scatter_dimension=1, tiled=True)  200 us
    reduce_scatter x2, waiting for transfers between devices, reduce(): lax.psum_scatter(rows, 'grp', scatter_dimension=0, tiled=True).astype(F32)  162 us
    psum x1, waiting for transfers between devices, small_sum(): return lax.psum(values, ('grp', 'fsdp'))  124 us
    all_gather x4, waiting for transfers between devices, group(): return lax.all_gather(owned, 'fsdp', axis=1, tiled=True)  81 us
    all_gather x2, waiting for transfers between devices, gather(): whole = lax.all_gather(low, 'fsdp', axis=1, tiled=True)  46 us
    pallas_call x2, Pallas kernels, attention_backward(): pl.pallas_call(functools.partial(attention_backward_kernel, dims, parts,...  40.3 us
    pallas_call x1, Pallas kernels, ffn_both(): pl.pallas_call(functools.partial(ffn_both_kernel, dims, parts, outs_parts...  25.6 us
  transfers between devices with their start and end apart: 13, of which 13 were waited for; matrix products, arithmetic and copies ran while one was open for 4% of the time, Pallas kernels for 2%

profile of v1, /device:TPU:0, one launch (start us, length us, event | category | flops | bytes accessed | tf_op | source)
XLA Modules:
  0.0 1200.3 jit_solution(6196548240402107751)
XLA Ops:
  10.5 23.1 %all-gather.11.cloned.1.call-done = bf16[6,384,384]{2,1,0:T(8,128)(2,1)} async-done(((bf16[6,96,384]{2,1,0:T(8,128)(2,1)}), bf16[6,384,384]{2,1,0:T(8,128)(2,1)}) %all-gather.11.cloned.1.call-update) | async-done | bytes 1769488 | tf_op jit(solution)/shard_map/all_gather | solution.py:603
  33.7 22.9 %all-gather.15.cloned.1.call-done = bf16[6,384,384]{2,1,0:T(8,128)(2,1)} async-done(((bf16[6,96,384]{2,1,0:T(8,128)(2,1)}), bf16[6,384,384]{2,1,0:T(8,128)(2,1)}) %all-gather.15.cloned.1.call-update) | async-done | bytes 1769488 | tf_op jit(solution)/shard_map/all_gather | solution.py:603
  57.3 197.1 %all-gather.13.cloned.1.call-done = bf16[48,384,384]{2,1,0:T(8,128)(2,1)} async-done(((bf16[6,384,384]{2,1,0:T(8,128)(2,1)}), bf16[48,384,384]{2,1,0:T(8,128)(2,1)}) %all-gather.13.cloned.1.call-update) | async-done | bytes 14155792 | tf_op jit(solution)/shard_map/all_gather | solution.py:604
  254.4 6.1 fusion.28
  260.5 4.2 copy_bitcast_fusion.4
  264.8 3.8 copy_bitcast_fusion.6
  269.1 11.9 attention_forward.2
  281.0 13.1 %ffn_forward.1 = (bf16[480,3072]{1,0:T(8,128)(2,1)}, bf16[480,3072]{1,0:T(8,128)(2,1)}, f32[480,768]{1,0:T(8,128)}, f32[480,1]{1,0:T(8,128)}, f32[480,768]{1,0:T(8,128)}) custom-call(s32[4]{0:T(128)} %broadcast_5_pos_ref.2.pos_ref, f32[480,768]{1,0:T(8,128)} %get-tuple-element.44.unit_ref, f32[1,9216]{1,0:T(1,128)} %get-tuple-element.94.small_ref, ...), custom_call_target="tpu_custom_call" | custom-call | flops 4529848320 | bytes 25165824 | tf_op jit(solution)/shard_map/ffn_forward/pallas_call | solution.py:297
  294.1 156.2 %all-gather.17.cloned.1.call-done = bf16[48,384,384]{2,1,0:T(8,128)(2,1)} async-done(((bf16[6,384,384]{2,1,0:T(8,128)(2,1)}), bf16[48,384,384]{2,1,0:T(8,128)(2,1)}) %all-gather.17.cloned.1.call-update) | async-done | bytes 14155792 | tf_op jit(solution)/shard_map/all_gather | solution.py:604
  450.3 6.1 fusion.27
  456.4 3.8 copy_bitcast_fusion
  460.2 3.7 copy_bitcast_fusion.2
  463.9 12.2 %attention_forward.3 = (bf16[480,2304]{1,0:T(8,128)(2,1)}, f32[3,12,160]{2,1,0:T(8,128)}, bf16[480,768]{1,0:T(8,128)(2,1)}, f32[480,768]{1,0:T(8,128)}, f32[480,1]{1,0:T(8,128)}) custom-call(s32[4]{0:T(128)} %broadcast_5_pos_ref.2.pos_ref, s32[3]{0:T(128)} %len_ref.9, f32[480,768]{1,0:T(8,128)} %get-tuple-element.45.x_ref, ...), custom_call_target="tpu_custom_call" | custom-call | flops 3397386240 | bytes 16777216 | tf_op jit(solution)/shard_map/attention_forward/pallas_call | solution.py:240
  476.1 25.6 %ffn_both.1 = (bf16[480,768]{1,0:T(8,128)(2,1)}, f32[480,768]{1,0:T(8,128)}, bf16[480,768]{1,0:T(8,128)(2,1)}, f32[1,9216]{1,0:T(1,128)}, bf16[2,2,3,6,96,384]{5...) custom-call(s32[4]{0:T(128)} %broadcast_5_pos_ref.2.pos_ref, s32[3]{0:T(128)} %len_ref.9, ...), custom_call_target="tpu_custom_call" | custom-call | flops 14722007040 | bytes 41943040 | tf_op jit(solution)/shard_map/ffn_both/pallas_call | solution.py:470
  501.7 20.3 %attention_backward.2 = (f32[480,768]{1,0:T(8,128)}, f32[1,1536]{1,0:T(1,128)}, bf16[2,2,1,6,96,384]{5,4,3,2,1,0:T(8,128)(2,1)}, bf16[2,2,1,6,96,384]{5,4,3,2,1,0:T(8,128)(2,1)}) custom-call(s32[4]{0:T(128)} %broadcast_5_pos_ref.2.pos_ref, s32[3]{0:T(128)} %len_ref.9, f32[480,768]{1,0:T(8,128)} %get-tuple-element.50.gz1_ref, ...), custom_call_target="tpu_custom_call" | custom-call | flops 6794772480 | bytes 25165824 | tf_op jit(solution)/shard_map/attention_backward/pallas_call | solution.py:570
  522.1 23.0 %ffn_backward.1 = (f32[480,768]{1,0:T(8,128)}, bf16[480,768]{1,0:T(8,128)(2,1)}, f32[1,9216]{1,0:T(1,128)}, bf16[2,2,3,6,96,384]{5,4,3,2,1,0:T(8,128)(2,1)}, bf16[2,2,3,6,96,384]{5,4,3,2,1,0:T(8,128)(2,1)}) custom-call(s32[4]{0:T(128)} %broadcast_5_pos_ref.2.pos_ref, f32[480,768]{1,0:T(8,128)} %get-tuple-element.54.gy_ref, ...), custom_call_target="tpu_custom_call" | custom-call | flops 10192158720 | bytes 41943040 | tf_op jit(solution)/shard_map/ffn_backward/pallas_call | solution.py:407
  545.1 20.0 %attention_backward.3 = (f32[480,768]{1,0:T(8,128)}, f32[1,1536]{1,0:T(1,128)}, bf16[2,2,1,6,96,384]{5,4,3,2,1,0:T(8,128)(2,1)}, bf16[2,2,1,6,96,384]{5,4,3,2,1,0:T(8,128)(2,1)}) custom-call(s32[4]{0:T(128)} %broadcast_5_pos_ref.2.pos_ref, s32[3]{0:T(128)} %len_ref.9, f32[480,768]{1,0:T(8,128)} %get-tuple-element.61.gz1_ref, ...), custom_call_target="tpu_custom_call" | custom-call | flops 6794772480 | bytes 25165824 | tf_op jit(solution)/shard_map/attention_backward/pallas_call | solution.py:570
  571.6 6.3 copy.47
  580.3 7.7 maximum_bitcast_fusion.1
  589.7 7.6 copy.49
  597.4 88.4 %reduce-scatter.5.cloned.1.call-done = bf16[48,96,384]{2,1,0:T(8,128)(2,1)} async-done(((bf16[48,384,384]{2,1,0:T(8,128)(2,1)}), bf16[48,96,384]{2,1,0:T(8,128)(2,1)}) %reduce-scatter.5.cloned.1.call-update) | async-done | bytes 3538960 | tf_op jit(solution)/shard_map/reduce_scatter | solution.py:616
  685.9 111.9 %reduce-scatter.9.cloned.1.call-done = bf16[48,96,384]{2,1,0:T(8,128)(2,1)} async-done(((bf16[48,384,384]{2,1,0:T(8,128)(2,1)}), bf16[48,96,384]{2,1,0:T(8,128)(2,1)}) %reduce-scatter.9.cloned.1.call-update) | async-done | bytes 3538960 | tf_op jit(solution)/shard_map/reduce_scatter | solution.py:616
  800.2 80.2 %reduce-scatter.7.cloned.1.call-done = bf16[6,96,384]{2,1,0:T(8,128)(2,1)} async-done(((bf16[48,96,384]{2,1,0:T(8,128)(2,1)}), bf16[6,96,384]{2,1,0:T(8,128)(2,1)}) %reduce-scatter.7.cloned.1.call-update) | async-done | bytes 442384 | tf_op jit(solution)/shard_map/reduce_scatter | solution.py:617
  881.0 81.7 %reduce-scatter.11.cloned.1.call-done = bf16[6,96,384]{2,1,0:T(8,128)(2,1)} async-done(((bf16[48,96,384]{2,1,0:T(8,128)(2,1)}), bf16[6,96,384]{2,1,0:T(8,128)(2,1)}) %reduce-scatter.11.cloned.1.call-update) | async-done | bytes 442384 | tf_op jit(solution)/shard_map/reduce_scatter | solution.py:617
  962.8 124.0 %all-reduce.2.cloned.1.call-done = f32[2,9216]{1,0:T(2,128)} async-done(((f32[2,9216]{1,0:T(2,128)}), f32[2,9216]{1,0:T(2,128)}) %all-reduce.2.cloned.1.call-update) | async-done | bytes 73744 | tf_op jit(solution)/shard_map/psum | solution.py:620
  1091.0 20.5 %all-gather.23.cloned.1.call-done = bf16[1,6,384,384]{3,2,1,0:T(8,128)(2,1)} async-done(((bf16[1,6,96,384]{3,2,1,0:T(8,128)(2,1)}), bf16[1,6,384,384]{3,2,1,0:T(8,128)(2,1)}) %all-gather.23.cloned.1.call-update) | async-done | bytes 1769488 | tf_op jit(solution)/shard_map/all_gather | solution.py:623
  1111.4 22.4 %all-gather.19.cloned.1.call-done = bf16[6,384,384]{2,1,0:T(8,128)(2,1)} async-done(((bf16[6,96,384]{2,1,0:T(8,128)(2,1)}), bf16[6,384,384]{2,1,0:T(8,128)(2,1)}) %all-gather.19.cloned.1.call-update) | async-done | bytes 1769488 | tf_op jit(solution)/shard_map/all_gather | solution.py:623
  1133.8 3.2 fusion.2
  1137.1 3.7 fusion.13
  1140.8 15.8 %all-gather.25.cloned.1.call-done = bf16[1,6,384,384]{3,2,1,0:T(8,128)(2,1)} async-done(((bf16[1,6,96,384]{3,2,1,0:T(8,128)(2,1)}), bf16[1,6,384,384]{3,2,1,0:T(8,128)(2,1)}) %all-gather.25.cloned.1.call-update) | async-done | bytes 1769488 | tf_op jit(solution)/shard_map/all_gather | solution.py:623
  1156.6 22.4 %all-gather.21.cloned.1.call-done = bf16[6,384,384]{2,1,0:T(8,128)(2,1)} async-done(((bf16[6,96,384]{2,1,0:T(8,128)(2,1)}), bf16[6,384,384]{2,1,0:T(8,128)(2,1)}) %all-gather.21.cloned.1.call-update) | async-done | bytes 1769488 | tf_op jit(solution)/shard_map/all_gather | solution.py:623
  1178.9 3.4 fusion
  (96 shorter events, 33.5 us)
Async XLA Ops:
  7.2 49.5 %copy-start.13 = (f32[2,9216]{1,0:T(2,128)S(1)}, f32[2,9216]{1,0:T(2,128)}, u32[]{:S(2)}) copy-start(f32[2,9216]{1,0:T(2,128)} %param.14) | copy-start | bytes 221188
  7.2 26.5 %all-gather.11.cloned.1.call-start = ((), (), s32[]{:S(2)}) async-start(), calls=%async_computation.4 | async-start | bytes 2211840 | tf_op jit(solution)/shard_map/all_gather | solution.py:603
  9.7 46.9 %all-gather.15.cloned.1.call-start = ((), (), s32[]{:S(2)}) async-start(), calls=%async_computation.6 | async-start | bytes 2211840 | tf_op jit(solution)/shard_map/all_gather | solution.py:603
  10.5 244.0 %all-gather.13.cloned.1.call-start = ((), (), s32[]{:S(2)}) async-start(), calls=%async_computation.5 | async-start | bytes 15925248 | tf_op jit(solution)/shard_map/all_gather | solution.py:604
  33.7 416.6 %all-gather.17.cloned.1.call-start = ((), (), s32[]{:S(2)}) async-start(), calls=%async_computation.7 | async-start | bytes 15925248 | tf_op jit(solution)/shard_map/all_gather | solution.py:604
  56.6 629.2 %reduce-scatter.5.cloned.1.call-start = ((), (), s32[]{:S(2)}) async-start(), calls=%async_computation.8 | async-start | bytes 17694720 | tf_op jit(solution)/shard_map/reduce_scatter | solution.py:616
  545.1 22.6 %copy-start.3 = (bf16[2,2,3,6,96,384]{5,4,3,2,1,0:T(8,128)(2,1)S(1)}, bf16[2,2,3,6,96,384]{5,4,3,2,1,0:T(8,128)(2,1)}, u32[]{:S(2)}) copy-start(bf16[2,2,3,6,96,384]{5,4,3,2,1,0:T(8,128)(2,1)} %get-tuple-element.69) | copy-start | bytes 15925252
  565.1 3.6 copy-start.2
  578.0 219.8 %reduce-scatter.9.cloned.1.call-start = ((), (), s32[]{:S(2)}) async-start(), calls=%async_computation.10 | async-start | bytes 17694720 | tf_op jit(solution)/shard_map/reduce_scatter | solution.py:616
  597.3 283.1 %reduce-scatter.7.cloned.1.call-start = ((), (), s32[]{:S(2)}) async-start(), calls=%async_computation.9 | async-start | bytes 3981312 | tf_op jit(solution)/shard_map/reduce_scatter | solution.py:617
  685.8 112.1 %copy-start.10 = (f32[2,6,96,384]{3,2,1,0:T(8,128)S(1)}, f32[2,6,96,384]{3,2,1,0:T(8,128)}, u32[]{:S(2)}) copy-start(f32[2,6,96,384]{3,2,1,0:T(8,128)} %param.19) | copy-start | bytes 5308420
  685.8 112.2 %copy-start.20 = (f32[1,1536]{1,0:T(1,128)S(1)}, f32[1,1536]{1,0:T(1,128)}, u32[]{:S(2)}) copy-start(f32[1,1536]{1,0:T(1,128)} %get-tuple-element.74) | copy-start | bytes 18436
  685.8 112.2 %copy-start.19 = (f32[1,1536]{1,0:T(1,128)S(1)}, f32[1,1536]{1,0:T(1,128)}, u32[]{:S(2)}) copy-start(f32[1,1536]{1,0:T(1,128)} %get-tuple-element.76) | copy-start | bytes 18436
  685.8 112.2 %copy-start.18 = (f32[1,9216]{1,0:T(1,128)S(1)}, f32[1,9216]{1,0:T(1,128)}, u32[]{:S(2)}) copy-start(f32[1,9216]{1,0:T(1,128)} %get-tuple-element.75) | copy-start | bytes 110596
  685.9 112.3 %copy-start.17 = (f32[1,9216]{1,0:T(1,128)S(1)}, f32[1,9216]{1,0:T(1,128)}, u32[]{:S(2)}) copy-start(f32[1,9216]{1,0:T(1,128)} %get-tuple-element.77) | copy-start | bytes 110596
  685.9 276.9 %reduce-scatter.11.cloned.1.call-start = ((), (), s32[]{:S(2)}) async-start(), calls=%async_computation.11 | async-start | bytes 3981312 | tf_op jit(solution)/shard_map/reduce_scatter | solution.py:617
  797.8 289.0 %copy-start.14 = (f32[2,9216]{1,0:T(2,128)S(1)}, f32[2,9216]{1,0:T(2,128)}, u32[]{:S(2)}) copy-start(f32[2,9216]{1,0:T(2,128)} %param.14) | copy-start | bytes 221188
  797.8 289.0 %copy-start.16 = (f32[2,9216]{1,0:T(2,128)S(1)}, f32[2,9216]{1,0:T(2,128)}, u32[]{:S(2)}) copy-start(f32[2,9216]{1,0:T(2,128)} %param.15) | copy-start | bytes 221188
  797.8 289.0 %all-reduce.2.cloned.1.call-start = ((), (), s32[]{:S(2)}) async-start(), calls=%async_computation.12 | async-start | bytes 147456 | tf_op jit(solution)/shard_map/psum | solution.py:620
  799.0 312.4 %all-gather.23.cloned.1.call-start = ((), (), s32[]{:S(2)}) async-start(), calls=%async_computation.15 | async-start | bytes 2211840 | tf_op jit(solution)/shard_map/all_gather | solution.py:623
  800.1 333.7 %all-gather.19.cloned.1.call-start = ((), (), s32[]{:S(2)}) async-start(), calls=%async_computation.13 | async-start | bytes 2211840 | tf_op jit(solution)/shard_map/all_gather | solution.py:623
  880.4 276.2 %all-gather.25.cloned.1.call-start = ((), (), s32[]{:S(2)}) async-start(), calls=%async_computation.16 | async-start | bytes 2211840 | tf_op jit(solution)/shard_map/all_gather | solution.py:623
  881.0 298.0 %all-gather.21.cloned.1.call-start = ((), (), s32[]{:S(2)}) async-start(), calls=%async_computation.14 | async-start | bytes 2211840 | tf_op jit(solution)/shard_map/all_gather | solution.py:623
  1091.0 46.1 %copy-start.4 = (f32[2,6,96,384]{3,2,1,0:T(8,128)S(1)}, f32[2,6,96,384]{3,2,1,0:T(8,128)}, u32[]{:S(2)}) copy-start(f32[2,6,96,384]{3,2,1,0:T(8,128)} %param.13) | copy-start | bytes 5308420
  1178.9 3.4 copy-start.9
  1182.3 4.5 copy-start.11
  1185.0 2.0 copy-start
  1185.0 3.0 copy-start.1
  1188.0 2.2 copy-start.5
  1188.0 2.2 copy-start.12
  1188.8 2.1 copy-start.6
  1190.9 2.1 copy-start.15
  (2 other events, 3.5 us)
Sparse Core Ops, SparseCore 0:
  10.2 23.4 all-gather.10
  35.8 20.7 all-gather.14
  58.8 195.5 all-gather.12
  256.5 193.7 all-gather.16
  578.1 107.6 reduce-scatter.4
  688.2 109.4 reduce-scatter.8
  801.4 78.9 reduce-scatter.6
  884.0 78.6 reduce-scatter.10
  968.9 117.8 all-reduce.1
  1088.8 22.6 all-gather.22
  1113.0 20.7 all-gather.18
  1135.8 20.7 all-gather.24
  1158.2 20.7 all-gather.20

commit v2 on v1

--- a/solution.py
+++ b/solution.py
@@ -623,6 +623,207 @@
         return lax.all_gather(owned, "fsdp", axis=1, tiled=True)
 
 
+def swap_of(axis):
+    def move(z, x, y, c):
+        return (z, x ^ (axis == "x"), y ^ (axis == "y"), c ^ (axis == "c"))
+
+    return move
+
+
+class SmallSlice:
+    def __init__(self, dims):
+        self.dims = dims
+        a, b = range(dims.own // 2), range(dims.own // 2, dims.own)
+        self.early = [Part((1, 2, 3), a, "y", None), Part((1, 2, 3), b, "x", None)]
+        self.late = [Part((0,), a, "y", None), Part((0,), b, "x", None)]
+        group, shard = lax.axis_index("grp"), lax.axis_index("fsdp")
+        self.z, self.x, self.y, self.c = group // 2, group % 2, shard // 2, shard % 2
+
+    def position(self):
+        return jnp.stack([self.z, self.x, self.y, self.c]).astype(jnp.int32)
+
+    def permute(self, array, move):
+        pairs = []
+        for flat in range(8 * Z_SLABS):
+            to = move(flat // 8, flat // 4 % 2, flat // 2 % 2, flat % 2)
+            if to is not None:
+                pairs.append((flat, ((to[0] * 2 + to[1]) * 2 + to[2]) * 2 + to[3]))
+        return lax.ppermute(array, ("grp", "fsdp"), pairs)
+
+    def swap(self, array, axis):
+        return self.permute(array, swap_of(axis))
+
+    def slabs(self, own):
+        got = [own] + [
+            self.permute(own, lambda z, x, y, c, k=k: ((z + k) % Z_SLABS, x, y, c)) for k in range(1, Z_SLABS)
+        ]
+        stacked = jnp.stack(got)
+        return [
+            lax.dynamic_index_in_dim(stacked, (self.z - z) % Z_SLABS, 0, keepdims=False)
+            for z in range(Z_SLABS)
+        ]
+
+    def spread(self, slabs, zs, js):
+        half = len(js) // 2
+        parts = []
+        for pick, first, second in ((slice(0, half), "x", "y"), (slice(half, None), "y", "x")):
+            own = jnp.stack([slabs[z][pick] for z in zs])
+            own = jnp.stack([own, self.swap(own, first)])
+            other = self.swap(own, second)
+            arrays = [[own, other], [self.swap(own, "c"), self.swap(other, "c")]]
+            parts.append(Part(zs, tuple(js)[pick], second, arrays))
+        return parts
+
+    def gather(self, low, layer):
+        own = self.dims.own
+        if layer == 0:
+            third = own // 3
+            parts = []
+            for js in (range(third), range(third, own)):
+                slabs = self.slabs(low[js.start : js.stop])
+                parts += self.spread(slabs, range(Z_SLABS), js)
+            return parts
+        slabs = self.slabs(low)
+        return self.spread(slabs, (0, 1), range(own)) + self.spread(slabs, (2, 3), range(own))
+
+    def add(self, a, b):
+        return (a.astype(F32) + b.astype(F32)).astype(BF)
+
+    def plane_sum(self, part):
+        keep, send = part.arrays
+        got = self.swap(send, "c")
+        first, second = (part.last, "x" if part.last == "y" else "y")
+        got1 = self.swap(self.add(keep[1], got[1]), first)
+        kept = self.add(keep[0], got[0])
+        got2 = self.swap(self.add(kept[1], got1[1]), second)
+        return self.add(self.add(kept[0], got1[0]), got2)
+
+    def reduce(self, early, late, layer):
+        z = self.z
+        first = jnp.concatenate([self.plane_sum(p) for p in late], axis=1)
+        rest = jnp.concatenate([self.plane_sum(p) for p in early], axis=1)
+        whole = jnp.concatenate([first, rest], axis=0)
+
+        def piece(k):
+            return lax.dynamic_index_in_dim(whole, (z + k) % Z_SLABS, 0, keepdims=False)
+
+        total = piece(0).astype(F32)
+        for k in range(1, Z_SLABS):
+            got = self.permute(piece(k), lambda z, x, y, c, k=k: ((z + k) % Z_SLABS, x, y, c))
+            total = total + got.astype(F32)
+        return total
+
+    def small_sum(self, values):
+        size = values.shape
+        values = values.reshape(-1, 128)
+        for axis in ("c", "x", "y"):
+            values = values + self.swap(values, axis)
+        for bit in (1, 2):
+            values = values + self.permute(values, lambda z, x, y, c, bit=bit: (z ^ bit, x, y, c))
+        return values.reshape(size)
+
+    def group(self, owned):
+        both = jnp.stack([owned, self.swap(owned, "y")])
+        return [both, self.swap(both, "c")]
+
+
+def update_kernel(layer, first, pos_ref, own_ref, left_ref, right_ref, roots_ref, masters_ref, *rest):
+    grads, roots, rest = rest[0:2], rest[2:4], rest[4:]
+    if not first:
+        rest = rest[5:]
+    outs, rest = rest[:5], rest[5:]
+    g_ref, r_ref, gram_ref, new_left, new_right, new_masters, new_copies, sem_in, sem_out = rest
+    y, c = pos_ref[2], pos_ref[3]
+    count, piece, block = own_ref.shape
+
+    def quarter(yq, cq):
+        return pl.ds(pl.multiple_of(piece * (2 * yq + cq), 16), piece)
+
+    for dc in range(2):
+        for dy in range(2):
+            rows = quarter(y ^ dy, c ^ dc)
+            pltpu.make_async_copy(grads[dc].at[dy], g_ref.at[:, rows, :], sem_in.at[0]).start()
+            pltpu.make_async_copy(roots[dc].at[dy], r_ref.at[:, rows, :], sem_in.at[1]).start()
+    copies = [pltpu.make_async_copy(own_ref, outs[0].at[layer], sem_out.at[0])]
+    copies[0].start()
+    wait_for(g_ref, sem_in.at[0])
+    wait_for(r_ref, sem_in.at[1])
+    own_rows = quarter(y, c)
+    for b in range(count):
+        g = g_ref[b]
+        mine = own_ref[b].astype(BF)
+        new_left[b] = decay_rate * left_ref[b] + (1.0 - decay_rate) * mm_bt(mine, g)
+        gram_ref[...] = mm_at(g, g)
+        new_right[b] = decay_rate * right_ref[b] + (1.0 - decay_rate) * gram_ref[own_rows, :]
+        mixed = mm(g, r_ref[b])
+        update = jnp.dot(
+            roots_ref[b], mixed, preferred_element_type=F32, precision=lax.Precision.HIGHEST
+        )
+        fresh = masters_ref[b] - matrix_rate * update
+        new_masters[b] = fresh
+        new_copies[b] = fresh.astype(BF)
+    for n, src in enumerate((new_left, new_right, new_masters, new_copies)):
+        copies.append(pltpu.make_async_copy(src, outs[n + 1].at[layer], sem_out.at[n + 1]))
+        copies[-1].start()
+    for copy in copies:
+        copy.wait()
+
+
+def update_layer(layer, pos, own, left, right, left_roots, masters, grads, roots, before):
+    count, piece, block = own.shape
+    whole = (LAYERS, count, piece, block)
+    ins = [pos, own, left, right, left_roots, masters, *grads, *roots]
+    specs = [SMEM] + [VMEM] * 5 + [HBM] * 4
+    aliases = {}
+    if before is not None:
+        aliases = {len(ins) + n: n for n in range(5)}
+        ins += list(before)
+        specs += [HBM] * 5
+    return pl.pallas_call(
+        functools.partial(update_kernel, layer, before is None),
+        in_specs=specs,
+        out_specs=[HBM] * 5,
+        out_shape=[shape(whole, F32)] * 4 + [shape(whole, BF)],
+        input_output_aliases=aliases,
+        scratch_shapes=[
+            pltpu.VMEM((count, block, block), BF),
+            pltpu.VMEM((count, block, block), BF),
+            pltpu.VMEM((block, block), F32),
+            pltpu.VMEM(own.shape, F32),
+            pltpu.VMEM(own.shape, F32),
+            pltpu.VMEM(own.shape, F32),
+            pltpu.VMEM(own.shape, BF),
+            pltpu.SemaphoreType.DMA((2,)),
+            pltpu.SemaphoreType.DMA((5,)),
+        ],
+        compiler_params=pltpu.CompilerParams(vmem_limit_bytes=VMEM_LIMIT),
+        cost_estimate=pl.CostEstimate(
+            flops=6 * count * block**3, bytes_accessed=16 << 20, transcendentals=0
+        ),
+        name="update_layer",
+    )(*ins)
+
+
+def update_plain(net, owned, masters, left_stats, right_stats, left_roots, right_roots):
+    own_rows = masters.shape[2]
+    first_row = lax.axis_index("fsdp") * own_rows
+    highest = lax.Precision.HIGHEST
+    grads = jnp.stack(owned)
+    whole = jnp.stack([net.group(g.astype(BF)) for g in owned]).astype(F32)
+    roots = jnp.stack([net.group(right_roots[n].astype(BF)) for n in range(LAYERS)]).astype(F32)
+    columns = lax.dynamic_slice_in_dim(whole, first_row, own_rows, 3)
+    new_left = decay_rate * left_stats + (1.0 - decay_rate) * jnp.einsum(
+        "lbrk,lbck->lbrc", grads, whole, precision=highest
+    )
+    new_right = decay_rate * right_stats + (1.0 - decay_rate) * jnp.einsum(
+        "lbkr,lbkc->lbrc", columns, whole, precision=highest
+    )
+    mixed = jnp.einsum("lbrk,lbkc->lbrc", whole, roots, precision=highest)
+    update = jnp.einsum("lbrk,lbkc->lbrc", left_roots, mixed, precision=highest)
+    new_masters = masters - matrix_rate * update
+    return grads, new_left, new_right, new_masters, new_masters.astype(BF)
+
+
 def local(
     inputs,
     lengths,
@@ -639,10 +840,10 @@
     rows = chains * seq
     groups, shards = lax.axis_size("grp"), lax.axis_size("fsdp")
     block = masters.shape[3]
-    own_rows = masters.shape[2]
     ffn = small_params.shape[1] - 8 * width
     dims = Dims(width, ffn, block, groups * masters.shape[1], rows)
-    net = AnySlice(dims)
+    small_slice = groups == 2 * Z_SLABS and shards == 4
+    net = SmallSlice(dims) if small_slice else AnySlice(dims)
     pos = net.position()
     low = [masters[n].astype(BF) for n in range(LAYERS)]
     weights = [net.gather(low[n], n) for n in range(LAYERS)]
@@ -659,13 +860,16 @@
             x = y
         else:
             saved.append((x, qkv, lse, ctx, unit, inv))
+    if small_slice:
+        low_roots, unit = lax.optimization_barrier((right_roots, unit))
+        roots = [net.group(low_roots[n].astype(BF)) for n in range(LAYERS)]
 
     owned = [None] * LAYERS
     sums = [None] * LAYERS
-    gy = None
+    gy, done = None, None
     for n in reversed(range(LAYERS)):
         if n == last:
-            x, qkv, lse, ctx, unit, inv = saved[n]
+            x, qkv, lse, ctx, _, inv = saved[n]
             cot = cotangent.reshape(rows, width)
             y, gz1, gctx, sums_a, early = ffn_both(
                 dims, weights[n], net.early, pos, lengths, cot, small[n], unit, inv, ctx
@@ -681,42 +885,30 @@
         )
         owned[n] = net.reduce(early, late, n)
         sums[n] = jnp.concatenate([sums_b[0], sums_a[0, 2 * width :]])
+        if small_slice:
+            done = update_layer(
+                n, pos, owned[n], left_stats[n], right_stats[n], left_roots[n], masters[n],
+                net.group(owned[n].astype(BF)), roots[n], done,
+            )
     input_grad = gy.reshape(chains, seq, width)
+    if not small_slice:
+        done = update_plain(net, owned, masters, left_stats, right_stats, left_roots, right_roots)
+    weight_grads, new_left, new_right, new_masters, new_copies = done
 
     small_grads = net.small_sum(jnp.stack(sums))
-    blocked_weight_gradients = jnp.stack(owned)
-    new_left, new_right, new_masters = [], [], []
-    first_row = lax.axis_index("fsdp") * own_rows
-    highest = lax.Precision.HIGHEST
-    for n in range(LAYERS):
-        whole = net.group(owned[n].astype(BF)).astype(F32)
-        roots = net.group(right_roots[n].astype(BF)).astype(F32)
-        columns = lax.dynamic_slice_in_dim(whole, first_row, own_rows, 2)
-        new_left.append(
-            decay_rate * left_stats[n]
-            + (1.0 - decay_rate) * jnp.einsum("brk,bck->brc", owned[n], whole, precision=highest)
-        )
-        new_right.append(
-            decay_rate * right_stats[n]
-            + (1.0 - decay_rate) * jnp.einsum("bkr,bkc->brc", columns, whole, precision=highest)
-        )
-        mixed = jnp.einsum("brk,bkc->brc", whole, roots, precision=highest)
-        update = jnp.einsum("brk,bkc->brc", left_roots[n], mixed, precision=highest)
-        new_masters.append(masters[n] - matrix_rate * update)
-    new_masters = jnp.stack(new_masters)
     new_moments = decay_rate * small_moments + (1.0 - decay_rate) * small_grads * small_grads
     new_small = small_params - small_rate * small_grads / (jnp.sqrt(new_moments) + moment_epsilon)
     return (
         activations,
         input_grad,
-        blocked_weight_gradients,
+        weight_grads,
         small_grads,
         new_moments,
         new_small,
-        jnp.stack(new_left),
-        jnp.stack(new_right),
+        new_left,
+        new_right,
         new_masters,
-        new_masters.astype(BF),
+        new_copies,
     )
 
 

time: 1210 us -> 619 us (0.51)
  the two profiles are of different devices: /device:TPU:0 before, /device:TPU:29 now
where the time goes in v2:
time: 619 us; the launch traced here: 610 us
  waiting for transfers between devices  244 us (39%)
  starting transfers between devices  178 us (29%)
  Pallas kernels  147 us (24%)
  other arithmetic  21.2 us (3%)
  local copies, waits for them, and re-layouts  18 us (3%)
    ppermute x84, waiting for transfers between devices, permute(): return lax.ppermute(array, ('grp', 'fsdp'), pairs)  244 us
    ppermute x84, starting transfers between devices, permute(): return lax.ppermute(array, ('grp', 'fsdp'), pairs)  178 us
    pallas_call x2, Pallas kernels, attention_backward(): pl.pallas_call(functools.partial(attention_backward_kernel, dims, parts,...  40.3 us
    pallas_call x1, Pallas kernels, ffn_both(): pl.pallas_call(functools.partial(ffn_both_kernel, dims, parts, outs_parts...  25.4 us
    pallas_call x2, Pallas kernels, attention_forward(): pl.pallas_call(functools.partial(attention_forward_kernel, dims, parts, c...  23.7 us
    pallas_call x1, Pallas kernels, ffn_backward(): pl.pallas_call(functools.partial(ffn_backward_kernel, dims, parts, outs_p...  22.5 us
    pallas_call x2, Pallas kernels, update_layer(): pl.pallas_call(functools.partial(update_kernel, layer, before is None), i...  22.3 us
    pallas_call x1, Pallas kernels, ffn_forward(): pl.pallas_call(functools.partial(ffn_forward_kernel, dims, parts), in_spe...  13.1 us
  transfers between devices with their start and end apart: 84, of which 30 were waited for; matrix products, arithmetic and copies ran while one was open for 5% of the time, Pallas kernels for 8%

profile of v2, /device:TPU:29, one launch (start us, length us, event | category | flops | bytes accessed | tf_op | source)
XLA Modules:
  0.0 610.4 jit_solution(531137819121402718)
XLA Ops:
  15.4 30.9 %collective-permute-start.13 = (bf16[4,96,384]{2,1,0:T(8,128)(2,1)S(1)}, bf16[4,96,384]{2,1,0:T(8,128)(2,1)S(1)}, u32[]{:S(2)}, u32[]{:S(2)}) collective-permute-start(bf16[4,96,384]{2,1,0:T(8,128)(2,1)S(1)} %get-tuple-element.200), channel_id=1, source_target_pairs={{0,24},{1,25},{2,26},{3,27},{4,28},{5,29},{6,30},{7,31},{8,0},{9,1... | collective-permute-start | bytes 884744 | tf_op jit(solution)/shard_map/ppermute | solution.py:651
  46.7 32.9 %collective-permute-done.12 = bf16[4,96,384]{2,1,0:T(8,128)(2,1)S(1)} collective-permute-done((bf16[4,96,384]{2,1,0:T(8,128)(2,1)S(1)}, bf16[4,96,384]{2,1,0:T(8,128)(2,1)S(1)}, u32[]{:S(2)}, u32[]{:S(2)}) %collective-permute-start.12) | collective-permute-done | bytes 294944 | tf_op jit(solution)/shard_map/ppermute | solution.py:651
  89.0 7.0 %collective-permute-done.37 = bf16[2,3,96,384]{3,2,1,0:T(8,128)(2,1)S(1)} collective-permute-done((bf16[2,3,96,384]{3,2,1,0:T(8,128)(2,1)S(1)}, bf16[2,3,96,384]{3,2,1,0:T(8,128)(2,1)S(1)}, u32[]{:S(2)}, u32[]{:S(2)}) %collective-permute-start.37) | collective-permute-done | bytes 442400 | tf_op jit(solution)/shard_map/ppermute | solution.py:651
  97.7 7.8 %collective-permute-done.29 = bf16[2,3,96,384]{3,2,1,0:T(8,128)(2,1)S(1)} collective-permute-done((bf16[2,3,96,384]{3,2,1,0:T(8,128)(2,1)S(1)}, bf16[2,3,96,384]{3,2,1,0:T(8,128)(2,1)S(1)}, u32[]{:S(2)}, u32[]{:S(2)}) %collective-permute-start.29) | collective-permute-done | bytes 442400 | tf_op jit(solution)/shard_map/ppermute | solution.py:651
  111.1 6.9 %collective-permute-done.25 = bf16[2,3,96,384]{3,2,1,0:T(8,128)(2,1)S(1)} collective-permute-done((bf16[2,3,96,384]{3,2,1,0:T(8,128)(2,1)S(1)}, bf16[2,3,96,384]{3,2,1,0:T(8,128)(2,1)S(1)}, u32[]{:S(2)}, u32[]{:S(2)}) %collective-permute-start.25) | collective-permute-done | bytes 442400 | tf_op jit(solution)/shard_map/ppermute | solution.py:651
  119.3 5.6 collective-permute-start.5
  141.4 7.6 %collective-permute-done.38.rest_13_ = bf16[2,2,3,96,384]{4,3,2,1,0:T(8,128)(2,1)S(1)} collective-permute-done((bf16[2,2,3,96,384]{4,3,2,1,0:T(8,128)(2,1)S(1)}, bf16[2,2,3,96,384]{4,3,2,1,0:T(8,128)(2,1)S(1)}, u32[]{:S(2)}, u32[]{:S(2)}) %collective-permute-start.38) | collective-permute-done | bytes 884768 | tf_op jit(solution)/shard_map/ppermute | solution.py:651
  149.0 7.1 %collective-permute-start.20 = (bf16[2,4,2,96,384]{4,3,2,1,0:T(8,128)(2,1)S(1)}, bf16[2,4,2,96,384]{4,3,2,1,0:T(8,128)(2,1)S(1)}, u32[]{:S(2)}, u32[]{:S(2)}) collective-permute-start(bf16[2,4,2,96,384]{4,3,2,1,0:T(8,128)(2,1)S(1)} %pad_maximum_fusion.3.rest_12_), channel_id=1, source_target_pairs={{0,1},{1,0},{2,3},{3,2},{4,5},{5,4},{6,7},{7,6},{8,9},{9,8},{10,11... | collective-permute-start | bytes 3538952 | tf_op jit(solution)/shard_map/ppermute | solution.py:651
  157.5 10.5 %collective-permute-done.30.rest_5_ = bf16[2,2,3,96,384]{4,3,2,1,0:T(8,128)(2,1)} collective-permute-done((bf16[2,2,3,96,384]{4,3,2,1,0:T(8,128)(2,1)S(1)}, bf16[2,2,3,96,384]{4,3,2,1,0:T(8,128)(2,1)}, u32[]{:S(2)}, u32[]{:S(2)}) %collective-permute-start.30) | collective-permute-done | bytes 884768 | tf_op jit(solution)/shard_map/ppermute | solution.py:651
  169.3 7.4 %collective-permute-start.27 = (bf16[2,2,3,96,384]{4,3,2,1,0:T(8,128)(2,1)S(1)}, bf16[2,2,3,96,384]{4,3,2,1,0:T(8,128)(2,1)S(1)}, u32[]{:S(2)}, u32[]{:S(2)}) collective-permute-start(bf16[2,2,3,96,384]{4,3,2,1,0:T(8,128)(2,1)S(1)} %pad_maximum_fusion.4.rest_0_), channel_id=1, source_target_pairs={{0,1},{1,0},{2,3},{3,2},{4,5},{5,4},{6,7},{7,6},{8,9},{9,8},{10,11... | collective-permute-start | bytes 2654216 | tf_op jit(solution)/shard_map/ppermute | solution.py:651
  176.7 26.0 %collective-permute-done.26.rest_1_ = bf16[2,2,3,96,384]{4,3,2,1,0:T(8,128)(2,1)} collective-permute-done((bf16[2,2,3,96,384]{4,3,2,1,0:T(8,128)(2,1)S(1)}, bf16[2,2,3,96,384]{4,3,2,1,0:T(8,128)(2,1)}, u32[]{:S(2)}, u32[]{:S(2)}) %collective-permute-start.26) | collective-permute-done | bytes 884768 | tf_op jit(solution)/shard_map/ppermute | solution.py:651
  215.3 11.7 %attention_forward.2 = (bf16[480,2304]{1,0:T(8,128)(2,1)}, f32[3,12,160]{2,1,0:T(8,128)}, bf16[480,768]{1,0:T(8,128)(2,1)}, f32[480,768]{1,0:T(8,128)}, f32[480,1]{1,0:T(8,128)}) custom-call(s32[4]{0:T(128)} %pad_add_fusion.pos_ref, s32[3]{0:T(128)} %len_ref.9, bf16[480,768]{1,0:T(8,128)(2,1)} %bitcast.269, f32[1,9216]{1,0:T(1,128)} %get-tuple-element.207.small_ref, ...), custom_call_target="tpu_custom_call" | custom-call | flops 3397386240 | bytes 16777216 | tf_op jit(solution)/shard_map/attention_forward/pallas_call | solution.py:240
  227.0 13.1 %ffn_forward.1 = (bf16[480,3072]{1,0:T(8,128)(2,1)}, bf16[480,3072]{1,0:T(8,128)(2,1)}, f32[480,768]{1,0:T(8,128)}, f32[480,1]{1,0:T(8,128)}, f32[480,768]{1,0:T(8,128)}) custom-call(s32[4]{0:T(128)} %pad_add_fusion.pos_ref, f32[480,768]{1,0:T(8,128)} %get-tuple-element.64.unit_ref, f32[1,9216]{1,0:T(1,128)} %get-tuple-element.207.small_ref, ...), custom_call_target="tpu_custom_call" | custom-call | flops 4529848320 | bytes 25165824 | tf_op jit(solution)/shard_map/ffn_forward/pallas_call | solution.py:297
  240.2 12.0 %attention_forward.3 = (bf16[480,2304]{1,0:T(8,128)(2,1)}, f32[3,12,160]{2,1,0:T(8,128)}, bf16[480,768]{1,0:T(8,128)(2,1)}, f32[480,768]{1,0:T(8,128)}, f32[480,1]{1,0:T(8,128)}) custom-call(s32[4]{0:T(128)} %pad_add_fusion.pos_ref, s32[3]{0:T(128)} %len_ref.9, f32[480,768]{1,0:T(8,128)} %get-tuple-element.65.x_ref, f32[1,9216]{1,0:T(1,128)} %get-tuple-element.208.small_ref, ...), custom_call_target="tpu_custom_call" | custom-call | flops 3397386240 | bytes 16777216 | tf_op jit(solution)/shard_map/attention_forward/pallas_call | solution.py:240
  254.0 25.4 %ffn_both.1 = (bf16[480,768]{1,0:T(8,128)(2,1)}, f32[480,768]{1,0:T(8,128)}, bf16[480,768]{1,0:T(8,128)(2,1)}, f32[1,9216]{1,0:T(1,128)}, bf16[2,2,3,3,96,384]{5...) custom-call(s32[4]{0:T(128)} %pad_add_fusion.pos_ref, ...), custom_call_target="tpu_custom_call" | custom-call | flops 14722007040 | bytes 41943040 | tf_op jit(solution)/shard_map/ffn_both/pallas_call | solution.py:470
  279.4 20.2 %attention_backward.2 = (f32[480,768]{1,0:T(8,128)}, f32[1,1536]{1,0:T(1,128)}, bf16[2,2,1,3,96,384]{5,4,3,2,1,0:T(8,128)(2,1)}, bf16[2,2,1,3,96,384]{5,4,3,2,1,...) custom-call(s32[4]{0:T(128)} %pad_add_fusion.pos_ref, s32[3]{0:T(128)} %len_ref.9, ...), custom_call_target="tpu_custom_call" | custom-call | flops 6794772480 | bytes 25165824 | tf_op jit(solution)/shard_map/attention_backward/pallas_call | solution.py:570
  299.6 22.5 %ffn_backward.1 = (f32[480,768]{1,0:T(8,128)}, bf16[480,768]{1,0:T(8,128)(2,1)}, f32[1,9216]{1,0:T(1,128)}, bf16[2,2,3,3,96,384]{5,4,3,2,1,0:T(8,128)(2,1)}, bf1...) custom-call(s32[4]{0:T(128)} %pad_add_fusion.pos_ref, ...), custom_call_target="tpu_custom_call" | custom-call | flops 10192158720 | bytes 41943040 | tf_op jit(solution)/shard_map/ffn_backward/pallas_call | solution.py:407
  323.0 20.1 %attention_backward.3 = (f32[480,768]{1,0:T(8,128)}, f32[1,1536]{1,0:T(1,128)}, bf16[2,2,1,3,96,384]{5,4,3,2,1,0:T(8,128)(2,1)}, bf16[2,2,1,3,96,384]{5,4,3,2,1,...) custom-call(s32[4]{0:T(128)} %pad_add_fusion.pos_ref, s32[3]{0:T(128)} %len_ref.9, ...), custom_call_target="tpu_custom_call" | custom-call | flops 6794772480 | bytes 25165824 | tf_op jit(solution)/shard_map/attention_backward/pallas_call | solution.py:570
  379.0 9.2 %collective-permute-done.42 = bf16[2,1,3,96,384]{4,3,2,1,0:T(8,128)(2,1)S(1)} collective-permute-done((bf16[2,1,3,96,384]{4,3,2,1,0:T(8,128)(2,1)S(1)}, bf16[2,1,3,96,384]{4,3,2,1,0:T(8,128)(2,1)S(1)}, u32[]{:S(2)}, u32[]{:S(2)}) %collective-permute-start.42) | collective-permute-done | bytes 442400 | tf_op jit(solution)/shard_map/ppermute | solution.py:651
  389.6 8.6 %collective-permute-done.45 = bf16[2,1,3,96,384]{4,3,2,1,0:T(8,128)(2,1)S(1)} collective-permute-done((bf16[2,1,3,96,384]{4,3,2,1,0:T(8,128)(2,1)S(1)}, bf16[2,1,3,96,384]{4,3,2,1,0:T(8,128)(2,1)S(1)}, u32[]{:S(2)}, u32[]{:S(2)}) %collective-permute-start.45) | collective-permute-done | bytes 442400 | tf_op jit(solution)/shard_map/ppermute | solution.py:651
  412.5 55.3 %collective-permute-done.46 = bf16[1,3,96,384]{3,2,1,0:T(8,128)(2,1)S(1)} collective-permute-done((bf16[1,3,96,384]{3,2,1,0:T(8,128)(2,1)S(1)}, bf16[1,3,96,384]{3,2,1,0:T(8,128)(2,1)S(1)}, u32[]{:S(2)}, u32[]{:S(2)}) %collective-permute-start.46) | collective-permute-done | bytes 221216 | tf_op jit(solution)/shard_map/ppermute | solution.py:651
  472.8 7.2 %collective-permute-done.68 = bf16[3,3,96,384]{3,2,1,0:T(8,128)(2,1)S(1)} collective-permute-done((bf16[3,3,96,384]{3,2,1,0:T(8,128)(2,1)S(1)}, bf16[3,3,96,384]{3,2,1,0:T(8,128)(2,1)S(1)}, u32[]{:S(2)}, u32[]{:S(2)}) %collective-permute-start.68) | collective-permute-done | bytes 663584 | tf_op jit(solution)/shard_map/ppermute | solution.py:651
  483.8 10.4 %collective-permute-done.49 = bf16[3,3,96,384]{3,2,1,0:T(8,128)(2,1)S(1)} collective-permute-done((bf16[3,3,96,384]{3,2,1,0:T(8,128)(2,1)S(1)}, bf16[3,3,96,384]{3,2,1,0:T(8,128)(2,1)S(1)}, u32[]{:S(2)}, u32[]{:S(2)}) %collective-permute-start.49) | collective-permute-done | bytes 663584 | tf_op jit(solution)/shard_map/ppermute | solution.py:651
  499.0 10.7 %collective-permute-done.73 = bf16[6,96,384]{2,1,0:T(8,128)(2,1)S(1)} collective-permute-done((bf16[6,96,384]{2,1,0:T(8,128)(2,1)S(1)}, bf16[6,96,384]{2,1,0:T(8,128)(2,1)S(1)}, u32[]{:S(2)}, u32[]{:S(2)}) %collective-permute-start.73) | collective-permute-done | bytes 442400 | tf_op jit(solution)/shard_map/ppermute | solution.py:651
  509.6 10.3 %collective-permute-start.77 = (bf16[6,96,384]{2,1,0:T(8,128)(2,1)S(1)}, bf16[6,96,384]{2,1,0:T(8,128)(2,1)S(1)}, u32[]{:S(2)}, u32[]{:S(2)}) collective-permute-start(bf16[6,96,384]{2,1,0:T(8,128)(2,1)S(1)} %bitcast.266), channel_id=1, source_target_pairs={{0,2},{1,3},{2,0},{3,1},{4,6},{5,7},{6,4},{7,5},{8,10},{9,11},{10,... | collective-permute-start | bytes 1327112 | tf_op jit(solution)/shard_map/ppermute | solution.py:651
  521.1 24.6 %collective-permute-start.83 = (f32[144,128]{1,0:T(8,128)S(1)}, f32[144,128]{1,0:T(8,128)S(1)}, u32[]{:S(2)}, u32[]{:S(2)}) collective-permute-start(f32[144,128]{1,0:T(8,128)S(1)} %add.485), channel_id=1, source_target_pairs={{0,16},{1,17},{2,18},{3,19},{4,20},{5,21},{6,22},{7,23},{8,24},{9,... | collective-permute-start | bytes 221192 | tf_op jit(solution)/shard_map/ppermute | solution.py:651
  545.6 7.8 %collective-permute-done.54 = bf16[6,96,384]{2,1,0:T(8,128)(2,1)S(1)} collective-permute-done((bf16[6,96,384]{2,1,0:T(8,128)(2,1)S(1)}, bf16[6,96,384]{2,1,0:T(8,128)(2,1)S(1)}, u32[]{:S(2)}, u32[]{:S(2)}) %collective-permute-start.54) | collective-permute-done | bytes 442400 | tf_op jit(solution)/shard_map/ppermute | solution.py:651
  553.4 5.2 collective-permute-start.75
  562.0 8.1 %collective-permute-start.78 = (bf16[2,6,96,384]{3,2,1,0:T(8,128)(2,1)S(1)}, bf16[2,6,96,384]{3,2,1,0:T(8,128)(2,1)S(1)}, u32[]{:S(2)}, u32[]{:S(2)}) collective-permute-start(bf16[2,6,96,384]{3,2,1,0:T(8,128)(2,1)S(1)} %pad_maximum_fusion.11.rest_2_), channel_id=1, source_target_pairs={{0,1},{1,0},{2,3},{3,2},{4,5},{5,4},{6,7},{7,6},{8,9},{9,8},{10,11... | collective-permute-start | bytes 2654216 | tf_op jit(solution)/shard_map/ppermute | solution.py:651
  570.5 7.5 %collective-permute-start.76 = (bf16[2,6,96,384]{3,2,1,0:T(8,128)(2,1)S(1)}, bf16[2,6,96,384]{3,2,1,0:T(8,128)(2,1)S(1)}, u32[]{:S(2)}, u32[]{:S(2)}) collective-permute-start(bf16[2,6,96,384]{3,2,1,0:T(8,128)(2,1)S(1)} %pad_maximum_fusion.10.rest_0_), channel_id=1, source_target_pairs={{0,1},{1,0},{2,3},{3,2},{4,5},{5,4},{6,7},{7,6},{8,9},{9,8},{10,11... | collective-permute-start | bytes 2654216 | tf_op jit(solution)/shard_map/ppermute | solution.py:651
  586.4 11.1 %update_layer.2 = (f32[2,6,96,384]{3,2,1,0:T(8,128)}, f32[2,6,96,384]{3,2,1,0:T(8,128)}, f32[2,6,96,384]{3,2,1,0:T(8,128)}, f32[2,6,96,384]{3,2,1,0:T(8,128)}, bf16[2,6,96,384]{3,2,1,0:T(8,128)(2,1)}) custom-call(s32[4]{0:T(128)} %pad_add_fusion.pos_ref, f32[6,96,384]{2,1,0:T(8,128)} %get-tuple-element.121.own_ref, ...), custom_call_target="tpu_custom_call" | custom-call | flops 2038431744 | bytes 16777216 | tf_op jit(solution)/shard_map/update_layer/pallas_call | solution.py:782
  598.8 11.1 %update_layer.3 = (f32[2,6,96,384]{3,2,1,0:T(8,128)}, f32[2,6,96,384]{3,2,1,0:T(8,128)}, f32[2,6,96,384]{3,2,1,0:T(8,128)}, f32[2,6,96,384]{3,2,1,0:T(8,128)}, bf16[2,6,96,384]{3,2,1,0:T(8,128)(2,1)}) custom-call(s32[4]{0:T(128)} %pad_add_fusion.pos_ref, ...), custom_call_target="tpu_custom_call", output_to_operand_aliasing={{0}: (10, {}), {1}: (11, {}), {2}: (12, {}), {3}: (13, {}),... | custom-call | flops 2038431744 | bytes 16777216 | tf_op jit(solution)/shard_map/update_layer/pallas_call | solution.py:782
  (331 shorter events, 146.4 us)
Async XLA Ops:
  5.6 40.9 %collective-permute-start.11 = (bf16[4,96,384]{2,1,0:T(8,128)(2,1)S(1)}, bf16[4,96,384]{2,1,0:T(8,128)(2,1)S(1)}, u32[]{:S(2)}, u32[]{:S(2)}) collective-permute-start(bf16[4,96,384]{2,1,0:T(8,128)(2,1)S(1)} %get-tuple-element.200), channel_id=1, source_target_pairs={{0,8},{1,9},{2,10},{3,11},{4,12},{5,13},{6,14},{7,15},{8,16},{9,17... | collective-permute-start | bytes 884744 | tf_op jit(solution)/shard_map/ppermute | solution.py:651
  6.1 75.3 %collective-permute-start.22 = (bf16[6,96,384]{2,1,0:T(8,128)(2,1)S(1)}, bf16[6,96,384]{2,1,0:T(8,128)(2,1)S(1)}, u32[]{:S(2)}, u32[]{:S(2)}) collective-permute-start(bf16[6,96,384]{2,1,0:T(8,128)(2,1)S(1)} %get-tuple-element.166), channel_id=1, source_target_pairs={{0,8},{1,9},{2,10},{3,11},{4,12},{5,13},{6,14},{7,15},{8,16},{9,17... | collective-permute-start | bytes 1327112 | tf_op jit(solution)/shard_map/ppermute | solution.py:651
  9.2 72.2 %collective-permute-start.23 = (bf16[6,96,384]{2,1,0:T(8,128)(2,1)S(1)}, bf16[6,96,384]{2,1,0:T(8,128)(2,1)S(1)}, u32[]{:S(2)}, u32[]{:S(2)}) collective-permute-start(bf16[6,96,384]{2,1,0:T(8,128)(2,1)S(1)} %get-tuple-element.166), channel_id=1, source_target_pairs={{0,16},{1,17},{2,18},{3,19},{4,20},{5,21},{6,22},{7,23},{8,24},{9,... | collective-permute-start | bytes 1327112 | tf_op jit(solution)/shard_map/ppermute | solution.py:651
  9.2 70.4 %collective-permute-start.12 = (bf16[4,96,384]{2,1,0:T(8,128)(2,1)S(1)}, bf16[4,96,384]{2,1,0:T(8,128)(2,1)S(1)}, u32[]{:S(2)}, u32[]{:S(2)}) collective-permute-start(bf16[4,96,384]{2,1,0:T(8,128)(2,1)S(1)} %get-tuple-element.200), channel_id=1, source_target_pairs={{0,16},{1,17},{2,18},{3,19},{4,20},{5,21},{6,22},{7,23},{8,24},{9,... | collective-permute-start | bytes 884744 | tf_op jit(solution)/shard_map/ppermute | solution.py:651
  15.4 64.4 %collective-permute-start.13 = (bf16[4,96,384]{2,1,0:T(8,128)(2,1)S(1)}, bf16[4,96,384]{2,1,0:T(8,128)(2,1)S(1)}, u32[]{:S(2)}, u32[]{:S(2)}) collective-permute-start(bf16[4,96,384]{2,1,0:T(8,128)(2,1)S(1)} %get-tuple-element.200), channel_id=1, source_target_pairs={{0,24},{1,25},{2,26},{3,27},{4,28},{5,29},{6,30},{7,31},{8,0},{9,1... | collective-permute-start | bytes 884744 | tf_op jit(solution)/shard_map/ppermute | solution.py:651
  46.5 34.9 %collective-permute-start.24 = (bf16[6,96,384]{2,1,0:T(8,128)(2,1)S(1)}, bf16[6,96,384]{2,1,0:T(8,128)(2,1)S(1)}, u32[]{:S(2)}, u32[]{:S(2)}) collective-permute-start(bf16[6,96,384]{2,1,0:T(8,128)(2,1)S(1)} %get-tuple-element.166), channel_id=1, source_target_pairs={{0,24},{1,25},{2,26},{3,27},{4,28},{5,29},{6,30},{7,31},{8,0},{9,1... | collective-permute-start | bytes 1327112 | tf_op jit(solution)/shard_map/ppermute | solution.py:651
  87.7 37.2 %collective-permute-start.8 = (bf16[2,4,1,96,384]{4,3,1,2,0:T(8,128)(2,1)S(1)}, bf16[2,4,1,96,384]{4,3,1,2,0:T(8,128)(2,1)S(1)}, u32[]{:S(2)}, u32[]{:S(2)}) collective-permute-start(bf16[2,4,1,96,384]{4,3,1,2,0:T(8,128)(2,1)S(1)} %get-tuple-element.179), channel_id=1, source_target_pairs={{0,4},{1,5},{2,6},{3,7},{4,0},{5,1},{6,2},{7,3},{8,12},{9,13},{10,... | collective-permute-start | bytes 1769480 | tf_op jit(solution)/shard_map/ppermute | solution.py:651
  133.3 34.8 %collective-permute-start.30 = (bf16[2,2,3,96,384]{4,3,2,1,0:T(8,128)(2,1)S(1)}, bf16[2,2,3,96,384]{4,3,2,1,0:T(8,128)(2,1)}, u32[]{:S(2)}, u32[]{:S(2)}) collective-permute-start(bf16[2,2,3,96,384]{4,3,2,1,0:T(8,128)(2,1)S(1)} %pad_maximum_fusion.5.rest_4_), channel_id=1, source_target_pairs={{0,4},{1,5},{2,6},{3,7},{4,0},{5,1},{6,2},{7,3},{8,12},{9,13},{10,... | collective-permute-start | bytes 2654216 | tf_op jit(solution)/shard_map/ppermute | solution.py:651
  133.6 35.7 %collective-permute-start.31 = (bf16[2,2,3,96,384]{4,3,2,1,0:T(8,128)(2,1)S(1)}, bf16[2,2,3,96,384]{4,3,2,1,0:T(8,128)(2,1)S(1)}, u32[]{:S(2)}, u32[]{:S(2)}) collective-permute-start(bf16[2,2,3,96,384]{4,3,2,1,0:T(8,128)(2,1)S(1)} %pad_maximum_fusion.5.rest_4_), channel_id=1, source_target_pairs={{0,1},{1,0},{2,3},{3,2},{4,5},{5,4},{6,7},{7,6},{8,9},{9,8},{10,11... | collective-permute-start | bytes 2654216 | tf_op jit(solution)/shard_map/ppermute | solution.py:651
  140.2 63.5 %collective-permute-start.19 = (bf16[2,4,2,96,384]{4,3,2,1,0:T(8,128)(2,1)S(1)}, bf16[2,4,2,96,384]{4,3,2,1,0:T(8,128)(2,1)S(1)}, u32[]{:S(2)}, u32[]{:S(2)}) collective-permute-start(bf16[2,4,2,96,384]{4,3,2,1,0:T(8,128)(2,1)S(1)} %pad_maximum_fusion.3.rest_12_), channel_id=1, source_target_pairs={{0,4},{1,5},{2,6},{3,7},{4,0},{5,1},{6,2},{7,3},{8,12},{9,13},{10,... | collective-permute-start | bytes 3538952 | tf_op jit(solution)/shard_map/ppermute | solution.py:651
  149.0 55.1 %collective-permute-start.20 = (bf16[2,4,2,96,384]{4,3,2,1,0:T(8,128)(2,1)S(1)}, bf16[2,4,2,96,384]{4,3,2,1,0:T(8,128)(2,1)S(1)}, u32[]{:S(2)}, u32[]{:S(2)}) collective-permute-start(bf16[2,4,2,96,384]{4,3,2,1,0:T(8,128)(2,1)S(1)} %pad_maximum_fusion.3.rest_12_), channel_id=1, source_target_pairs={{0,1},{1,0},{2,3},{3,2},{4,5},{5,4},{6,7},{7,6},{8,9},{9,8},{10,11... | collective-permute-start | bytes 3538952 | tf_op jit(solution)/shard_map/ppermute | solution.py:651
  156.1 48.1 %collective-permute-start.15 = (bf16[2,4,2,96,384]{4,3,2,1,0:T(8,128)(2,1)S(1)}, bf16[2,4,2,96,384]{4,3,2,1,0:T(8,128)(2,1)}, u32[]{:S(2)}, u32[]{:S(2)}) collective-permute-start(bf16[2,4,2,96,384]{4,3,2,1,0:T(8,128)(2,1)S(1)} %pad_maximum_fusion.2.rest_8_), channel_id=1, source_target_pairs={{0,2},{1,3},{2,0},{3,1},{4,6},{5,7},{6,4},{7,5},{8,10},{9,11},{10,... | collective-permute-start | bytes 3538952 | tf_op jit(solution)/shard_map/ppermute | solution.py:651
  168.1 34.7 %collective-permute-start.26 = (bf16[2,2,3,96,384]{4,3,2,1,0:T(8,128)(2,1)S(1)}, bf16[2,2,3,96,384]{4,3,2,1,0:T(8,128)(2,1)}, u32[]{:S(2)}, u32[]{:S(2)}) collective-permute-start(bf16[2,2,3,96,384]{4,3,2,1,0:T(8,128)(2,1)S(1)} %pad_maximum_fusion.4.rest_0_), channel_id=1, source_target_pairs={{0,2},{1,3},{2,0},{3,1},{4,6},{5,7},{6,4},{7,5},{8,10},{9,11},{10,... | collective-permute-start | bytes 2654216 | tf_op jit(solution)/shard_map/ppermute | solution.py:651
  203.7 36.5 %collective-permute-start.28 = (bf16[2,2,3,96,384]{4,3,2,1,0:T(8,128)(2,1)}, bf16[2,2,3,96,384]{4,3,2,1,0:T(8,128)(2,1)}, u32[]{:S(2)}, u32[]{:S(2)}) collective-permute-start(bf16[2,2,3,96,384]{4,3,2,1,0:T(8,128)(2,1)} %collective-permute-done.26.rest_1_), channel_id=1, source_target_pairs={{0,1},{1,0},{2,3},{3,2},{4,5},{5,4},{6,7},{7,6},{8,9},{9,8},{10,11... | collective-permute-start | bytes 2654216 | tf_op jit(solution)/shard_map/ppermute | solution.py:651
  207.1 45.0 %collective-permute-start.39 = (bf16[2,2,3,96,384]{4,3,2,1,0:T(8,128)(2,1)}, bf16[2,2,3,96,384]{4,3,2,1,0:T(8,128)(2,1)S(1)}, u32[]{:S(2)}, u32[]{:S(2)}) collective-permute-start(bf16[2,2,3,96,384]{4,3,2,1,0:T(8,128)(2,1)} %copy-done.14), channel_id=1, source_target_pairs={{0,1},{1,0},{2,3},{3,2},{4,5},{5,4},{6,7},{7,6},{8,9},{9,8},{10,11... | collective-permute-start | bytes 2654216 | tf_op jit(solution)/shard_map/ppermute | solution.py:651
  208.8 43.3 %collective-permute-start.35 = (bf16[2,2,3,96,384]{4,3,2,1,0:T(8,128)(2,1)}, bf16[2,2,3,96,384]{4,3,2,1,0:T(8,128)(2,1)S(1)}, u32[]{:S(2)}, u32[]{:S(2)}) collective-permute-start(bf16[2,2,3,96,384]{4,3,2,1,0:T(8,128)(2,1)} %copy-done.15), channel_id=1, source_target_pairs={{0,1},{1,0},{2,3},{3,2},{4,5},{5,4},{6,7},{7,6},{8,9},{9,8},{10,11... | collective-permute-start | bytes 2654216 | tf_op jit(solution)/shard_map/ppermute | solution.py:651
  210.6 41.6 %collective-permute-start.40 = (bf16[2,2,3,96,384]{4,3,2,1,0:T(8,128)(2,1)}, bf16[2,2,3,96,384]{4,3,2,1,0:T(8,128)(2,1)S(1)}, u32[]{:S(2)}, u32[]{:S(2)}) collective-permute-start(bf16[2,2,3,96,384]{4,3,2,1,0:T(8,128)(2,1)} %copy-done.45), channel_id=1, source_target_pairs={{0,1},{1,0},{2,3},{3,2},{4,5},{5,4},{6,7},{7,6},{8,9},{9,8},{10,11... | collective-permute-start | bytes 2654216 | tf_op jit(solution)/shard_map/ppermute | solution.py:651
  215.1 37.0 %collective-permute-start.36 = (bf16[2,2,3,96,384]{4,3,2,1,0:T(8,128)(2,1)}, bf16[2,2,3,96,384]{4,3,2,1,0:T(8,128)(2,1)S(1)}, u32[]{:S(2)}, u32[]{:S(2)}) collective-permute-start(bf16[2,2,3,96,384]{4,3,2,1,0:T(8,128)(2,1)} %copy-done.46), channel_id=1, source_target_pairs={{0,1},{1,0},{2,3},{3,2},{4,5},{5,4},{6,7},{7,6},{8,9},{9,8},{10,11... | collective-permute-start | bytes 2654216 | tf_op jit(solution)/shard_map/ppermute | solution.py:651
  353.9 49.4 %collective-permute-start.66 = (bf16[2,2,3,3,96,384]{5,4,3,2,1,0:T(8,128)(2,1)}, bf16[2,2,3,3,96,384]{5,4,3,2,1,0:T(8,128)(2,1)S(1)}, u32[]{:S(2)}, u32[]{:S(2)}) collective-permute-start(bf16[2,2,3,3,96,384]{5,4,3,2,1,0:T(8,128)(2,1)} %get-tuple-element.101), channel_id=1, source_target_pairs={{0,1},{1,0},{2,3},{3,2},{4,5},{5,4},{6,7},{7,6},{8,9},{9,8},{10,11... | collective-permute-start | bytes 7962632 | tf_op jit(solution)/shard_map/ppermute | solution.py:651
  360.3 44.9 %collective-permute-start.69 = (bf16[2,2,3,3,96,384]{5,4,3,2,1,0:T(8,128)(2,1)}, bf16[2,2,3,3,96,384]{5,4,3,2,1,0:T(8,128)(2,1)S(1)}, u32[]{:S(2)}, u32[]{:S(2)}) collective-permute-start(bf16[2,2,3,3,96,384]{5,4,3,2,1,0:T(8,128)(2,1)} %get-tuple-element.103), channel_id=1, source_target_pairs={{0,1},{1,0},{2,3},{3,2},{4,5},{5,4},{6,7},{7,6},{8,9},{9,8},{10,11... | collective-permute-start | bytes 7962632 | tf_op jit(solution)/shard_map/ppermute | solution.py:651
  364.8 42.5 %collective-permute-start.47 = (bf16[2,2,3,3,96,384]{5,4,3,2,1,0:T(8,128)(2,1)S(1)}, bf16[2,2,3,3,96,384]{5,4,3,2,1,0:T(8,128)(2,1)S(1)}, u32[]{:S(2)}, u32[]{:S(2)}) collective-permute-start(bf16[2,2,3,3,96,384]{5,4,3,2,1,0:T(8,128)(2,1)S(1)} %copy-done.44), channel_id=1, source_target_pairs={{0,1},{1,0},{2,3},{3,2},{4,5},{5,4},{6,7},{7,6},{8,9},{9,8},{10,11... | collective-permute-start | bytes 7962632 | tf_op jit(solution)/shard_map/ppermute | solution.py:651
  373.3 35.7 %collective-permute-start.50 = (bf16[2,2,3,3,96,384]{5,4,3,2,1,0:T(8,128)(2,1)S(1)}, bf16[2,2,3,3,96,384]{5,4,3,2,1,0:T(8,128)(2,1)S(1)}, u32[]{:S(2)}, u32[]{:S(2)}) collective-permute-start(bf16[2,2,3,3,96,384]{5,4,3,2,1,0:T(8,128)(2,1)S(1)} %copy-done.43), channel_id=1, source_target_pairs={{0,1},{1,0},{2,3},{3,2},{4,5},{5,4},{6,7},{7,6},{8,9},{9,8},{10,11... | collective-permute-start | bytes 7962632 | tf_op jit(solution)/shard_map/ppermute | solution.py:651
  405.3 62.7 %collective-permute-start.67 = (bf16[2,3,3,96,384]{4,3,2,1,0:T(8,128)(2,1)S(1)}, bf16[2,3,3,96,384]{4,3,2,1,0:T(8,128)(2,1)S(1)}, u32[]{:S(2)}, u32[]{:S(2)}) collective-permute-start(bf16[2,3,3,96,384]{4,3,2,1,0:T(8,128)(2,1)S(1)} %get-tuple-element.125), channel_id=1, source_target_pairs={{0,2},{1,3},{2,0},{3,1},{4,6},{5,7},{6,4},{7,5},{8,10},{9,11},{10,... | collective-permute-start | bytes 3981320 | tf_op jit(solution)/shard_map/ppermute | solution.py:651
  407.3 61.8 %collective-permute-start.70 = (bf16[2,3,3,96,384]{4,3,2,1,0:T(8,128)(2,1)S(1)}, bf16[2,3,3,96,384]{4,3,2,1,0:T(8,128)(2,1)S(1)}, u32[]{:S(2)}, u32[]{:S(2)}) collective-permute-start(bf16[2,3,3,96,384]{4,3,2,1,0:T(8,128)(2,1)S(1)} %get-tuple-element.127), channel_id=1, source_target_pairs={{0,4},{1,5},{2,6},{3,7},{4,0},{5,1},{6,2},{7,3},{8,12},{9,13},{10,... | collective-permute-start | bytes 3981320 | tf_op jit(solution)/shard_map/ppermute | solution.py:651
  409.0 61.6 %collective-permute-start.48 = (bf16[2,3,3,96,384]{4,3,2,1,0:T(8,128)(2,1)S(1)}, bf16[2,3,3,96,384]{4,3,2,1,0:T(8,128)(2,1)S(1)}, u32[]{:S(2)}, u32[]{:S(2)}) collective-permute-start(bf16[2,3,3,96,384]{4,3,2,1,0:T(8,128)(2,1)S(1)} %get-tuple-element.129), channel_id=1, source_target_pairs={{0,2},{1,3},{2,0},{3,1},{4,6},{5,7},{6,4},{7,5},{8,10},{9,11},{10,... | collective-permute-start | bytes 3981320 | tf_op jit(solution)/shard_map/ppermute | solution.py:651
  410.8 61.6 %collective-permute-start.51 = (bf16[2,3,3,96,384]{4,3,2,1,0:T(8,128)(2,1)S(1)}, bf16[2,3,3,96,384]{4,3,2,1,0:T(8,128)(2,1)S(1)}, u32[]{:S(2)}, u32[]{:S(2)}) collective-permute-start(bf16[2,3,3,96,384]{4,3,2,1,0:T(8,128)(2,1)S(1)} %get-tuple-element.131), channel_id=1, source_target_pairs={{0,4},{1,5},{2,6},{3,7},{4,0},{5,1},{6,2},{7,3},{8,12},{9,13},{10,... | collective-permute-start | bytes 3981320 | tf_op jit(solution)/shard_map/ppermute | solution.py:651
  411.4 56.4 %collective-permute-start.46 = (bf16[1,3,96,384]{3,2,1,0:T(8,128)(2,1)S(1)}, bf16[1,3,96,384]{3,2,1,0:T(8,128)(2,1)S(1)}, u32[]{:S(2)}, u32[]{:S(2)}) collective-permute-start(bf16[1,3,96,384]{3,2,1,0:T(8,128)(2,1)S(1)} %fusion.47), channel_id=1, source_target_pairs={{0,2},{1,3},{2,0},{3,1},{4,6},{5,7},{6,4},{7,5},{8,10},{9,11},{10,... | collective-permute-start | bytes 663560 | tf_op jit(solution)/shard_map/ppermute | solution.py:651
  498.5 55.0 %collective-permute-start.54 = (bf16[6,96,384]{2,1,0:T(8,128)(2,1)S(1)}, bf16[6,96,384]{2,1,0:T(8,128)(2,1)S(1)}, u32[]{:S(2)}, u32[]{:S(2)}) collective-permute-start(bf16[6,96,384]{2,1,0:T(8,128)(2,1)S(1)} %get-tuple-element.151), channel_id=1, source_target_pairs={{0,16},{1,17},{2,18},{3,19},{4,20},{5,21},{6,22},{7,23},{8,24},{9,... | collective-permute-start | bytes 1327112 | tf_op jit(solution)/shard_map/ppermute | solution.py:651
  498.5 60.1 %collective-permute-start.55 = (bf16[6,96,384]{2,1,0:T(8,128)(2,1)S(1)}, bf16[6,96,384]{2,1,0:T(8,128)(2,1)S(1)}, u32[]{:S(2)}, u32[]{:S(2)}) collective-permute-start(bf16[6,96,384]{2,1,0:T(8,128)(2,1)S(1)} %get-tuple-element.150), channel_id=1, source_target_pairs={{0,24},{1,25},{2,26},{3,27},{4,28},{5,29},{6,30},{7,31},{8,0},{9,1... | collective-permute-start | bytes 1327112 | tf_op jit(solution)/shard_map/ppermute | solution.py:651
  509.6 52.2 %collective-permute-start.77 = (bf16[6,96,384]{2,1,0:T(8,128)(2,1)S(1)}, bf16[6,96,384]{2,1,0:T(8,128)(2,1)S(1)}, u32[]{:S(2)}, u32[]{:S(2)}) collective-permute-start(bf16[6,96,384]{2,1,0:T(8,128)(2,1)S(1)} %bitcast.266), channel_id=1, source_target_pairs={{0,2},{1,3},{2,0},{3,1},{4,6},{5,7},{6,4},{7,5},{8,10},{9,11},{10,... | collective-permute-start | bytes 1327112 | tf_op jit(solution)/shard_map/ppermute | solution.py:651
  519.9 50.2 %collective-permute-start.58 = (bf16[6,96,384]{2,1,0:T(8,128)(2,1)S(1)}, bf16[6,96,384]{2,1,0:T(8,128)(2,1)S(1)}, u32[]{:S(2)}, u32[]{:S(2)}) collective-permute-start(bf16[6,96,384]{2,1,0:T(8,128)(2,1)S(1)} %bitcast.265), channel_id=1, source_target_pairs={{0,2},{1,3},{2,0},{3,1},{4,6},{5,7},{6,4},{7,5},{8,10},{9,11},{10,... | collective-permute-start | bytes 1327112 | tf_op jit(solution)/shard_map/ppermute | solution.py:651
  521.1 40.1 %collective-permute-start.83 = (f32[144,128]{1,0:T(8,128)S(1)}, f32[144,128]{1,0:T(8,128)S(1)}, u32[]{:S(2)}, u32[]{:S(2)}) collective-permute-start(f32[144,128]{1,0:T(8,128)S(1)} %add.485), channel_id=1, source_target_pairs={{0,16},{1,17},{2,18},{3,19},{4,20},{5,21},{6,22},{7,23},{8,24},{9,... | collective-permute-start | bytes 221192 | tf_op jit(solution)/shard_map/ppermute | solution.py:651
  (105 other events, 1492.4 us)

commit v3 on v1

v3 whole, which is shorter than its diff:
```python
import functools

import jax
import jax.numpy as jnp
from jax import lax
from jax.experimental import pallas as pl
from jax.experimental.pallas import tpu as pltpu
from jax.sharding import PartitionSpec as P

HEADS = 12
LAYERS = 2
Z_SLABS = 4
BF = jnp.bfloat16
F32 = jnp.float32

norm_epsilon = 1e-05
matrix_rate = 1.0
small_rate = 0.3
decay_rate = 0.5
moment_epsilon = 1e-08

VMEM = pl.BlockSpec(memory_space=pltpu.VMEM)
SMEM = pl.BlockSpec(memory_space=pltpu.SMEM)
ANY = pl.BlockSpec(memory_space=pl.ANY)


def shape(dims, dtype):
    return jax.ShapeDtypeStruct(tuple(dims), dtype)


def mm(a, b):
    return jnp.dot(a, b, preferred_element_type=F32)


def mm_bt(a, b):
    return lax.dot_general(a, b, (((1,), (1,)), ((), ())), preferred_element_type=F32)


def mm_at(a, b):
    return lax.dot_general(a, b, (((0,), (0,)), ((), ())), preferred_element_type=F32)


class Part:
    def __init__(self, zs, js, order, arrays=None):
        self.zs, self.js, self.order, self.arrays = tuple(zs), tuple(js), order, arrays

    def index(self, first, second, z, j):
        place = self.zs.index(z) * len(self.js) + self.js.index(j)
        return (first * 2 + second) * len(self.zs) * len(self.js) + place

    def count(self):
        return 4 * len(self.zs) * len(self.js)


def launch(body, name, ins, out_shape, out_specs, deps=(), scratch=(), cost=None, aliases=None, limit=16, **grid):
    count, extra = len(ins), len(deps)

    def kernel(*refs):
        body(*refs[:count], *refs[count + extra :])

    flops, moved, special = cost or (0, 0, 0)
    return pl.pallas_call(
        kernel,
        in_specs=[spec for _, spec in ins] + [ANY] * extra,
        out_specs=out_specs,
        out_shape=out_shape,
        scratch_shapes=list(scratch),
        input_output_aliases=aliases or {},
        compiler_params=pltpu.CompilerParams(vmem_limit_bytes=limit << 20),
        cost_estimate=pl.CostEstimate(flops=flops, bytes_accessed=moved, transcendentals=special),
        name=name,
        **grid,
    )(*[array for array, _ in ins], *deps)


class Dims:
    def __init__(self, model, ffn, block, blocks, rows):
        self.model, self.ffn, self.block, self.blocks, self.rows = model, ffn, block, blocks, rows
        self.own = blocks // (2 * Z_SLABS)
        self.piece = block // 4
        wide, tall = model // block, ffn // block
        self.places = {}
        at = 0
        for name, rows_, cols_ in (
            ("q", wide, wide),
            ("k", wide, wide),
            ("v", wide, wide),
            ("o", wide, wide),
            ("up", wide, tall),
            ("down", tall, wide),
        ):
            self.places[name] = [
                (at + r * cols_ + c, r * block, c * block) for r in range(rows_) for c in range(cols_)
            ]
            at += rows_ * cols_

    def where(self, b):
        return b // (2 * self.own), (b // self.own) % 2, b % self.own


def find_part(parts, z, j):
    for number, part in enumerate(parts):
        if z in part.zs and j in part.js:
            return number
    raise ValueError("no part")


def needed_parts(dims, parts, names):
    used = set()
    for name in names:
        for b, _, _ in dims.places[name]:
            z, _, j = dims.where(b)
            used.add(find_part(parts, z, j))
    return [parts[n] for n in sorted(used)]


def start_loads(dims, parts, refs, pos, name, dst, row0, col0, sem):
    x, y, c = pos
    by_x = []

    def start(src, row, quarter, col):
        rows = pl.ds(pl.multiple_of(row0 + row + dims.piece * quarter, 16), dims.piece)
        pltpu.make_async_copy(src, dst.at[rows, pl.ds(col0 + col, dims.block)], sem).start()

    for b, row, col in dims.places[name]:
        z, xq, j = dims.where(b)
        number = find_part(parts, z, j)
        if parts[number].order == "xy":
            by_x.append((number, z, xq, j, row, col))
            continue
        for dc in range(2):
            for dy in range(2):
                src = refs[number][2 * dc + dy].at[parts[number].index(0, x ^ xq, z, j)]
                start(src, row, 2 * (y ^ dy) + (c ^ dc), col)
    if by_x:
        for own_x in range(2):

            @pl.when(x == own_x)
            def _(own_x=own_x):
                for number, z, xq, j, row, col in by_x:
                    for dc in range(2):
                        for yq in range(2):
                            src = refs[number][2 * dc + (own_x ^ xq)].at[parts[number].index(0, y ^ yq, z, j)]
                            start(src, row, 2 * yq + (c ^ dc), col)


def wait_for(ref, sem):
    pltpu.make_async_copy(ref, ref, sem).wait()


def start_stores(dims, parts, outs, pos, places, src, sem):
    x, y, c = pos
    for b, row, col in places:
        z, xq, j = dims.where(b)
        number = find_part(parts, z, j)
        for dc in range(2):
            for yq in range(2):
                ends = (x ^ xq, y ^ yq) if parts[number].order == "xy" else (y ^ yq, x ^ xq)
                rows = pl.ds(pl.multiple_of(row + dims.piece * (2 * yq + (c ^ dc)), 16), dims.piece)
                dst = outs[number][dc].at[parts[number].index(*ends, z, j)]
                pltpu.make_async_copy(src.at[rows, pl.ds(col, dims.block)], dst, sem).start()


def norm_forward(values):
    center = values - jnp.mean(values, axis=-1, keepdims=True)
    spread = jnp.mean(center * center, axis=-1, keepdims=True)
    inverse = lax.rsqrt(spread + norm_epsilon)
    return center * inverse, inverse


def norm_backward(gradient, unit, inverse, gain):
    scaled = gradient * gain
    inner = (
        scaled
        - jnp.mean(scaled, axis=-1, keepdims=True)
        - unit * jnp.mean(scaled * unit, axis=-1, keepdims=True)
    )
    return inverse * inner


def col_sum(values):
    return jnp.sum(values.astype(F32), axis=0, keepdims=True)


def put_rows(sums_ref, number, values):
    count = values.shape[1] // 128
    for n in range(count):
        at = number * count + n
        sums_ref[at : at + 1, :] = values[:, 128 * n : 128 * (n + 1)]


def segment(small_ref, number, width):
    return small_ref[0:1, number * width : (number + 1) * width]


def unflatten(refs, parts):
    return [refs[4 * n : 4 * n + 4] for n in range(len(parts))], refs[4 * len(parts) :]


def weight_ins(parts):
    return [(a, ANY) for p in parts for a in p.arrays]


def half_masks(head):
    lane = lax.broadcasted_iota(jnp.int32, (1, 2 * head), 1)
    low = lane < head
    ones = jnp.where(low, 1.0, 0.0).astype(F32)
    return low, (ones.astype(BF), (1.0 - ones).astype(BF))


def attention_forward_kernel(dims, parts, chains, pos_ref, len_ref, x_ref, small_ref, *rest):
    refs, rest = unflatten(rest, parts)
    qkv_ref, lse_ref, ctx_ref, unit_ref, inv_ref, w, sems = rest
    width, seq = dims.model, dims.rows // chains
    head = width // HEADS
    pos = (pos_ref[1], pos_ref[2], pos_ref[3])
    for n, name in enumerate(("q", "k", "v", "o")):
        start_loads(dims, parts, refs, pos, name, w, 0, n * width, sems.at[n])
    xb = x_ref[...].astype(BF)
    for n, bias in ((0, 0), (1, None), (2, 1)):
        cols = slice(n * width, (n + 1) * width)
        wait_for(w.at[:, cols], sems.at[n])
        out = mm(xb, w[:, cols])
        if bias is not None:
            out = out + segment(small_ref, bias, width)
        qkv_ref[:, cols] = out.astype(BF)
    low, masks = half_masks(head)
    scale = head**-0.5

    def chain(i, carry):
        rows = pl.ds(pl.multiple_of(i * seq, 16), seq)
        valid = lax.broadcasted_iota(jnp.int32, (seq, seq), 0) < len_ref[i]
        for pair in range(HEADS // 2):
            at = pair * 2 * head
            q = qkv_ref[rows, at : at + 2 * head]
            k = qkv_ref[rows, width + at : width + at + 2 * head]
            v = qkv_ref[rows, 2 * width + at : 2 * width + at + 2 * head]
            outs = []
            for h in range(2):
                s = jnp.where(valid, mm_bt(k, q * masks[h]) * scale, -1000000000.0)
                top = jnp.max(s, axis=0, keepdims=True)
                e = jnp.exp(s - top)
                total = jnp.sum(e, axis=0, keepdims=True)
                lse_ref[i, 2 * pair + h : 2 * pair + h + 1, :] = top + jnp.log(total)
                outs.append(mm_at((e * (1.0 / total)).astype(BF), v))
            ctx_ref[rows, at : at + 2 * head] = jnp.where(low, outs[0], outs[1]).astype(BF)
        return carry

    lax.fori_loop(0, chains, chain, 0)
    wait_for(w.at[:, 3 * width :], sems.at[3])
    attended = mm(ctx_ref[...], w[:, 3 * width :]) + segment(small_ref, 2, width)
    unit, inverse = norm_forward(x_ref[...].astype(F32) + attended)
    unit_ref[...] = unit
    inv_ref[...] = inverse


def attention_forward(dims, parts, pos, lengths, x, small, deps=()):
    parts = needed_parts(dims, parts, ("q", "k", "v", "o"))
    chains = lengths.shape[0]
    rows, width = dims.rows, dims.model
    return launch(
        functools.partial(attention_forward_kernel, dims, parts, chains),
        "attention_forward",
        [(pos, SMEM), (lengths, SMEM), (x, VMEM), (small, VMEM)] + weight_ins(parts),
        [
            shape((rows, 3 * width), BF),
            shape((chains, HEADS, rows // chains), F32),
            shape((rows, width), BF),
            shape((rows, width), F32),
            shape((rows, 1), F32),
        ],
        [VMEM] * 5,
        deps,
        [pltpu.VMEM((width, 4 * width), BF), pltpu.SemaphoreType.DMA((4,))],
        (12 * rows * width * width, 16 << 20, 1 << 20),
        limit=56,
    )


def ffn_forward_body(dims, small_ref, unit_ref, up, down, sems, act_ref, slope_ref):
    width = dims.model
    h1 = unit_ref[...] * segment(small_ref, 4, width) + segment(small_ref, 5, width)
    hb = h1.astype(BF)
    total = h1 + segment(small_ref, 3, width)
    wait_for(up, sems.at[0])
    for n in range(dims.ffn // width):
        cols = slice(n * width, (n + 1) * width)
        u = mm(hb, up[:, cols]) + segment(small_ref, 8 + n, width)
        cdf = 0.5 * (1.0 + lax.erf(u * 0.7071067811865476))
        act = (u * cdf).astype(BF)
        act_ref[:, cols] = act
        slope_ref[:, cols] = (cdf + u * (0.3989422804014327 * jnp.exp(-0.5 * u * u))).astype(BF)
        if n == 0:
            wait_for(down, sems.at[1])
        total = total + mm(act, down[cols, :])
    return total


def ffn_forward_kernel(dims, parts, pos_ref, unit_ref, small_ref, *rest):
    refs, rest = unflatten(rest, parts)
    act_ref, slope_ref, unit2_ref, inv2_ref, y_ref, up, down, sems = rest
    pos = (pos_ref[1], pos_ref[2], pos_ref[3])
    start_loads(dims, parts, refs, pos, "up", up, 0, 0, sems.at[0])
    start_loads(dims, parts, refs, pos, "down", down, 0, 0, sems.at[1])
    width = dims.model
    total = ffn_forward_body(dims, small_ref, unit_ref, up, down, sems, act_ref, slope_ref)
    unit, inverse = norm_forward(total)
    unit2_ref[...] = unit
    inv2_ref[...] = inverse
    y_ref[...] = unit * segment(small_ref, 6, width) + segment(small_ref, 7, width)


def ffn_forward(dims, parts, pos, unit, small, deps=()):
    parts = needed_parts(dims, parts, ("up", "down"))
    rows, width, ffn = dims.rows, dims.model, dims.ffn
    return launch(
        functools.partial(ffn_forward_kernel, dims, parts),
        "ffn_forward",
        [(pos, SMEM), (unit, VMEM), (small, VMEM)] + weight_ins(parts),
        [
            shape((rows, ffn), BF),
            shape((rows, ffn), BF),
            shape((rows, width), F32),
            shape((rows, 1), F32),
            shape((rows, width), F32),
        ],
        [VMEM] * 5,
        deps,
        [pltpu.VMEM((width, ffn), BF), pltpu.VMEM((ffn, width), BF), pltpu.SemaphoreType.DMA((2,))],
        (4 * rows * width * ffn, 24 << 20, 3 << 20),
        limit=56,
    )


def ffn_backward_body(
    dims, outs_parts, outs, pos, gy, small_ref, unit_ref, inv_ref, ctx_ref, unit2, inv2, act_ref, slope_ref,
    up, down, wo, grad_up, grad_down, grad_o, sem_out, gz1_ref, gctx_ref, sums_ref, wait_o,
):
    width = dims.model
    gain1, gain2 = segment(small_ref, 4, width), segment(small_ref, 6, width)

    def put(number, values):
        put_rows(sums_ref, number, values)

    put(6, col_sum(gy * unit2))
    put(7, col_sum(gy))
    gz2 = norm_backward(gy, unit2, inv2, gain2)
    gf = gz2.astype(BF)
    put(3, col_sum(gf))
    hb = (unit_ref[...] * gain1 + segment(small_ref, 5, width)).astype(BF)
    gh1 = gz2
    block = dims.block
    for n in range(dims.ffn // width):
        cols = slice(n * width, (n + 1) * width)
        gu = (slope_ref[:, cols].astype(F32) * mm_bt(gf, down[cols, :])).astype(BF)
        put(8 + n, col_sum(gu))
        grad_up[:, cols] = mm_at(hb, gu).astype(BF)
        grad_down[cols, :] = mm_at(act_ref[:, cols], gf).astype(BF)
        low, high = n * width, (n + 1) * width
        start_stores(
            dims, outs_parts, outs, pos,
            [p for p in dims.places["up"] if low <= p[2] < high], grad_up, sem_out.at[0],
        )
        start_stores(
            dims, outs_parts, outs, pos,
            [p for p in dims.places["down"] if low <= p[1] < high], grad_down, sem_out.at[1],
        )
        gh1 = gh1 + mm_bt(gu, up[:, cols])
    unit = unit_ref[...]
    put(4, col_sum(gh1 * unit))
    put(5, col_sum(gh1))
    gz1 = norm_backward(gh1, unit, inv_ref[...], gain1)
    gz1_ref[...] = gz1
    ga = gz1.astype(BF)
    put(2, col_sum(ga))
    grad_o[...] = mm_at(ctx_ref[...], ga).astype(BF)
    start_stores(dims, outs_parts, outs, pos, dims.places["o"], grad_o, sem_out.at[2])
    wait_o()
    gctx_ref[...] = mm_bt(ga, wo[...]).astype(BF)
    put(0, jnp.zeros((1, width), F32))
    put(1, jnp.zeros((1, width), F32))
    wait_for(grad_up, sem_out.at[0])
    wait_for(grad_down, sem_out.at[1])
    wait_for(grad_o, sem_out.at[2])


def grad_shapes(dims, parts):
    return [shape((p.count(), dims.piece, dims.block), BF) for p in parts for _ in range(2)]


def pair_up(arrays, parts):
    return [Part(p.zs, p.js, p.order, list(arrays[2 * n : 2 * n + 2])) for n, p in enumerate(parts)]


def ffn_scratch(dims):
    width, ffn = dims.model, dims.ffn
    matrices = [(width, ffn), (ffn, width), (width, width)] * 2
    return [pltpu.VMEM(m, BF) for m in matrices] + [pltpu.SemaphoreType.DMA((3,))] * 2


def ffn_backward_kernel(dims, parts, outs_parts, pos_ref, gy_ref, small_ref, unit_ref, inv_ref, ctx_ref, unit2_ref, inv2_ref, act_ref, slope_ref, *rest):
    refs, rest = unflatten(rest, parts)
    gz1_ref, gctx_ref, sums_ref, *rest = rest
    count = 2 * len(outs_parts)
    outs = [rest[2 * n : 2 * n + 2] for n in range(len(outs_parts))]
    up, down, wo, grad_up, grad_down, grad_o, sems, sem_out = rest[count:]
    pos = (pos_ref[1], pos_ref[2], pos_ref[3])
    start_loads(dims, parts, refs, pos, "down", down, 0, 0, sems.at[1])
    start_loads(dims, parts, refs, pos, "up", up, 0, 0, sems.at[0])
    start_loads(dims, parts, refs, pos, "o", wo, 0, 0, sems.at[2])
    wait_for(down, sems.at[1])
    wait_for(up, sems.at[0])
    ffn_backward_body(
        dims, outs_parts, outs, pos, gy_ref[...], small_ref, unit_ref, inv_ref, ctx_ref,
        unit2_ref[...], inv2_ref[...], act_ref, slope_ref, up, down, wo, grad_up, grad_down, grad_o,
        sem_out, gz1_ref, gctx_ref, sums_ref, lambda: wait_for(wo, sems.at[2]),
    )


def ffn_backward(dims, parts, outs_parts, pos, gy, small, unit, inv, ctx, unit2, inv2, act, slope, deps=()):
    parts = needed_parts(dims, parts, ("up", "down", "o"))
    rows, width, ffn = dims.rows, dims.model, dims.ffn
    grads = grad_shapes(dims, outs_parts)
    out = launch(
        functools.partial(ffn_backward_kernel, dims, parts, outs_parts),
        "ffn_backward",
        [(pos, SMEM)]
        + [(a, VMEM) for a in (gy, small, unit, inv, ctx, unit2, inv2, act, slope)]
        + weight_ins(parts),
        [shape((rows, width), F32), shape((rows, width), BF), shape((small.shape[1] // 128, 128), F32)] + grads,
        [VMEM] * 3 + [ANY] * len(grads),
        deps,
        ffn_scratch(dims),
        (8 * rows * width * ffn + 4 * rows * width * width, 40 << 20, 0),
        limit=56,
    )
    return out[0], out[1], out[2], pair_up(out[3:], outs_parts)


def ffn_both_kernel(dims, parts, outs_parts, chains, pos_ref, len_ref, cot_ref, small_ref, unit_ref, inv_ref, ctx_ref, *rest):
    refs, rest = unflatten(rest, parts)
    y_ref, gz1_ref, gctx_ref, sums_ref, *rest = rest
    count = 2 * len(outs_parts)
    outs = [rest[2 * n : 2 * n + 2] for n in range(len(outs_parts))]
    up, down, wo, grad_up, grad_down, grad_o, sems, sem_out, act_ref, slope_ref = rest[count:]
    pos = (pos_ref[1], pos_ref[2], pos_ref[3])
    start_loads(dims, parts, refs, pos, "up", up, 0, 0, sems.at[0])
    start_loads(dims, parts, refs, pos, "down", down, 0, 0, sems.at[1])
    start_loads(dims, parts, refs, pos, "o", wo, 0, 0, sems.at[2])
    width, seq = dims.model, dims.rows // chains
    total = ffn_forward_body(dims, small_ref, unit_ref, up, down, sems, act_ref, slope_ref)
    unit2, inv2 = norm_forward(total)
    y_ref[...] = (unit2 * segment(small_ref, 6, width) + segment(small_ref, 7, width)).astype(BF)
    place = lax.broadcasted_iota(jnp.int32, (seq, width), 0)
    gy = jnp.concatenate(
        [
            jnp.where(place < len_ref[i], cot_ref[i * seq : (i + 1) * seq, :].astype(F32), 0.0)
            for i in range(chains)
        ],
        axis=0,
    )
    ffn_backward_body(
        dims, outs_parts, outs, pos, gy, small_ref, unit_ref, inv_ref, ctx_ref,
        unit2, inv2, act_ref, slope_ref, up, down, wo, grad_up, grad_down, grad_o,
        sem_out, gz1_ref, gctx_ref, sums_ref, lambda: wait_for(wo, sems.at[2]),
    )


def ffn_both(dims, parts, outs_parts, pos, lengths, cot, small, unit, inv, ctx, deps=()):
    parts = needed_parts(dims, parts, ("up", "down", "o"))
    rows, width, ffn = dims.rows, dims.model, dims.ffn
    grads = grad_shapes(dims, outs_parts)
    out = launch(
        functools.partial(ffn_both_kernel, dims, parts, outs_parts, lengths.shape[0]),
        "ffn_both",
        [(pos, SMEM), (lengths, SMEM)]
        + [(a, VMEM) for a in (cot, small, unit, inv, ctx)]
        + weight_ins(parts),
        [
            shape((rows, width), BF),
            shape((rows, width), F32),
            shape((rows, width), BF),
            shape((small.shape[1] // 128, 128), F32),
        ]
        + grads,
        [VMEM] * 4 + [ANY] * len(grads),
        deps,
        ffn_scratch(dims) + [pltpu.VMEM((rows, ffn), BF)] * 2,
        (12 * rows * width * ffn + 4 * rows * width * width, 40 << 20, 3 << 20),
        limit=56,
    )
    return out[0], out[1], out[2], out[3], pair_up(out[4:], outs_parts)


def attention_backward_kernel(dims, parts, outs_parts, chains, given, pos_ref, len_ref, gz1_ref, gctx_ref, qkv_ref, lse_ref, x_ref, *rest):
    given_refs, rest = rest[:given], rest[given:]
    refs, rest = unflatten(rest, parts)
    gx_ref, sums_ref, *rest = rest
    count = 2 * len(outs_parts)
    outs = [rest[2 * n : 2 * n + 2] for n in range(len(outs_parts))]
    w, grads_ref, grad_w, sems, sem_out = rest[count:]
    pos = (pos_ref[1], pos_ref[2], pos_ref[3])
    width, seq = dims.model, dims.rows // chains
    head = width // HEADS
    names = ("q", "k", "v")
    for n, name in enumerate(names):
        start_loads(dims, parts, refs, pos, name, w, 0, n * width, sems.at[n])
    low, masks = half_masks(head)
    scale = head**-0.5

    def chain(i, carry):
        rows = pl.ds(pl.multiple_of(i * seq, 16), seq)
        valid = lax.broadcasted_iota(jnp.int32, (seq, seq), 0) < len_ref[i]
        for pair in range(HEADS // 2):
            at = pair * 2 * head
            q = qkv_ref[rows, at : at + 2 * head]
            k = qkv_ref[rows, width + at : width + at + 2 * head]
            v = qkv_ref[rows, 2 * width + at : 2 * width + at + 2 * head]
            g = gctx_ref[rows, at : at + 2 * head]
            gq, gk, gv = [], [], []
            for h in range(2):
                s = jnp.where(valid, mm_bt(k, q * masks[h]) * scale, -1000000000.0)
                p = jnp.exp(s - lse_ref[i, 2 * pair + h : 2 * pair + h + 1, :])
                gp = mm_bt(v, g * masks[h])
                inner = jnp.sum(p * gp, axis=0, keepdims=True)
                gs = (p * (gp - inner)).astype(BF)
                gv.append(mm(p.astype(BF), g))
                gk.append(mm(gs, q))
                gq.append(mm_at(gs, k))
            grads_ref[rows, at : at + 2 * head] = (jnp.where(low, gq[0], gq[1]) * scale).astype(BF)
            grads_ref[rows, width + at : width + at + 2 * head] = (
                jnp.where(low, gk[0], gk[1]) * scale
            ).astype(BF)
            grads_ref[rows, 2 * width + at : 2 * width + at + 2 * head] = jnp.where(
                low, gv[0], gv[1]
            ).astype(BF)
        return carry

    lax.fori_loop(0, chains, chain, 0)
    xb = x_ref[...].astype(BF)
    for n, name in enumerate(names):
        cols = slice(n * width, (n + 1) * width)
        grad_w[:, cols] = mm_at(xb, grads_ref[:, cols]).astype(BF)
        places = [(b, r, c + n * width) for b, r, c in dims.places[name]]
        start_stores(dims, outs_parts, outs, pos, places, grad_w, sem_out)
    at = 0
    for ref in given_refs:
        sums_ref[at : at + ref.shape[0], :] = ref[...]
        at += ref.shape[0]
    put_rows(sums_ref, 0, col_sum(grads_ref[:, :width]))
    put_rows(sums_ref, 1, col_sum(grads_ref[:, 2 * width :]))
    gx = gz1_ref[...]
    for n in range(3):
        cols = slice(n * width, (n + 1) * width)
        wait_for(w.at[:, cols], sems.at[n])
        gx = gx + mm_bt(grads_ref[:, cols], w[:, cols])
    gx_ref[...] = gx
    wait_for(grad_w, sem_out)


def attention_backward(dims, parts, outs_parts, pos, lengths, gz1, gctx, qkv, lse, x, sums, deps=()):
    parts = needed_parts(dims, parts, ("q", "k", "v"))
    rows, width = dims.rows, dims.model
    grads = grad_shapes(dims, outs_parts)
    out = launch(
        functools.partial(attention_backward_kernel, dims, parts, outs_parts, lengths.shape[0], len(sums)),
        "attention_backward",
        [(pos, SMEM), (lengths, SMEM)] + [(a, VMEM) for a in (gz1, gctx, qkv, lse, x, *sums)] + weight_ins(parts),
        [shape((rows, width), F32), shape((sum(a.shape[0] for a in sums), 128), F32)] + grads,
        [VMEM] * 2 + [ANY] * len(grads),
        deps,
        [
            pltpu.VMEM((width, 3 * width), BF),
            pltpu.VMEM((rows, 3 * width), BF),
            pltpu.VMEM((width, 3 * width), BF),
            pltpu.SemaphoreType.DMA((3,)),
            pltpu.SemaphoreType.DMA,
        ],
        (24 * rows * width * width, 24 << 20, 1 << 20),
        limit=56,
    )
    return out[0], out[1], pair_up(out[2:], outs_parts)


class AnySlice:
    def __init__(self, dims):
        self.dims = dims
        own = range(dims.own)
        self.early = [Part((1, 2, 3), own, "yx")]
        self.late = [Part((0,), own, "yx")]

    def position(self):
        return jnp.zeros((4,), jnp.int32)

    def gather(self, low):
        dims = self.dims
        whole = lax.all_gather(low, "fsdp", axis=1, tiled=True)
        whole = lax.all_gather(whole, "grp", axis=0, tiled=True)
        split = whole.reshape(Z_SLABS, 2, dims.own, 2, 2, dims.piece, dims.block)
        order = split.transpose(4, 3, 1, 0, 2, 5, 6).reshape(4, -1, dims.piece, dims.block)
        return [Part(range(Z_SLABS), range(dims.own), "yx", [order[n] for n in range(4)])]

    def reduce(self, early, late):
        dims = self.dims
        pieces = []
        for part in (late[0], early[0]):
            stacked = jnp.stack(part.arrays)
            split = stacked.reshape(2, 2, 2, len(part.zs), dims.own, dims.piece, dims.block)
            pieces.append(split.transpose(3, 2, 4, 1, 0, 5, 6))
        whole = jnp.concatenate(pieces, axis=0).reshape(dims.blocks, dims.block, dims.block)
        rows = lax.psum_scatter(whole, "fsdp", scatter_dimension=1, tiled=True)
        return lax.psum_scatter(rows, "grp", scatter_dimension=0, tiled=True).astype(F32)

    def small_sum(self, values):
        return lax.psum(values, ("grp", "fsdp"))

    def group(self, owned):
        return lax.all_gather(owned, "fsdp", axis=1, tiled=True)


def swap_of(axis):
    def move(z, x, y, c):
        return (z, x ^ (axis == "x"), y ^ (axis == "y"), c ^ (axis == "c"))

    return move


def join_kernel(ranges, *refs):
    pairs = len(ranges)
    ins, outs, holds, sems = refs[: 2 * pairs], refs[2 * pairs : 3 * pairs], refs[3 * pairs : -2], refs[-2:]
    for n, (low, count) in enumerate(ranges):
        for half in range(2):
            src = ins[2 * n + half].at[pl.ds(low, count)]
            dst = holds[n].at[pl.ds(half * count, count)]
            pltpu.make_async_copy(src, dst, sems[0].at[n]).start()
    for n in range(pairs):
        wait_for(holds[n], sems[0].at[n])
        pltpu.make_async_copy(holds[n], outs[n], sems[1].at[n]).start()
    for n in range(pairs):
        wait_for(holds[n], sems[1].at[n])


def stack_kernel(zs, halves, pos_ref, *refs):
    ins, outs, holds, sems = refs[:Z_SLABS], refs[Z_SLABS:-4], refs[-4:-2], refs[-2:]
    z = pos_ref[0]
    for n, (low, high) in enumerate(halves):
        for place, want in enumerate(zs):
            for k in range(Z_SLABS):

                @pl.when(lax.rem(z - want + Z_SLABS, Z_SLABS) == k)
                def _(n=n, low=low, high=high, place=place, k=k):
                    dst = holds[n].at[pl.ds(place * (high - low), high - low)]
                    pltpu.make_async_copy(ins[k].at[pl.ds(low, high - low)], dst, sems[0].at[n]).start()

    for n in range(2):
        wait_for(holds[n], sems[0].at[n])
        pltpu.make_async_copy(holds[n], outs[n], sems[1].at[n]).start()
    for n in range(2):
        wait_for(holds[n], sems[1].at[n])


def round_kernel(src_ref, dst_ref):
    dst_ref[...] = src_ref[...].astype(BF)


def add_kernel(a_ref, b_ref, first_ref, second_ref):
    half = first_ref.shape[0]

    def piece(i, carry):
        for out, at in ((first_ref, i), (second_ref, i + half)):
            out[i] = (a_ref[at].astype(F32) + b_ref[at].astype(F32)).astype(BF)
        return carry

    lax.fori_loop(0, half, piece, 0)


def collect_kernel(zs, *refs):
    ins, out = refs[:-1], refs[-1]
    base = min(min(z_list) for z_list in zs)
    half = ins[0].shape[0] // len(zs[0])
    for n, z_list in enumerate(zs):
        for place, want in enumerate(z_list):
            piece = pl.ds(place * half, half)
            total = ins[2 * n][piece].astype(F32) + ins[2 * n + 1][piece].astype(F32)
            out[pl.ds((2 * (want - base) + n % 2) * half, half)] = total.astype(BF)


def pick_kernel(places, src_ref, *refs):
    outs, holds, sems = refs[: len(places)], refs[len(places) : -2], refs[-2:]
    for n, runs in enumerate(places):
        at = 0
        for low, count in runs:
            dst = holds[n].at[pl.ds(at, count)]
            pltpu.make_async_copy(src_ref.at[pl.ds(low, count)], dst, sems[0].at[n]).start()
            at += count
    for n in range(len(places)):
        wait_for(holds[n], sems[0].at[n])
        pltpu.make_async_copy(holds[n], outs[n], sems[1].at[n]).start()
    for n in range(len(places)):
        wait_for(holds[n], sems[1].at[n])


def pass_kernel(*refs):
    pass


def total_kernel(own_ref, *refs):
    *got, wide_ref, low_ref = refs
    total = own_ref[...].astype(F32)
    for ref in got:
        total = total + ref[...].astype(F32)
    wide_ref[...] = total
    low_ref[...] = total.astype(BF)


class SmallSlice:
    def __init__(self, dims):
        self.dims = dims
        a, b = range(dims.own // 2), range(dims.own // 2, dims.own)
        self.early = [Part((1, 2, 3), a, "yx"), Part((1, 2, 3), b, "xy")]
        self.late = [Part((0,), a, "yx"), Part((0,), b, "xy")]
        group, shard = lax.axis_index("grp"), lax.axis_index("fsdp")
        self.z, self.x, self.y, self.c = group // 2, group % 2, shard // 2, shard % 2
        self.pos = jnp.stack([self.z, self.x, self.y, self.c]).astype(jnp.int32)

    def position(self):
        return self.pos

    def pieces(self, count):
        return shape((count, self.dims.piece, self.dims.block), BF)

    def permute(self, array, move):
        pairs = []
        for flat in range(8 * Z_SLABS):
            to = move(flat // 8, flat // 4 % 2, flat // 2 % 2, flat % 2)
            if to is not None:
                pairs.append((flat, ((to[0] * 2 + to[1]) * 2 + to[2]) * 2 + to[3]))
        return lax.ppermute(array, ("grp", "fsdp"), pairs)

    def swap(self, array, axis):
        return self.permute(array, swap_of(axis))

    def rounded(self, wide, deps=()):
        return launch(round_kernel, "rounded", [(wide, VMEM)], shape(wide.shape, BF), VMEM, deps)

    def from_slabs(self, own):
        return [own] + [
            self.permute(own, lambda z, x, y, c, k=k: ((z + k) % Z_SLABS, x, y, c)) for k in range(1, Z_SLABS)
        ]

    def lot(self, slabs, zs, js, deps=()):
        half = len(js) // 2
        halves = [(0, half), (half, len(js))]
        sizes = [self.pieces(len(zs) * (high - low)) for low, high in halves]
        arrays = launch(
            functools.partial(stack_kernel, zs, halves),
            "stack",
            [(self.pos, SMEM)] + [(a, ANY) for a in slabs],
            sizes,
            [ANY] * 2,
            deps,
            [pltpu.VMEM(s.shape, BF) for s in sizes] + [pltpu.SemaphoreType.DMA((2,))] * 2,
        )
        return [(Part(zs, js[low:high], order), a) for (low, high), order, a in zip(halves, ("yx", "xy"), arrays)]

    def columns(self):
        return [[2 * z + x for z in range(Z_SLABS)] for x in range(2)]

    def whole_column(self, own):
        return lax.all_gather(own, "grp", axis_index_groups=self.columns(), axis=0, tiled=True)

    def whole_lot(self, whole, zs, js, deps=()):
        half, count = len(js) // 2, self.dims.own
        places = [[(z * count + js[low], half) for z in zs] for low in (0, half)]
        sizes = [self.pieces(len(zs) * half)] * 2
        arrays = launch(
            functools.partial(pick_kernel, places),
            "pick",
            [(whole, ANY)],
            sizes,
            [ANY] * 2,
            deps,
            [pltpu.VMEM(s.shape, BF) for s in sizes] + [pltpu.SemaphoreType.DMA((2,))] * 2,
        )
        halves = ((js[:half], "yx"), (js[half:], "xy"))
        return [(Part(zs, j, order), a) for (j, order), a in zip(halves, arrays)]

    def gate(self, arrays, deps):
        return launch(
            pass_kernel,
            "gate",
            [(a, ANY) for a in arrays],
            [shape(a.shape, a.dtype) for a in arrays],
            [ANY] * len(arrays),
            deps,
            aliases={n: n for n in range(len(arrays))},
        )

    def hold(self, parts, deps):
        for part, array in zip(parts, self.gate([p.arrays[1] for p in parts], deps)):
            part.arrays[1] = array

    def first_swap(self, lot):
        return [self.swap(a, part.order[1]) for part, a in lot]

    def joined(self, lot, got, zs, deps=()):
        ins, ranges, sizes = [], [], []
        for (part, own), g in zip(lot, got):
            count = len(part.js)
            ranges.append((part.zs.index(zs[0]) * count, len(zs) * count))
            sizes.append(self.pieces(2 * len(zs) * count))
            ins += [own, g]
        return launch(
            functools.partial(join_kernel, ranges),
            "join",
            [(a, ANY) for a in ins],
            sizes,
            [ANY] * len(lot),
            deps,
            [pltpu.VMEM(s.shape, BF) for s in sizes] + [pltpu.SemaphoreType.DMA((2,))] * 2,
        )

    def second_swap(self, lot, both):
        return [self.swap(b, part.order[0]) for (part, _), b in zip(lot, both)]

    def core_swap(self, lot, zs, both, got):
        return [
            Part(zs, part.js, part.order, [b, g, self.swap(b, "c"), self.swap(g, "c")])
            for (part, _), b, g in zip(lot, both, got)
        ]

    def add(self, keep, got, deps=()):
        sums = []
        for own, other in zip(keep, got):
            out = [self.pieces(own.shape[0] // 2)] * 2
            sums.append(launch(add_kernel, "add", [(own, VMEM), (other, VMEM)], out, [VMEM] * 2, deps))
        return [kept for kept, _ in sums], [sent for _, sent in sums]

    def core_sum(self, parts, deps=()):
        got = [self.swap(p.arrays[1], "c") for p in parts]
        return self.add([p.arrays[0] for p in parts], got, deps)

    def swaps(self, sums, axes):
        return [self.swap(a, axis) for a, axis in zip(sums[1], axes)]

    def collect(self, zs, sums, got, deps=()):
        ins = []
        for (kept, _), others in zip(sums, got):
            for own, other in zip(kept, others):
                ins += [own, other]
        return launch(
            functools.partial(collect_kernel, [z for z in zs for _ in range(2)]),
            "collect",
            [(a, VMEM) for a in ins],
            self.pieces(sum(len(z) for z in zs) * self.dims.own),
            VMEM,
            deps,
        )

    def deal(self, whole):
        split = whole.reshape((Z_SLABS, self.dims.own) + whole.shape[1:])
        got = []
        for k in range(Z_SLABS):
            mine = lax.dynamic_index_in_dim(split, (self.z + k) % Z_SLABS, 0, keepdims=False)
            if k > 0:
                mine = self.permute(mine, lambda z, x, y, c, k=k: ((z + k) % Z_SLABS, x, y, c))
            got.append(mine)
        return got

    def slab_sum(self, dealt, deps=()):
        size = dealt[0].shape
        return launch(
            total_kernel,
            "total",
            [(a, VMEM) for a in dealt],
            [shape(size, F32), shape(size, BF)],
            [VMEM] * 2,
            deps,
        )

    def column_sum(self, whole):
        return lax.psum_scatter(
            whole, "grp", axis_index_groups=self.columns(), scatter_dimension=0, tiled=True
        )

    def whole_group(self, own):
        return [lax.all_gather(own, "fsdp", axis=0, tiled=True)]

    def small_sum_column(self, values):
        for bit in (1, 2):
            values = values + self.permute(values, lambda z, x, y, c, bit=bit: (z ^ bit, x, y, c))
        return values

    def small_sum_plane(self, values):
        for axis in ("c", "x", "y"):
            values = values + self.swap(values, axis)
        return values

    def group(self, own):
        other = self.swap(own, "y")
        return [own, other, self.swap(own, "c"), self.swap(other, "c")]


def update_kernel(layer, first, count_grads, pos_ref, own_ref, *rest):
    stats, grads, rest = rest[:4], rest[4 : 4 + count_grads], rest[4 + count_grads :]
    roots, rest = rest[:4], rest[4:]
    if not first:
        rest = rest[5:]
    outs, rest = rest[:5], rest[5:]
    g_ref, r_ref, gram_ref, own, held, fresh, low_ref, sem_g, sem_r, sem_in, sem_out = rest
    y, c = pos_ref[2], pos_ref[3]
    count, piece, block = own_ref.shape

    def quarter(yq, cq):
        return pl.ds(pl.multiple_of(piece * (2 * yq + cq), 16), piece)

    for n in range(count_grads):
        rows = quarter(y ^ (n % 2), c ^ (n // 2)) if count_grads == 4 else pl.ds(0, block)
        if count_grads == 4:
            pltpu.make_async_copy(grads[n], g_ref.at[:, rows, :], sem_g).start()
    if count_grads == 1:
        for n in range(4):
            mine = grads[0].at[pl.ds(n * count, count)]
            pltpu.make_async_copy(mine, g_ref.at[:, pl.ds(n * piece, piece), :], sem_g).start()
    for n in range(4):
        mine = roots[n].at[pl.ds(layer * count, count)]
        pltpu.make_async_copy(mine, r_ref.at[:, quarter(y ^ (n % 2), c ^ (n // 2)), :], sem_r).start()
    for n in range(4):
        pltpu.make_async_copy(stats[n].at[layer], held.at[n], sem_in.at[n]).start()
    pltpu.make_async_copy(own_ref, own, sem_in.at[4]).start()
    own_rows = quarter(y, c)
    wait_for(g_ref, sem_g)
    for b in range(count):
        g = g_ref[b]
        if b == 0:
            wait_for(held.at[0], sem_in.at[0])
        fresh[1, b] = decay_rate * held[0, b] + (1.0 - decay_rate) * mm_bt(g_ref[b, own_rows, :], g)
        gram_ref[...] = mm_at(g, g)
        if b == 0:
            wait_for(held.at[1], sem_in.at[1])
        fresh[2, b] = decay_rate * held[1, b] + (1.0 - decay_rate) * gram_ref[own_rows, :]
        if b == 0:
            wait_for(r_ref, sem_r)
        mixed = mm(g, r_ref[b])
        if b == 0:
            wait_for(held.at[2], sem_in.at[2])
        update = jnp.dot(held[2, b], mixed, preferred_element_type=F32, precision=lax.Precision.HIGHEST)
        if b == 0:
            wait_for(held.at[3], sem_in.at[3])
            wait_for(own, sem_in.at[4])
        master = held[3, b] - matrix_rate * update
        fresh[3, b] = master
        low_ref[b] = master.astype(BF)
        fresh[0, b] = own[b].astype(F32)
        for n in range(4):
            pltpu.make_async_copy(fresh.at[n, b], outs[n].at[layer, b], sem_out.at[0]).start()
        pltpu.make_async_copy(low_ref.at[b], outs[4].at[layer, b], sem_out.at[1]).start()
    wait_for(fresh, sem_out.at[0])
    wait_for(low_ref, sem_out.at[1])


def update_layer(layer, pos, own, left, right, left_roots, masters, grads, roots, before, deps=()):
    count, piece, block = own.shape
    whole = (LAYERS, count, piece, block)
    ins = [(pos, SMEM), (own, ANY)] + [(a, ANY) for a in (left, right, left_roots, masters)]
    ins += [(a, ANY) for a in grads] + [(a, ANY) for a in roots]
    aliases = {}
    if before is not None:
        aliases = {len(ins) + n: n for n in range(5)}
        ins += [(a, ANY) for a in before]
    return launch(
        functools.partial(update_kernel, layer, before is None, len(grads)),
        "update_layer",
        ins,
        [shape(whole, F32)] * 4 + [shape(whole, BF)],
        [ANY] * 5,
        deps,
        [
            pltpu.VMEM((count, block, block), BF),
            pltpu.VMEM((count, block, block), BF),
            pltpu.VMEM((block, block), F32),
            pltpu.VMEM(own.shape, own.dtype),
            pltpu.VMEM((4,) + own.shape, F32),
            pltpu.VMEM((4,) + own.shape, F32),
            pltpu.VMEM(own.shape, BF),
            pltpu.SemaphoreType.DMA,
            pltpu.SemaphoreType.DMA,
            pltpu.SemaphoreType.DMA((5,)),
            pltpu.SemaphoreType.DMA((2,)),
        ],
        (0, 0, 0),
        aliases,
        limit=56,
    )


def update_plain(net, owned, masters, left_stats, right_stats, left_roots, right_roots):
    own_rows = masters.shape[2]
    first_row = lax.axis_index("fsdp") * own_rows
    highest = lax.Precision.HIGHEST
    grads = jnp.stack(owned)
    whole = jnp.stack([net.group(g.astype(BF)) for g in owned]).astype(F32)
    roots = jnp.stack([net.group(right_roots[n].astype(BF)) for n in range(LAYERS)]).astype(F32)
    columns = lax.dynamic_slice_in_dim(whole, first_row, own_rows, 3)
    new_left = decay_rate * left_stats + (1.0 - decay_rate) * jnp.einsum(
        "lbrk,lbck->lbrc", grads, whole, precision=highest
    )
    new_right = decay_rate * right_stats + (1.0 - decay_rate) * jnp.einsum(
        "lbkr,lbkc->lbrc", columns, whole, precision=highest
    )
    mixed = jnp.einsum("lbrk,lbkc->lbrc", whole, roots, precision=highest)
    update = jnp.einsum("lbrk,lbkc->lbrc", left_roots, mixed, precision=highest)
    new_masters = masters - matrix_rate * update
    return grads, new_left, new_right, new_masters, new_masters.astype(BF)


def update_small_kernel(sums_ref, moments_ref, params_ref, grads_out, moments_out, params_out):
    count = moments_ref.shape[1] // 128
    for layer in range(LAYERS):
        for n in range(count):
            at, cols = layer * count + n, slice(128 * n, 128 * (n + 1))
            grads_out[layer : layer + 1, cols] = sums_ref[at : at + 1, :]
    grads = grads_out[...]
    moments = decay_rate * moments_ref[...] + (1.0 - decay_rate) * grads * grads
    moments_out[...] = moments
    params_out[...] = params_ref[...] - small_rate * grads / (jnp.sqrt(moments) + moment_epsilon)


def update_small(sums, moments, params):
    return launch(
        update_small_kernel,
        "update_small",
        [(a, VMEM) for a in (sums, moments, params)],
        [shape(moments.shape, F32)] * 3,
        [VMEM] * 3,
    )


def run_any(net, dims, small, lengths, x, cot, low):
    pos = net.position()
    weights = [net.gather(low[n]) for n in range(LAYERS)]
    last = LAYERS - 1
    saved = []
    for n in range(LAYERS):
        qkv, lse, ctx, unit, inv = attention_forward(dims, weights[n], pos, lengths, x, small[n])
        saved.append([x, qkv, lse, ctx, unit, inv])
        if n < last:
            *rest, x = ffn_forward(dims, weights[n], pos, unit, small[n])
            saved[n] += rest
    owned = [None] * LAYERS
    for n in reversed(range(LAYERS)):
        x, qkv, lse, ctx, unit, inv, *rest = saved[n]
        if n == last:
            y, gz1, gctx, sums_a, early = ffn_both(
                dims, weights[n], net.early, pos, lengths, cot, small[n], unit, inv, ctx
            )
        else:
            act, slope, unit2, inv2 = rest
            gz1, gctx, sums_a, early = ffn_backward(
                dims, weights[n], net.early, pos, gy, small[n], unit, inv, ctx, unit2, inv2, act, slope
            )
        sums = [sums_a] if n == last else [sums_a, sums]
        gy, sums, late = attention_backward(
            dims, weights[n], net.late, pos, lengths, gz1, gctx, qkv, lse, x, sums
        )
        owned[n] = net.reduce(early, late)
    return y, gy, owned, net.small_sum(sums)


def run_small(net, dims, small, lengths, x, cot, left_stats, right_stats, left_roots, right_roots, masters):
    pos = net.position()
    own, every = tuple(range(dims.own)), tuple(range(Z_SLABS))
    third = dims.own // 3

    low_zs, high_zs = every[: Z_SLABS // 2], every[Z_SLABS // 2 :]
    slabs = net.from_slabs(masters[0].astype(BF))
    low1 = net.rounded(masters[1], slabs[1:])
    whole1 = net.whole_column(low1)
    lot = net.lot(slabs, every, own, [low1])
    got = net.first_swap(lot)
    both = net.joined(lot, got, low_zs)
    both_b = net.joined(lot, got, high_zs, both)
    got = net.second_swap(lot, both)
    weights0 = net.core_swap(lot, low_zs, both, got)
    got = net.second_swap(lot, both_b)
    lot_b = net.whole_lot(whole1, every, own, both_b)
    qkv0, lse0, ctx0, unit0, inv0 = attention_forward(dims, weights0, pos, lengths, x, small[0], both_b)
    weights0 += net.core_swap(lot, high_zs, both_b, net.gate(got, [inv0]))

    lot = lot_b
    got = net.first_swap(lot)
    act0, slope0, unit0b, inv0b, y0 = ffn_forward(
        dims, weights0, pos, unit0, small[0], [a for _, a in lot]
    )
    both = net.joined(lot, got, low_zs, [inv0b])
    both_b = net.joined(lot, got, high_zs, both)
    got = net.second_swap(lot, both)
    weights1 = net.core_swap(lot, low_zs, both, got)
    got = net.second_swap(lot, both_b)
    qkv1, lse1, ctx1, unit1, inv1 = attention_forward(dims, weights1, pos, lengths, y0, small[1], both_b)
    got = net.gate(got, [inv1])
    weights1 += net.core_swap(lot, high_zs, both_b, got)

    roots = net.rounded(right_roots.reshape((-1,) + right_roots.shape[2:]), got)
    y1, gz1, gctx, sums, early1 = ffn_both(
        dims, weights1, net.early, pos, lengths, cot, small[1], unit1, inv1, ctx1, [roots]
    )
    roots_y = net.swap(roots, "y")
    net.hold(early1, [roots_y])
    roots = [roots, roots_y, net.swap(roots, "c"), net.swap(roots_y, "c")]

    split = ((0,), (1, 2, 3))
    early1 = net.core_sum(early1)
    gx1, sums1, late1 = attention_backward(
        dims, weights1, net.late, pos, lengths, gz1, gctx, qkv1, lse1, y0, [sums], early1[1]
    )
    got = net.swaps(early1, "yx")
    net.hold(late1, got)
    early1 = net.add(early1[0], got, [gx1])
    late1 = net.core_sum(late1, early1[1])
    got_l, got_e = net.swaps(late1, "yx"), net.swaps(early1, "xy")
    gz0, gctx0, sums, early0 = ffn_backward(
        dims, weights0, net.early, pos, gx1, small[0], unit0, inv0, ctx0, unit0b, inv0b, act0, slope0,
        [*early1[1], *late1[1]],
    )
    net.hold(early0, [*got_l, *got_e])
    late1 = net.add(late1[0], got_l)
    got_l = net.swaps(late1, "xy")
    early0 = net.core_sum(early0, late1[1])
    whole1 = net.collect(split, (late1, early1), (got_l, got_e), early0[1])
    gx0, sums, late0 = attention_backward(
        dims, weights0, net.late, pos, lengths, gz0, gctx0, qkv0, lse0, x, [sums, sums1], [whole1]
    )

    got = net.swaps(early0, "yx")
    net.hold(late0, got)
    early0 = net.add(early0[0], got, [gx0])
    late0 = net.core_sum(late0, early0[1])
    got_l, got_e = net.swaps(late0, "yx"), net.swaps(early0, "xy")
    late0 = net.add(late0[0], got_l, got_e)
    got_l = net.swaps(late0, "xy")
    whole0 = net.collect(split, (late0, early0), (got_l, got_e))
    (low1,) = net.gate([net.column_sum(whole1)], late0[1])
    dealt = net.deal(whole0)
    (sums,) = net.gate([sums], [whole0])
    sums = net.small_sum_plane(sums)

    def update(n, wide, grads, before):
        return update_layer(
            n, pos, wide, left_stats, right_stats, left_roots, masters, grads, roots, before, [whole0]
        )

    done = update(1, low1, net.whole_group(low1), None)
    wide0, low0 = net.slab_sum(dealt, [done[0], sums])
    (sums,) = net.gate([sums], [low0])
    sums = net.small_sum_column(sums)
    done = update(0, wide0, net.group(low0), done)
    return y1, gx0, done, sums


def local(
    inputs,
    lengths,
    cotangent,
    masters,
    small_params,
    small_moments,
    left_stats,
    right_stats,
    left_roots,
    right_roots,
):
    chains, seq, width = inputs.shape
    rows = chains * seq
    groups, shards = lax.axis_size("grp"), lax.axis_size("fsdp")
    block = masters.shape[3]
    ffn = small_params.shape[1] - 8 * width
    dims = Dims(width, ffn, block, groups * masters.shape[1], rows)
    small = [small_params[n : n + 1] for n in range(LAYERS)]
    x, cot = inputs.reshape(rows, width), cotangent.reshape(rows, width)
    if groups == 2 * Z_SLABS and shards == 4:
        net = SmallSlice(dims)
        y, gx, done, sums = run_small(
            net, dims, small, lengths, x, cot, left_stats, right_stats, left_roots, right_roots, masters
        )
    else:
        net = AnySlice(dims)
        low = [masters[n].astype(BF) for n in range(LAYERS)]
        y, gx, owned, sums = run_any(net, dims, small, lengths, x, cot, low)
        done = update_plain(net, owned, masters, left_stats, right_stats, left_roots, right_roots)
    weight_grads, new_left, new_right, new_masters, new_copies = done
    small_grads, new_moments, new_small = update_small(sums, small_moments, small_params)
    return (
        y.reshape(chains, seq, width),
        gx.reshape(chains, seq, width),
        weight_grads,
        small_grads,
        new_moments,
        new_small,
        new_left,
        new_right,
        new_masters,
        new_copies,
    )


def solution(mesh):
    tokens, blocks = P(("grp", "fsdp"), None, None), P(None, "grp", "fsdp", None)
    return jax.shard_map(
        local,
        mesh=mesh,
        in_specs=(tokens, P(("grp", "fsdp")), tokens, blocks, P(), P(), blocks, blocks, blocks, blocks),
        out_specs=(tokens, tokens, blocks, P(), P(), P(), blocks, blocks, blocks, blocks),
        check_vma=False,
    )
```

time: 1210 us -> 503 us (0.42)
  waiting for transfers between devices: 968 us -> 202 us
  starting transfers between devices: 0.51 us -> 67.7 us
  Pallas kernels: 126 us -> 172 us
  other arithmetic: 24.8 us -> 1.68 us
  matrix products: 16.1 us -> 0 us
    all_gather x8 -> x2, waiting for transfers between devices: 480 us -> 5.46 us  [the longest x1 5.44 us: whole_column(): lax.all_gather(own, 'grp', axis_index_groups=self.columns(), axis=0, tile...]
    reduce_scatter x4 -> x1, waiting for transfers between devices: 362 us -> 0.01 us  [column_sum(): lax.psum_scatter(whole, 'grp', axis_index_groups=self.columns(), scatter_...]
    ppermute x0 -> x69, waiting for transfers between devices: none -> 196 us  [permute(): return lax.ppermute(array, ('grp', 'fsdp'), pairs)]
    psum x1 -> x0, waiting for transfers between devices: 124 us -> none  [small_sum(): return lax.psum(values, ('grp', 'fsdp'))]
    ppermute x0 -> x69, starting transfers between devices: none -> 67.6 us  [permute(): return lax.ppermute(array, ('grp', 'fsdp'), pairs)]
    pallas_call x7 -> x46, Pallas kernels: 126 us -> 172 us  [launch(): pl.pallas_call(kernel, in_specs=[spec for _, spec in ins] + [ANY] * extra...]
    unnamed x43 -> x166, local copies, waits for them, and re-layouts: 4.01 us -> 34.4 us
    dot_general x8 -> x0, matrix products: 16.1 us -> none  [the longest x2 6.61 us: local(): mixed = jnp.einsum('brk,bkc->brc', whole, roots, precision=highest)]
  transfers between devices with their start and end apart: 13 -> 72, of which waited for: 13 -> 36; matrix products, arithmetic and copies ran while one was open for 4% -> 1% of each run, Pallas kernels for 2% -> 30%
where the time goes in v3:
time: 503 us; the launch traced here: 496 us
  waiting for transfers between devices  202 us (40%)
  Pallas kernels  172 us (34%)
  starting transfers between devices  67.7 us (13%)
  local copies, waits for them, and re-layouts  38.8 us (8%)
  between operations  14.9 us (3%)
    ppermute x69, waiting for transfers between devices, permute(): return lax.ppermute(array, ('grp', 'fsdp'), pairs)  196 us
    pallas_call x46, Pallas kernels, launch(): pl.pallas_call(kernel, in_specs=[spec for _, spec in ins] + [ANY] * extra...  172 us
    ppermute x69, starting transfers between devices, permute(): return lax.ppermute(array, ('grp', 'fsdp'), pairs)  67.6 us
    unnamed x166, local copies, waits for them, and re-layouts  34.4 us
  transfers between devices with their start and end apart: 72, of which 36 were waited for; matrix products, arithmetic and copies ran while one was open for 1% of the time, Pallas kernels for 30%

profile of v3, /device:TPU:0, one launch (start us, length us, event | category | flops | bytes accessed | tf_op | source)
XLA Modules:
  0.0 496.4 jit_solution(18054101943221547561)
XLA Ops:
  16.8 7.9 %collective-permute-done.refs_1_.refs_2_ = bf16[6,96,384]{2,1,0:T(8,128)(2,1)S(1)} collective-permute-done((bf16[6,96,384]{2,1,0:T(8,128)(2,1)S(1)}, bf16[6,96,384]{2,1,0:T(8,128)(2,1)S(1)}, u32[]{:S(2)}, u32[]{:S(2)}) %collective-permute-start) | collective-permute-done | bytes 442400 | tf_op jit(solution)/shard_map/ppermute | solution.py:738
  24.7 18.1 %collective-permute-done.1.refs_2_.refs_3_ = bf16[6,96,384]{2,1,0:T(8,128)(2,1)S(1)} collective-permute-done((bf16[6,96,384]{2,1,0:T(8,128)(2,1)S(1)}, bf16[6,96,384]{2,1,0:T(8,128)(2,1)S(1)}, u32[]{:S(2)}, u32[]{:S(2)}) %collective-permute-start.1) | collective-permute-done | bytes 442400 | tf_op jit(solution)/shard_map/ppermute | solution.py:738
  43.6 3.4 stack.21
  50.1 18.5 %collective-permute-done.3.refs_1_ = bf16[12,96,384]{2,1,0:T(8,128)(2,1)S(1)} collective-permute-done((bf16[12,96,384]{2,1,0:T(8,128)(2,1)S(1)}, bf16[12,96,384]{2,1,0:T(8,128)(2,1)S(1)}, u32[]{:S(2)}, u32[]{:S(2)}) %collective-permute-start.3) | collective-permute-done | bytes 884768 | tf_op jit(solution)/shard_map/ppermute | solution.py:738
  77.6 15.1 %collective-permute-done.8.refs_9_.refs_8_.refs_15_.refs_14_ = bf16[12,96,384]{2,1,0:T(8,128)(2,1)} collective-permute-done((bf16[12,96,384]{2,1,0:T(8,128)(2,1)}, bf16[12,96,384]{2,1,0:T(8,128)(2,1)}, u32[]{:S(2)}, u32[]{:S(2)}) %collective-permute-start.8) | collective-permute-done | bytes 884768 | tf_op jit(solution)/shard_map/ppermute | solution.py:738
  101.9 11.7 %attention_forward.2 = (bf16[480,2304]{1,0:T(8,128)(2,1)}, f32[3,12,160]{2,1,0:T(8,128)}, bf16[480,768]{1,0:T(8,128)(2,1)}, f32[480,768]{1,0:T(8,128)}, f32[480,1]{1,0:T(8,128)}) custom-call(s32[4]{0:T(128)} %copy-done.60, s32[3]{0:T(128)} %refs_1_.10, bf16[480,768]{1,0:T(8,128)(2,1)} %bitcast.26, f32[1,9216]{1,0:T(1,128)} %get-tuple-element.240.refs_3_.refs_2_, ...), custom_call_target="tpu_custom_call" | custom-call | flops 3397386240 | bytes 16777216 | tf_op jit(solution)/shard_map/attention_forward/pallas_call | solution.py:62
  116.5 5.4 %all-gather.3.cloned.1.call-done.refs_0_ = bf16[24,96,384]{2,1,0:T(8,128)(2,1)} async-done(((bf16[6,96,384]{2,1,0:T(8,128)(2,1)}), bf16[24,96,384]{2,1,0:T(8,128)(2,1)}) %all-gather.3.cloned.1.call-update) | async-done | bytes 1769488 | tf_op jit(solution)/shard_map/all_gather | solution.py:770
  130.3 13.1 %ffn_forward.1 = (bf16[480,3072]{1,0:T(8,128)(2,1)}, bf16[480,3072]{1,0:T(8,128)(2,1)}, f32[480,768]{1,0:T(8,128)}, f32[480,1]{1,0:T(8,128)}, f32[480,768]{1,0:T(8,128)}) custom-call(s32[4]{0:T(128)} %copy-done.60, f32[480,768]{1,0:T(8,128)} %get-tuple-element.129.refs_1_.refs_3_, f32[1,9216]{1,0:T(1,128)} %get-tuple-element.240.refs_3_.refs_2_, ...), custom_call_target="tpu_custom_call" | custom-call | flops 4529848320 | bytes 25165824 | tf_op jit(solution)/shard_map/ffn_forward/pallas_call | solution.py:62
  143.4 4.1 collective-permute-done.17.refs_1_
  156.0 17.7 %collective-permute-done.19.refs_5_.refs_8_.refs_9_ = bf16[12,96,384]{2,1,0:T(8,128)(2,1)S(1)} collective-permute-done((bf16[12,96,384]{2,1,0:T(8,128)(2,1)S(1)}, bf16[12,96,384]{2,1,0:T(8,128)(2,1)S(1)}, u32[]{:S(2)}, u32[]{:S(2)}) %collective-permute-start.19) | collective-permute-done | bytes 884768 | tf_op jit(solution)/shard_map/ppermute | solution.py:738
  179.3 12.0 %attention_forward.3 = (bf16[480,2304]{1,0:T(8,128)(2,1)}, f32[3,12,160]{2,1,0:T(8,128)}, bf16[480,768]{1,0:T(8,128)(2,1)}, f32[480,768]{1,0:T(8,128)}, f32[480,1]{1,0:T(8,128)}) custom-call(s32[4]{0:T(128)} %copy-done.60, s32[3]{0:T(128)} %refs_1_.10, f32[480,768]{1,0:T(8,128)} %get-tuple-element.135.refs_2_.refs_6_, f32[1,9216]{1,0:T(1,128)} %get-tuple-element.241.refs_3_, ...), custom_call_target="tpu_custom_call" | custom-call | flops 3397386240 | bytes 16777216 | tf_op jit(solution)/shard_map/attention_forward/pallas_call | solution.py:62
  191.3 7.2 %collective-permute-done.25.refs_0_ = bf16[12,96,384]{2,1,0:T(8,128)(2,1)S(1)} collective-permute-done((bf16[12,96,384]{2,1,0:T(8,128)(2,1)S(1)}, bf16[12,96,384]{2,1,0:T(8,128)(2,1)S(1)}, u32[]{:S(2)}, u32[]{:S(2)}) %collective-permute-start.25) | collective-permute-done | bytes 884768 | tf_op jit(solution)/shard_map/ppermute | solution.py:738
  204.4 25.4 %ffn_both.1 = (bf16[480,768]{1,0:T(8,128)(2,1)}, f32[480,768]{1,0:T(8,128)}, bf16[480,768]{1,0:T(8,128)(2,1)}, f32[72,128]{1,0:T(8,128)}, bf16[36,96,384]{2,1,0:...) custom-call(s32[4]{0:T(128)} %copy-done.60, s32[3]{0:T(128)} %refs_1_.10, ...), custom_call_target="tpu_custom_call" | custom-call | flops 14722007040 | bytes 41943040 | tf_op jit(solution)/shard_map/ffn_both/pallas_call | solution.py:62
  230.4 4.7 collective-permute-done.33.refs_1_
  242.1 20.2 %attention_backward.2 = (f32[480,768]{1,0:T(8,128)}, f32[72,128]{1,0:T(8,128)}, bf16[12,96,384]{2,1,0:T(8,128)(2,1)}, bf16[12,96,384]{2,1,0:T(8,128)(2,1)}, bf16...) custom-call(s32[4]{0:T(128)} %copy-done.60, s32[3]{0:T(128)} %refs_1_.10, f32[480,768]{1,0:T(8,128)} %get-tuple-element.147.refs_2_, ...), custom_call_target="tpu_custom_call" | custom-call | flops 6794772480 | bytes 25165824 | tf_op jit(solution)/shard_map/attention_backward/pallas_call | solution.py:62
  262.3 4.7 collective-permute-done.35.refs_1_.refs_3_
  267.0 5.0 %collective-permute-done.34.refs_1_.refs_2_ = bf16[18,96,384]{2,1,0:T(8,128)(2,1)S(1)} collective-permute-done((bf16[18,96,384]{2,1,0:T(8,128)(2,1)}, bf16[18,96,384]{2,1,0:T(8,128)(2,1)S(1)}, u32[]{:S(2)}, u32[]{:S(2)}) %collective-permute-start.34) | collective-permute-done | bytes 1327136 | tf_op jit(solution)/shard_map/ppermute | solution.py:738
  280.7 22.5 %ffn_backward.1 = (f32[480,768]{1,0:T(8,128)}, bf16[480,768]{1,0:T(8,128)(2,1)}, f32[72,128]{1,0:T(8,128)}, bf16[36,96,384]{2,1,0:T(8,128)(2,1)}, bf16[36,96,384...) custom-call(s32[4]{0:T(128)} %copy-done.60, ...), custom_call_target="tpu_custom_call" | custom-call | flops 10192158720 | bytes 41943040 | tf_op jit(solution)/shard_map/ffn_backward/pallas_call | solution.py:62
  308.2 5.5 %collective-permute-done.45.refs_1_ = bf16[36,96,384]{2,1,0:T(8,128)(2,1)S(1)} collective-permute-done((bf16[36,96,384]{2,1,0:T(8,128)(2,1)S(1)}, bf16[36,96,384]{2,1,0:T(8,128)(2,1)S(1)}, u32[]{:S(2)}, u32[]{:S(2)}) %collective-permute-start.45) | collective-permute-done | bytes 2654240 | tf_op jit(solution)/shard_map/ppermute | solution.py:738
  321.7 19.9 %attention_backward.3 = (f32[480,768]{1,0:T(8,128)}, f32[144,128]{1,0:T(8,128)}, bf16[12,96,384]{2,1,0:T(8,128)(2,1)}, bf16[12,96,384]{2,1,0:T(8,128)(2,1)}, bf1...) custom-call(s32[4]{0:T(128)} %copy-done.60, s32[3]{0:T(128)} %refs_1_.10, f32[480,768]{1,0:T(8,128)} %get-tuple-element.177.refs_2_, ...), custom_call_target="tpu_custom_call" | custom-call | flops 6794772480 | bytes 25165824 | tf_op jit(solution)/shard_map/attention_backward/pallas_call | solution.py:62
  341.6 9.5 %collective-permute-done.47.refs_3_.refs_1_ = bf16[18,96,384]{2,1,0:T(8,128)(2,1)S(1)} collective-permute-done((bf16[18,96,384]{2,1,0:T(8,128)(2,1)}, bf16[18,96,384]{2,1,0:T(8,128)(2,1)S(1)}, u32[]{:S(2)}, u32[]{:S(2)}) %collective-permute-start.47) | collective-permute-done | bytes 1327136 | tf_op jit(solution)/shard_map/ppermute | solution.py:738
  359.9 12.0 %collective-permute-done.51.refs_3_.refs_7_ = bf16[9,96,384]{2,1,0:T(8,128)(2,1)S(1)} collective-permute-done((bf16[9,96,384]{2,1,0:T(8,128)(2,1)S(1)}, bf16[9,96,384]{2,1,0:T(8,128)(2,1)S(1)}, u32[]{:S(2)}, u32[]{:S(2)}) %collective-permute-start.51) | collective-permute-done | bytes 663584 | tf_op jit(solution)/shard_map/ppermute | solution.py:738
  374.4 7.3 %collective-permute-done.54.refs_1_ = bf16[6,96,384]{2,1,0:T(8,128)(2,1)S(1)} collective-permute-done((bf16[6,96,384]{2,1,0:T(8,128)(2,1)S(1)}, bf16[6,96,384]{2,1,0:T(8,128)(2,1)S(1)}, u32[]{:S(2)}, u32[]{:S(2)}) %collective-permute-start.54) | collective-permute-done | bytes 442400 | tf_op jit(solution)/shard_map/ppermute | solution.py:738
  387.9 3.3 collective-permute-done.55.refs_3_
  402.5 3.1 collective-permute-done.62
  409.4 4.9 collective-permute-start.56
  416.8 10.6 %update_layer.2 = (f32[2,6,96,384]{3,2,1,0:T(8,128)}, f32[2,6,96,384]{3,2,1,0:T(8,128)}, f32[2,6,96,384]{3,2,1,0:T(8,128)}, f32[2,6,96,384]{3,2,1,0:T(8,128)}, bf16[2,6,96,384]{3,2,1,0:T(8,128)(2,1)}) custom-call(s32[4]{0:T(128)} %copy-done.60, bf16[6,96,384]{2,1,0:T(8,128)(2,1)} %copy-done.16, f32[2,6,96,384]{3,2,1,0:T(8,128)} %refs_2_.4, ...), custom_call_target="tpu_custom_call" | custom-call | tf_op jit(solution)/shard_map/update_layer/pallas_call | solution.py:62
  427.5 14.0 %collective-permute-done.57.refs_2_ = bf16[6,96,384]{2,1,0:T(8,128)(2,1)S(1)} collective-permute-done((bf16[6,96,384]{2,1,0:T(8,128)(2,1)}, bf16[6,96,384]{2,1,0:T(8,128)(2,1)S(1)}, u32[]{:S(2)}, u32[]{:S(2)}) %collective-permute-start.57) | collective-permute-done | bytes 442400 | tf_op jit(solution)/shard_map/ppermute | solution.py:738
  446.3 11.0 %collective-permute-done.64.refs_7_ = bf16[6,96,384]{2,1,0:T(8,128)(2,1)S(1)} collective-permute-done((bf16[6,96,384]{2,1,0:T(8,128)(2,1)S(1)}, bf16[6,96,384]{2,1,0:T(8,128)(2,1)S(1)}, u32[]{:S(2)}, u32[]{:S(2)}) %collective-permute-start.64) | collective-permute-done | bytes 442400 | tf_op jit(solution)/shard_map/ppermute | solution.py:738
  457.3 10.1 %collective-permute-start.67 = (f32[144,128]{1,0:T(8,128)S(1)}, f32[144,128]{1,0:T(8,128)S(1)}, u32[]{:S(2)}, u32[]{:S(2)}) collective-permute-start(f32[144,128]{1,0:T(8,128)S(1)} %gate.17), channel_id=1, source_target_pairs={{0,8},{1,9},{2,10},{3,11},{4,12},{5,13},{6,14},{7,15},{8,0},{9,1},... | collective-permute-start | bytes 221192 | tf_op jit(solution)/shard_map/ppermute | solution.py:738
  471.8 5.4 %collective-permute-done.68 = f32[144,128]{1,0:T(8,128)S(1)} collective-permute-done((f32[144,128]{1,0:T(8,128)S(1)}, f32[144,128]{1,0:T(8,128)S(1)}, u32[]{:S(2)}, u32[]{:S(2)}) %collective-permute-start.68) | collective-permute-done | bytes 73760 | tf_op jit(solution)/shard_map/ppermute | solution.py:738
  478.9 10.8 %update_layer.3 = (f32[2,6,96,384]{3,2,1,0:T(8,128)}, f32[2,6,96,384]{3,2,1,0:T(8,128)}, f32[2,6,96,384]{3,2,1,0:T(8,128)}, f32[2,6,96,384]{3,2,1,0:T(8,128)}, bf16[2,6,96,384]{3,2,1,0:T(8,128)(2,1)}) custom-call(s32[4]{0:T(128)} %copy-done.60, ...), custom_call_target="tpu_custom_call", output_to_operand_aliasing={{0}: (14, {}), {1}: (15, {}), {2}: (16, {}), {3}: (17, {}),... | custom-call | tf_op jit(solution)/shard_map/update_layer/pallas_call | solution.py:62
  (337 shorter events, 137.4 us)
Async XLA Ops:
  7.2 114.7 %all-gather.3.cloned.1.call-start = ((), (), s32[]{:S(2)}) async-start(), calls=%async_computation.1 | async-start | bytes 2211840 | tf_op jit(solution)/shard_map/all_gather | solution.py:770
  11.5 31.3 %collective-permute-start.1 = (bf16[6,96,384]{2,1,0:T(8,128)(2,1)S(1)}, bf16[6,96,384]{2,1,0:T(8,128)(2,1)S(1)}, u32[]{:S(2)}, u32[]{:S(2)}) collective-permute-start(bf16[6,96,384]{2,1,0:T(8,128)(2,1)S(1)} %fusion.refs_1_), channel_id=1, source_target_pairs={{0,16},{1,17},{2,18},{3,19},{4,20},{5,21},{6,22},{7,23},{8,24},{9,... | collective-permute-start | bytes 1327112 | tf_op jit(solution)/shard_map/ppermute | solution.py:738
  14.1 28.7 %collective-permute-start.2 = (bf16[6,96,384]{2,1,0:T(8,128)(2,1)S(1)}, bf16[6,96,384]{2,1,0:T(8,128)(2,1)S(1)}, u32[]{:S(2)}, u32[]{:S(2)}) collective-permute-start(bf16[6,96,384]{2,1,0:T(8,128)(2,1)S(1)} %fusion.refs_1_), channel_id=1, source_target_pairs={{0,24},{1,25},{2,26},{3,27},{4,28},{5,29},{6,30},{7,31},{8,0},{9,1... | collective-permute-start | bytes 1327112 | tf_op jit(solution)/shard_map/ppermute | solution.py:738
  72.6 22.9 %collective-permute-start.5 = (bf16[12,96,384]{2,1,0:T(8,128)(2,1)}, bf16[12,96,384]{2,1,0:T(8,128)(2,1)}, u32[]{:S(2)}, u32[]{:S(2)}) collective-permute-start(bf16[12,96,384]{2,1,0:T(8,128)(2,1)} %get-tuple-element.125.refs_4_.refs_3_.refs_10_.refs_9_), channel_id=1, source_target_pairs={{0,2},{1,3},{2,0},{3,1},{4,6},{5,7},{6,4},{7,5},{8,10},{9,11},{10,... | collective-permute-start | bytes 2654216 | tf_op jit(solution)/shard_map/ppermute | solution.py:738
  74.2 22.9 %collective-permute-start.6 = (bf16[12,96,384]{2,1,0:T(8,128)(2,1)}, bf16[12,96,384]{2,1,0:T(8,128)(2,1)}, u32[]{:S(2)}, u32[]{:S(2)}) collective-permute-start(bf16[12,96,384]{2,1,0:T(8,128)(2,1)} %get-tuple-element.125.refs_4_.refs_3_.refs_10_.refs_9_), channel_id=1, source_target_pairs={{0,1},{1,0},{2,3},{3,2},{4,5},{5,4},{6,7},{7,6},{8,9},{9,8},{10,11... | collective-permute-start | bytes 2654216 | tf_op jit(solution)/shard_map/ppermute | solution.py:738
  74.2 22.9 %collective-permute-start.9 = (bf16[12,96,384]{2,1,0:T(8,128)(2,1)}, bf16[12,96,384]{2,1,0:T(8,128)(2,1)}, u32[]{:S(2)}, u32[]{:S(2)}) collective-permute-start(bf16[12,96,384]{2,1,0:T(8,128)(2,1)} %get-tuple-element.126.refs_5_.refs_8_.refs_7_.refs_14_.refs_13_), channel_id=1, source_target_pairs={{0,1},{1,0},{2,3},{3,2},{4,5},{5,4},{6,7},{7,6},{8,9},{9,8},{10,11... | collective-permute-start | bytes 2654216 | tf_op jit(solution)/shard_map/ppermute | solution.py:738
  74.7 308.7 %reduce-scatter.2.cloned.1.call-start = ((), (), s32[]{:S(2)}) async-start(), calls=%async_computation.2 | async-start | bytes 2211840 | tf_op jit(solution)/shard_map/reduce_scatter | solution.py:882
  77.0 36.6 %collective-permute-start.11 = (bf16[12,96,384]{2,1,0:T(8,128)(2,1)}, bf16[12,96,384]{2,1,0:T(8,128)(2,1)S(1)}, u32[]{:S(2)}, u32[]{:S(2)}) collective-permute-start(bf16[12,96,384]{2,1,0:T(8,128)(2,1)} %get-tuple-element.127.refs_12_.refs_1_.refs_11_.refs_18_), channel_id=1, source_target_pairs={{0,2},{1,3},{2,0},{3,1},{4,6},{5,7},{6,4},{7,5},{8,10},{9,11},{10,... | collective-permute-start | bytes 2654216 | tf_op jit(solution)/shard_map/ppermute | solution.py:738
  92.7 34.9 %collective-permute-start.13 = (bf16[12,96,384]{2,1,0:T(8,128)(2,1)}, bf16[12,96,384]{2,1,0:T(8,128)(2,1)}, u32[]{:S(2)}, u32[]{:S(2)}) collective-permute-start(bf16[12,96,384]{2,1,0:T(8,128)(2,1)} %get-tuple-element.127.refs_12_.refs_1_.refs_11_.refs_18_), channel_id=1, source_target_pairs={{0,1},{1,0},{2,3},{3,2},{4,5},{5,4},{6,7},{7,6},{8,9},{9,8},{10,11... | collective-permute-start | bytes 2654216 | tf_op jit(solution)/shard_map/ppermute | solution.py:738
  99.7 29.4 %collective-permute-start.15 = (bf16[12,96,384]{2,1,0:T(8,128)(2,1)}, bf16[12,96,384]{2,1,0:T(8,128)(2,1)}, u32[]{:S(2)}, u32[]{:S(2)}) collective-permute-start(bf16[12,96,384]{2,1,0:T(8,128)(2,1)} %get-tuple-element.128.refs_13_.refs_2_.refs_15_.refs_22_), channel_id=1, source_target_pairs={{0,1},{1,0},{2,3},{3,2},{4,5},{5,4},{6,7},{7,6},{8,9},{9,8},{10,11... | collective-permute-start | bytes 2654216 | tf_op jit(solution)/shard_map/ppermute | solution.py:738
  155.5 21.7 %collective-permute-start.20 = (bf16[12,96,384]{2,1,0:T(8,128)(2,1)S(1)}, bf16[12,96,384]{2,1,0:T(8,128)(2,1)S(1)}, u32[]{:S(2)}, u32[]{:S(2)}) collective-permute-start(bf16[12,96,384]{2,1,0:T(8,128)(2,1)S(1)} %get-tuple-element.137.refs_4_.refs_7_.refs_8_), channel_id=1, source_target_pairs={{0,1},{1,0},{2,3},{3,2},{4,5},{5,4},{6,7},{7,6},{8,9},{9,8},{10,11... | collective-permute-start | bytes 2654216 | tf_op jit(solution)/shard_map/ppermute | solution.py:738
  155.5 22.3 %collective-permute-start.23 = (bf16[12,96,384]{2,1,0:T(8,128)(2,1)S(1)}, bf16[12,96,384]{2,1,0:T(8,128)(2,1)S(1)}, u32[]{:S(2)}, u32[]{:S(2)}) collective-permute-start(bf16[12,96,384]{2,1,0:T(8,128)(2,1)S(1)} %get-tuple-element.138.refs_5_.refs_8_.refs_11_.refs_12_), channel_id=1, source_target_pairs={{0,1},{1,0},{2,3},{3,2},{4,5},{5,4},{6,7},{7,6},{8,9},{9,8},{10,11... | collective-permute-start | bytes 2654216 | tf_op jit(solution)/shard_map/ppermute | solution.py:738
  176.4 22.1 %collective-permute-start.25 = (bf16[12,96,384]{2,1,0:T(8,128)(2,1)S(1)}, bf16[12,96,384]{2,1,0:T(8,128)(2,1)S(1)}, u32[]{:S(2)}, u32[]{:S(2)}) collective-permute-start(bf16[12,96,384]{2,1,0:T(8,128)(2,1)S(1)} %get-tuple-element.139.refs_12_.refs_15_), channel_id=1, source_target_pairs={{0,2},{1,3},{2,0},{3,1},{4,6},{5,7},{6,4},{7,5},{8,10},{9,11},{10,... | collective-permute-start | bytes 2654216 | tf_op jit(solution)/shard_map/ppermute | solution.py:738
  177.8 24.6 %collective-permute-start.27 = (bf16[12,96,384]{2,1,0:T(8,128)(2,1)S(1)}, bf16[12,96,384]{2,1,0:T(8,128)(2,1)S(1)}, u32[]{:S(2)}, u32[]{:S(2)}) collective-permute-start(bf16[12,96,384]{2,1,0:T(8,128)(2,1)S(1)} %get-tuple-element.139.refs_12_.refs_15_), channel_id=1, source_target_pairs={{0,1},{1,0},{2,3},{3,2},{4,5},{5,4},{6,7},{7,6},{8,9},{9,8},{10,11... | collective-permute-start | bytes 2654216 | tf_op jit(solution)/shard_map/ppermute | solution.py:738
  177.8 24.6 %collective-permute-start.29 = (bf16[12,96,384]{2,1,0:T(8,128)(2,1)S(1)}, bf16[12,96,384]{2,1,0:T(8,128)(2,1)S(1)}, u32[]{:S(2)}, u32[]{:S(2)}) collective-permute-start(bf16[12,96,384]{2,1,0:T(8,128)(2,1)S(1)} %get-tuple-element.140.refs_13_.refs_19_), channel_id=1, source_target_pairs={{0,1},{1,0},{2,3},{3,2},{4,5},{5,4},{6,7},{7,6},{8,9},{9,8},{10,11... | collective-permute-start | bytes 2654216 | tf_op jit(solution)/shard_map/ppermute | solution.py:738
  200.9 28.8 %collective-permute-start.31 = (bf16[12,96,384]{2,1,0:T(8,128)(2,1)S(1)}, bf16[12,96,384]{2,1,0:T(8,128)(2,1)S(1)}, u32[]{:S(2)}, u32[]{:S(2)}) collective-permute-start(bf16[12,96,384]{2,1,0:T(8,128)(2,1)S(1)} %rounded.3.refs_23_.refs_7_.refs_10_), channel_id=1, source_target_pairs={{0,2},{1,3},{2,0},{3,1},{4,6},{5,7},{6,4},{7,5},{8,10},{9,11},{10,... | collective-permute-start | bytes 2654216 | tf_op jit(solution)/shard_map/ppermute | solution.py:738
  235.8 31.2 %collective-permute-start.35 = (bf16[18,96,384]{2,1,0:T(8,128)(2,1)S(1)}, bf16[18,96,384]{2,1,0:T(8,128)(2,1)S(1)}, u32[]{:S(2)}, u32[]{:S(2)}) collective-permute-start(bf16[18,96,384]{2,1,0:T(8,128)(2,1)S(1)} %get-tuple-element.159.refs_17_), channel_id=1, source_target_pairs={{0,4},{1,5},{2,6},{3,7},{4,0},{5,1},{6,2},{7,3},{8,12},{9,13},{10,... | collective-permute-start | bytes 3981320 | tf_op jit(solution)/shard_map/ppermute | solution.py:738
  240.6 31.4 %collective-permute-start.34 = (bf16[18,96,384]{2,1,0:T(8,128)(2,1)}, bf16[18,96,384]{2,1,0:T(8,128)(2,1)S(1)}, u32[]{:S(2)}, u32[]{:S(2)}) collective-permute-start(bf16[18,96,384]{2,1,0:T(8,128)(2,1)} %get-tuple-element.156.refs_16_), channel_id=1, source_target_pairs={{0,2},{1,3},{2,0},{3,1},{4,6},{5,7},{6,4},{7,5},{8,10},{9,11},{10,... | collective-permute-start | bytes 3981320 | tf_op jit(solution)/shard_map/ppermute | solution.py:738
  274.6 28.6 %collective-permute-start.43 = (bf16[9,96,384]{2,1,0:T(8,128)(2,1)S(1)}, bf16[9,96,384]{2,1,0:T(8,128)(2,1)S(1)}, u32[]{:S(2)}, u32[]{:S(2)}) collective-permute-start(bf16[9,96,384]{2,1,0:T(8,128)(2,1)S(1)} %get-tuple-element.168.refs_3_.refs_27_), channel_id=1, source_target_pairs={{0,2},{1,3},{2,0},{3,1},{4,6},{5,7},{6,4},{7,5},{8,10},{9,11},{10,... | collective-permute-start | bytes 1990664 | tf_op jit(solution)/shard_map/ppermute | solution.py:738
  277.3 25.9 %collective-permute-start.42 = (bf16[9,96,384]{2,1,0:T(8,128)(2,1)S(1)}, bf16[9,96,384]{2,1,0:T(8,128)(2,1)S(1)}, u32[]{:S(2)}, u32[]{:S(2)}) collective-permute-start(bf16[9,96,384]{2,1,0:T(8,128)(2,1)S(1)} %get-tuple-element.166.refs_2_.refs_26_), channel_id=1, source_target_pairs={{0,4},{1,5},{2,6},{3,7},{4,0},{5,1},{6,2},{7,3},{8,12},{9,13},{10,... | collective-permute-start | bytes 1990664 | tf_op jit(solution)/shard_map/ppermute | solution.py:738
  278.1 25.1 %collective-permute-start.40 = (bf16[6,96,384]{2,1,0:T(8,128)(2,1)S(1)}, bf16[6,96,384]{2,1,0:T(8,128)(2,1)S(1)}, u32[]{:S(2)}, u32[]{:S(2)}) collective-permute-start(bf16[6,96,384]{2,1,0:T(8,128)(2,1)S(1)} %get-tuple-element.176.refs_29_), channel_id=1, source_target_pairs={{0,4},{1,5},{2,6},{3,7},{4,0},{5,1},{6,2},{7,3},{8,12},{9,13},{10,... | collective-permute-start | bytes 1327112 | tf_op jit(solution)/shard_map/ppermute | solution.py:738
  279.9 23.3 %collective-permute-start.38 = (bf16[6,96,384]{2,1,0:T(8,128)(2,1)S(1)}, bf16[6,96,384]{2,1,0:T(8,128)(2,1)S(1)}, u32[]{:S(2)}, u32[]{:S(2)}) collective-permute-start(bf16[6,96,384]{2,1,0:T(8,128)(2,1)S(1)} %get-tuple-element.173.refs_28_), channel_id=1, source_target_pairs={{0,2},{1,3},{2,0},{3,1},{4,6},{5,7},{6,4},{7,5},{8,10},{9,11},{10,... | collective-permute-start | bytes 1327112 | tf_op jit(solution)/shard_map/ppermute | solution.py:738
  319.6 97.2 %all-gather.5.cloned.1.call-start = ((), (), s32[]{:S(2)}) async-start(), calls=%async_computation.3 | async-start | bytes 2211840 | tf_op jit(solution)/shard_map/all_gather | solution.py:887
  319.7 31.4 %collective-permute-start.47 = (bf16[18,96,384]{2,1,0:T(8,128)(2,1)}, bf16[18,96,384]{2,1,0:T(8,128)(2,1)S(1)}, u32[]{:S(2)}, u32[]{:S(2)}) collective-permute-start(bf16[18,96,384]{2,1,0:T(8,128)(2,1)} %copy-done.32), channel_id=1, source_target_pairs={{0,4},{1,5},{2,6},{3,7},{4,0},{5,1},{6,2},{7,3},{8,12},{9,13},{10,... | collective-permute-start | bytes 3981320 | tf_op jit(solution)/shard_map/ppermute | solution.py:738
  320.3 31.1 %collective-permute-start.46 = (bf16[18,96,384]{2,1,0:T(8,128)(2,1)}, bf16[18,96,384]{2,1,0:T(8,128)(2,1)S(1)}, u32[]{:S(2)}, u32[]{:S(2)}) collective-permute-start(bf16[18,96,384]{2,1,0:T(8,128)(2,1)} %copy-done.33), channel_id=1, source_target_pairs={{0,2},{1,3},{2,0},{3,1},{4,6},{5,7},{6,4},{7,5},{8,10},{9,11},{10,... | collective-permute-start | bytes 3981320 | tf_op jit(solution)/shard_map/ppermute | solution.py:738
  358.3 23.5 %collective-permute-start.54 = (bf16[6,96,384]{2,1,0:T(8,128)(2,1)S(1)}, bf16[6,96,384]{2,1,0:T(8,128)(2,1)S(1)}, u32[]{:S(2)}, u32[]{:S(2)}) collective-permute-start(bf16[6,96,384]{2,1,0:T(8,128)(2,1)S(1)} %get-tuple-element.215), channel_id=1, source_target_pairs={{0,4},{1,5},{2,6},{3,7},{4,0},{5,1},{6,2},{7,3},{8,12},{9,13},{10,... | collective-permute-start | bytes 1327112 | tf_op jit(solution)/shard_map/ppermute | solution.py:738
  359.1 23.4 %collective-permute-start.49 = (bf16[6,96,384]{2,1,0:T(8,128)(2,1)S(1)}, bf16[6,96,384]{2,1,0:T(8,128)(2,1)S(1)}, u32[]{:S(2)}, u32[]{:S(2)}) collective-permute-start(bf16[6,96,384]{2,1,0:T(8,128)(2,1)S(1)} %get-tuple-element.209), channel_id=1, source_target_pairs={{0,2},{1,3},{2,0},{3,1},{4,6},{5,7},{6,4},{7,5},{8,10},{9,11},{10,... | collective-permute-start | bytes 1327112 | tf_op jit(solution)/shard_map/ppermute | solution.py:738
  387.4 29.4 %collective-permute-start.59 = (bf16[12,96,384]{2,1,0:T(8,128)(2,1)S(1)}, bf16[12,96,384]{2,1,0:T(8,128)(2,1)}, u32[]{:S(2)}, u32[]{:S(2)}) collective-permute-start(bf16[12,96,384]{2,1,0:T(8,128)(2,1)S(1)} %copy-done.3), channel_id=1, source_target_pairs={{0,1},{1,0},{2,3},{3,2},{4,5},{5,4},{6,7},{7,6},{8,9},{9,8},{10,11... | collective-permute-start | bytes 2654216 | tf_op jit(solution)/shard_map/ppermute | solution.py:738
  387.4 29.4 %collective-permute-start.60 = (bf16[12,96,384]{2,1,0:T(8,128)(2,1)S(1)}, bf16[12,96,384]{2,1,0:T(8,128)(2,1)}, u32[]{:S(2)}, u32[]{:S(2)}) collective-permute-start(bf16[12,96,384]{2,1,0:T(8,128)(2,1)S(1)} %collective-permute-done.31.refs_2_.refs_8_.refs_11_), channel_id=1, source_target_pairs={{0,1},{1,0},{2,3},{3,2},{4,5},{5,4},{6,7},{7,6},{8,9},{9,8},{10,11... | collective-permute-start | bytes 2654216 | tf_op jit(solution)/shard_map/ppermute | solution.py:738
  414.2 27.3 %collective-permute-start.57 = (bf16[6,96,384]{2,1,0:T(8,128)(2,1)}, bf16[6,96,384]{2,1,0:T(8,128)(2,1)S(1)}, u32[]{:S(2)}, u32[]{:S(2)}) collective-permute-start(bf16[6,96,384]{2,1,0:T(8,128)(2,1)} %get-tuple-element.237), channel_id=1, source_target_pairs={{0,16},{1,17},{2,18},{3,19},{4,20},{5,21},{6,22},{7,23},{8,24},{9,... | collective-permute-start | bytes 1327112 | tf_op jit(solution)/shard_map/ppermute | solution.py:738
  414.2 27.6 %collective-permute-start.58 = (bf16[6,96,384]{2,1,0:T(8,128)(2,1)}, bf16[6,96,384]{2,1,0:T(8,128)(2,1)}, u32[]{:S(2)}, u32[]{:S(2)}) collective-permute-start(bf16[6,96,384]{2,1,0:T(8,128)(2,1)} %get-tuple-element.236), channel_id=1, source_target_pairs={{0,24},{1,25},{2,26},{3,27},{4,28},{5,29},{6,30},{7,31},{8,0},{9,1... | collective-permute-start | bytes 1327112 | tf_op jit(solution)/shard_map/ppermute | solution.py:738
  446.3 31.7 %collective-permute-start.65 = (bf16[6,96,384]{2,1,0:T(8,128)(2,1)S(1)}, bf16[6,96,384]{2,1,0:T(8,128)(2,1)S(1)}, u32[]{:S(2)}, u32[]{:S(2)}) collective-permute-start(bf16[6,96,384]{2,1,0:T(8,128)(2,1)S(1)} %get-tuple-element.223.refs_6_.refs_1_), channel_id=1, source_target_pairs={{0,1},{1,0},{2,3},{3,2},{4,5},{5,4},{6,7},{7,6},{8,9},{9,8},{10,11... | collective-permute-start | bytes 1327112 | tf_op jit(solution)/shard_map/ppermute | solution.py:738
  (123 other events, 1040.6 us)
Sparse Core Ops, SparseCore 0:
  74.8 47.0 all-gather.2
  319.8 40.0 reduce-scatter.1
  385.3 21.8 all-gather.4

commit v4 on v3

--- a/solution.py
+++ b/solution.py
@@ -41,8 +41,9 @@
 
 
 class Part:
-    def __init__(self, zs, js, order, arrays=None):
-        self.zs, self.js, self.order, self.arrays = tuple(zs), tuple(js), order, arrays
+    def __init__(self, zs, js, order, arrays=None, offsets=(0, 0, 0, 0)):
+        self.zs, self.js, self.order = tuple(zs), tuple(js), order
+        self.arrays, self.offsets = arrays, offsets
 
     def index(self, first, second, z, j):
         place = self.zs.index(z) * len(self.js) + self.js.index(j)
@@ -58,7 +59,7 @@
     def kernel(*refs):
         body(*refs[:count], *refs[count + extra :])
 
-    flops, moved, special = cost or (0, 0, 0)
+    flops, moved, special = 0, 0, 0
     return pl.pallas_call(
         kernel,
         in_specs=[spec for _, spec in ins] + [ANY] * extra,
@@ -130,7 +131,8 @@
             continue
         for dc in range(2):
             for dy in range(2):
-                src = refs[number][2 * dc + dy].at[parts[number].index(0, x ^ xq, z, j)]
+                n = 2 * dc + dy
+                src = refs[number][n].at[parts[number].offsets[n] + parts[number].index(0, x ^ xq, z, j)]
                 start(src, row, 2 * (y ^ dy) + (c ^ dc), col)
     if by_x:
         for own_x in range(2):
@@ -140,8 +142,9 @@
                 for number, z, xq, j, row, col in by_x:
                     for dc in range(2):
                         for yq in range(2):
-                            src = refs[number][2 * dc + (own_x ^ xq)].at[parts[number].index(0, y ^ yq, z, j)]
-                            start(src, row, 2 * yq + (c ^ dc), col)
+                            n = 2 * dc + (own_x ^ xq)
+                            at = parts[number].offsets[n] + parts[number].index(0, y ^ yq, z, j)
+                            start(refs[number][n].at[at], row, 2 * yq + (c ^ dc), col)
 
 
 def wait_for(ref, sem):
@@ -187,6 +190,10 @@
     for n in range(count):
         at = number * count + n
         sums_ref[at : at + 1, :] = values[:, 128 * n : 128 * (n + 1)]
+
+
+def launch_list(*args, **kwargs):
+    return list(launch(*args, **kwargs))
 
 
 def segment(small_ref, number, width):
@@ -627,36 +634,21 @@
 
 def join_kernel(ranges, *refs):
     pairs = len(ranges)
-    ins, outs, holds, sems = refs[: 2 * pairs], refs[2 * pairs : 3 * pairs], refs[3 * pairs : -2], refs[-2:]
+    ins, outs, hold, sems = refs[: 2 * pairs], refs[2 * pairs : 3 * pairs + 1], refs[-3], refs[-2:]
+    runs, at = [], 0
     for n, (low, count) in enumerate(ranges):
+        runs.append(hold.at[pl.ds(at, 2 * count)])
         for half in range(2):
             src = ins[2 * n + half].at[pl.ds(low, count)]
-            dst = holds[n].at[pl.ds(half * count, count)]
-            pltpu.make_async_copy(src, dst, sems[0].at[n]).start()
+            pltpu.make_async_copy(src, hold.at[pl.ds(at + half * count, count)], sems[0].at[n]).start()
+        at += 2 * count
     for n in range(pairs):
-        wait_for(holds[n], sems[0].at[n])
-        pltpu.make_async_copy(holds[n], outs[n], sems[1].at[n]).start()
+        wait_for(runs[n], sems[0].at[n])
+        pltpu.make_async_copy(runs[n], outs[n], sems[1].at[n]).start()
+    pltpu.make_async_copy(hold, outs[pairs], sems[1].at[pairs]).start()
     for n in range(pairs):
-        wait_for(holds[n], sems[1].at[n])
-
-
-def stack_kernel(zs, halves, pos_ref, *refs):
-    ins, outs, holds, sems = refs[:Z_SLABS], refs[Z_SLABS:-4], refs[-4:-2], refs[-2:]
-    z = pos_ref[0]
-    for n, (low, high) in enumerate(halves):
-        for place, want in enumerate(zs):
-            for k in range(Z_SLABS):
-
-                @pl.when(lax.rem(z - want + Z_SLABS, Z_SLABS) == k)
-                def _(n=n, low=low, high=high, place=place, k=k):
-                    dst = holds[n].at[pl.ds(place * (high - low), high - low)]
-                    pltpu.make_async_copy(ins[k].at[pl.ds(low, high - low)], dst, sems[0].at[n]).start()
-
-    for n in range(2):
-        wait_for(holds[n], sems[0].at[n])
-        pltpu.make_async_copy(holds[n], outs[n], sems[1].at[n]).start()
-    for n in range(2):
-        wait_for(holds[n], sems[1].at[n])
+        wait_for(runs[n], sems[1].at[n])
+    wait_for(hold, sems[1].at[pairs])
 
 
 def round_kernel(src_ref, dst_ref):
@@ -675,14 +667,22 @@
 
 
 def collect_kernel(zs, *refs):
-    ins, out = refs[:-1], refs[-1]
-    base = min(min(z_list) for z_list in zs)
-    half = ins[0].shape[0] // len(zs[0])
+    pairs = len(zs)
+    ins, out, total, holds, sems = refs[: 2 * pairs], refs[2 * pairs], refs[2 * pairs + 1], refs[2 * pairs + 2 : -1], refs[-1]
+    for n in range(2 * pairs):
+        pltpu.make_async_copy(ins[n], holds[n], sems.at[n]).start()
+    half = holds[0].shape[0] // len(zs[0])
+    copies = []
     for n, z_list in enumerate(zs):
+        wait_for(holds[2 * n], sems.at[2 * n])
+        wait_for(holds[2 * n + 1], sems.at[2 * n + 1])
         for place, want in enumerate(z_list):
-            piece = pl.ds(place * half, half)
-            total = ins[2 * n][piece].astype(F32) + ins[2 * n + 1][piece].astype(F32)
-            out[pl.ds((2 * (want - base) + n % 2) * half, half)] = total.astype(BF)
+            piece, at = pl.ds(place * half, half), pl.ds((2 * want + n % 2) * half, half)
+            value = holds[2 * n][piece].astype(F32) + holds[2 * n + 1][piece].astype(F32)
+            total[at] = value.astype(BF)
+            copies.append(pltpu.make_async_copy(total.at[at], out.at[at], sems.at[2 * pairs]))
+            copies[-1].start()
+    wait_for(total, sems.at[2 * pairs])
 
 
 def pick_kernel(places, src_ref, *refs):
@@ -704,15 +704,6 @@
     pass
 
 
-def total_kernel(own_ref, *refs):
-    *got, wide_ref, low_ref = refs
-    total = own_ref[...].astype(F32)
-    for ref in got:
-        total = total + ref[...].astype(F32)
-    wide_ref[...] = total
-    low_ref[...] = total.astype(BF)
-
-
 class SmallSlice:
     def __init__(self, dims):
         self.dims = dims
@@ -743,26 +734,6 @@
     def rounded(self, wide, deps=()):
         return launch(round_kernel, "rounded", [(wide, VMEM)], shape(wide.shape, BF), VMEM, deps)
 
-    def from_slabs(self, own):
-        return [own] + [
-            self.permute(own, lambda z, x, y, c, k=k: ((z + k) % Z_SLABS, x, y, c)) for k in range(1, Z_SLABS)
-        ]
-
-    def lot(self, slabs, zs, js, deps=()):
-        half = len(js) // 2
-        halves = [(0, half), (half, len(js))]
-        sizes = [self.pieces(len(zs) * (high - low)) for low, high in halves]
-        arrays = launch(
-            functools.partial(stack_kernel, zs, halves),
-            "stack",
-            [(self.pos, SMEM)] + [(a, ANY) for a in slabs],
-            sizes,
-            [ANY] * 2,
-            deps,
-            [pltpu.VMEM(s.shape, BF) for s in sizes] + [pltpu.SemaphoreType.DMA((2,))] * 2,
-        )
-        return [(Part(zs, js[low:high], order), a) for (low, high), order, a in zip(halves, ("yx", "xy"), arrays)]
-
     def columns(self):
         return [[2 * z + x for z in range(Z_SLABS)] for x in range(2)]
 
@@ -770,8 +741,8 @@
         return lax.all_gather(own, "grp", axis_index_groups=self.columns(), axis=0, tiled=True)
 
     def whole_lot(self, whole, zs, js, deps=()):
-        half, count = len(js) // 2, self.dims.own
-        places = [[(z * count + js[low], half) for z in zs] for low in (0, half)]
+        half, count = len(js) // 2, len(js)
+        places = [[(z * count + low, half) for z in zs] for low in (0, half)]
         sizes = [self.pieces(len(zs) * half)] * 2
         arrays = launch(
             functools.partial(pick_kernel, places),
@@ -781,6 +752,7 @@
             [ANY] * 2,
             deps,
             [pltpu.VMEM(s.shape, BF) for s in sizes] + [pltpu.SemaphoreType.DMA((2,))] * 2,
+            limit=60,
         )
         halves = ((js[:half], "yx"), (js[half:], "xy"))
         return [(Part(zs, j, order), a) for (j, order), a in zip(halves, arrays)]
@@ -794,6 +766,7 @@
             [ANY] * len(arrays),
             deps,
             aliases={n: n for n in range(len(arrays))},
+            limit=60,
         )
 
     def hold(self, parts, deps):
@@ -810,24 +783,27 @@
             ranges.append((part.zs.index(zs[0]) * count, len(zs) * count))
             sizes.append(self.pieces(2 * len(zs) * count))
             ins += [own, g]
-        return launch(
+        return launch_list(
             functools.partial(join_kernel, ranges),
             "join",
             [(a, ANY) for a in ins],
-            sizes,
-            [ANY] * len(lot),
+            sizes + [self.pieces(sum(a.shape[0] for a in sizes))],
+            [ANY] * (len(lot) + 1),
             deps,
-            [pltpu.VMEM(s.shape, BF) for s in sizes] + [pltpu.SemaphoreType.DMA((2,))] * 2,
+            [pltpu.VMEM((sum(a.shape[0] for a in sizes),) + sizes[0].shape[1:], BF)]
+            + [pltpu.SemaphoreType.DMA((2,)), pltpu.SemaphoreType.DMA((3,))],
         )
 
     def second_swap(self, lot, both):
         return [self.swap(b, part.order[0]) for (part, _), b in zip(lot, both)]
 
     def core_swap(self, lot, zs, both, got):
-        return [
-            Part(zs, part.js, part.order, [b, g, self.swap(b, "c"), self.swap(g, "c")])
-            for (part, _), b, g in zip(lot, both, got)
-        ]
+        others = self.swap(both[-1], "c")
+        parts, at = [], 0
+        for (part, _), b, g in zip(lot, both, got):
+            parts.append(Part(zs, part.js, part.order, [b, g, others, self.swap(g, "c")], (0, 0, at, 0)))
+            at += b.shape[0]
+        return parts
 
     def add(self, keep, got, deps=()):
         sums = []
@@ -851,31 +827,13 @@
         return launch(
             functools.partial(collect_kernel, [z for z in zs for _ in range(2)]),
             "collect",
-            [(a, VMEM) for a in ins],
-            self.pieces(sum(len(z) for z in zs) * self.dims.own),
-            VMEM,
+            [(a, ANY) for a in ins],
+            self.pieces(Z_SLABS * self.dims.own),
+            ANY,
             deps,
-        )
-
-    def deal(self, whole):
-        split = whole.reshape((Z_SLABS, self.dims.own) + whole.shape[1:])
-        got = []
-        for k in range(Z_SLABS):
-            mine = lax.dynamic_index_in_dim(split, (self.z + k) % Z_SLABS, 0, keepdims=False)
-            if k > 0:
-                mine = self.permute(mine, lambda z, x, y, c, k=k: ((z + k) % Z_SLABS, x, y, c))
-            got.append(mine)
-        return got
-
-    def slab_sum(self, dealt, deps=()):
-        size = dealt[0].shape
-        return launch(
-            total_kernel,
-            "total",
-            [(a, VMEM) for a in dealt],
-            [shape(size, F32), shape(size, BF)],
-            [VMEM] * 2,
-            deps,
+            [pltpu.VMEM((Z_SLABS * self.dims.own,) + ins[0].shape[1:], BF)]
+            + [pltpu.VMEM(a.shape, BF) for a in ins]
+            + [pltpu.SemaphoreType.DMA((len(ins) + 1,))],
         )
 
     def column_sum(self, whole):
@@ -883,17 +841,11 @@
             whole, "grp", axis_index_groups=self.columns(), scatter_dimension=0, tiled=True
         )
 
-    def whole_group(self, own):
-        return [lax.all_gather(own, "fsdp", axis=0, tiled=True)]
-
-    def small_sum_column(self, values):
-        for bit in (1, 2):
+    def small_sum(self, values, axes, bits):
+        for axis in axes:
+            values = values + self.swap(values, axis)
+        for bit in bits:
             values = values + self.permute(values, lambda z, x, y, c, bit=bit: (z ^ bit, x, y, c))
-        return values
-
-    def small_sum_plane(self, values):
-        for axis in ("c", "x", "y"):
-            values = values + self.swap(values, axis)
         return values
 
     def group(self, own):
@@ -907,7 +859,7 @@
     if not first:
         rest = rest[5:]
     outs, rest = rest[:5], rest[5:]
-    g_ref, r_ref, gram_ref, own, held, fresh, low_ref, sem_g, sem_r, sem_in, sem_out = rest
+    g_ref, r_ref, turned, own, held, fresh, low_ref, sem_g, sem_r, sem_in, sem_out = rest
     y, c = pos_ref[2], pos_ref[3]
     count, piece, block = own_ref.shape
 
@@ -930,21 +882,26 @@
     pltpu.make_async_copy(own_ref, own, sem_in.at[4]).start()
     own_rows = quarter(y, c)
     wait_for(g_ref, sem_g)
+    def halves(value):
+        high = value.astype(BF)
+        return [high, (value - high.astype(F32)).astype(BF)]
+
     for b in range(count):
         g = g_ref[b]
+        turned[...] = g.T
         if b == 0:
             wait_for(held.at[0], sem_in.at[0])
         fresh[1, b] = decay_rate * held[0, b] + (1.0 - decay_rate) * mm_bt(g_ref[b, own_rows, :], g)
-        gram_ref[...] = mm_at(g, g)
         if b == 0:
             wait_for(held.at[1], sem_in.at[1])
-        fresh[2, b] = decay_rate * held[1, b] + (1.0 - decay_rate) * gram_ref[own_rows, :]
+            wait_for(held.at[2], sem_in.at[2])
+        products = mm(jnp.concatenate([turned[own_rows, :], *halves(held[2, b])], axis=0), g)
+        fresh[2, b] = decay_rate * held[1, b] + (1.0 - decay_rate) * products[:piece]
         if b == 0:
             wait_for(r_ref, sem_r)
-        mixed = mm(g, r_ref[b])
-        if b == 0:
-            wait_for(held.at[2], sem_in.at[2])
-        update = jnp.dot(held[2, b], mixed, preferred_element_type=F32, precision=lax.Precision.HIGHEST)
+        mixed = products[piece : 2 * piece] + products[2 * piece :]
+        products = mm(jnp.concatenate(halves(mixed), axis=0), r_ref[b])
+        update = products[:piece] + products[piece:]
         if b == 0:
             wait_for(held.at[3], sem_in.at[3])
             wait_for(own, sem_in.at[4])
@@ -978,7 +935,7 @@
         [
             pltpu.VMEM((count, block, block), BF),
             pltpu.VMEM((count, block, block), BF),
-            pltpu.VMEM((block, block), F32),
+            pltpu.VMEM((block, block), BF),
             pltpu.VMEM(own.shape, own.dtype),
             pltpu.VMEM((4,) + own.shape, F32),
             pltpu.VMEM((4,) + own.shape, F32),
@@ -1073,31 +1030,32 @@
     third = dims.own // 3
 
     low_zs, high_zs = every[: Z_SLABS // 2], every[Z_SLABS // 2 :]
-    slabs = net.from_slabs(masters[0].astype(BF))
-    low1 = net.rounded(masters[1], slabs[1:])
-    whole1 = net.whole_column(low1)
-    lot = net.lot(slabs, every, own, [low1])
-    got = net.first_swap(lot)
-    both = net.joined(lot, got, low_zs)
-    both_b = net.joined(lot, got, high_zs, both)
+    third = dims.own // 3
+    whole_a = net.whole_column(masters[0, :third].astype(BF))
+    whole_b = net.whole_column(masters[0, third:].astype(BF))
+    whole1 = net.whole_column(masters[1].astype(BF))
+    lot = net.whole_lot(whole_a, every, own[:third])
+    both = net.joined(lot, net.first_swap(lot), every)
     got = net.second_swap(lot, both)
-    weights0 = net.core_swap(lot, low_zs, both, got)
-    got = net.second_swap(lot, both_b)
-    lot_b = net.whole_lot(whole1, every, own, both_b)
-    qkv0, lse0, ctx0, unit0, inv0 = attention_forward(dims, weights0, pos, lengths, x, small[0], both_b)
-    weights0 += net.core_swap(lot, high_zs, both_b, net.gate(got, [inv0]))
+    weights0 = net.core_swap(lot, every, both, got)
+    lot = net.whole_lot(whole_b, every, own[third:], both)
+    both = net.joined(lot, net.first_swap(lot), every, got)
+    got = net.second_swap(lot, both)
+    lot_b = net.whole_lot(whole1, every, own, both)
+    weights0 += net.core_swap(lot, every, both, net.gate(got, [a for _, a in lot_b]))
 
     lot = lot_b
     got = net.first_swap(lot)
-    act0, slope0, unit0b, inv0b, y0 = ffn_forward(
-        dims, weights0, pos, unit0, small[0], [a for _, a in lot]
-    )
-    both = net.joined(lot, got, low_zs, [inv0b])
+    qkv0, lse0, ctx0, unit0, inv0 = attention_forward(
+        dims, weights0, pos, lengths, x, small[0], [a for _, a in lot]
+    )
+    both = net.joined(lot, got, low_zs, [inv0])
     both_b = net.joined(lot, got, high_zs, both)
-    got = net.second_swap(lot, both)
+    act0, slope0, unit0b, inv0b, y0 = ffn_forward(dims, weights0, pos, unit0, small[0], both_b)
+    got = net.gate(net.second_swap(lot, both), [inv0b])
     weights1 = net.core_swap(lot, low_zs, both, got)
     got = net.second_swap(lot, both_b)
-    qkv1, lse1, ctx1, unit1, inv1 = attention_forward(dims, weights1, pos, lengths, y0, small[1], both_b)
+    qkv1, lse1, ctx1, unit1, inv1 = attention_forward(dims, weights1, pos, lengths, y0, small[1])
     got = net.gate(got, [inv1])
     weights1 += net.core_swap(lot, high_zs, both_b, got)
 
@@ -1137,24 +1095,25 @@
     early0 = net.add(early0[0], got, [gx0])
     late0 = net.core_sum(late0, early0[1])
     got_l, got_e = net.swaps(late0, "yx"), net.swaps(early0, "xy")
-    late0 = net.add(late0[0], got_l, got_e)
+    (sums,) = net.gate([sums], late0[1])
+    sums = net.small_sum(sums, ("c",), (1, 2))
+    late0 = net.add(late0[0], got_l, [*got_e, sums])
     got_l = net.swaps(late0, "xy")
     whole0 = net.collect(split, (late0, early0), (got_l, got_e))
-    (low1,) = net.gate([net.column_sum(whole1)], late0[1])
-    dealt = net.deal(whole0)
+    low0 = net.column_sum(whole0)
+    (low1,) = net.gate([net.column_sum(whole1)], [whole0])
+    grads1 = net.group(low1)
     (sums,) = net.gate([sums], [whole0])
-    sums = net.small_sum_plane(sums)
+    sums = net.small_sum(sums, ("x", "y"), ())
 
     def update(n, wide, grads, before):
         return update_layer(
             n, pos, wide, left_stats, right_stats, left_roots, masters, grads, roots, before, [whole0]
         )
 
-    done = update(1, low1, net.whole_group(low1), None)
-    wide0, low0 = net.slab_sum(dealt, [done[0], sums])
-    (sums,) = net.gate([sums], [low0])
-    sums = net.small_sum_column(sums)
-    done = update(0, wide0, net.group(low0), done)
+    done = update(1, low1, grads1, None)
+    (low0,) = net.gate([low0], [done[0], sums])
+    done = update(0, low0, net.group(low0), done)
     return y1, gx0, done, sums
 
 

time: 503 us -> 460 us (0.915)
  waiting for transfers between devices: 202 us -> 141 us
  blocking collectives: 0 us -> 24.2 us
  starting transfers between devices: 67.7 us -> 46 us
  local copies, waits for them, and re-layouts: 38.8 us -> 49.6 us
    ppermute x69 -> x64, waiting for transfers between devices: 196 us -> 137 us  [permute(): return lax.ppermute(array, ('grp', 'fsdp'), pairs)]
    all_gather x0 -> x1, blocking collectives: none -> 24.2 us  [whole_column(): lax.all_gather(own, 'grp', axis_index_groups=self.columns(), axis=0, tile...]
    ppermute x69 -> x64, starting transfers between devices: 67.6 us -> 45.8 us  [permute(): return lax.ppermute(array, ('grp', 'fsdp'), pairs)]
    unnamed x166 -> x197, local copies, waits for them, and re-layouts: 34.4 us -> 45.7 us
    all_gather x1 -> x2, waiting for transfers between devices: 5.44 us -> 0.01 us  [whole_column(): lax.all_gather(own, 'grp', axis_index_groups=self.columns(), axis=0, tile...]
    pallas_call x46 -> x47, Pallas kernels: 172 us -> 173 us  [launch(): pl.pallas_call(kernel, in_specs=[spec for _, spec in ins] + [ANY] * extra...]
  transfers between devices with their start and end apart: 72 -> 68, of which waited for: 36 -> 36; matrix products, arithmetic and copies ran while one was open for 1% -> 2% of each run, Pallas kernels for 30% -> 35%
where the time goes in v4:
time: 460 us; the launch traced here: 452 us
  Pallas kernels  173 us (38%)
  waiting for transfers between devices  141 us (31%)
  local copies, waits for them, and re-layouts  49.6 us (11%)
  starting transfers between devices  46 us (10%)
  blocking collectives  24.2 us (5%)
  between operations  14.9 us (3%)
    pallas_call x47, Pallas kernels, launch(): pl.pallas_call(kernel, in_specs=[spec for _, spec in ins] + [ANY] * extra...  173 us
    ppermute x64, waiting for transfers between devices, permute(): return lax.ppermute(array, ('grp', 'fsdp'), pairs)  137 us
    ppermute x64, starting transfers between devices, permute(): return lax.ppermute(array, ('grp', 'fsdp'), pairs)  45.8 us
    unnamed x197, local copies, waits for them, and re-layouts  45.7 us
    all_gather x1, blocking collectives, whole_column(): lax.all_gather(own, 'grp', axis_index_groups=self.columns(), axis=0, tile...  24.2 us
  transfers between devices with their start and end apart: 68, of which 36 were waited for; matrix products, arithmetic and copies ran while one was open for 2% of the time, Pallas kernels for 35%

profile of v4, /device:TPU:0, one launch (start us, length us, event | category | flops | bytes accessed | tf_op | source)
XLA Modules:
  0.0 452.1 jit_solution(17296730157360204406)
XLA Ops:
  12.3 24.2 %all-gather = bf16[1,8,96,384]{3,2,0,1:T(8,128)(2,1)} all-gather(bf16[1,2,96,384]{3,2,0,1:T(8,128)(2,1)S(1)} %copy.46), channel_id=2, replica_groups={{0,8,16,24},{4,12,20,28},{1,9,17,25},{5,13,21,29},{2,10,18,26},{6,14,22..., dimensions={1}, use_global_device_ids=true | all-gather | bytes 737280 | tf_op jit(solution)/shard_map/all_gather | solution.py:741
  41.3 4.0 collective-permute-done.refs_1_
  56.6 10.0 %collective-permute-done.2.refs_4_.refs_5_.refs_11_.refs_10_ = bf16[8,96,384]{2,1,0:T(8,128)(2,1)} collective-permute-done((bf16[8,96,384]{2,1,0:T(8,128)(2,1)S(1)}, bf16[8,96,384]{2,1,0:T(8,128)(2,1)}, u32[]{:S(2)}, u32[]{:S(2)}) %collective-permute-start.2) | collective-permute-done | bytes 589856 | tf_op jit(solution)/shard_map/ppermute | solution.py:729
  68.1 6.2 %collective-permute-done.7.refs_1_ = bf16[8,96,384]{2,1,0:T(8,128)(2,1)S(1)} collective-permute-done((bf16[8,96,384]{2,1,0:T(8,128)(2,1)}, bf16[8,96,384]{2,1,0:T(8,128)(2,1)S(1)}, u32[]{:S(2)}, u32[]{:S(2)}) %collective-permute-start.7) | collective-permute-done | bytes 589856 | tf_op jit(solution)/shard_map/ppermute | solution.py:729
  80.7 20.0 %collective-permute-done.10.refs_1_ = bf16[16,96,384]{2,1,0:T(8,128)(2,1)S(1)} collective-permute-done((bf16[16,96,384]{2,1,0:T(8,128)(2,1)S(1)}, bf16[16,96,384]{2,1,0:T(8,128)(2,1)S(1)}, u32[]{:S(2)}, u32[]{:S(2)}) %collective-permute-start.10) | collective-permute-done | bytes 1179680 | tf_op jit(solution)/shard_map/ppermute | solution.py:729
  100.7 2.9 pick.5
  111.0 11.8 %attention_forward.2 = (bf16[480,2304]{1,0:T(8,128)(2,1)}, f32[3,12,160]{2,1,0:T(8,128)}, bf16[480,768]{1,0:T(8,128)(2,1)}, f32[480,768]{1,0:T(8,128)}, f32[480,1]{1,0:T(8,128)}) custom-call(s32[4]{0:T(128)} %pad_add_fusion.refs_0_, s32[3]{0:T(128)} %refs_1_.10, bf16[480,768]{1,0:T(8,128)(2,1)} %bitcast.14, f32[1,9216]{1,0:T(1,128)} %get-tuple-element.248.refs_3_.refs_2_, ...), custom_call_target="tpu_custom_call" | custom-call | tf_op jit(solution)/shard_map/attention_forward/pallas_call | solution.py:63
  122.9 2.7 collective-permute-done.14.refs_1_
  139.5 13.1 %ffn_forward.1 = (bf16[480,3072]{1,0:T(8,128)(2,1)}, bf16[480,3072]{1,0:T(8,128)(2,1)}, f32[480,768]{1,0:T(8,128)}, f32[480,1]{1,0:T(8,128)}, f32[480,768]{1,0:T(8,128)}) custom-call(s32[4]{0:T(128)} %pad_add_fusion.refs_0_, f32[480,768]{1,0:T(8,128)} %get-tuple-element.143.refs_1_.refs_3_, f32[1,9216]{1,0:T(1,128)} %get-tuple-element.248.refs_3_.refs_2_, ...), custom_call_target="tpu_custom_call" | custom-call | tf_op jit(solution)/shard_map/ffn_forward/pallas_call | solution.py:63
  158.8 12.0 %attention_forward.3 = (bf16[480,2304]{1,0:T(8,128)(2,1)}, f32[3,12,160]{2,1,0:T(8,128)}, bf16[480,768]{1,0:T(8,128)(2,1)}, f32[480,768]{1,0:T(8,128)}, f32[480,1]{1,0:T(8,128)}) custom-call(s32[4]{0:T(128)} %pad_add_fusion.refs_0_, s32[3]{0:T(128)} %refs_1_.10, f32[480,768]{1,0:T(8,128)} %get-tuple-element.151.refs_2_.refs_6_, ...), custom_call_target="tpu_custom_call" | custom-call | tf_op jit(solution)/shard_map/attention_forward/pallas_call | solution.py:63
  170.7 5.4 %collective-permute-done.21.refs_0_ = bf16[12,96,384]{2,1,0:T(8,128)(2,1)S(1)} collective-permute-done((bf16[12,96,384]{2,1,0:T(8,128)(2,1)S(1)}, bf16[12,96,384]{2,1,0:T(8,128)(2,1)S(1)}, u32[]{:S(2)}, u32[]{:S(2)}) %collective-permute-start.21) | collective-permute-done | bytes 884768 | tf_op jit(solution)/shard_map/ppermute | solution.py:729
  184.5 25.4 %ffn_both.1 = (bf16[480,768]{1,0:T(8,128)(2,1)}, f32[480,768]{1,0:T(8,128)}, bf16[480,768]{1,0:T(8,128)(2,1)}, f32[72,128]{1,0:T(8,128)}, bf16[36,96,384]{2,1,0:...) custom-call(s32[4]{0:T(128)} %pad_add_fusion.refs_0_, ...), custom_call_target="tpu_custom_call" | custom-call | tf_op jit(solution)/shard_map/ffn_both/pallas_call | solution.py:63
  211.3 4.7 %collective-permute-done.28.refs_1_ = bf16[36,96,384]{2,1,0:T(8,128)(2,1)S(1)} collective-permute-done((bf16[36,96,384]{2,1,0:T(8,128)(2,1)}, bf16[36,96,384]{2,1,0:T(8,128)(2,1)S(1)}, u32[]{:S(2)}, u32[]{:S(2)}) %collective-permute-start.28) | collective-permute-done | bytes 2654240 | tf_op jit(solution)/shard_map/ppermute | solution.py:729
  222.9 20.2 %attention_backward.2 = (f32[480,768]{1,0:T(8,128)}, f32[72,128]{1,0:T(8,128)}, bf16[12,96,384]{2,1,0:T(8,128)(2,1)}, bf16[12,96,384]{2,1,0:T(8,128)(2,1)}, bf16...) custom-call(s32[4]{0:T(128)} %pad_add_fusion.refs_0_, s32[3]{0:T(128)} %refs_1_.10, ...), custom_call_target="tpu_custom_call" | custom-call | tf_op jit(solution)/shard_map/attention_backward/pallas_call | solution.py:63
  243.1 4.9 %collective-permute-done.30.refs_1_.refs_3_ = bf16[18,96,384]{2,1,0:T(8,128)(2,1)S(1)} collective-permute-done((bf16[18,96,384]{2,1,0:T(8,128)(2,1)S(1)}, bf16[18,96,384]{2,1,0:T(8,128)(2,1)S(1)}, u32[]{:S(2)}, u32[]{:S(2)}) %collective-permute-start.30) | collective-permute-done | bytes 1327136 | tf_op jit(solution)/shard_map/ppermute | solution.py:729
  248.0 4.8 %collective-permute-done.29.refs_1_.refs_2_ = bf16[18,96,384]{2,1,0:T(8,128)(2,1)S(1)} collective-permute-done((bf16[18,96,384]{2,1,0:T(8,128)(2,1)S(1)}, bf16[18,96,384]{2,1,0:T(8,128)(2,1)S(1)}, u32[]{:S(2)}, u32[]{:S(2)}) %collective-permute-start.29) | collective-permute-done | bytes 1327136 | tf_op jit(solution)/shard_map/ppermute | solution.py:729
  265.1 22.5 %ffn_backward.1 = (f32[480,768]{1,0:T(8,128)}, bf16[480,768]{1,0:T(8,128)(2,1)}, f32[72,128]{1,0:T(8,128)}, bf16[36,96,384]{2,1,0:T(8,128)(2,1)}, bf16[36,96,384...) custom-call(s32[4]{0:T(128)} %pad_add_fusion.refs_0_, ...), custom_call_target="tpu_custom_call" | custom-call | tf_op jit(solution)/shard_map/ffn_backward/pallas_call | solution.py:63
  300.6 3.3 collect.2.refs_25_
  306.0 19.9 %attention_backward.3 = (f32[480,768]{1,0:T(8,128)}, f32[144,128]{1,0:T(8,128)}, bf16[12,96,384]{2,1,0:T(8,128)(2,1)}, bf16[12,96,384]{2,1,0:T(8,128)(2,1)}, bf1...) custom-call(s32[4]{0:T(128)} %pad_add_fusion.refs_0_, s32[3]{0:T(128)} %refs_1_.10, ...), custom_call_target="tpu_custom_call" | custom-call | tf_op jit(solution)/shard_map/attention_backward/pallas_call | solution.py:63
  326.0 8.5 %collective-permute-done.42.refs_3_.refs_1_ = bf16[18,96,384]{2,1,0:T(8,128)(2,1)S(1)} collective-permute-done((bf16[18,96,384]{2,1,0:T(8,128)(2,1)S(1)}, bf16[18,96,384]{2,1,0:T(8,128)(2,1)S(1)}, u32[]{:S(2)}, u32[]{:S(2)}) %collective-permute-start.42) | collective-permute-done | bytes 1327136 | tf_op jit(solution)/shard_map/ppermute | solution.py:729
  352.4 3.0 collective-permute-done.49
  355.4 2.7 collective-permute-start.50
  358.1 3.7 collective-permute-done.50
  362.2 7.7 %collective-permute-done.52.refs_1_ = bf16[6,96,384]{2,1,0:T(8,128)(2,1)} collective-permute-done((bf16[6,96,384]{2,1,0:T(8,128)(2,1)S(1)}, bf16[6,96,384]{2,1,0:T(8,128)(2,1)}, u32[]{:S(2)}, u32[]{:S(2)}) %collective-permute-start.52) | collective-permute-done | bytes 442400 | tf_op jit(solution)/shard_map/ppermute | solution.py:729
  380.3 3.5 collect.3.refs_1_.refs_14_.refs_19_
  386.7 11.5 %collective-permute-done.54.refs_7_ = bf16[6,96,384]{2,1,0:T(8,128)(2,1)S(1)} collective-permute-done((bf16[6,96,384]{2,1,0:T(8,128)(2,1)}, bf16[6,96,384]{2,1,0:T(8,128)(2,1)S(1)}, u32[]{:S(2)}, u32[]{:S(2)}) %collective-permute-start.54) | collective-permute-done | bytes 442400 | tf_op jit(solution)/shard_map/ppermute | solution.py:729
  399.3 3.7 collective-permute-done.59
  405.1 3.3 collective-permute-done.60
  410.2 7.9 %update_layer.2 = (f32[2,6,96,384]{3,2,1,0:T(8,128)}, f32[2,6,96,384]{3,2,1,0:T(8,128)}, f32[2,6,96,384]{3,2,1,0:T(8,128)}, f32[2,6,96,384]{3,2,1,0:T(8,128)}, bf16[2,6,96,384]{3,2,1,0:T(8,128)(2,1)}) custom-call(s32[4]{0:T(128)} %pad_add_fusion.refs_0_, bf16[6,96,384]{2,1,0:T(8,128)(2,1)} %gate.19.refs_1_.refs_6_, f32[2,6,96,384]{3,2,1,0:T(8,128)} %refs_2_.4, ...), custom_call_target="tpu_custom_call" | custom-call | tf_op jit(solution)/shard_map/update_layer/pallas_call | solution.py:63
  418.2 4.7 %reduce-scatter.3.cloned.1.call-done.refs_0_ = bf16[6,96,384]{2,1,0:T(8,128)(2,1)} async-done(((bf16[24,96,384]{2,1,0:T(8,128)(2,1)}), bf16[6,96,384]{2,1,0:T(8,128)(2,1)}) %reduce-scatter.3.cloned.1.call-update) | async-done | bytes 442384 | tf_op jit(solution)/shard_map/reduce_scatter | solution.py:840
  424.4 10.5 %collective-permute-done.61.refs_7_ = bf16[6,96,384]{2,1,0:T(8,128)(2,1)S(1)} collective-permute-done((bf16[6,96,384]{2,1,0:T(8,128)(2,1)}, bf16[6,96,384]{2,1,0:T(8,128)(2,1)S(1)}, u32[]{:S(2)}, u32[]{:S(2)}) %collective-permute-start.61) | collective-permute-done | bytes 442400 | tf_op jit(solution)/shard_map/ppermute | solution.py:729
  437.4 7.9 %update_layer.3 = (f32[2,6,96,384]{3,2,1,0:T(8,128)}, f32[2,6,96,384]{3,2,1,0:T(8,128)}, f32[2,6,96,384]{3,2,1,0:T(8,128)}, f32[2,6,96,384]{3,2,1,0:T(8,128)}, bf16[2,6,96,384]{3,2,1,0:T(8,128)(2,1)}) custom-call(s32[4]{0:T(128)} %pad_add_fusion.refs_0_, ...), custom_call_target="tpu_custom_call", output_to_operand_aliasing={{0}: (14, {}), {1}: (15, {}), {2}: (16, {}), {3}: (17, {}),... | custom-call | tf_op jit(solution)/shard_map/update_layer/pallas_call | solution.py:63
  (363 shorter events, 140.6 us)
Async XLA Ops:
  7.2 45.2 %all-gather.6.cloned.1.call-start = ((), (), s32[]{:S(2)}) async-start(), calls=%async_computation.4 | async-start | bytes 1474560 | tf_op jit(solution)/shard_map/all_gather | solution.py:741
  9.1 91.6 %all-gather.8.cloned.1.call-start = ((), (), s32[]{:S(2)}) async-start(), calls=%async_computation.5 | async-start | bytes 2211840 | tf_op jit(solution)/shard_map/all_gather | solution.py:741
  11.2 374.4 %reduce-scatter.5.cloned.1.call-start = ((), (), s32[]{:S(2)}) async-start(), calls=%async_computation.3 | async-start | bytes 2211840 | tf_op jit(solution)/shard_map/reduce_scatter | solution.py:840
  79.0 21.7 %collective-permute-start.10 = (bf16[16,96,384]{2,1,0:T(8,128)(2,1)S(1)}, bf16[16,96,384]{2,1,0:T(8,128)(2,1)S(1)}, u32[]{:S(2)}, u32[]{:S(2)}) collective-permute-start(bf16[16,96,384]{2,1,0:T(8,128)(2,1)S(1)} %get-tuple-element.137.refs_2_.refs_16_.refs_15_.refs_22_.refs_21_), channel_id=1, source_target_pairs={{0,4},{1,5},{2,6},{3,7},{4,0},{5,1},{6,2},{7,3},{8,12},{9,13},{10,... | collective-permute-start | bytes 3538952 | tf_op jit(solution)/shard_map/ppermute | solution.py:729
  79.6 24.1 %collective-permute-start.9 = (bf16[16,96,384]{2,1,0:T(8,128)(2,1)S(1)}, bf16[16,96,384]{2,1,0:T(8,128)(2,1)}, u32[]{:S(2)}, u32[]{:S(2)}) collective-permute-start(bf16[16,96,384]{2,1,0:T(8,128)(2,1)S(1)} %get-tuple-element.136.refs_1_.refs_12_.refs_11_.refs_18_.refs_17_), channel_id=1, source_target_pairs={{0,2},{1,3},{2,0},{3,1},{4,6},{5,7},{6,4},{7,5},{8,10},{9,11},{10,... | collective-permute-start | bytes 3538952 | tf_op jit(solution)/shard_map/ppermute | solution.py:729
  80.2 26.0 %collective-permute-start.3 = (bf16[16,96,384]{2,1,0:T(8,128)(2,1)}, bf16[16,96,384]{2,1,0:T(8,128)(2,1)}, u32[]{:S(2)}, u32[]{:S(2)}) collective-permute-start(bf16[16,96,384]{2,1,0:T(8,128)(2,1)} %get-tuple-element.132.refs_3_), channel_id=1, source_target_pairs={{0,1},{1,0},{2,3},{3,2},{4,5},{5,4},{6,7},{7,6},{8,9},{9,8},{10,11... | collective-permute-start | bytes 3538952 | tf_op jit(solution)/shard_map/ppermute | solution.py:729
  80.2 24.1 %collective-permute-start.4 = (bf16[8,96,384]{2,1,0:T(8,128)(2,1)}, bf16[8,96,384]{2,1,0:T(8,128)(2,1)}, u32[]{:S(2)}, u32[]{:S(2)}) collective-permute-start(bf16[8,96,384]{2,1,0:T(8,128)(2,1)} %collective-permute-done.2.refs_4_.refs_5_.refs_11_.refs_10_), channel_id=1, source_target_pairs={{0,1},{1,0},{2,3},{3,2},{4,5},{5,4},{6,7},{7,6},{8,9},{9,8},{10,11... | collective-permute-start | bytes 1769480 | tf_op jit(solution)/shard_map/ppermute | solution.py:729
  80.7 25.5 %collective-permute-start.6 = (bf16[8,96,384]{2,1,0:T(8,128)(2,1)}, bf16[8,96,384]{2,1,0:T(8,128)(2,1)}, u32[]{:S(2)}, u32[]{:S(2)}) collective-permute-start(bf16[8,96,384]{2,1,0:T(8,128)(2,1)} %collective-permute-done.5.refs_5_.refs_9_.refs_8_.refs_15_.refs_14_), channel_id=1, source_target_pairs={{0,1},{1,0},{2,3},{3,2},{4,5},{5,4},{6,7},{7,6},{8,9},{9,8},{10,11... | collective-permute-start | bytes 1769480 | tf_op jit(solution)/shard_map/ppermute | solution.py:729
  103.6 21.9 %collective-permute-start.14 = (bf16[12,96,384]{2,1,0:T(8,128)(2,1)}, bf16[12,96,384]{2,1,0:T(8,128)(2,1)S(1)}, u32[]{:S(2)}, u32[]{:S(2)}) collective-permute-start(bf16[12,96,384]{2,1,0:T(8,128)(2,1)} %get-tuple-element.139.refs_2_.refs_20_.refs_0_), channel_id=1, source_target_pairs={{0,4},{1,5},{2,6},{3,7},{4,0},{5,1},{6,2},{7,3},{8,12},{9,13},{10,... | collective-permute-start | bytes 2654216 | tf_op jit(solution)/shard_map/ppermute | solution.py:729
  105.5 21.4 %collective-permute-start.15 = (bf16[12,96,384]{2,1,0:T(8,128)(2,1)S(1)}, bf16[12,96,384]{2,1,0:T(8,128)(2,1)S(1)}, u32[]{:S(2)}, u32[]{:S(2)}) collective-permute-start(bf16[12,96,384]{2,1,0:T(8,128)(2,1)S(1)} %copy-done.5), channel_id=1, source_target_pairs={{0,2},{1,3},{2,0},{3,1},{4,6},{5,7},{6,4},{7,5},{8,10},{9,11},{10,... | collective-permute-start | bytes 2654216 | tf_op jit(solution)/shard_map/ppermute | solution.py:729
  132.5 20.5 %collective-permute-start.16 = (bf16[12,96,384]{2,1,0:T(8,128)(2,1)S(1)}, bf16[12,96,384]{2,1,0:T(8,128)(2,1)S(1)}, u32[]{:S(2)}, u32[]{:S(2)}) collective-permute-start(bf16[12,96,384]{2,1,0:T(8,128)(2,1)S(1)} %get-tuple-element.145.refs_4_.refs_7_.refs_8_), channel_id=1, source_target_pairs={{0,2},{1,3},{2,0},{3,1},{4,6},{5,7},{6,4},{7,5},{8,10},{9,11},{10,... | collective-permute-start | bytes 2654216 | tf_op jit(solution)/shard_map/ppermute | solution.py:729
  133.2 20.3 %collective-permute-start.17 = (bf16[12,96,384]{2,1,0:T(8,128)(2,1)S(1)}, bf16[12,96,384]{2,1,0:T(8,128)(2,1)}, u32[]{:S(2)}, u32[]{:S(2)}) collective-permute-start(bf16[12,96,384]{2,1,0:T(8,128)(2,1)S(1)} %get-tuple-element.146.refs_5_.refs_8_.refs_11_.refs_12_), channel_id=1, source_target_pairs={{0,4},{1,5},{2,6},{3,7},{4,0},{5,1},{6,2},{7,3},{8,12},{9,13},{10,... | collective-permute-start | bytes 2654216 | tf_op jit(solution)/shard_map/ppermute | solution.py:729
  134.7 23.2 %collective-permute-start.18 = (bf16[24,96,384]{2,1,0:T(8,128)(2,1)}, bf16[24,96,384]{2,1,0:T(8,128)(2,1)}, u32[]{:S(2)}, u32[]{:S(2)}) collective-permute-start(bf16[24,96,384]{2,1,0:T(8,128)(2,1)} %get-tuple-element.147.refs_6_), channel_id=1, source_target_pairs={{0,1},{1,0},{2,3},{3,2},{4,5},{5,4},{6,7},{7,6},{8,9},{9,8},{10,11... | collective-permute-start | bytes 5308424 | tf_op jit(solution)/shard_map/ppermute | solution.py:729
  154.5 21.7 %collective-permute-start.21 = (bf16[12,96,384]{2,1,0:T(8,128)(2,1)S(1)}, bf16[12,96,384]{2,1,0:T(8,128)(2,1)S(1)}, u32[]{:S(2)}, u32[]{:S(2)}) collective-permute-start(bf16[12,96,384]{2,1,0:T(8,128)(2,1)S(1)} %copy-done.30), channel_id=1, source_target_pairs={{0,2},{1,3},{2,0},{3,1},{4,6},{5,7},{6,4},{7,5},{8,10},{9,11},{10,... | collective-permute-start | bytes 2654216 | tf_op jit(solution)/shard_map/ppermute | solution.py:729
  155.5 21.8 %collective-permute-start.22 = (bf16[12,96,384]{2,1,0:T(8,128)(2,1)S(1)}, bf16[12,96,384]{2,1,0:T(8,128)(2,1)S(1)}, u32[]{:S(2)}, u32[]{:S(2)}) collective-permute-start(bf16[12,96,384]{2,1,0:T(8,128)(2,1)S(1)} %copy-done.32), channel_id=1, source_target_pairs={{0,4},{1,5},{2,6},{3,7},{4,0},{5,1},{6,2},{7,3},{8,12},{9,13},{10,... | collective-permute-start | bytes 2654216 | tf_op jit(solution)/shard_map/ppermute | solution.py:729
  156.8 26.5 %collective-permute-start.23 = (bf16[24,96,384]{2,1,0:T(8,128)(2,1)}, bf16[24,96,384]{2,1,0:T(8,128)(2,1)}, u32[]{:S(2)}, u32[]{:S(2)}) collective-permute-start(bf16[24,96,384]{2,1,0:T(8,128)(2,1)} %copy-done.47), channel_id=1, source_target_pairs={{0,1},{1,0},{2,3},{3,2},{4,5},{5,4},{6,7},{7,6},{8,9},{9,8},{10,11... | collective-permute-start | bytes 5308424 | tf_op jit(solution)/shard_map/ppermute | solution.py:729
  182.6 27.3 %collective-permute-start.26 = (bf16[12,96,384]{2,1,0:T(8,128)(2,1)S(1)}, bf16[12,96,384]{2,1,0:T(8,128)(2,1)S(1)}, u32[]{:S(2)}, u32[]{:S(2)}) collective-permute-start(bf16[12,96,384]{2,1,0:T(8,128)(2,1)S(1)} %rounded.1.refs_23_.refs_10_), channel_id=1, source_target_pairs={{0,2},{1,3},{2,0},{3,1},{4,6},{5,7},{6,4},{7,5},{8,10},{9,11},{10,... | collective-permute-start | bytes 2654216 | tf_op jit(solution)/shard_map/ppermute | solution.py:729
  216.7 31.2 %collective-permute-start.30 = (bf16[18,96,384]{2,1,0:T(8,128)(2,1)S(1)}, bf16[18,96,384]{2,1,0:T(8,128)(2,1)S(1)}, u32[]{:S(2)}, u32[]{:S(2)}) collective-permute-start(bf16[18,96,384]{2,1,0:T(8,128)(2,1)S(1)} %get-tuple-element.173.refs_17_), channel_id=1, source_target_pairs={{0,4},{1,5},{2,6},{3,7},{4,0},{5,1},{6,2},{7,3},{8,12},{9,13},{10,... | collective-permute-start | bytes 3981320 | tf_op jit(solution)/shard_map/ppermute | solution.py:729
  221.6 31.2 %collective-permute-start.29 = (bf16[18,96,384]{2,1,0:T(8,128)(2,1)S(1)}, bf16[18,96,384]{2,1,0:T(8,128)(2,1)S(1)}, u32[]{:S(2)}, u32[]{:S(2)}) collective-permute-start(bf16[18,96,384]{2,1,0:T(8,128)(2,1)S(1)} %get-tuple-element.170.refs_16_), channel_id=1, source_target_pairs={{0,2},{1,3},{2,0},{3,1},{4,6},{5,7},{6,4},{7,5},{8,10},{9,11},{10,... | collective-permute-start | bytes 3981320 | tf_op jit(solution)/shard_map/ppermute | solution.py:729
  259.1 28.6 %collective-permute-start.38 = (bf16[9,96,384]{2,1,0:T(8,128)(2,1)S(1)}, bf16[9,96,384]{2,1,0:T(8,128)(2,1)S(1)}, u32[]{:S(2)}, u32[]{:S(2)}) collective-permute-start(bf16[9,96,384]{2,1,0:T(8,128)(2,1)S(1)} %get-tuple-element.182.refs_3_.refs_27_), channel_id=1, source_target_pairs={{0,2},{1,3},{2,0},{3,1},{4,6},{5,7},{6,4},{7,5},{8,10},{9,11},{10,... | collective-permute-start | bytes 1990664 | tf_op jit(solution)/shard_map/ppermute | solution.py:729
  261.6 26.0 %collective-permute-start.37 = (bf16[9,96,384]{2,1,0:T(8,128)(2,1)S(1)}, bf16[9,96,384]{2,1,0:T(8,128)(2,1)S(1)}, u32[]{:S(2)}, u32[]{:S(2)}) collective-permute-start(bf16[9,96,384]{2,1,0:T(8,128)(2,1)S(1)} %get-tuple-element.180.refs_2_.refs_26_), channel_id=1, source_target_pairs={{0,4},{1,5},{2,6},{3,7},{4,0},{5,1},{6,2},{7,3},{8,12},{9,13},{10,... | collective-permute-start | bytes 1990664 | tf_op jit(solution)/shard_map/ppermute | solution.py:729
  262.7 24.9 %collective-permute-start.35 = (bf16[6,96,384]{2,1,0:T(8,128)(2,1)S(1)}, bf16[6,96,384]{2,1,0:T(8,128)(2,1)S(1)}, u32[]{:S(2)}, u32[]{:S(2)}) collective-permute-start(bf16[6,96,384]{2,1,0:T(8,128)(2,1)S(1)} %get-tuple-element.190.refs_29_), channel_id=1, source_target_pairs={{0,4},{1,5},{2,6},{3,7},{4,0},{5,1},{6,2},{7,3},{8,12},{9,13},{10,... | collective-permute-start | bytes 1327112 | tf_op jit(solution)/shard_map/ppermute | solution.py:729
  264.3 23.4 %collective-permute-start.33 = (bf16[6,96,384]{2,1,0:T(8,128)(2,1)S(1)}, bf16[6,96,384]{2,1,0:T(8,128)(2,1)S(1)}, u32[]{:S(2)}, u32[]{:S(2)}) collective-permute-start(bf16[6,96,384]{2,1,0:T(8,128)(2,1)S(1)} %get-tuple-element.187.refs_28_), channel_id=1, source_target_pairs={{0,2},{1,3},{2,0},{3,1},{4,6},{5,7},{6,4},{7,5},{8,10},{9,11},{10,... | collective-permute-start | bytes 1327112 | tf_op jit(solution)/shard_map/ppermute | solution.py:729
  304.0 118.9 %reduce-scatter.3.cloned.1.call-start = ((), (), s32[]{:S(2)}) async-start(), calls=%async_computation.2 | async-start | bytes 2211840 | tf_op jit(solution)/shard_map/reduce_scatter | solution.py:840
  304.0 30.4 %collective-permute-start.42 = (bf16[18,96,384]{2,1,0:T(8,128)(2,1)S(1)}, bf16[18,96,384]{2,1,0:T(8,128)(2,1)S(1)}, u32[]{:S(2)}, u32[]{:S(2)}) collective-permute-start(bf16[18,96,384]{2,1,0:T(8,128)(2,1)S(1)} %get-tuple-element.212.refs_9_), channel_id=1, source_target_pairs={{0,4},{1,5},{2,6},{3,7},{4,0},{5,1},{6,2},{7,3},{8,12},{9,13},{10,... | collective-permute-start | bytes 3981320 | tf_op jit(solution)/shard_map/ppermute | solution.py:729
  304.9 30.4 %collective-permute-start.41 = (bf16[18,96,384]{2,1,0:T(8,128)(2,1)S(1)}, bf16[18,96,384]{2,1,0:T(8,128)(2,1)S(1)}, u32[]{:S(2)}, u32[]{:S(2)}) collective-permute-start(bf16[18,96,384]{2,1,0:T(8,128)(2,1)S(1)} %get-tuple-element.209.refs_8_), channel_id=1, source_target_pairs={{0,2},{1,3},{2,0},{3,1},{4,6},{5,7},{6,4},{7,5},{8,10},{9,11},{10,... | collective-permute-start | bytes 3981320 | tf_op jit(solution)/shard_map/ppermute | solution.py:729
  340.8 21.0 %collective-permute-start.46 = (bf16[9,96,384]{2,1,0:T(8,128)(2,1)S(1)}, bf16[9,96,384]{2,1,0:T(8,128)(2,1)S(1)}, u32[]{:S(2)}, u32[]{:S(2)}) collective-permute-start(bf16[9,96,384]{2,1,0:T(8,128)(2,1)S(1)} %get-tuple-element.221.refs_3_), channel_id=1, source_target_pairs={{0,2},{1,3},{2,0},{3,1},{4,6},{5,7},{6,4},{7,5},{8,10},{9,11},{10,... | collective-permute-start | bytes 1990664 | tf_op jit(solution)/shard_map/ppermute | solution.py:729
  346.1 23.9 %collective-permute-start.52 = (bf16[6,96,384]{2,1,0:T(8,128)(2,1)S(1)}, bf16[6,96,384]{2,1,0:T(8,128)(2,1)}, u32[]{:S(2)}, u32[]{:S(2)}) collective-permute-start(bf16[6,96,384]{2,1,0:T(8,128)(2,1)S(1)} %get-tuple-element.227.refs_2_), channel_id=1, source_target_pairs={{0,4},{1,5},{2,6},{3,7},{4,0},{5,1},{6,2},{7,3},{8,12},{9,13},{10,... | collective-permute-start | bytes 1327112 | tf_op jit(solution)/shard_map/ppermute | solution.py:729
  347.5 25.7 %collective-permute-start.44 = (bf16[6,96,384]{2,1,0:T(8,128)(2,1)S(1)}, bf16[6,96,384]{2,1,0:T(8,128)(2,1)}, u32[]{:S(2)}, u32[]{:S(2)}) collective-permute-start(bf16[6,96,384]{2,1,0:T(8,128)(2,1)S(1)} %get-tuple-element.223.refs_1_), channel_id=1, source_target_pairs={{0,2},{1,3},{2,0},{3,1},{4,6},{5,7},{6,4},{7,5},{8,10},{9,11},{10,... | collective-permute-start | bytes 1327112 | tf_op jit(solution)/shard_map/ppermute | solution.py:729
  385.1 23.9 %collective-permute-start.57 = (bf16[12,96,384]{2,1,0:T(8,128)(2,1)S(1)}, bf16[12,96,384]{2,1,0:T(8,128)(2,1)S(1)}, u32[]{:S(2)}, u32[]{:S(2)}) collective-permute-start(bf16[12,96,384]{2,1,0:T(8,128)(2,1)S(1)} %copy-done.8), channel_id=1, source_target_pairs={{0,1},{1,0},{2,3},{3,2},{4,5},{5,4},{6,7},{7,6},{8,9},{9,8},{10,11... | collective-permute-start | bytes 2654216 | tf_op jit(solution)/shard_map/ppermute | solution.py:729
  385.3 23.7 %collective-permute-start.58 = (bf16[12,96,384]{2,1,0:T(8,128)(2,1)S(1)}, bf16[12,96,384]{2,1,0:T(8,128)(2,1)S(1)}, u32[]{:S(2)}, u32[]{:S(2)}) collective-permute-start(bf16[12,96,384]{2,1,0:T(8,128)(2,1)S(1)} %copy-done.86), channel_id=1, source_target_pairs={{0,1},{1,0},{2,3},{3,2},{4,5},{5,4},{6,7},{7,6},{8,9},{9,8},{10,11... | collective-permute-start | bytes 2654216 | tf_op jit(solution)/shard_map/ppermute | solution.py:729
  386.7 22.3 %collective-permute-start.55 = (bf16[6,96,384]{2,1,0:T(8,128)(2,1)}, bf16[6,96,384]{2,1,0:T(8,128)(2,1)}, u32[]{:S(2)}, u32[]{:S(2)}) collective-permute-start(bf16[6,96,384]{2,1,0:T(8,128)(2,1)} %gate.19.refs_1_.refs_6_), channel_id=1, source_target_pairs={{0,1},{1,0},{2,3},{3,2},{4,5},{5,4},{6,7},{7,6},{8,9},{9,8},{10,11... | collective-permute-start | bytes 1327112 | tf_op jit(solution)/shard_map/ppermute | solution.py:729
  (133 other events, 613.5 us)
Sparse Core Ops, SparseCore 0:
  10.2 38.0 all-gather.5
  50.3 40.3 all-gather.7
  304.1 38.7 reduce-scatter.4
  384.1 38.7 reduce-scatter.2

commit v5 on v4

--- a/solution.py
+++ b/solution.py
@@ -41,25 +41,27 @@
 
 
 class Part:
-    def __init__(self, zs, js, order, arrays=None, offsets=(0, 0, 0, 0)):
+    def __init__(self, zs, js, order, arrays=None, offsets=(0, 0, 0, 0), strides=None):
         self.zs, self.js, self.order = tuple(zs), tuple(js), order
         self.arrays, self.offsets = arrays, offsets
+        many = len(self.zs) * len(self.js)
+        self.strides = strides or (2 * many, many, len(self.js), 1)
 
     def index(self, first, second, z, j):
-        place = self.zs.index(z) * len(self.js) + self.js.index(j)
-        return (first * 2 + second) * len(self.zs) * len(self.js) + place
+        of_first, of_second, of_z, of_j = self.strides
+        return first * of_first + second * of_second + self.zs.index(z) * of_z + self.js.index(j) * of_j
 
     def count(self):
         return 4 * len(self.zs) * len(self.js)
 
 
-def launch(body, name, ins, out_shape, out_specs, deps=(), scratch=(), cost=None, aliases=None, limit=16, **grid):
+def launch(body, name, ins, out_shape, out_specs, deps=(), scratch=(), cost=None, aliases=None, limit=16, weight=0, **grid):
     count, extra = len(ins), len(deps)
 
     def kernel(*refs):
         body(*refs[:count], *refs[count + extra :])
 
-    flops, moved, special = 0, 0, 0
+    flops, moved, special = weight, 0, 0
     return pl.pallas_call(
         kernel,
         in_specs=[spec for _, spec in ins] + [ANY] * extra,
@@ -192,10 +194,6 @@
         sums_ref[at : at + 1, :] = values[:, 128 * n : 128 * (n + 1)]
 
 
-def launch_list(*args, **kwargs):
-    return list(launch(*args, **kwargs))
-
-
 def segment(small_ref, number, width):
     return small_ref[0:1, number * width : (number + 1) * width]
 
@@ -215,13 +213,18 @@
     return low, (ones.astype(BF), (1.0 - ones).astype(BF))
 
 
-def attention_forward_kernel(dims, parts, chains, pos_ref, len_ref, x_ref, small_ref, *rest):
+def project(small_ref, x, ctx, wo):
+    attended = mm(ctx, wo) + segment(small_ref, 2, x.shape[1])
+    return norm_forward(x.astype(F32) + attended)
+
+
+def attention_forward_kernel(dims, parts, names, chains, pos_ref, len_ref, x_ref, small_ref, *rest):
     refs, rest = unflatten(rest, parts)
-    qkv_ref, lse_ref, ctx_ref, unit_ref, inv_ref, w, sems = rest
+    qkv_ref, lse_ref, ctx_ref, *normed, w, sems = rest
     width, seq = dims.model, dims.rows // chains
     head = width // HEADS
     pos = (pos_ref[1], pos_ref[2], pos_ref[3])
-    for n, name in enumerate(("q", "k", "v", "o")):
+    for n, name in enumerate(names):
         start_loads(dims, parts, refs, pos, name, w, 0, n * width, sems.at[n])
     xb = x_ref[...].astype(BF)
     for n, bias in ((0, 0), (1, None), (2, 1)):
@@ -254,32 +257,33 @@
         return carry
 
     lax.fori_loop(0, chains, chain, 0)
-    wait_for(w.at[:, 3 * width :], sems.at[3])
-    attended = mm(ctx_ref[...], w[:, 3 * width :]) + segment(small_ref, 2, width)
-    unit, inverse = norm_forward(x_ref[...].astype(F32) + attended)
-    unit_ref[...] = unit
-    inv_ref[...] = inverse
-
-
-def attention_forward(dims, parts, pos, lengths, x, small, deps=()):
-    parts = needed_parts(dims, parts, ("q", "k", "v", "o"))
+    if normed:
+        wait_for(w.at[:, 3 * width :], sems.at[3])
+        unit, inverse = project(small_ref, x_ref[...], ctx_ref[...], w[:, 3 * width :])
+        normed[0][...] = unit
+        normed[1][...] = inverse
+
+
+def attention_forward(dims, parts, pos, lengths, x, small, deps=(), projected=True):
+    names = ("q", "k", "v", "o") if projected else ("q", "k", "v")
+    parts = needed_parts(dims, parts, names)
     chains = lengths.shape[0]
     rows, width = dims.rows, dims.model
+    outs = [
+        shape((rows, 3 * width), BF),
+        shape((chains, HEADS, rows // chains), F32),
+        shape((rows, width), BF),
+    ]
+    if projected:
+        outs += [shape((rows, width), F32), shape((rows, 1), F32)]
     return launch(
-        functools.partial(attention_forward_kernel, dims, parts, chains),
+        functools.partial(attention_forward_kernel, dims, parts, names, chains),
         "attention_forward",
         [(pos, SMEM), (lengths, SMEM), (x, VMEM), (small, VMEM)] + weight_ins(parts),
-        [
-            shape((rows, 3 * width), BF),
-            shape((chains, HEADS, rows // chains), F32),
-            shape((rows, width), BF),
-            shape((rows, width), F32),
-            shape((rows, 1), F32),
-        ],
-        [VMEM] * 5,
+        outs,
+        [VMEM] * len(outs),
         deps,
-        [pltpu.VMEM((width, 4 * width), BF), pltpu.SemaphoreType.DMA((4,))],
-        (12 * rows * width * width, 16 << 20, 1 << 20),
+        [pltpu.VMEM((width, len(names) * width), BF), pltpu.SemaphoreType.DMA((4,))],
         limit=56,
     )
 
@@ -317,7 +321,7 @@
     y_ref[...] = unit * segment(small_ref, 6, width) + segment(small_ref, 7, width)
 
 
-def ffn_forward(dims, parts, pos, unit, small, deps=()):
+def ffn_forward(dims, parts, pos, unit, small, deps=(), weight=0):
     parts = needed_parts(dims, parts, ("up", "down"))
     rows, width, ffn = dims.rows, dims.model, dims.ffn
     return launch(
@@ -335,6 +339,7 @@
         deps,
         [pltpu.VMEM((width, ffn), BF), pltpu.VMEM((ffn, width), BF), pltpu.SemaphoreType.DMA((2,))],
         (4 * rows * width * ffn, 24 << 20, 3 << 20),
+        weight=weight,
         limit=56,
     )
 
@@ -444,17 +449,21 @@
     return out[0], out[1], out[2], pair_up(out[3:], outs_parts)
 
 
-def ffn_both_kernel(dims, parts, outs_parts, chains, pos_ref, len_ref, cot_ref, small_ref, unit_ref, inv_ref, ctx_ref, *rest):
+def ffn_both_kernel(dims, parts, outs_parts, chains, pos_ref, len_ref, cot_ref, small_ref, x_ref, ctx_ref, *rest):
     refs, rest = unflatten(rest, parts)
     y_ref, gz1_ref, gctx_ref, sums_ref, *rest = rest
     count = 2 * len(outs_parts)
     outs = [rest[2 * n : 2 * n + 2] for n in range(len(outs_parts))]
-    up, down, wo, grad_up, grad_down, grad_o, sems, sem_out, act_ref, slope_ref = rest[count:]
+    up, down, wo, grad_up, grad_down, grad_o, sems, sem_out, act_ref, slope_ref, unit_ref, inv_ref = rest[count:]
     pos = (pos_ref[1], pos_ref[2], pos_ref[3])
+    start_loads(dims, parts, refs, pos, "o", wo, 0, 0, sems.at[2])
     start_loads(dims, parts, refs, pos, "up", up, 0, 0, sems.at[0])
     start_loads(dims, parts, refs, pos, "down", down, 0, 0, sems.at[1])
-    start_loads(dims, parts, refs, pos, "o", wo, 0, 0, sems.at[2])
     width, seq = dims.model, dims.rows // chains
+    wait_for(wo, sems.at[2])
+    unit, inverse = project(small_ref, x_ref[...], ctx_ref[...], wo[...])
+    unit_ref[...] = unit
+    inv_ref[...] = inverse
     total = ffn_forward_body(dims, small_ref, unit_ref, up, down, sems, act_ref, slope_ref)
     unit2, inv2 = norm_forward(total)
     y_ref[...] = (unit2 * segment(small_ref, 6, width) + segment(small_ref, 7, width)).astype(BF)
@@ -469,11 +478,11 @@
     ffn_backward_body(
         dims, outs_parts, outs, pos, gy, small_ref, unit_ref, inv_ref, ctx_ref,
         unit2, inv2, act_ref, slope_ref, up, down, wo, grad_up, grad_down, grad_o,
-        sem_out, gz1_ref, gctx_ref, sums_ref, lambda: wait_for(wo, sems.at[2]),
-    )
-
-
-def ffn_both(dims, parts, outs_parts, pos, lengths, cot, small, unit, inv, ctx, deps=()):
+        sem_out, gz1_ref, gctx_ref, sums_ref, lambda: None,
+    )
+
+
+def ffn_both(dims, parts, outs_parts, pos, lengths, cot, small, x, ctx, deps=()):
     parts = needed_parts(dims, parts, ("up", "down", "o"))
     rows, width, ffn = dims.rows, dims.model, dims.ffn
     grads = grad_shapes(dims, outs_parts)
@@ -481,7 +490,7 @@
         functools.partial(ffn_both_kernel, dims, parts, outs_parts, lengths.shape[0]),
         "ffn_both",
         [(pos, SMEM), (lengths, SMEM)]
-        + [(a, VMEM) for a in (cot, small, unit, inv, ctx)]
+        + [(a, VMEM) for a in (cot, small, x, ctx)]
         + weight_ins(parts),
         [
             shape((rows, width), BF),
@@ -492,7 +501,9 @@
         + grads,
         [VMEM] * 4 + [ANY] * len(grads),
         deps,
-        ffn_scratch(dims) + [pltpu.VMEM((rows, ffn), BF)] * 2,
+        ffn_scratch(dims)
+        + [pltpu.VMEM((rows, ffn), BF)] * 2
+        + [pltpu.VMEM((rows, width), F32), pltpu.VMEM((rows, 1), F32)],
         (12 * rows * width * ffn + 4 * rows * width * width, 40 << 20, 3 << 20),
         limit=56,
     )
@@ -651,6 +662,14 @@
     wait_for(hold, sems[1].at[pairs])
 
 
+def stack_kernel(*refs):
+    *ins, out, sem = refs
+    count = ins[0].shape[0]
+    for n, ref in enumerate(ins):
+        pltpu.make_async_copy(ref, out.at[pl.ds(n * count, count)], sem).start()
+    wait_for(out, sem)
+
+
 def round_kernel(src_ref, dst_ref):
     dst_ref[...] = src_ref[...].astype(BF)
 
@@ -779,11 +798,11 @@
     def joined(self, lot, got, zs, deps=()):
         ins, ranges, sizes = [], [], []
         for (part, own), g in zip(lot, got):
-            count = len(part.js)
+            count = own.shape[0] // len(part.zs)
             ranges.append((part.zs.index(zs[0]) * count, len(zs) * count))
             sizes.append(self.pieces(2 * len(zs) * count))
             ins += [own, g]
-        return launch_list(
+        return launch(
             functools.partial(join_kernel, ranges),
             "join",
             [(a, ANY) for a in ins],
@@ -792,10 +811,27 @@
             deps,
             [pltpu.VMEM((sum(a.shape[0] for a in sizes),) + sizes[0].shape[1:], BF)]
             + [pltpu.SemaphoreType.DMA((2,)), pltpu.SemaphoreType.DMA((3,))],
+            limit=60,
         )
 
     def second_swap(self, lot, both):
         return [self.swap(b, part.order[0]) for (part, _), b in zip(lot, both)]
+
+    def plane(self, own, js, deps):
+        got = [self.swap(own, "x"), self.swap(own, "y")]
+        got.append(self.permute(own, lambda z, x, y, c: (z, 1 - x, 1 - y, c)))
+        count = own.shape[0]
+        whole = launch(
+            stack_kernel,
+            "stack",
+            [(a, ANY) for a in [own, *got]],
+            self.pieces(4 * count),
+            VMEM,
+            deps,
+            [pltpu.SemaphoreType.DMA],
+        )
+        part = Part(range(Z_SLABS), js, "yx", None, (0, 2 * count) * 2, (2 * count, count, 4 * count, 1))
+        return part, whole
 
     def core_swap(self, lot, zs, both, got):
         others = self.swap(both[-1], "c")
@@ -805,21 +841,21 @@
             at += b.shape[0]
         return parts
 
-    def add(self, keep, got, deps=()):
+    def add(self, keep, got, deps=(), weight=0):
         sums = []
         for own, other in zip(keep, got):
             out = [self.pieces(own.shape[0] // 2)] * 2
-            sums.append(launch(add_kernel, "add", [(own, VMEM), (other, VMEM)], out, [VMEM] * 2, deps))
+            sums.append(launch(add_kernel, "add", [(own, VMEM), (other, VMEM)], out, [VMEM] * 2, deps, weight=weight))
         return [kept for kept, _ in sums], [sent for _, sent in sums]
 
-    def core_sum(self, parts, deps=()):
+    def core_sum(self, parts, deps=(), weight=0):
         got = [self.swap(p.arrays[1], "c") for p in parts]
-        return self.add([p.arrays[0] for p in parts], got, deps)
+        return self.add([p.arrays[0] for p in parts], got, deps, weight)
 
     def swaps(self, sums, axes):
         return [self.swap(a, axis) for a, axis in zip(sums[1], axes)]
 
-    def collect(self, zs, sums, got, deps=()):
+    def collect(self, zs, sums, got, deps=(), weight=0):
         ins = []
         for (kept, _), others in zip(sums, got):
             for own, other in zip(kept, others):
@@ -834,6 +870,8 @@
             [pltpu.VMEM((Z_SLABS * self.dims.own,) + ins[0].shape[1:], BF)]
             + [pltpu.VMEM(a.shape, BF) for a in ins]
             + [pltpu.SemaphoreType.DMA((len(ins) + 1,))],
+            weight=weight,
+            limit=60,
         )
 
     def column_sum(self, whole):
@@ -848,8 +886,8 @@
             values = values + self.permute(values, lambda z, x, y, c, bit=bit: (z ^ bit, x, y, c))
         return values
 
-    def group(self, own):
-        other = self.swap(own, "y")
+    def group(self, own, deps=()):
+        (other,) = self.gate([self.swap(own, "y")], deps)
         return [own, other, self.swap(own, "c"), self.swap(other, "c")]
 
 
@@ -999,20 +1037,22 @@
     last = LAYERS - 1
     saved = []
     for n in range(LAYERS):
-        qkv, lse, ctx, unit, inv = attention_forward(dims, weights[n], pos, lengths, x, small[n])
-        saved.append([x, qkv, lse, ctx, unit, inv])
+        qkv, lse, ctx, *normed = attention_forward(
+            dims, weights[n], pos, lengths, x, small[n], projected=n < last
+        )
+        saved.append([x, qkv, lse, ctx, *normed])
         if n < last:
-            *rest, x = ffn_forward(dims, weights[n], pos, unit, small[n])
+            *rest, x = ffn_forward(dims, weights[n], pos, normed[0], small[n])
             saved[n] += rest
     owned = [None] * LAYERS
     for n in reversed(range(LAYERS)):
-        x, qkv, lse, ctx, unit, inv, *rest = saved[n]
+        x, qkv, lse, ctx, *rest = saved[n]
         if n == last:
             y, gz1, gctx, sums_a, early = ffn_both(
-                dims, weights[n], net.early, pos, lengths, cot, small[n], unit, inv, ctx
+                dims, weights[n], net.early, pos, lengths, cot, small[n], x, ctx
             )
         else:
-            act, slope, unit2, inv2 = rest
+            unit, inv, act, slope, unit2, inv2 = rest
             gz1, gctx, sums_a, early = ffn_backward(
                 dims, weights[n], net.early, pos, gy, small[n], unit, inv, ctx, unit2, inv2, act, slope
             )
@@ -1029,19 +1069,22 @@
     own, every = tuple(range(dims.own)), tuple(range(Z_SLABS))
     third = dims.own // 3
 
-    low_zs, high_zs = every[: Z_SLABS // 2], every[Z_SLABS // 2 :]
+    low_zs, high_zs = every[:1], every[1:]
     third = dims.own // 3
     whole_a = net.whole_column(masters[0, :third].astype(BF))
     whole_b = net.whole_column(masters[0, third:].astype(BF))
-    whole1 = net.whole_column(masters[1].astype(BF))
-    lot = net.whole_lot(whole_a, every, own[:third])
+    most = 2 * third
+    whole1 = net.whole_column(masters[1, :most].astype(BF))
+    part1, plane1 = net.plane(masters[1, most:].astype(BF), own[most:], [whole_a])
+    lot = net.whole_lot(whole_a, every, own[:third], [plane1])
+    plane1 = net.whole_column(plane1)
     both = net.joined(lot, net.first_swap(lot), every)
     got = net.second_swap(lot, both)
     weights0 = net.core_swap(lot, every, both, got)
     lot = net.whole_lot(whole_b, every, own[third:], both)
     both = net.joined(lot, net.first_swap(lot), every, got)
     got = net.second_swap(lot, both)
-    lot_b = net.whole_lot(whole1, every, own, both)
+    lot_b = net.whole_lot(whole1, every, own[:most], both)
     weights0 += net.core_swap(lot, every, both, net.gate(got, [a for _, a in lot_b]))
 
     lot = lot_b
@@ -1051,17 +1094,19 @@
     )
     both = net.joined(lot, got, low_zs, [inv0])
     both_b = net.joined(lot, got, high_zs, both)
-    act0, slope0, unit0b, inv0b, y0 = ffn_forward(dims, weights0, pos, unit0, small[0], both_b)
-    got = net.gate(net.second_swap(lot, both), [inv0b])
-    weights1 = net.core_swap(lot, low_zs, both, got)
+    act0, slope0, unit0b, inv0b, y0 = ffn_forward(dims, weights0, pos, unit0, small[0], both_b, 10**11)
+    (plane1,) = net.gate([plane1], both_b[:1])
+    other1, *got = net.gate([net.swap(plane1, "c"), *net.second_swap(lot, both)], [inv0b])
+    part1.arrays = [plane1, plane1, other1, other1]
+    weights1 = [part1] + net.core_swap(lot, low_zs, both, got)
     got = net.second_swap(lot, both_b)
-    qkv1, lse1, ctx1, unit1, inv1 = attention_forward(dims, weights1, pos, lengths, y0, small[1])
-    got = net.gate(got, [inv1])
+    qkv1, lse1, ctx1 = attention_forward(dims, weights1, pos, lengths, y0, small[1], projected=False)
+    got = net.gate(got, [lse1])
     weights1 += net.core_swap(lot, high_zs, both_b, got)
 
     roots = net.rounded(right_roots.reshape((-1,) + right_roots.shape[2:]), got)
     y1, gz1, gctx, sums, early1 = ffn_both(
-        dims, weights1, net.early, pos, lengths, cot, small[1], unit1, inv1, ctx1, [roots]
+        dims, weights1, net.early, pos, lengths, cot, small[1], y0, ctx1, [roots]
     )
     roots_y = net.swap(roots, "y")
     net.hold(early1, [roots_y])
@@ -1073,9 +1118,8 @@
         dims, weights1, net.late, pos, lengths, gz1, gctx, qkv1, lse1, y0, [sums], early1[1]
     )
     got = net.swaps(early1, "yx")
-    net.hold(late1, got)
-    early1 = net.add(early1[0], got, [gx1])
-    late1 = net.core_sum(late1, early1[1])
+    late1 = net.core_sum(late1)
+    early1 = net.add(early1[0], got, late1[1])
     got_l, got_e = net.swaps(late1, "yx"), net.swaps(early1, "xy")
     gz0, gctx0, sums, early0 = ffn_backward(
         dims, weights0, net.early, pos, gx1, small[0], unit0, inv0, ctx0, unit0b, inv0b, act0, slope0,
@@ -1084,27 +1128,24 @@
     net.hold(early0, [*got_l, *got_e])
     late1 = net.add(late1[0], got_l)
     got_l = net.swaps(late1, "xy")
-    early0 = net.core_sum(early0, late1[1])
-    whole1 = net.collect(split, (late1, early1), (got_l, got_e), early0[1])
+    early0 = net.core_sum(early0, got_l)
     gx0, sums, late0 = attention_backward(
-        dims, weights0, net.late, pos, lengths, gz0, gctx0, qkv0, lse0, x, [sums, sums1], [whole1]
-    )
+        dims, weights0, net.late, pos, lengths, gz0, gctx0, qkv0, lse0, x, [sums, sums1],
+        early0[1],
+    )
+    whole1 = net.collect(split, (late1, early1), (got_l, got_e), [gx0])
 
     got = net.swaps(early0, "yx")
-    net.hold(late0, got)
-    early0 = net.add(early0[0], got, [gx0])
-    late0 = net.core_sum(late0, early0[1])
+    late0 = net.core_sum(late0, [*got, whole1], 10**11)
+    early0 = net.add(early0[0], got, late0[1])
     got_l, got_e = net.swaps(late0, "yx"), net.swaps(early0, "xy")
-    (sums,) = net.gate([sums], late0[1])
-    sums = net.small_sum(sums, ("c",), (1, 2))
-    late0 = net.add(late0[0], got_l, [*got_e, sums])
+    late0 = net.add(late0[0], got_l, early0[1])
     got_l = net.swaps(late0, "xy")
     whole0 = net.collect(split, (late0, early0), (got_l, got_e))
     low0 = net.column_sum(whole0)
-    (low1,) = net.gate([net.column_sum(whole1)], [whole0])
+    low1, sums = net.gate([net.column_sum(whole1), sums], [whole0])
+    sums = net.small_sum(sums, ("c", "x", "y"), ())
     grads1 = net.group(low1)
-    (sums,) = net.gate([sums], [whole0])
-    sums = net.small_sum(sums, ("x", "y"), ())
 
     def update(n, wide, grads, before):
         return update_layer(
@@ -1112,8 +1153,9 @@
         )
 
     done = update(1, low1, grads1, None)
-    (low0,) = net.gate([low0], [done[0], sums])
-    done = update(0, low0, net.group(low0), done)
+    low0, sums = net.gate([low0, sums], [done[0]])
+    sums = net.small_sum(sums, (), (1, 2))
+    done = update(0, low0, net.group(low0, [sums]), done)
     return y1, gx0, done, sums
 
 

time: 460 us -> 431 us (0.937)
  waiting for transfers between devices: 141 us -> 117 us
  local copies, waits for them, and re-layouts: 49.6 us -> 32.1 us
  Pallas kernels: 173 us -> 180 us
    ppermute x64 -> x68, waiting for transfers between devices: 137 us -> 116 us  [permute(): return lax.ppermute(array, ('grp', 'fsdp'), pairs)]
    unnamed x197 -> x158, local copies, waits for them, and re-layouts: 45.7 us -> 30.5 us
    pallas_call x47, Pallas kernels: 173 us -> 180 us  [launch(): pl.pallas_call(kernel, in_specs=[spec for _, spec in ins] + [ANY] * extra...]
    ppermute x64 -> x68, starting transfers between devices: 45.8 us -> 49.2 us  [permute(): return lax.ppermute(array, ('grp', 'fsdp'), pairs)]
  transfers between devices with their start and end apart: 68 -> 73, of which waited for: 36 -> 34; matrix products, arithmetic and copies ran while one was open for 2% -> 1% of each run, Pallas kernels for 35% -> 41%
where the time goes in v5:
time: 431 us; the launch traced here: 423 us
  Pallas kernels  180 us (42%)
  waiting for transfers between devices  117 us (27%)
  starting transfers between devices  49.4 us (11%)
  local copies, waits for them, and re-layouts  32.1 us (7%)
  blocking collectives  24.5 us (6%)
  between operations  15 us (3%)
  other arithmetic  5.3 us (1%)
    pallas_call x47, Pallas kernels, launch(): pl.pallas_call(kernel, in_specs=[spec for _, spec in ins] + [ANY] * extra...  180 us
    ppermute x68, waiting for transfers between devices, permute(): return lax.ppermute(array, ('grp', 'fsdp'), pairs)  116 us
    ppermute x68, starting transfers between devices, permute(): return lax.ppermute(array, ('grp', 'fsdp'), pairs)  49.2 us
    unnamed x158, local copies, waits for them, and re-layouts  30.5 us
    all_gather x1, blocking collectives, whole_column(): lax.all_gather(own, 'grp', axis_index_groups=self.columns(), axis=0, tile...  24.5 us
  transfers between devices with their start and end apart: 73, of which 34 were waited for; matrix products, arithmetic and copies ran while one was open for 1% of the time, Pallas kernels for 41%

profile of v5, /device:TPU:0, one launch (start us, length us, event | category | flops | bytes accessed | tf_op | source)
XLA Modules:
  0.0 423.5 jit_solution(9297770314980599774)
XLA Ops:
  10.5 3.0 collective-permute-start
  15.1 24.5 %all-gather = bf16[1,8,96,384]{3,2,0,1:T(8,128)(2,1)S(1)} all-gather(bf16[1,2,96,384]{3,2,0,1:T(8,128)(2,1)S(1)} %get-tuple-element.249), channel_id=2, replica_groups={{0,8,16,24},{4,12,20,28},{1,9,17,25},{5,13,21,29},{2,10,18,26},{6,14,22..., dimensions={1}, use_global_device_ids=true | all-gather | bytes 737280 | tf_op jit(solution)/shard_map/all_gather | solution.py:760
  46.2 3.9 collective-permute-done.3.refs_1_
  52.7 2.5 join.4
  57.1 2.2 pick.4
  61.6 8.9 %collective-permute-done.5.refs_4_.refs_5_.refs_11_.refs_10_ = bf16[8,96,384]{2,1,0:T(8,128)(2,1)S(1)} collective-permute-done((bf16[8,96,384]{2,1,0:T(8,128)(2,1)}, bf16[8,96,384]{2,1,0:T(8,128)(2,1)S(1)}, u32[]{:S(2)}, u32[]{:S(2)}) %collective-permute-start.5) | collective-permute-done | bytes 589856 | tf_op jit(solution)/shard_map/ppermute | solution.py:748
  71.4 6.3 %collective-permute-done.10.refs_1_ = bf16[8,96,384]{2,1,0:T(8,128)(2,1)S(1)} collective-permute-done((bf16[8,96,384]{2,1,0:T(8,128)(2,1)}, bf16[8,96,384]{2,1,0:T(8,128)(2,1)S(1)}, u32[]{:S(2)}, u32[]{:S(2)}) %collective-permute-start.10) | collective-permute-done | bytes 589856 | tf_op jit(solution)/shard_map/ppermute | solution.py:748
  79.4 3.5 join.5
  85.0 18.3 %collective-permute-done.12.refs_0_ = bf16[16,96,384]{2,1,0:T(8,128)(2,1)} collective-permute-done((bf16[16,96,384]{2,1,0:T(8,128)(2,1)}, bf16[16,96,384]{2,1,0:T(8,128)(2,1)}, u32[]{:S(2)}, u32[]{:S(2)}) %collective-permute-start.12) | collective-permute-done | bytes 1179680 | tf_op jit(solution)/shard_map/ppermute | solution.py:748
  113.8 11.7 %attention_forward.2 = (bf16[480,2304]{1,0:T(8,128)(2,1)}, f32[3,12,160]{2,1,0:T(8,128)}, bf16[480,768]{1,0:T(8,128)(2,1)}, f32[480,768]{1,0:T(8,128)}, f32[480,1]{1,0:T(8,128)}) custom-call(s32[4]{0:T(128)} %pad_add_fusion.refs_0_, s32[3]{0:T(128)} %refs_1_.10, bf16[480,768]{1,0:T(8,128)(2,1)} %bitcast.23, f32[1,9216]{1,0:T(1,128)} %get-tuple-element.250.refs_3_.refs_2_, ...), custom_call_target="tpu_custom_call" | custom-call | tf_op jit(solution)/shard_map/attention_forward/pallas_call | solution.py:65
  129.8 3.0 join.7
  134.6 3.0 collective-permute-done.20.refs_1_
  138.4 13.2 %ffn_forward.1 = (bf16[480,3072]{1,0:T(8,128)(2,1)}, bf16[480,3072]{1,0:T(8,128)(2,1)}, f32[480,768]{1,0:T(8,128)}, f32[480,1]{1,0:T(8,128)}, f32[480,768]{1,0:T(8,128)}) custom-call(s32[4]{0:T(128)} %pad_add_fusion.refs_0_, f32[480,768]{1,0:T(8,128)} %get-tuple-element.142.refs_1_.refs_3_, f32[1,9216]{1,0:T(1,128)} %get-tuple-element.250.refs_3_.refs_2_, ...), custom_call_target="tpu_custom_call" | custom-call | flops 99999997952 | tf_op jit(solution)/shard_map/ffn_forward/pallas_call | solution.py:65
  154.7 10.6 %attention_forward.3 = (bf16[480,2304]{1,0:T(8,128)(2,1)}, f32[3,12,160]{2,1,0:T(8,128)}, bf16[480,768]{1,0:T(8,128)(2,1)}) custom-call(s32[4]{0:T(128)} %pad_add_fusion.refs_0_, s32[3]{0:T(128)} %refs_1_.10, f32[480,768]{1,0:T(8,128)} %get-tuple-element.150.refs_2_.refs_4_.refs_6_, f32[1,9216]{1,0:T(1,128)} %get-tuple-element.251.refs_3_, ...), custom_call_target="tpu_custom_call" | custom-call | tf_op jit(solution)/shard_map/attention_forward/pallas_call | solution.py:65
  172.6 26.1 %ffn_both.1 = (bf16[480,768]{1,0:T(8,128)(2,1)}, f32[480,768]{1,0:T(8,128)}, bf16[480,768]{1,0:T(8,128)(2,1)}, f32[72,128]{1,0:T(8,128)}, bf16[36,96,384]{2,1,0:...) custom-call(s32[4]{0:T(128)} %pad_add_fusion.refs_0_, ...), custom_call_target="tpu_custom_call" | custom-call | tf_op jit(solution)/shard_map/ffn_both/pallas_call | solution.py:65
  200.2 4.7 %collective-permute-done.32.refs_1_ = bf16[36,96,384]{2,1,0:T(8,128)(2,1)S(1)} collective-permute-done((bf16[36,96,384]{2,1,0:T(8,128)(2,1)}, bf16[36,96,384]{2,1,0:T(8,128)(2,1)S(1)}, u32[]{:S(2)}, u32[]{:S(2)}) %collective-permute-start.32) | collective-permute-done | bytes 2654240 | tf_op jit(solution)/shard_map/ppermute | solution.py:748
  210.4 20.2 %attention_backward.2 = (f32[480,768]{1,0:T(8,128)}, f32[72,128]{1,0:T(8,128)}, bf16[12,96,384]{2,1,0:T(8,128)(2,1)}, bf16[12,96,384]{2,1,0:T(8,128)(2,1)}, bf16...) custom-call(s32[4]{0:T(128)} %pad_add_fusion.refs_0_, s32[3]{0:T(128)} %refs_1_.10, ...), custom_call_target="tpu_custom_call" | custom-call | tf_op jit(solution)/shard_map/attention_backward/pallas_call | solution.py:65
  244.0 22.5 %ffn_backward.1 = (f32[480,768]{1,0:T(8,128)}, bf16[480,768]{1,0:T(8,128)(2,1)}, f32[72,128]{1,0:T(8,128)}, bf16[36,96,384]{2,1,0:T(8,128)(2,1)}, bf16[36,96,384...) custom-call(s32[4]{0:T(128)} %pad_add_fusion.refs_0_, ...), custom_call_target="tpu_custom_call" | custom-call | tf_op jit(solution)/shard_map/ffn_backward/pallas_call | solution.py:65
  278.9 3.6 collective-permute-done.42.refs_2_.refs_1_
  289.7 19.9 %attention_backward.3 = (f32[480,768]{1,0:T(8,128)}, f32[144,128]{1,0:T(8,128)}, bf16[12,96,384]{2,1,0:T(8,128)(2,1)}, bf16[12,96,384]{2,1,0:T(8,128)(2,1)}, bf1...) custom-call(s32[4]{0:T(128)} %pad_add_fusion.refs_0_, s32[3]{0:T(128)} %refs_1_.10, ...), custom_call_target="tpu_custom_call" | custom-call | tf_op jit(solution)/shard_map/attention_backward/pallas_call | solution.py:65
  310.2 3.2 collect.2.refs_4_
  314.3 4.1 collective-permute-done.46.refs_2_.refs_1_
  328.3 4.5 %collective-permute-done.51.refs_1_ = bf16[6,96,384]{2,1,0:T(8,128)(2,1)S(1)} collective-permute-done((bf16[6,96,384]{2,1,0:T(8,128)(2,1)S(1)}, bf16[6,96,384]{2,1,0:T(8,128)(2,1)S(1)}, u32[]{:S(2)}, u32[]{:S(2)}) %collective-permute-start.51) | collective-permute-done | bytes 442400 | tf_op jit(solution)/shard_map/ppermute | solution.py:748
  336.5 13.0 %collective-permute-done.52.refs_3_ = bf16[3,96,384]{2,1,0:T(8,128)(2,1)S(1)} collective-permute-done((bf16[3,96,384]{2,1,0:T(8,128)(2,1)S(1)}, bf16[3,96,384]{2,1,0:T(8,128)(2,1)S(1)}, u32[]{:S(2)}, u32[]{:S(2)}) %collective-permute-start.52) | collective-permute-done | bytes 221216 | tf_op jit(solution)/shard_map/ppermute | solution.py:748
  350.7 3.2 collect.3.refs_2_.refs_14_.refs_19_
  356.6 11.6 %collective-permute-done.58.refs_0_ = bf16[6,96,384]{2,1,0:T(8,128)(2,1)S(1)} collective-permute-done((bf16[6,96,384]{2,1,0:T(8,128)(2,1)}, bf16[6,96,384]{2,1,0:T(8,128)(2,1)S(1)}, u32[]{:S(2)}, u32[]{:S(2)}) %collective-permute-start.58) | collective-permute-done | bytes 442400 | tf_op jit(solution)/shard_map/ppermute | solution.py:748
  373.2 3.1 collective-permute-done.56
  377.4 3.4 collective-permute-done.57
  383.4 7.9 %update_layer.2 = (f32[2,6,96,384]{3,2,1,0:T(8,128)}, f32[2,6,96,384]{3,2,1,0:T(8,128)}, f32[2,6,96,384]{3,2,1,0:T(8,128)}, f32[2,6,96,384]{3,2,1,0:T(8,128)}, bf16[2,6,96,384]{3,2,1,0:T(8,128)(2,1)}) custom-call(s32[4]{0:T(128)} %pad_add_fusion.refs_0_, bf16[6,96,384]{2,1,0:T(8,128)(2,1)} %get-tuple-element.230.refs_1_.refs_6_, f32[2,6,96,384]{3,2,1,0:T(8,128)} %refs_2_.4, ...), custom_call_target="tpu_custom_call" | custom-call | tf_op jit(solution)/shard_map/update_layer/pallas_call | solution.py:65
  393.5 4.0 collective-permute-done.64
  400.2 4.3 %collective-permute-done.65 = f32[144,128]{1,0:T(8,128)S(1)} collective-permute-done((f32[144,128]{1,0:T(8,128)S(1)}, f32[144,128]{1,0:T(8,128)S(1)}, u32[]{:S(2)}, u32[]{:S(2)}) %collective-permute-start.65) | collective-permute-done | bytes 73760 | tf_op jit(solution)/shard_map/ppermute | solution.py:748
  408.7 7.9 %update_layer.3 = (f32[2,6,96,384]{3,2,1,0:T(8,128)}, f32[2,6,96,384]{3,2,1,0:T(8,128)}, f32[2,6,96,384]{3,2,1,0:T(8,128)}, f32[2,6,96,384]{3,2,1,0:T(8,128)}, bf16[2,6,96,384]{3,2,1,0:T(8,128)(2,1)}) custom-call(s32[4]{0:T(128)} %pad_add_fusion.refs_0_, ...), custom_call_target="tpu_custom_call", output_to_operand_aliasing={{0}: (14, {}), {1}: (15, {}), {2}: (16, {}), {3}: (17, {}),... | custom-call | tf_op jit(solution)/shard_map/update_layer/pallas_call | solution.py:65
  (335 shorter events, 126.6 us)
Async XLA Ops:
  7.2 49.9 %all-gather.9.cloned.1.call-start = ((), (), s32[]{:S(2)}) async-start(), calls=%async_computation.5 | async-start | bytes 1474560 | tf_op jit(solution)/shard_map/all_gather | solution.py:760
  9.7 93.6 %all-gather.11.cloned.1.call-start = ((), (), s32[]{:S(2)}) async-start(), calls=%async_computation.6 | async-start | bytes 1474560 | tf_op jit(solution)/shard_map/all_gather | solution.py:760
  10.5 124.1 %all-gather.7.cloned.1.call-start = ((), (), s32[]{:S(2)}) async-start(), calls=%async_computation.2 | async-start | bytes 2949120 | tf_op jit(solution)/shard_map/all_gather | solution.py:760
  10.5 29.0 %collective-permute-start = (bf16[2,96,384]{2,1,0:T(8,128)(2,1)S(1)}, bf16[2,96,384]{2,1,0:T(8,128)(2,1)S(1)}, u32[]{:S(2)}, u32[]{:S(2)}) collective-permute-start(bf16[2,96,384]{2,1,0:T(8,128)(2,1)S(1)} %get-tuple-element.248.refs_0_), channel_id=1, source_target_pairs={{0,4},{1,5},{2,6},{3,7},{4,0},{5,1},{6,2},{7,3},{8,12},{9,13},{10,... | collective-permute-start | bytes 442376 | tf_op jit(solution)/shard_map/ppermute | solution.py:748
  13.5 26.0 %collective-permute-start.1 = (bf16[2,96,384]{2,1,0:T(8,128)(2,1)S(1)}, bf16[2,96,384]{2,1,0:T(8,128)(2,1)S(1)}, u32[]{:S(2)}, u32[]{:S(2)}) collective-permute-start(bf16[2,96,384]{2,1,0:T(8,128)(2,1)S(1)} %get-tuple-element.248.refs_0_), channel_id=1, source_target_pairs={{0,2},{1,3},{2,0},{3,1},{4,6},{5,7},{6,4},{7,5},{8,10},{9,11},{10,... | collective-permute-start | bytes 442376 | tf_op jit(solution)/shard_map/ppermute | solution.py:748
  15.1 24.5 %collective-permute-start.2 = (bf16[2,96,384]{2,1,0:T(8,128)(2,1)S(1)}, bf16[2,96,384]{2,1,0:T(8,128)(2,1)S(1)}, u32[]{:S(2)}, u32[]{:S(2)}) collective-permute-start(bf16[2,96,384]{2,1,0:T(8,128)(2,1)S(1)} %get-tuple-element.248.refs_0_), channel_id=1, source_target_pairs={{0,6},{1,7},{2,4},{3,5},{4,2},{5,3},{6,0},{7,1},{8,14},{9,15},{10,... | collective-permute-start | bytes 442376 | tf_op jit(solution)/shard_map/ppermute | solution.py:748
  82.9 20.4 %collective-permute-start.12 = (bf16[16,96,384]{2,1,0:T(8,128)(2,1)}, bf16[16,96,384]{2,1,0:T(8,128)(2,1)}, u32[]{:S(2)}, u32[]{:S(2)}) collective-permute-start(bf16[16,96,384]{2,1,0:T(8,128)(2,1)} %get-tuple-element.135.refs_1_.refs_12_.refs_11_.refs_18_.refs_17_), channel_id=1, source_target_pairs={{0,2},{1,3},{2,0},{3,1},{4,6},{5,7},{6,4},{7,5},{8,10},{9,11},{10,... | collective-permute-start | bytes 3538952 | tf_op jit(solution)/shard_map/ppermute | solution.py:748
  83.3 22.2 %collective-permute-start.13 = (bf16[16,96,384]{2,1,0:T(8,128)(2,1)}, bf16[16,96,384]{2,1,0:T(8,128)(2,1)}, u32[]{:S(2)}, u32[]{:S(2)}) collective-permute-start(bf16[16,96,384]{2,1,0:T(8,128)(2,1)} %get-tuple-element.136.refs_2_.refs_16_.refs_15_.refs_22_.refs_21_), channel_id=1, source_target_pairs={{0,4},{1,5},{2,6},{3,7},{4,0},{5,1},{6,2},{7,3},{8,12},{9,13},{10,... | collective-permute-start | bytes 3538952 | tf_op jit(solution)/shard_map/ppermute | solution.py:748
  84.3 23.2 %collective-permute-start.6 = (bf16[16,96,384]{2,1,0:T(8,128)(2,1)}, bf16[16,96,384]{2,1,0:T(8,128)(2,1)S(1)}, u32[]{:S(2)}, u32[]{:S(2)}) collective-permute-start(bf16[16,96,384]{2,1,0:T(8,128)(2,1)} %get-tuple-element.131.refs_3_), channel_id=1, source_target_pairs={{0,1},{1,0},{2,3},{3,2},{4,5},{5,4},{6,7},{7,6},{8,9},{9,8},{10,11... | collective-permute-start | bytes 3538952 | tf_op jit(solution)/shard_map/ppermute | solution.py:748
  84.3 271.3 %reduce-scatter.5.cloned.1.call-start = ((), (), s32[]{:S(2)}) async-start(), calls=%async_computation.4 | async-start | bytes 2211840 | tf_op jit(solution)/shard_map/reduce_scatter | solution.py:878
  84.4 22.8 %collective-permute-start.7 = (bf16[8,96,384]{2,1,0:T(8,128)(2,1)}, bf16[8,96,384]{2,1,0:T(8,128)(2,1)}, u32[]{:S(2)}, u32[]{:S(2)}) collective-permute-start(bf16[8,96,384]{2,1,0:T(8,128)(2,1)} %copy-done.52), channel_id=1, source_target_pairs={{0,1},{1,0},{2,3},{3,2},{4,5},{5,4},{6,7},{7,6},{8,9},{9,8},{10,11... | collective-permute-start | bytes 1769480 | tf_op jit(solution)/shard_map/ppermute | solution.py:748
  85.0 22.5 %collective-permute-start.9 = (bf16[8,96,384]{2,1,0:T(8,128)(2,1)}, bf16[8,96,384]{2,1,0:T(8,128)(2,1)}, u32[]{:S(2)}, u32[]{:S(2)}) collective-permute-start(bf16[8,96,384]{2,1,0:T(8,128)(2,1)} %copy-done.53), channel_id=1, source_target_pairs={{0,1},{1,0},{2,3},{3,2},{4,5},{5,4},{6,7},{7,6},{8,9},{9,8},{10,11... | collective-permute-start | bytes 1769480 | tf_op jit(solution)/shard_map/ppermute | solution.py:748
  105.5 19.9 %collective-permute-start.17 = (bf16[8,96,384]{2,1,0:T(8,128)(2,1)}, bf16[8,96,384]{2,1,0:T(8,128)(2,1)}, u32[]{:S(2)}, u32[]{:S(2)}) collective-permute-start(bf16[8,96,384]{2,1,0:T(8,128)(2,1)} %get-tuple-element.138.refs_2_.refs_20_.refs_0_), channel_id=1, source_target_pairs={{0,4},{1,5},{2,6},{3,7},{4,0},{5,1},{6,2},{7,3},{8,12},{9,13},{10,... | collective-permute-start | bytes 1769480 | tf_op jit(solution)/shard_map/ppermute | solution.py:748
  129.8 22.3 %collective-permute-start.22 = (bf16[8,96,384]{2,1,0:T(8,128)(2,1)}, bf16[8,96,384]{2,1,0:T(8,128)(2,1)S(1)}, u32[]{:S(2)}, u32[]{:S(2)}) collective-permute-start(bf16[8,96,384]{2,1,0:T(8,128)(2,1)} %get-tuple-element.146.refs_6_), channel_id=1, source_target_pairs={{0,1},{1,0},{2,3},{3,2},{4,5},{5,4},{6,7},{7,6},{8,9},{9,8},{10,11... | collective-permute-start | bytes 1769480 | tf_op jit(solution)/shard_map/ppermute | solution.py:748
  132.8 32.4 %collective-permute-start.25 = (bf16[12,96,384]{2,1,0:T(8,128)(2,1)}, bf16[12,96,384]{2,1,0:T(8,128)(2,1)S(1)}, u32[]{:S(2)}, u32[]{:S(2)}) collective-permute-start(bf16[12,96,384]{2,1,0:T(8,128)(2,1)} %get-tuple-element.147.refs_19_.refs_1_.refs_10_), channel_id=1, source_target_pairs={{0,2},{1,3},{2,0},{3,1},{4,6},{5,7},{6,4},{7,5},{8,10},{9,11},{10,... | collective-permute-start | bytes 2654216 | tf_op jit(solution)/shard_map/ppermute | solution.py:748
  137.6 27.7 %collective-permute-start.26 = (bf16[12,96,384]{2,1,0:T(8,128)(2,1)}, bf16[12,96,384]{2,1,0:T(8,128)(2,1)S(1)}, u32[]{:S(2)}, u32[]{:S(2)}) collective-permute-start(bf16[12,96,384]{2,1,0:T(8,128)(2,1)} %get-tuple-element.148.refs_20_.refs_14_), channel_id=1, source_target_pairs={{0,4},{1,5},{2,6},{3,7},{4,0},{5,1},{6,2},{7,3},{8,12},{9,13},{10,... | collective-permute-start | bytes 2654216 | tf_op jit(solution)/shard_map/ppermute | solution.py:748
  138.4 33.0 %collective-permute-start.27 = (bf16[24,96,384]{2,1,0:T(8,128)(2,1)}, bf16[24,96,384]{2,1,0:T(8,128)(2,1)}, u32[]{:S(2)}, u32[]{:S(2)}) collective-permute-start(bf16[24,96,384]{2,1,0:T(8,128)(2,1)} %get-tuple-element.149.refs_21_), channel_id=1, source_target_pairs={{0,1},{1,0},{2,3},{3,2},{4,5},{5,4},{6,7},{7,6},{8,9},{9,8},{10,11... | collective-permute-start | bytes 5308424 | tf_op jit(solution)/shard_map/ppermute | solution.py:748
  169.8 28.9 %collective-permute-start.30 = (bf16[12,96,384]{2,1,0:T(8,128)(2,1)S(1)}, bf16[12,96,384]{2,1,0:T(8,128)(2,1)S(1)}, u32[]{:S(2)}, u32[]{:S(2)}) collective-permute-start(bf16[12,96,384]{2,1,0:T(8,128)(2,1)S(1)} %rounded.1.refs_18_.refs_10_), channel_id=1, source_target_pairs={{0,2},{1,3},{2,0},{3,1},{4,6},{5,7},{6,4},{7,5},{8,10},{9,11},{10,... | collective-permute-start | bytes 2654216 | tf_op jit(solution)/shard_map/ppermute | solution.py:748
  205.6 31.3 %collective-permute-start.36 = (bf16[18,96,384]{2,1,0:T(8,128)(2,1)S(1)}, bf16[18,96,384]{2,1,0:T(8,128)(2,1)}, u32[]{:S(2)}, u32[]{:S(2)}) collective-permute-start(bf16[18,96,384]{2,1,0:T(8,128)(2,1)S(1)} %get-tuple-element.171.refs_21_), channel_id=1, source_target_pairs={{0,4},{1,5},{2,6},{3,7},{4,0},{5,1},{6,2},{7,3},{8,12},{9,13},{10,... | collective-permute-start | bytes 3981320 | tf_op jit(solution)/shard_map/ppermute | solution.py:748
  209.4 31.2 %collective-permute-start.33 = (bf16[18,96,384]{2,1,0:T(8,128)(2,1)S(1)}, bf16[18,96,384]{2,1,0:T(8,128)(2,1)S(1)}, u32[]{:S(2)}, u32[]{:S(2)}) collective-permute-start(bf16[18,96,384]{2,1,0:T(8,128)(2,1)S(1)} %get-tuple-element.168.refs_20_), channel_id=1, source_target_pairs={{0,2},{1,3},{2,0},{3,1},{4,6},{5,7},{6,4},{7,5},{8,10},{9,11},{10,... | collective-permute-start | bytes 3981320 | tf_op jit(solution)/shard_map/ppermute | solution.py:748
  239.5 27.2 %collective-permute-start.40 = (bf16[9,96,384]{2,1,0:T(8,128)(2,1)S(1)}, bf16[9,96,384]{2,1,0:T(8,128)(2,1)S(1)}, u32[]{:S(2)}, u32[]{:S(2)}) collective-permute-start(bf16[9,96,384]{2,1,0:T(8,128)(2,1)S(1)} %get-tuple-element.186.refs_27_), channel_id=1, source_target_pairs={{0,2},{1,3},{2,0},{3,1},{4,6},{5,7},{6,4},{7,5},{8,10},{9,11},{10,... | collective-permute-start | bytes 1990664 | tf_op jit(solution)/shard_map/ppermute | solution.py:748
  241.0 25.7 %collective-permute-start.39 = (bf16[9,96,384]{2,1,0:T(8,128)(2,1)S(1)}, bf16[9,96,384]{2,1,0:T(8,128)(2,1)S(1)}, u32[]{:S(2)}, u32[]{:S(2)}) collective-permute-start(bf16[9,96,384]{2,1,0:T(8,128)(2,1)S(1)} %get-tuple-element.184.refs_26_), channel_id=1, source_target_pairs={{0,4},{1,5},{2,6},{3,7},{4,0},{5,1},{6,2},{7,3},{8,12},{9,13},{10,... | collective-permute-start | bytes 1990664 | tf_op jit(solution)/shard_map/ppermute | solution.py:748
  242.6 24.0 %collective-permute-start.38 = (bf16[6,96,384]{2,1,0:T(8,128)(2,1)S(1)}, bf16[6,96,384]{2,1,0:T(8,128)(2,1)S(1)}, u32[]{:S(2)}, u32[]{:S(2)}) collective-permute-start(bf16[6,96,384]{2,1,0:T(8,128)(2,1)S(1)} %get-tuple-element.183.refs_3_.refs_29_), channel_id=1, source_target_pairs={{0,4},{1,5},{2,6},{3,7},{4,0},{5,1},{6,2},{7,3},{8,12},{9,13},{10,... | collective-permute-start | bytes 1327112 | tf_op jit(solution)/shard_map/ppermute | solution.py:748
  243.1 23.6 %collective-permute-start.37 = (bf16[6,96,384]{2,1,0:T(8,128)(2,1)S(1)}, bf16[6,96,384]{2,1,0:T(8,128)(2,1)S(1)}, u32[]{:S(2)}, u32[]{:S(2)}) collective-permute-start(bf16[6,96,384]{2,1,0:T(8,128)(2,1)S(1)} %get-tuple-element.180.refs_2_.refs_28_), channel_id=1, source_target_pairs={{0,2},{1,3},{2,0},{3,1},{4,6},{5,7},{6,4},{7,5},{8,10},{9,11},{10,... | collective-permute-start | bytes 1327112 | tf_op jit(solution)/shard_map/ppermute | solution.py:748
  284.3 30.0 %collective-permute-start.47 = (bf16[18,96,384]{2,1,0:T(8,128)(2,1)}, bf16[18,96,384]{2,1,0:T(8,128)(2,1)}, u32[]{:S(2)}, u32[]{:S(2)}) collective-permute-start(bf16[18,96,384]{2,1,0:T(8,128)(2,1)} %get-tuple-element.204.refs_26_), channel_id=1, source_target_pairs={{0,4},{1,5},{2,6},{3,7},{4,0},{5,1},{6,2},{7,3},{8,12},{9,13},{10,... | collective-permute-start | bytes 3981320 | tf_op jit(solution)/shard_map/ppermute | solution.py:748
  288.7 29.7 %collective-permute-start.46 = (bf16[18,96,384]{2,1,0:T(8,128)(2,1)}, bf16[18,96,384]{2,1,0:T(8,128)(2,1)}, u32[]{:S(2)}, u32[]{:S(2)}) collective-permute-start(bf16[18,96,384]{2,1,0:T(8,128)(2,1)} %get-tuple-element.201.refs_25_), channel_id=1, source_target_pairs={{0,2},{1,3},{2,0},{3,1},{4,6},{5,7},{6,4},{7,5},{8,10},{9,11},{10,... | collective-permute-start | bytes 3981320 | tf_op jit(solution)/shard_map/ppermute | solution.py:748
  313.5 78.0 %reduce-scatter.3.cloned.1.call-start = ((), (), s32[]{:S(2)}) async-start(), calls=%async_computation.3 | async-start | bytes 2211840 | tf_op jit(solution)/shard_map/reduce_scatter | solution.py:878
  324.1 25.4 %collective-permute-start.54 = (bf16[9,96,384]{2,1,0:T(8,128)(2,1)S(1)}, bf16[9,96,384]{2,1,0:T(8,128)(2,1)S(1)}, u32[]{:S(2)}, u32[]{:S(2)}) collective-permute-start(bf16[9,96,384]{2,1,0:T(8,128)(2,1)S(1)} %get-tuple-element.220.refs_3_), channel_id=1, source_target_pairs={{0,2},{1,3},{2,0},{3,1},{4,6},{5,7},{6,4},{7,5},{8,10},{9,11},{10,... | collective-permute-start | bytes 1990664 | tf_op jit(solution)/shard_map/ppermute | solution.py:748
  326.9 22.7 %collective-permute-start.53 = (bf16[9,96,384]{2,1,0:T(8,128)(2,1)S(1)}, bf16[9,96,384]{2,1,0:T(8,128)(2,1)S(1)}, u32[]{:S(2)}, u32[]{:S(2)}) collective-permute-start(bf16[9,96,384]{2,1,0:T(8,128)(2,1)S(1)} %get-tuple-element.218.refs_2_), channel_id=1, source_target_pairs={{0,4},{1,5},{2,6},{3,7},{4,0},{5,1},{6,2},{7,3},{8,12},{9,13},{10,... | collective-permute-start | bytes 1990664 | tf_op jit(solution)/shard_map/ppermute | solution.py:748
  355.1 26.3 %collective-permute-start.61 = (bf16[12,96,384]{2,1,0:T(8,128)(2,1)S(1)}, bf16[12,96,384]{2,1,0:T(8,128)(2,1)S(1)}, u32[]{:S(2)}, u32[]{:S(2)}) collective-permute-start(bf16[12,96,384]{2,1,0:T(8,128)(2,1)S(1)} %copy-done.1), channel_id=1, source_target_pairs={{0,1},{1,0},{2,3},{3,2},{4,5},{5,4},{6,7},{7,6},{8,9},{9,8},{10,11... | collective-permute-start | bytes 2654216 | tf_op jit(solution)/shard_map/ppermute | solution.py:748
  355.3 26.1 %collective-permute-start.62 = (bf16[12,96,384]{2,1,0:T(8,128)(2,1)S(1)}, bf16[12,96,384]{2,1,0:T(8,128)(2,1)S(1)}, u32[]{:S(2)}, u32[]{:S(2)}) collective-permute-start(bf16[12,96,384]{2,1,0:T(8,128)(2,1)S(1)} %copy-done.55), channel_id=1, source_target_pairs={{0,1},{1,0},{2,3},{3,2},{4,5},{5,4},{6,7},{7,6},{8,9},{9,8},{10,11... | collective-permute-start | bytes 2654216 | tf_op jit(solution)/shard_map/ppermute | solution.py:748
  356.6 24.9 %collective-permute-start.59 = (bf16[6,96,384]{2,1,0:T(8,128)(2,1)}, bf16[6,96,384]{2,1,0:T(8,128)(2,1)}, u32[]{:S(2)}, u32[]{:S(2)}) collective-permute-start(bf16[6,96,384]{2,1,0:T(8,128)(2,1)} %get-tuple-element.230.refs_1_.refs_6_), channel_id=1, source_target_pairs={{0,1},{1,0},{2,3},{3,2},{4,5},{5,4},{6,7},{7,6},{8,9},{9,8},{10,11... | collective-permute-start | bytes 1327112 | tf_op jit(solution)/shard_map/ppermute | solution.py:748
  (120 other events, 643.6 us)
Sparse Core Ops, SparseCore 0:
  9.8 38.7 all-gather.8
  50.7 30.8 all-gather.10
  84.5 50.0 all-gather.6
  313.6 37.1 reduce-scatter.4
  354.1 37.3 reduce-scatter.2

commit v6 on v5

--- a/solution.py
+++ b/solution.py
@@ -69,7 +69,7 @@
         out_shape=out_shape,
         scratch_shapes=list(scratch),
         input_output_aliases=aliases or {},
-        compiler_params=pltpu.CompilerParams(vmem_limit_bytes=limit << 20),
+        compiler_params=pltpu.CompilerParams(vmem_limit_bytes=int(limit * 2**20)),
         cost_estimate=pl.CostEstimate(flops=flops, bytes_accessed=moved, transcendentals=special),
         name=name,
         **grid,
@@ -346,7 +346,7 @@
 
 def ffn_backward_body(
     dims, outs_parts, outs, pos, gy, small_ref, unit_ref, inv_ref, ctx_ref, unit2, inv2, act_ref, slope_ref,
-    up, down, wo, grad_up, grad_down, grad_o, sem_out, gz1_ref, gctx_ref, sums_ref, wait_o,
+    up, down, wo, grad_up, grad_down, grad_o, sem_out, gz1_ref, gctx_ref, sums_ref, wait_o, ready=lambda: None,
 ):
     width = dims.model
     gain1, gain2 = segment(small_ref, 4, width), segment(small_ref, 6, width)
@@ -359,6 +359,7 @@
     gz2 = norm_backward(gy, unit2, inv2, gain2)
     gf = gz2.astype(BF)
     put(3, col_sum(gf))
+    ready()
     hb = (unit_ref[...] * gain1 + segment(small_ref, 5, width)).astype(BF)
     gh1 = gz2
     block = dims.block
@@ -410,22 +411,33 @@
     return [pltpu.VMEM(m, BF) for m in matrices] + [pltpu.SemaphoreType.DMA((3,))] * 2
 
 
-def ffn_backward_kernel(dims, parts, outs_parts, pos_ref, gy_ref, small_ref, unit_ref, inv_ref, ctx_ref, unit2_ref, inv2_ref, act_ref, slope_ref, *rest):
+def ffn_backward_kernel(dims, parts, outs_parts, pos_ref, gy_ref, small_ref, inv_ref, unit2_ref, inv2_ref, *rest):
+    far, rest = rest[:4], rest[4:]
     refs, rest = unflatten(rest, parts)
     gz1_ref, gctx_ref, sums_ref, *rest = rest
     count = 2 * len(outs_parts)
     outs = [rest[2 * n : 2 * n + 2] for n in range(len(outs_parts))]
-    up, down, wo, grad_up, grad_down, grad_o, sems, sem_out = rest[count:]
+    up, down, wo, grad_up, grad_down, grad_o, sems, sem_out, *near, sem_far = rest[count:]
+    unit_ref, slope_ref, act_ref, ctx_ref = near
     pos = (pos_ref[1], pos_ref[2], pos_ref[3])
+    pltpu.make_async_copy(far[0], near[0], sem_far.at[0]).start()
     start_loads(dims, parts, refs, pos, "down", down, 0, 0, sems.at[1])
+    for n in range(1, 4):
+        pltpu.make_async_copy(far[n], near[n], sem_far.at[n]).start()
     start_loads(dims, parts, refs, pos, "up", up, 0, 0, sems.at[0])
     start_loads(dims, parts, refs, pos, "o", wo, 0, 0, sems.at[2])
-    wait_for(down, sems.at[1])
-    wait_for(up, sems.at[0])
+
+    def ready():
+        wait_for(unit_ref, sem_far.at[0])
+        wait_for(down, sems.at[1])
+        for n in range(1, 4):
+            wait_for(near[n], sem_far.at[n])
+        wait_for(up, sems.at[0])
+
     ffn_backward_body(
         dims, outs_parts, outs, pos, gy_ref[...], small_ref, unit_ref, inv_ref, ctx_ref,
         unit2_ref[...], inv2_ref[...], act_ref, slope_ref, up, down, wo, grad_up, grad_down, grad_o,
-        sem_out, gz1_ref, gctx_ref, sums_ref, lambda: wait_for(wo, sems.at[2]),
+        sem_out, gz1_ref, gctx_ref, sums_ref, lambda: wait_for(wo, sems.at[2]), ready,
     )
 
 
@@ -437,12 +449,15 @@
         functools.partial(ffn_backward_kernel, dims, parts, outs_parts),
         "ffn_backward",
         [(pos, SMEM)]
-        + [(a, VMEM) for a in (gy, small, unit, inv, ctx, unit2, inv2, act, slope)]
+        + [(a, VMEM) for a in (gy, small, inv, unit2, inv2)]
+        + [(a, ANY) for a in (unit, slope, act, ctx)]
         + weight_ins(parts),
         [shape((rows, width), F32), shape((rows, width), BF), shape((small.shape[1] // 128, 128), F32)] + grads,
         [VMEM] * 3 + [ANY] * len(grads),
         deps,
-        ffn_scratch(dims),
+        ffn_scratch(dims)
+        + [pltpu.VMEM(a.shape, a.dtype) for a in (unit, slope, act, ctx)]
+        + [pltpu.SemaphoreType.DMA((4,))],
         (8 * rows * width * ffn + 4 * rows * width * width, 40 << 20, 0),
         limit=56,
     )
@@ -505,7 +520,7 @@
         + [pltpu.VMEM((rows, ffn), BF)] * 2
         + [pltpu.VMEM((rows, width), F32), pltpu.VMEM((rows, 1), F32)],
         (12 * rows * width * ffn + 4 * rows * width * width, 40 << 20, 3 << 20),
-        limit=56,
+        limit=62,
     )
     return out[0], out[1], out[2], out[3], pair_up(out[4:], outs_parts)
 
@@ -685,6 +700,19 @@
     lax.fori_loop(0, half, piece, 0)
 
 
+def add_both_kernel(*refs):
+    ins, outs, hold, sems = refs[:4], refs[4:8], refs[8], refs[9]
+    for n in range(4):
+        pltpu.make_async_copy(ins[n], hold.at[n], sems.at[n]).start()
+    half = outs[0].shape[0]
+    for n in range(2):
+        wait_for(hold.at[2 * n], sems.at[2 * n])
+        wait_for(hold.at[2 * n + 1], sems.at[2 * n + 1])
+        for i in range(half):
+            for out, at in ((outs[2 * n], i), (outs[2 * n + 1], i + half)):
+                out[i] = (hold[2 * n, at].astype(F32) + hold[2 * n + 1, at].astype(F32)).astype(BF)
+
+
 def collect_kernel(zs, *refs):
     pairs = len(zs)
     ins, out, total, holds, sems = refs[: 2 * pairs], refs[2 * pairs], refs[2 * pairs + 1], refs[2 * pairs + 2 : -1], refs[-1]
@@ -848,6 +876,20 @@
             sums.append(launch(add_kernel, "add", [(own, VMEM), (other, VMEM)], out, [VMEM] * 2, deps, weight=weight))
         return [kept for kept, _ in sums], [sent for _, sent in sums]
 
+    def add_both(self, keep, got, deps=()):
+        ins = [a for pair in zip(keep, got) for a in pair]
+        out = launch(
+            add_both_kernel,
+            "add_both",
+            [(a, ANY) for a in ins],
+            [self.pieces(keep[0].shape[0] // 2)] * 4,
+            [VMEM] * 4,
+            deps,
+            [pltpu.VMEM((4,) + keep[0].shape, BF), pltpu.SemaphoreType.DMA((4,))],
+            limit=16,
+        )
+        return out[0::2], out[1::2]
+
     def core_sum(self, parts, deps=(), weight=0):
         got = [self.swap(p.arrays[1], "c") for p in parts]
         return self.add([p.arrays[0] for p in parts], got, deps, weight)
@@ -879,12 +921,16 @@
             whole, "grp", axis_index_groups=self.columns(), scatter_dimension=0, tiled=True
         )
 
-    def small_sum(self, values, axes, bits):
+    def small_sum(self, values, axes):
         for axis in axes:
             values = values + self.swap(values, axis)
-        for bit in bits:
-            values = values + self.permute(values, lambda z, x, y, c, bit=bit: (z ^ bit, x, y, c))
         return values
+
+    def small_sum_slabs(self, values):
+        one, two, three = (
+            self.permute(values, lambda z, x, y, c, bits=bits: (z ^ bits, x, y, c)) for bits in (1, 2, 3)
+        )
+        return (values + one) + (two + three)
 
     def group(self, own, deps=()):
         (other,) = self.gate([self.swap(own, "y")], deps)
@@ -985,7 +1031,7 @@
         ],
         (0, 0, 0),
         aliases,
-        limit=56,
+        limit=63.5,
     )
 
 
@@ -1126,7 +1172,7 @@
         [*early1[1], *late1[1]],
     )
     net.hold(early0, [*got_l, *got_e])
-    late1 = net.add(late1[0], got_l)
+    late1 = net.add_both(late1[0], got_l)
     got_l = net.swaps(late1, "xy")
     early0 = net.core_sum(early0, got_l)
     gx0, sums, late0 = attention_backward(
@@ -1144,7 +1190,7 @@
     whole0 = net.collect(split, (late0, early0), (got_l, got_e))
     low0 = net.column_sum(whole0)
     low1, sums = net.gate([net.column_sum(whole1), sums], [whole0])
-    sums = net.small_sum(sums, ("c", "x", "y"), ())
+    sums = net.small_sum(sums, ("c", "x", "y"))
     grads1 = net.group(low1)
 
     def update(n, wide, grads, before):
@@ -1154,7 +1200,7 @@
 
     done = update(1, low1, grads1, None)
     low0, sums = net.gate([low0, sums], [done[0]])
-    sums = net.small_sum(sums, (), (1, 2))
+    sums = net.small_sum_slabs(sums)
     done = update(0, low0, net.group(low0, [sums]), done)
     return y1, gx0, done, sums
 

time: 431 us -> 427 us (level)
    ppermute x68 -> x69, waiting for transfers between devices: 116 us -> 111 us  [permute(): return lax.ppermute(array, ('grp', 'fsdp'), pairs)]
    ppermute x68 -> x69, starting transfers between devices: 49.2 us -> 53 us  [permute(): return lax.ppermute(array, ('grp', 'fsdp'), pairs)]
    unnamed x158 -> x152, local copies, waits for them, and re-layouts: 30.5 us -> 27.8 us
    pallas_call x47 -> x46, Pallas kernels: 180 us -> 180 us  [launch(): pl.pallas_call(kernel, in_specs=[spec for _, spec in ins] + [ANY] * extra...]
  transfers between devices with their start and end apart: 73 -> 74, of which waited for: 34 -> 33; matrix products, arithmetic and copies ran while one was open for 1% -> 1% of each run, Pallas kernels for 41% -> 41%
where the time goes in v6:
time: 427 us; the launch traced here: 420 us
  Pallas kernels  180 us (42%)
  waiting for transfers between devices  113 us (26%)
  starting transfers between devices  53.2 us (12%)
  local copies, waits for them, and re-layouts  29.4 us (7%)
  blocking collectives  24.5 us (6%)
  between operations  14.9 us (3%)
  other arithmetic  5.32 us (1%)
    pallas_call x46, Pallas kernels, launch(): pl.pallas_call(kernel, in_specs=[spec for _, spec in ins] + [ANY] * extra...  180 us
    ppermute x69, waiting for transfers between devices, permute(): return lax.ppermute(array, ('grp', 'fsdp'), pairs)  111 us
    ppermute x69, starting transfers between devices, permute(): return lax.ppermute(array, ('grp', 'fsdp'), pairs)  53 us
    unnamed x152, local copies, waits for them, and re-layouts  27.8 us
    all_gather x1, blocking collectives, whole_column(): lax.all_gather(own, 'grp', axis_index_groups=self.columns(), axis=0, tile...  24.5 us
  transfers between devices with their start and end apart: 74, of which 33 were waited for; matrix products, arithmetic and copies ran while one was open for 1% of the time, Pallas kernels for 41%

profile of v6, /device:TPU:0, one launch (start us, length us, event | category | flops | bytes accessed | tf_op | source)
XLA Modules:
  0.0 420.2 jit_solution(13514369297508012531)
XLA Ops:
  10.5 3.0 collective-permute-start
  15.1 24.5 %all-gather = bf16[1,8,96,384]{3,2,0,1:T(8,128)(2,1)S(1)} all-gather(bf16[1,2,96,384]{3,2,0,1:T(8,128)(2,1)S(1)} %get-tuple-element.249), channel_id=2, replica_groups={{0,8,16,24},{4,12,20,28},{1,9,17,25},{5,13,21,29},{2,10,18,26},{6,14,22..., dimensions={1}, use_global_device_ids=true | all-gather | bytes 737280 | tf_op jit(solution)/shard_map/all_gather | solution.py:788
  46.2 3.9 collective-permute-done.3.refs_1_
  52.7 2.5 join.4
  57.1 2.2 pick.4
  61.6 8.9 %collective-permute-done.5.refs_4_.refs_5_.refs_11_.refs_10_ = bf16[8,96,384]{2,1,0:T(8,128)(2,1)S(1)} collective-permute-done((bf16[8,96,384]{2,1,0:T(8,128)(2,1)}, bf16[8,96,384]{2,1,0:T(8,128)(2,1)S(1)}, u32[]{:S(2)}, u32[]{:S(2)}) %collective-permute-start.5) | collective-permute-done | bytes 589856 | tf_op jit(solution)/shard_map/ppermute | solution.py:776
  71.4 6.3 %collective-permute-done.10.refs_1_ = bf16[8,96,384]{2,1,0:T(8,128)(2,1)S(1)} collective-permute-done((bf16[8,96,384]{2,1,0:T(8,128)(2,1)}, bf16[8,96,384]{2,1,0:T(8,128)(2,1)S(1)}, u32[]{:S(2)}, u32[]{:S(2)}) %collective-permute-start.10) | collective-permute-done | bytes 589856 | tf_op jit(solution)/shard_map/ppermute | solution.py:776
  79.4 3.5 join.5
  85.0 18.3 %collective-permute-done.12.refs_0_ = bf16[16,96,384]{2,1,0:T(8,128)(2,1)} collective-permute-done((bf16[16,96,384]{2,1,0:T(8,128)(2,1)}, bf16[16,96,384]{2,1,0:T(8,128)(2,1)}, u32[]{:S(2)}, u32[]{:S(2)}) %collective-permute-start.12) | collective-permute-done | bytes 1179680 | tf_op jit(solution)/shard_map/ppermute | solution.py:776
  113.7 11.7 %attention_forward.2 = (bf16[480,2304]{1,0:T(8,128)(2,1)}, f32[3,12,160]{2,1,0:T(8,128)}, bf16[480,768]{1,0:T(8,128)(2,1)}, f32[480,768]{1,0:T(8,128)}, f32[480,1]{1,0:T(8,128)}) custom-call(s32[4]{0:T(128)} %pad_add_fusion.refs_0_, s32[3]{0:T(128)} %refs_1_.10, bf16[480,768]{1,0:T(8,128)(2,1)} %bitcast.23, f32[1,9216]{1,0:T(1,128)} %get-tuple-element.250.refs_3_.refs_2_, ...), custom_call_target="tpu_custom_call" | custom-call | tf_op jit(solution)/shard_map/attention_forward/pallas_call | solution.py:65
  129.8 3.0 join.7
  134.6 3.0 collective-permute-done.20.refs_1_
  138.4 13.2 %ffn_forward.1 = (bf16[480,3072]{1,0:T(8,128)(2,1)}, bf16[480,3072]{1,0:T(8,128)(2,1)}, f32[480,768]{1,0:T(8,128)}, f32[480,1]{1,0:T(8,128)}, f32[480,768]{1,0:T(8,128)}) custom-call(s32[4]{0:T(128)} %pad_add_fusion.refs_0_, f32[480,768]{1,0:T(8,128)} %get-tuple-element.142.refs_1_.refs_6_, f32[1,9216]{1,0:T(1,128)} %get-tuple-element.250.refs_3_.refs_2_, ...), custom_call_target="tpu_custom_call" | custom-call | flops 99999997952 | tf_op jit(solution)/shard_map/ffn_forward/pallas_call | solution.py:65
  154.7 10.6 %attention_forward.3 = (bf16[480,2304]{1,0:T(8,128)(2,1)}, f32[3,12,160]{2,1,0:T(8,128)}, bf16[480,768]{1,0:T(8,128)(2,1)}) custom-call(s32[4]{0:T(128)} %pad_add_fusion.refs_0_, s32[3]{0:T(128)} %refs_1_.10, f32[480,768]{1,0:T(8,128)} %get-tuple-element.150.refs_2_.refs_4_.refs_6_, f32[1,9216]{1,0:T(1,128)} %get-tuple-element.251.refs_3_, ...), custom_call_target="tpu_custom_call" | custom-call | tf_op jit(solution)/shard_map/attention_forward/pallas_call | solution.py:65
  172.5 26.1 %ffn_both.1 = (bf16[480,768]{1,0:T(8,128)(2,1)}, f32[480,768]{1,0:T(8,128)}, bf16[480,768]{1,0:T(8,128)(2,1)}, f32[72,128]{1,0:T(8,128)}, bf16[36,96,384]{2,1,0:...) custom-call(s32[4]{0:T(128)} %pad_add_fusion.refs_0_, ...), custom_call_target="tpu_custom_call" | custom-call | tf_op jit(solution)/shard_map/ffn_both/pallas_call | solution.py:65
  200.1 4.7 %collective-permute-done.32.refs_1_ = bf16[36,96,384]{2,1,0:T(8,128)(2,1)S(1)} collective-permute-done((bf16[36,96,384]{2,1,0:T(8,128)(2,1)}, bf16[36,96,384]{2,1,0:T(8,128)(2,1)S(1)}, u32[]{:S(2)}, u32[]{:S(2)}) %collective-permute-start.32) | collective-permute-done | bytes 2654240 | tf_op jit(solution)/shard_map/ppermute | solution.py:776
  210.3 20.1 %attention_backward.2 = (f32[480,768]{1,0:T(8,128)}, f32[72,128]{1,0:T(8,128)}, bf16[12,96,384]{2,1,0:T(8,128)(2,1)}, bf16[12,96,384]{2,1,0:T(8,128)(2,1)}, bf16...) custom-call(s32[4]{0:T(128)} %pad_add_fusion.refs_0_, s32[3]{0:T(128)} %refs_1_.10, ...), custom_call_target="tpu_custom_call" | custom-call | tf_op jit(solution)/shard_map/attention_backward/pallas_call | solution.py:65
  244.1 21.5 %ffn_backward.1 = (f32[480,768]{1,0:T(8,128)}, bf16[480,768]{1,0:T(8,128)(2,1)}, f32[72,128]{1,0:T(8,128)}, bf16[36,96,384]{2,1,0:T(8,128)(2,1)}, bf16[36,96,384...) custom-call(s32[4]{0:T(128)} %pad_add_fusion.refs_0_, ...), custom_call_target="tpu_custom_call" | custom-call | tf_op jit(solution)/shard_map/ffn_backward/pallas_call | solution.py:65
  276.3 4.0 collective-permute-done.42.refs_2_.refs_1_
  288.1 19.9 %attention_backward.3 = (f32[480,768]{1,0:T(8,128)}, f32[144,128]{1,0:T(8,128)}, bf16[12,96,384]{2,1,0:T(8,128)(2,1)}, bf16[12,96,384]{2,1,0:T(8,128)(2,1)}, bf1...) custom-call(s32[4]{0:T(128)} %pad_add_fusion.refs_0_, s32[3]{0:T(128)} %refs_1_.10, ...), custom_call_target="tpu_custom_call" | custom-call | tf_op jit(solution)/shard_map/attention_backward/pallas_call | solution.py:65
  308.6 3.2 collect.2.refs_4_
  313.2 3.2 collective-permute-done.46.refs_2_.refs_1_
  326.6 3.5 collective-permute-done.51.refs_1_
  334.6 13.2 %collective-permute-done.52.refs_3_ = bf16[3,96,384]{2,1,0:T(8,128)(2,1)S(1)} collective-permute-done((bf16[3,96,384]{2,1,0:T(8,128)(2,1)S(1)}, bf16[3,96,384]{2,1,0:T(8,128)(2,1)S(1)}, u32[]{:S(2)}, u32[]{:S(2)}) %collective-permute-start.52) | collective-permute-done | bytes 221216 | tf_op jit(solution)/shard_map/ppermute | solution.py:776
  349.0 3.2 collect.3.refs_2_.refs_14_.refs_19_
  355.2 11.2 %collective-permute-done.58.refs_0_ = bf16[6,96,384]{2,1,0:T(8,128)(2,1)S(1)} collective-permute-done((bf16[6,96,384]{2,1,0:T(8,128)(2,1)}, bf16[6,96,384]{2,1,0:T(8,128)(2,1)S(1)}, u32[]{:S(2)}, u32[]{:S(2)}) %collective-permute-start.58) | collective-permute-done | bytes 442400 | tf_op jit(solution)/shard_map/ppermute | solution.py:776
  370.8 3.7 collective-permute-done.56
  375.9 3.0 collective-permute-done.57
  381.4 7.9 %update_layer.2 = (f32[2,6,96,384]{3,2,1,0:T(8,128)}, f32[2,6,96,384]{3,2,1,0:T(8,128)}, f32[2,6,96,384]{3,2,1,0:T(8,128)}, f32[2,6,96,384]{3,2,1,0:T(8,128)}, bf16[2,6,96,384]{3,2,1,0:T(8,128)(2,1)}) custom-call(s32[4]{0:T(128)} %pad_add_fusion.refs_0_, bf16[6,96,384]{2,1,0:T(8,128)(2,1)} %get-tuple-element.230.refs_1_.refs_6_, f32[2,6,96,384]{3,2,1,0:T(8,128)} %refs_2_.4, ...), custom_call_target="tpu_custom_call" | custom-call | tf_op jit(solution)/shard_map/update_layer/pallas_call | solution.py:65
  393.3 2.4 collective-permute-start.66
  396.0 4.3 %collective-permute-done.65 = f32[144,128]{1,0:T(8,128)S(1)} collective-permute-done((f32[144,128]{1,0:T(8,128)}, f32[144,128]{1,0:T(8,128)S(1)}, u32[]{:S(2)}, u32[]{:S(2)}) %collective-permute-start.65) | collective-permute-done | bytes 73760 | tf_op jit(solution)/shard_map/ppermute | solution.py:776
  405.4 7.9 %update_layer.3 = (f32[2,6,96,384]{3,2,1,0:T(8,128)}, f32[2,6,96,384]{3,2,1,0:T(8,128)}, f32[2,6,96,384]{3,2,1,0:T(8,128)}, f32[2,6,96,384]{3,2,1,0:T(8,128)}, bf16[2,6,96,384]{3,2,1,0:T(8,128)(2,1)}) custom-call(s32[4]{0:T(128)} %pad_add_fusion.refs_0_, ...), custom_call_target="tpu_custom_call", output_to_operand_aliasing={{0}: (14, {}), {1}: (15, {}), {2}: (16, {}), {3}: (17, {}),... | custom-call | tf_op jit(solution)/shard_map/update_layer/pallas_call | solution.py:65
  (329 shorter events, 127.5 us)
Async XLA Ops:
  7.2 49.9 %all-gather.9.cloned.1.call-start = ((), (), s32[]{:S(2)}) async-start(), calls=%async_computation.5 | async-start | bytes 1474560 | tf_op jit(solution)/shard_map/all_gather | solution.py:788
  9.7 93.6 %all-gather.11.cloned.1.call-start = ((), (), s32[]{:S(2)}) async-start(), calls=%async_computation.6 | async-start | bytes 1474560 | tf_op jit(solution)/shard_map/all_gather | solution.py:788
  10.5 124.1 %all-gather.7.cloned.1.call-start = ((), (), s32[]{:S(2)}) async-start(), calls=%async_computation.2 | async-start | bytes 2949120 | tf_op jit(solution)/shard_map/all_gather | solution.py:788
  10.5 29.0 %collective-permute-start = (bf16[2,96,384]{2,1,0:T(8,128)(2,1)S(1)}, bf16[2,96,384]{2,1,0:T(8,128)(2,1)S(1)}, u32[]{:S(2)}, u32[]{:S(2)}) collective-permute-start(bf16[2,96,384]{2,1,0:T(8,128)(2,1)S(1)} %get-tuple-element.248.refs_0_), channel_id=1, source_target_pairs={{0,4},{1,5},{2,6},{3,7},{4,0},{5,1},{6,2},{7,3},{8,12},{9,13},{10,... | collective-permute-start | bytes 442376 | tf_op jit(solution)/shard_map/ppermute | solution.py:776
  13.6 26.0 %collective-permute-start.1 = (bf16[2,96,384]{2,1,0:T(8,128)(2,1)S(1)}, bf16[2,96,384]{2,1,0:T(8,128)(2,1)S(1)}, u32[]{:S(2)}, u32[]{:S(2)}) collective-permute-start(bf16[2,96,384]{2,1,0:T(8,128)(2,1)S(1)} %get-tuple-element.248.refs_0_), channel_id=1, source_target_pairs={{0,2},{1,3},{2,0},{3,1},{4,6},{5,7},{6,4},{7,5},{8,10},{9,11},{10,... | collective-permute-start | bytes 442376 | tf_op jit(solution)/shard_map/ppermute | solution.py:776
  15.1 24.5 %collective-permute-start.2 = (bf16[2,96,384]{2,1,0:T(8,128)(2,1)S(1)}, bf16[2,96,384]{2,1,0:T(8,128)(2,1)S(1)}, u32[]{:S(2)}, u32[]{:S(2)}) collective-permute-start(bf16[2,96,384]{2,1,0:T(8,128)(2,1)S(1)} %get-tuple-element.248.refs_0_), channel_id=1, source_target_pairs={{0,6},{1,7},{2,4},{3,5},{4,2},{5,3},{6,0},{7,1},{8,14},{9,15},{10,... | collective-permute-start | bytes 442376 | tf_op jit(solution)/shard_map/ppermute | solution.py:776
  82.9 20.4 %collective-permute-start.12 = (bf16[16,96,384]{2,1,0:T(8,128)(2,1)}, bf16[16,96,384]{2,1,0:T(8,128)(2,1)}, u32[]{:S(2)}, u32[]{:S(2)}) collective-permute-start(bf16[16,96,384]{2,1,0:T(8,128)(2,1)} %get-tuple-element.135.refs_1_.refs_12_.refs_11_.refs_18_.refs_17_), channel_id=1, source_target_pairs={{0,2},{1,3},{2,0},{3,1},{4,6},{5,7},{6,4},{7,5},{8,10},{9,11},{10,... | collective-permute-start | bytes 3538952 | tf_op jit(solution)/shard_map/ppermute | solution.py:776
  83.3 22.2 %collective-permute-start.13 = (bf16[16,96,384]{2,1,0:T(8,128)(2,1)}, bf16[16,96,384]{2,1,0:T(8,128)(2,1)}, u32[]{:S(2)}, u32[]{:S(2)}) collective-permute-start(bf16[16,96,384]{2,1,0:T(8,128)(2,1)} %get-tuple-element.136.refs_2_.refs_16_.refs_15_.refs_22_.refs_21_), channel_id=1, source_target_pairs={{0,4},{1,5},{2,6},{3,7},{4,0},{5,1},{6,2},{7,3},{8,12},{9,13},{10,... | collective-permute-start | bytes 3538952 | tf_op jit(solution)/shard_map/ppermute | solution.py:776
  84.3 23.2 %collective-permute-start.6 = (bf16[16,96,384]{2,1,0:T(8,128)(2,1)}, bf16[16,96,384]{2,1,0:T(8,128)(2,1)S(1)}, u32[]{:S(2)}, u32[]{:S(2)}) collective-permute-start(bf16[16,96,384]{2,1,0:T(8,128)(2,1)} %get-tuple-element.131.refs_3_), channel_id=1, source_target_pairs={{0,1},{1,0},{2,3},{3,2},{4,5},{5,4},{6,7},{7,6},{8,9},{9,8},{10,11... | collective-permute-start | bytes 3538952 | tf_op jit(solution)/shard_map/ppermute | solution.py:776
  84.3 269.6 %reduce-scatter.5.cloned.1.call-start = ((), (), s32[]{:S(2)}) async-start(), calls=%async_computation.4 | async-start | bytes 2211840 | tf_op jit(solution)/shard_map/reduce_scatter | solution.py:920
  84.4 22.8 %collective-permute-start.7 = (bf16[8,96,384]{2,1,0:T(8,128)(2,1)}, bf16[8,96,384]{2,1,0:T(8,128)(2,1)}, u32[]{:S(2)}, u32[]{:S(2)}) collective-permute-start(bf16[8,96,384]{2,1,0:T(8,128)(2,1)} %copy-done.52), channel_id=1, source_target_pairs={{0,1},{1,0},{2,3},{3,2},{4,5},{5,4},{6,7},{7,6},{8,9},{9,8},{10,11... | collective-permute-start | bytes 1769480 | tf_op jit(solution)/shard_map/ppermute | solution.py:776
  84.9 22.5 %collective-permute-start.9 = (bf16[8,96,384]{2,1,0:T(8,128)(2,1)}, bf16[8,96,384]{2,1,0:T(8,128)(2,1)}, u32[]{:S(2)}, u32[]{:S(2)}) collective-permute-start(bf16[8,96,384]{2,1,0:T(8,128)(2,1)} %copy-done.53), channel_id=1, source_target_pairs={{0,1},{1,0},{2,3},{3,2},{4,5},{5,4},{6,7},{7,6},{8,9},{9,8},{10,11... | collective-permute-start | bytes 1769480 | tf_op jit(solution)/shard_map/ppermute | solution.py:776
  105.5 19.9 %collective-permute-start.17 = (bf16[8,96,384]{2,1,0:T(8,128)(2,1)}, bf16[8,96,384]{2,1,0:T(8,128)(2,1)}, u32[]{:S(2)}, u32[]{:S(2)}) collective-permute-start(bf16[8,96,384]{2,1,0:T(8,128)(2,1)} %get-tuple-element.138.refs_2_.refs_20_.refs_0_), channel_id=1, source_target_pairs={{0,4},{1,5},{2,6},{3,7},{4,0},{5,1},{6,2},{7,3},{8,12},{9,13},{10,... | collective-permute-start | bytes 1769480 | tf_op jit(solution)/shard_map/ppermute | solution.py:776
  129.8 22.3 %collective-permute-start.22 = (bf16[8,96,384]{2,1,0:T(8,128)(2,1)}, bf16[8,96,384]{2,1,0:T(8,128)(2,1)S(1)}, u32[]{:S(2)}, u32[]{:S(2)}) collective-permute-start(bf16[8,96,384]{2,1,0:T(8,128)(2,1)} %get-tuple-element.146.refs_6_), channel_id=1, source_target_pairs={{0,1},{1,0},{2,3},{3,2},{4,5},{5,4},{6,7},{7,6},{8,9},{9,8},{10,11... | collective-permute-start | bytes 1769480 | tf_op jit(solution)/shard_map/ppermute | solution.py:776
  132.8 32.4 %collective-permute-start.25 = (bf16[12,96,384]{2,1,0:T(8,128)(2,1)}, bf16[12,96,384]{2,1,0:T(8,128)(2,1)S(1)}, u32[]{:S(2)}, u32[]{:S(2)}) collective-permute-start(bf16[12,96,384]{2,1,0:T(8,128)(2,1)} %get-tuple-element.147.refs_19_.refs_1_.refs_10_), channel_id=1, source_target_pairs={{0,2},{1,3},{2,0},{3,1},{4,6},{5,7},{6,4},{7,5},{8,10},{9,11},{10,... | collective-permute-start | bytes 2654216 | tf_op jit(solution)/shard_map/ppermute | solution.py:776
  137.6 27.7 %collective-permute-start.26 = (bf16[12,96,384]{2,1,0:T(8,128)(2,1)S(1)}, bf16[12,96,384]{2,1,0:T(8,128)(2,1)S(1)}, u32[]{:S(2)}, u32[]{:S(2)}) collective-permute-start(bf16[12,96,384]{2,1,0:T(8,128)(2,1)S(1)} %copy-done.66), channel_id=1, source_target_pairs={{0,4},{1,5},{2,6},{3,7},{4,0},{5,1},{6,2},{7,3},{8,12},{9,13},{10,... | collective-permute-start | bytes 2654216 | tf_op jit(solution)/shard_map/ppermute | solution.py:776
  138.4 34.1 %collective-permute-start.27 = (bf16[24,96,384]{2,1,0:T(8,128)(2,1)}, bf16[24,96,384]{2,1,0:T(8,128)(2,1)}, u32[]{:S(2)}, u32[]{:S(2)}) collective-permute-start(bf16[24,96,384]{2,1,0:T(8,128)(2,1)} %get-tuple-element.149.refs_21_), channel_id=1, source_target_pairs={{0,1},{1,0},{2,3},{3,2},{4,5},{5,4},{6,7},{7,6},{8,9},{9,8},{10,11... | collective-permute-start | bytes 5308424 | tf_op jit(solution)/shard_map/ppermute | solution.py:776
  170.9 27.7 %collective-permute-start.30 = (bf16[12,96,384]{2,1,0:T(8,128)(2,1)S(1)}, bf16[12,96,384]{2,1,0:T(8,128)(2,1)S(1)}, u32[]{:S(2)}, u32[]{:S(2)}) collective-permute-start(bf16[12,96,384]{2,1,0:T(8,128)(2,1)S(1)} %rounded.1.refs_18_.refs_10_), channel_id=1, source_target_pairs={{0,2},{1,3},{2,0},{3,1},{4,6},{5,7},{6,4},{7,5},{8,10},{9,11},{10,... | collective-permute-start | bytes 2654216 | tf_op jit(solution)/shard_map/ppermute | solution.py:776
  205.5 31.3 %collective-permute-start.36 = (bf16[18,96,384]{2,1,0:T(8,128)(2,1)S(1)}, bf16[18,96,384]{2,1,0:T(8,128)(2,1)}, u32[]{:S(2)}, u32[]{:S(2)}) collective-permute-start(bf16[18,96,384]{2,1,0:T(8,128)(2,1)S(1)} %get-tuple-element.171.refs_21_), channel_id=1, source_target_pairs={{0,4},{1,5},{2,6},{3,7},{4,0},{5,1},{6,2},{7,3},{8,12},{9,13},{10,... | collective-permute-start | bytes 3981320 | tf_op jit(solution)/shard_map/ppermute | solution.py:776
  209.3 31.2 %collective-permute-start.33 = (bf16[18,96,384]{2,1,0:T(8,128)(2,1)S(1)}, bf16[18,96,384]{2,1,0:T(8,128)(2,1)S(1)}, u32[]{:S(2)}, u32[]{:S(2)}) collective-permute-start(bf16[18,96,384]{2,1,0:T(8,128)(2,1)S(1)} %get-tuple-element.168.refs_20_), channel_id=1, source_target_pairs={{0,2},{1,3},{2,0},{3,1},{4,6},{5,7},{6,4},{7,5},{8,10},{9,11},{10,... | collective-permute-start | bytes 3981320 | tf_op jit(solution)/shard_map/ppermute | solution.py:776
  239.4 27.1 %collective-permute-start.40 = (bf16[9,96,384]{2,1,0:T(8,128)(2,1)S(1)}, bf16[9,96,384]{2,1,0:T(8,128)(2,1)S(1)}, u32[]{:S(2)}, u32[]{:S(2)}) collective-permute-start(bf16[9,96,384]{2,1,0:T(8,128)(2,1)S(1)} %get-tuple-element.186.refs_27_), channel_id=1, source_target_pairs={{0,2},{1,3},{2,0},{3,1},{4,6},{5,7},{6,4},{7,5},{8,10},{9,11},{10,... | collective-permute-start | bytes 1990664 | tf_op jit(solution)/shard_map/ppermute | solution.py:776
  240.9 25.7 %collective-permute-start.39 = (bf16[9,96,384]{2,1,0:T(8,128)(2,1)S(1)}, bf16[9,96,384]{2,1,0:T(8,128)(2,1)S(1)}, u32[]{:S(2)}, u32[]{:S(2)}) collective-permute-start(bf16[9,96,384]{2,1,0:T(8,128)(2,1)S(1)} %get-tuple-element.184.refs_26_), channel_id=1, source_target_pairs={{0,4},{1,5},{2,6},{3,7},{4,0},{5,1},{6,2},{7,3},{8,12},{9,13},{10,... | collective-permute-start | bytes 1990664 | tf_op jit(solution)/shard_map/ppermute | solution.py:776
  242.5 24.0 %collective-permute-start.38 = (bf16[6,96,384]{2,1,0:T(8,128)(2,1)S(1)}, bf16[6,96,384]{2,1,0:T(8,128)(2,1)S(1)}, u32[]{:S(2)}, u32[]{:S(2)}) collective-permute-start(bf16[6,96,384]{2,1,0:T(8,128)(2,1)S(1)} %get-tuple-element.183.refs_3_.refs_29_), channel_id=1, source_target_pairs={{0,4},{1,5},{2,6},{3,7},{4,0},{5,1},{6,2},{7,3},{8,12},{9,13},{10,... | collective-permute-start | bytes 1327112 | tf_op jit(solution)/shard_map/ppermute | solution.py:776
  243.0 23.6 %collective-permute-start.37 = (bf16[6,96,384]{2,1,0:T(8,128)(2,1)S(1)}, bf16[6,96,384]{2,1,0:T(8,128)(2,1)S(1)}, u32[]{:S(2)}, u32[]{:S(2)}) collective-permute-start(bf16[6,96,384]{2,1,0:T(8,128)(2,1)S(1)} %get-tuple-element.180.refs_2_.refs_28_), channel_id=1, source_target_pairs={{0,2},{1,3},{2,0},{3,1},{4,6},{5,7},{6,4},{7,5},{8,10},{9,11},{10,... | collective-permute-start | bytes 1327112 | tf_op jit(solution)/shard_map/ppermute | solution.py:776
  283.5 29.7 %collective-permute-start.47 = (bf16[18,96,384]{2,1,0:T(8,128)(2,1)}, bf16[18,96,384]{2,1,0:T(8,128)(2,1)}, u32[]{:S(2)}, u32[]{:S(2)}) collective-permute-start(bf16[18,96,384]{2,1,0:T(8,128)(2,1)} %get-tuple-element.204.refs_26_), channel_id=1, source_target_pairs={{0,4},{1,5},{2,6},{3,7},{4,0},{5,1},{6,2},{7,3},{8,12},{9,13},{10,... | collective-permute-start | bytes 3981320 | tf_op jit(solution)/shard_map/ppermute | solution.py:776
  286.8 29.6 %collective-permute-start.46 = (bf16[18,96,384]{2,1,0:T(8,128)(2,1)}, bf16[18,96,384]{2,1,0:T(8,128)(2,1)}, u32[]{:S(2)}, u32[]{:S(2)}) collective-permute-start(bf16[18,96,384]{2,1,0:T(8,128)(2,1)} %get-tuple-element.201.refs_25_), channel_id=1, source_target_pairs={{0,2},{1,3},{2,0},{3,1},{4,6},{5,7},{6,4},{7,5},{8,10},{9,11},{10,... | collective-permute-start | bytes 3981320 | tf_op jit(solution)/shard_map/ppermute | solution.py:776
  311.9 78.0 %reduce-scatter.3.cloned.1.call-start = ((), (), s32[]{:S(2)}) async-start(), calls=%async_computation.3 | async-start | bytes 2211840 | tf_op jit(solution)/shard_map/reduce_scatter | solution.py:920
  323.0 24.8 %collective-permute-start.54 = (bf16[9,96,384]{2,1,0:T(8,128)(2,1)S(1)}, bf16[9,96,384]{2,1,0:T(8,128)(2,1)S(1)}, u32[]{:S(2)}, u32[]{:S(2)}) collective-permute-start(bf16[9,96,384]{2,1,0:T(8,128)(2,1)S(1)} %get-tuple-element.220.refs_3_), channel_id=1, source_target_pairs={{0,2},{1,3},{2,0},{3,1},{4,6},{5,7},{6,4},{7,5},{8,10},{9,11},{10,... | collective-permute-start | bytes 1990664 | tf_op jit(solution)/shard_map/ppermute | solution.py:776
  325.8 22.0 %collective-permute-start.53 = (bf16[9,96,384]{2,1,0:T(8,128)(2,1)S(1)}, bf16[9,96,384]{2,1,0:T(8,128)(2,1)S(1)}, u32[]{:S(2)}, u32[]{:S(2)}) collective-permute-start(bf16[9,96,384]{2,1,0:T(8,128)(2,1)S(1)} %get-tuple-element.218.refs_2_), channel_id=1, source_target_pairs={{0,4},{1,5},{2,6},{3,7},{4,0},{5,1},{6,2},{7,3},{8,12},{9,13},{10,... | collective-permute-start | bytes 1990664 | tf_op jit(solution)/shard_map/ppermute | solution.py:776
  353.4 26.2 %collective-permute-start.61 = (bf16[12,96,384]{2,1,0:T(8,128)(2,1)S(1)}, bf16[12,96,384]{2,1,0:T(8,128)(2,1)S(1)}, u32[]{:S(2)}, u32[]{:S(2)}) collective-permute-start(bf16[12,96,384]{2,1,0:T(8,128)(2,1)S(1)} %copy-done.1), channel_id=1, source_target_pairs={{0,1},{1,0},{2,3},{3,2},{4,5},{5,4},{6,7},{7,6},{8,9},{9,8},{10,11... | collective-permute-start | bytes 2654216 | tf_op jit(solution)/shard_map/ppermute | solution.py:776
  353.7 25.9 %collective-permute-start.62 = (bf16[12,96,384]{2,1,0:T(8,128)(2,1)S(1)}, bf16[12,96,384]{2,1,0:T(8,128)(2,1)S(1)}, u32[]{:S(2)}, u32[]{:S(2)}) collective-permute-start(bf16[12,96,384]{2,1,0:T(8,128)(2,1)S(1)} %copy-done.55), channel_id=1, source_target_pairs={{0,1},{1,0},{2,3},{3,2},{4,5},{5,4},{6,7},{7,6},{8,9},{9,8},{10,11... | collective-permute-start | bytes 2654216 | tf_op jit(solution)/shard_map/ppermute | solution.py:776
  355.2 25.3 %collective-permute-start.59 = (bf16[6,96,384]{2,1,0:T(8,128)(2,1)}, bf16[6,96,384]{2,1,0:T(8,128)(2,1)}, u32[]{:S(2)}, u32[]{:S(2)}) collective-permute-start(bf16[6,96,384]{2,1,0:T(8,128)(2,1)} %get-tuple-element.230.refs_1_.refs_6_), channel_id=1, source_target_pairs={{0,1},{1,0},{2,3},{3,2},{4,5},{5,4},{6,7},{7,6},{8,9},{9,8},{10,11... | collective-permute-start | bytes 1327112 | tf_op jit(solution)/shard_map/ppermute | solution.py:776
  (118 other events, 661.6 us)
Sparse Core Ops, SparseCore 0:
  9.8 38.7 all-gather.8
  50.7 30.8 all-gather.10
  84.4 50.0 all-gather.6
  312.0 37.4 reduce-scatter.4
  352.4 37.4 reduce-scatter.2

commit v7 on v6

--- a/solution.py
+++ b/solution.py
@@ -943,52 +943,57 @@
     if not first:
         rest = rest[5:]
     outs, rest = rest[:5], rest[5:]
-    g_ref, r_ref, turned, own, held, fresh, low_ref, sem_g, sem_r, sem_in, sem_out = rest
+    g_ref, r_ref, turned, own, held, fresh, low_ref, sem_in, sem_out = rest
     y, c = pos_ref[2], pos_ref[3]
     count, piece, block = own_ref.shape
 
     def quarter(yq, cq):
         return pl.ds(pl.multiple_of(piece * (2 * yq + cq), 16), piece)
 
-    for n in range(count_grads):
-        rows = quarter(y ^ (n % 2), c ^ (n // 2)) if count_grads == 4 else pl.ds(0, block)
-        if count_grads == 4:
-            pltpu.make_async_copy(grads[n], g_ref.at[:, rows, :], sem_g).start()
-    if count_grads == 1:
+    groups = [(0, 1), (1, (count - 1) // 2), (1 + (count - 1) // 2, count - 1 - (count - 1) // 2)]
+    for number, (low, many) in enumerate(groups):
+        some = pl.ds(low, many)
         for n in range(4):
-            mine = grads[0].at[pl.ds(n * count, count)]
-            pltpu.make_async_copy(mine, g_ref.at[:, pl.ds(n * piece, piece), :], sem_g).start()
-    for n in range(4):
-        mine = roots[n].at[pl.ds(layer * count, count)]
-        pltpu.make_async_copy(mine, r_ref.at[:, quarter(y ^ (n % 2), c ^ (n // 2)), :], sem_r).start()
-    for n in range(4):
-        pltpu.make_async_copy(stats[n].at[layer], held.at[n], sem_in.at[n]).start()
-    pltpu.make_async_copy(own_ref, own, sem_in.at[4]).start()
+            rows = quarter(y ^ (n % 2), c ^ (n // 2))
+            mine = grads[n].at[some]
+            pltpu.make_async_copy(mine, g_ref.at[some, rows, :], sem_in.at[number, 5]).start()
+        for n in range(3):
+            pltpu.make_async_copy(stats[n].at[layer, some], held.at[n, some], sem_in.at[number, n]).start()
+        for n in range(4):
+            rows = quarter(y ^ (n % 2), c ^ (n // 2))
+            mine = roots[n].at[pl.ds(layer * count + low, many)]
+            pltpu.make_async_copy(mine, r_ref.at[some, rows, :], sem_in.at[number, 6]).start()
+        pltpu.make_async_copy(stats[3].at[layer, some], held.at[3, some], sem_in.at[number, 3]).start()
+        pltpu.make_async_copy(own_ref.at[some], own.at[some], sem_in.at[number, 4]).start()
     own_rows = quarter(y, c)
-    wait_for(g_ref, sem_g)
+
+    def arrived(b, n):
+        for number, (low, many) in enumerate(groups):
+            if low == b:
+                some = pl.ds(low, many)
+                ref = held.at[n, some] if n < 4 else (own, g_ref, r_ref)[n - 4].at[some]
+                wait_for(ref, sem_in.at[number, n])
+
     def halves(value):
         high = value.astype(BF)
         return [high, (value - high.astype(F32)).astype(BF)]
 
     for b in range(count):
+        arrived(b, 5)
         g = g_ref[b]
         turned[...] = g.T
-        if b == 0:
-            wait_for(held.at[0], sem_in.at[0])
+        arrived(b, 0)
         fresh[1, b] = decay_rate * held[0, b] + (1.0 - decay_rate) * mm_bt(g_ref[b, own_rows, :], g)
-        if b == 0:
-            wait_for(held.at[1], sem_in.at[1])
-            wait_for(held.at[2], sem_in.at[2])
+        arrived(b, 1)
+        arrived(b, 2)
         products = mm(jnp.concatenate([turned[own_rows, :], *halves(held[2, b])], axis=0), g)
         fresh[2, b] = decay_rate * held[1, b] + (1.0 - decay_rate) * products[:piece]
-        if b == 0:
-            wait_for(r_ref, sem_r)
+        arrived(b, 6)
         mixed = products[piece : 2 * piece] + products[2 * piece :]
         products = mm(jnp.concatenate(halves(mixed), axis=0), r_ref[b])
         update = products[:piece] + products[piece:]
-        if b == 0:
-            wait_for(held.at[3], sem_in.at[3])
-            wait_for(own, sem_in.at[4])
+        arrived(b, 3)
+        arrived(b, 4)
         master = held[3, b] - matrix_rate * update
         fresh[3, b] = master
         low_ref[b] = master.astype(BF)
@@ -1024,9 +1029,7 @@
             pltpu.VMEM((4,) + own.shape, F32),
             pltpu.VMEM((4,) + own.shape, F32),
             pltpu.VMEM(own.shape, BF),
-            pltpu.SemaphoreType.DMA,
-            pltpu.SemaphoreType.DMA,
-            pltpu.SemaphoreType.DMA((5,)),
+            pltpu.SemaphoreType.DMA((3, 7)),
             pltpu.SemaphoreType.DMA((2,)),
         ],
         (0, 0, 0),

time: 427 us -> 427 us (level)
  no operation moved by 1% of the time
where the time goes in v7:
time: 427 us; the launch traced here: 420 us
  Pallas kernels  179 us (42%)
  waiting for transfers between devices  114 us (27%)
  starting transfers between devices  53.2 us (12%)
  local copies, waits for them, and re-layouts  29.4 us (7%)
  blocking collectives  24.5 us (6%)
  between operations  14.9 us (3%)
  other arithmetic  5.32 us (1%)
    pallas_call x46, Pallas kernels, launch(): pl.pallas_call(kernel, in_specs=[spec for _, spec in ins] + [ANY] * extra...  179 us
    ppermute x69, waiting for transfers between devices, permute(): return lax.ppermute(array, ('grp', 'fsdp'), pairs)  111 us
    ppermute x69, starting transfers between devices, permute(): return lax.ppermute(array, ('grp', 'fsdp'), pairs)  53 us
    unnamed x152, local copies, waits for them, and re-layouts  27.8 us
    all_gather x1, blocking collectives, whole_column(): lax.all_gather(own, 'grp', axis_index_groups=self.columns(), axis=0, tile...  24.5 us
  transfers between devices with their start and end apart: 74, of which 33 were waited for; matrix products, arithmetic and copies ran while one was open for 1% of the time, Pallas kernels for 41%

profile of v7, /device:TPU:0, one launch (start us, length us, event | category | flops | bytes accessed | tf_op | source)
XLA Modules:
  0.0 419.6 jit_solution(883319879114620564)
XLA Ops:
  10.5 3.0 collective-permute-start
  15.1 24.5 %all-gather = bf16[1,8,96,384]{3,2,0,1:T(8,128)(2,1)S(1)} all-gather(bf16[1,2,96,384]{3,2,0,1:T(8,128)(2,1)S(1)} %get-tuple-element.249), channel_id=2, replica_groups={{0,8,16,24},{4,12,20,28},{1,9,17,25},{5,13,21,29},{2,10,18,26},{6,14,22..., dimensions={1}, use_global_device_ids=true | all-gather | bytes 737280 | tf_op jit(solution)/shard_map/all_gather | solution.py:788
  46.2 3.9 collective-permute-done.3.refs_1_
  52.7 2.5 join.4
  57.1 2.2 pick.4
  61.6 8.9 %collective-permute-done.5.refs_4_.refs_5_.refs_11_.refs_10_ = bf16[8,96,384]{2,1,0:T(8,128)(2,1)S(1)} collective-permute-done((bf16[8,96,384]{2,1,0:T(8,128)(2,1)}, bf16[8,96,384]{2,1,0:T(8,128)(2,1)S(1)}, u32[]{:S(2)}, u32[]{:S(2)}) %collective-permute-start.5) | collective-permute-done | bytes 589856 | tf_op jit(solution)/shard_map/ppermute | solution.py:776
  71.4 6.3 %collective-permute-done.10.refs_1_ = bf16[8,96,384]{2,1,0:T(8,128)(2,1)S(1)} collective-permute-done((bf16[8,96,384]{2,1,0:T(8,128)(2,1)}, bf16[8,96,384]{2,1,0:T(8,128)(2,1)S(1)}, u32[]{:S(2)}, u32[]{:S(2)}) %collective-permute-start.10) | collective-permute-done | bytes 589856 | tf_op jit(solution)/shard_map/ppermute | solution.py:776
  79.4 3.5 join.5
  85.0 18.3 %collective-permute-done.12.refs_0_ = bf16[16,96,384]{2,1,0:T(8,128)(2,1)} collective-permute-done((bf16[16,96,384]{2,1,0:T(8,128)(2,1)}, bf16[16,96,384]{2,1,0:T(8,128)(2,1)}, u32[]{:S(2)}, u32[]{:S(2)}) %collective-permute-start.12) | collective-permute-done | bytes 1179680 | tf_op jit(solution)/shard_map/ppermute | solution.py:776
  113.7 11.7 %attention_forward.2 = (bf16[480,2304]{1,0:T(8,128)(2,1)}, f32[3,12,160]{2,1,0:T(8,128)}, bf16[480,768]{1,0:T(8,128)(2,1)}, f32[480,768]{1,0:T(8,128)}, f32[480,1]{1,0:T(8,128)}) custom-call(s32[4]{0:T(128)} %pad_add_fusion.refs_0_, s32[3]{0:T(128)} %refs_1_.10, bf16[480,768]{1,0:T(8,128)(2,1)} %bitcast.23, f32[1,9216]{1,0:T(1,128)} %get-tuple-element.250.refs_3_.refs_2_, ...), custom_call_target="tpu_custom_call" | custom-call | tf_op jit(solution)/shard_map/attention_forward/pallas_call | solution.py:65
  129.8 3.0 join.7
  134.6 3.0 collective-permute-done.20.refs_1_
  138.4 13.2 %ffn_forward.1 = (bf16[480,3072]{1,0:T(8,128)(2,1)}, bf16[480,3072]{1,0:T(8,128)(2,1)}, f32[480,768]{1,0:T(8,128)}, f32[480,1]{1,0:T(8,128)}, f32[480,768]{1,0:T(8,128)}) custom-call(s32[4]{0:T(128)} %pad_add_fusion.refs_0_, f32[480,768]{1,0:T(8,128)} %get-tuple-element.142.refs_1_.refs_6_, f32[1,9216]{1,0:T(1,128)} %get-tuple-element.250.refs_3_.refs_2_, ...), custom_call_target="tpu_custom_call" | custom-call | flops 99999997952 | tf_op jit(solution)/shard_map/ffn_forward/pallas_call | solution.py:65
  154.6 10.6 %attention_forward.3 = (bf16[480,2304]{1,0:T(8,128)(2,1)}, f32[3,12,160]{2,1,0:T(8,128)}, bf16[480,768]{1,0:T(8,128)(2,1)}) custom-call(s32[4]{0:T(128)} %pad_add_fusion.refs_0_, s32[3]{0:T(128)} %refs_1_.10, f32[480,768]{1,0:T(8,128)} %get-tuple-element.150.refs_2_.refs_4_.refs_6_, f32[1,9216]{1,0:T(1,128)} %get-tuple-element.251.refs_3_, ...), custom_call_target="tpu_custom_call" | custom-call | tf_op jit(solution)/shard_map/attention_forward/pallas_call | solution.py:65
  172.5 25.8 %ffn_both.1 = (bf16[480,768]{1,0:T(8,128)(2,1)}, f32[480,768]{1,0:T(8,128)}, bf16[480,768]{1,0:T(8,128)(2,1)}, f32[72,128]{1,0:T(8,128)}, bf16[36,96,384]{2,1,0:...) custom-call(s32[4]{0:T(128)} %pad_add_fusion.refs_0_, ...), custom_call_target="tpu_custom_call" | custom-call | tf_op jit(solution)/shard_map/ffn_both/pallas_call | solution.py:65
  199.8 4.7 %collective-permute-done.32.refs_1_ = bf16[36,96,384]{2,1,0:T(8,128)(2,1)S(1)} collective-permute-done((bf16[36,96,384]{2,1,0:T(8,128)(2,1)}, bf16[36,96,384]{2,1,0:T(8,128)(2,1)S(1)}, u32[]{:S(2)}, u32[]{:S(2)}) %collective-permute-start.32) | collective-permute-done | bytes 2654240 | tf_op jit(solution)/shard_map/ppermute | solution.py:776
  210.0 20.1 %attention_backward.2 = (f32[480,768]{1,0:T(8,128)}, f32[72,128]{1,0:T(8,128)}, bf16[12,96,384]{2,1,0:T(8,128)(2,1)}, bf16[12,96,384]{2,1,0:T(8,128)(2,1)}, bf16...) custom-call(s32[4]{0:T(128)} %pad_add_fusion.refs_0_, s32[3]{0:T(128)} %refs_1_.10, ...), custom_call_target="tpu_custom_call" | custom-call | tf_op jit(solution)/shard_map/attention_backward/pallas_call | solution.py:65
  243.8 21.5 %ffn_backward.1 = (f32[480,768]{1,0:T(8,128)}, bf16[480,768]{1,0:T(8,128)(2,1)}, f32[72,128]{1,0:T(8,128)}, bf16[36,96,384]{2,1,0:T(8,128)(2,1)}, bf16[36,96,384...) custom-call(s32[4]{0:T(128)} %pad_add_fusion.refs_0_, ...), custom_call_target="tpu_custom_call" | custom-call | tf_op jit(solution)/shard_map/ffn_backward/pallas_call | solution.py:65
  276.2 4.1 collective-permute-done.42.refs_2_.refs_1_
  288.0 19.9 %attention_backward.3 = (f32[480,768]{1,0:T(8,128)}, f32[144,128]{1,0:T(8,128)}, bf16[12,96,384]{2,1,0:T(8,128)(2,1)}, bf16[12,96,384]{2,1,0:T(8,128)(2,1)}, bf1...) custom-call(s32[4]{0:T(128)} %pad_add_fusion.refs_0_, s32[3]{0:T(128)} %refs_1_.10, ...), custom_call_target="tpu_custom_call" | custom-call | tf_op jit(solution)/shard_map/attention_backward/pallas_call | solution.py:65
  308.5 3.2 collect.2.refs_4_
  313.1 3.2 collective-permute-done.46.refs_2_.refs_1_
  326.4 3.5 collective-permute-done.51.refs_1_
  334.5 13.2 %collective-permute-done.52.refs_3_ = bf16[3,96,384]{2,1,0:T(8,128)(2,1)S(1)} collective-permute-done((bf16[3,96,384]{2,1,0:T(8,128)(2,1)S(1)}, bf16[3,96,384]{2,1,0:T(8,128)(2,1)S(1)}, u32[]{:S(2)}, u32[]{:S(2)}) %collective-permute-start.52) | collective-permute-done | bytes 221216 | tf_op jit(solution)/shard_map/ppermute | solution.py:776
  348.8 3.2 collect.3.refs_2_.refs_14_.refs_19_
  355.0 11.2 %collective-permute-done.58.refs_0_ = bf16[6,96,384]{2,1,0:T(8,128)(2,1)S(1)} collective-permute-done((bf16[6,96,384]{2,1,0:T(8,128)(2,1)}, bf16[6,96,384]{2,1,0:T(8,128)(2,1)S(1)}, u32[]{:S(2)}, u32[]{:S(2)}) %collective-permute-start.58) | collective-permute-done | bytes 442400 | tf_op jit(solution)/shard_map/ppermute | solution.py:776
  370.6 3.7 collective-permute-done.56
  375.7 3.0 collective-permute-done.57
  381.2 7.4 %update_layer.2 = (f32[2,6,96,384]{3,2,1,0:T(8,128)}, f32[2,6,96,384]{3,2,1,0:T(8,128)}, f32[2,6,96,384]{3,2,1,0:T(8,128)}, f32[2,6,96,384]{3,2,1,0:T(8,128)}, bf16[2,6,96,384]{3,2,1,0:T(8,128)(2,1)}) custom-call(s32[4]{0:T(128)} %pad_add_fusion.refs_0_, bf16[6,96,384]{2,1,0:T(8,128)(2,1)} %get-tuple-element.230.refs_1_.refs_6_, f32[2,6,96,384]{3,2,1,0:T(8,128)} %refs_2_.4, ...), custom_call_target="tpu_custom_call" | custom-call | tf_op jit(solution)/shard_map/update_layer/pallas_call | solution.py:65
  393.2 2.4 collective-permute-start.66
  395.8 4.4 %collective-permute-done.65 = f32[144,128]{1,0:T(8,128)S(1)} collective-permute-done((f32[144,128]{1,0:T(8,128)}, f32[144,128]{1,0:T(8,128)S(1)}, u32[]{:S(2)}, u32[]{:S(2)}) %collective-permute-start.65) | collective-permute-done | bytes 73760 | tf_op jit(solution)/shard_map/ppermute | solution.py:776
  405.3 7.5 %update_layer.3 = (f32[2,6,96,384]{3,2,1,0:T(8,128)}, f32[2,6,96,384]{3,2,1,0:T(8,128)}, f32[2,6,96,384]{3,2,1,0:T(8,128)}, f32[2,6,96,384]{3,2,1,0:T(8,128)}, bf16[2,6,96,384]{3,2,1,0:T(8,128)(2,1)}) custom-call(s32[4]{0:T(128)} %pad_add_fusion.refs_0_, ...), custom_call_target="tpu_custom_call", output_to_operand_aliasing={{0}: (14, {}), {1}: (15, {}), {2}: (16, {}), {3}: (17, {}),... | custom-call | tf_op jit(solution)/shard_map/update_layer/pallas_call | solution.py:65
  (329 shorter events, 128.1 us)
Async XLA Ops:
  7.2 49.9 %all-gather.9.cloned.1.call-start = ((), (), s32[]{:S(2)}) async-start(), calls=%async_computation.5 | async-start | bytes 1474560 | tf_op jit(solution)/shard_map/all_gather | solution.py:788
  9.7 93.6 %all-gather.11.cloned.1.call-start = ((), (), s32[]{:S(2)}) async-start(), calls=%async_computation.6 | async-start | bytes 1474560 | tf_op jit(solution)/shard_map/all_gather | solution.py:788
  10.5 124.1 %all-gather.7.cloned.1.call-start = ((), (), s32[]{:S(2)}) async-start(), calls=%async_computation.2 | async-start | bytes 2949120 | tf_op jit(solution)/shard_map/all_gather | solution.py:788
  10.5 29.0 %collective-permute-start = (bf16[2,96,384]{2,1,0:T(8,128)(2,1)S(1)}, bf16[2,96,384]{2,1,0:T(8,128)(2,1)S(1)}, u32[]{:S(2)}, u32[]{:S(2)}) collective-permute-start(bf16[2,96,384]{2,1,0:T(8,128)(2,1)S(1)} %get-tuple-element.248.refs_0_), channel_id=1, source_target_pairs={{0,4},{1,5},{2,6},{3,7},{4,0},{5,1},{6,2},{7,3},{8,12},{9,13},{10,... | collective-permute-start | bytes 442376 | tf_op jit(solution)/shard_map/ppermute | solution.py:776
  13.6 26.0 %collective-permute-start.1 = (bf16[2,96,384]{2,1,0:T(8,128)(2,1)S(1)}, bf16[2,96,384]{2,1,0:T(8,128)(2,1)S(1)}, u32[]{:S(2)}, u32[]{:S(2)}) collective-permute-start(bf16[2,96,384]{2,1,0:T(8,128)(2,1)S(1)} %get-tuple-element.248.refs_0_), channel_id=1, source_target_pairs={{0,2},{1,3},{2,0},{3,1},{4,6},{5,7},{6,4},{7,5},{8,10},{9,11},{10,... | collective-permute-start | bytes 442376 | tf_op jit(solution)/shard_map/ppermute | solution.py:776
  15.1 24.5 %collective-permute-start.2 = (bf16[2,96,384]{2,1,0:T(8,128)(2,1)S(1)}, bf16[2,96,384]{2,1,0:T(8,128)(2,1)S(1)}, u32[]{:S(2)}, u32[]{:S(2)}) collective-permute-start(bf16[2,96,384]{2,1,0:T(8,128)(2,1)S(1)} %get-tuple-element.248.refs_0_), channel_id=1, source_target_pairs={{0,6},{1,7},{2,4},{3,5},{4,2},{5,3},{6,0},{7,1},{8,14},{9,15},{10,... | collective-permute-start | bytes 442376 | tf_op jit(solution)/shard_map/ppermute | solution.py:776
  82.9 20.4 %collective-permute-start.12 = (bf16[16,96,384]{2,1,0:T(8,128)(2,1)}, bf16[16,96,384]{2,1,0:T(8,128)(2,1)}, u32[]{:S(2)}, u32[]{:S(2)}) collective-permute-start(bf16[16,96,384]{2,1,0:T(8,128)(2,1)} %get-tuple-element.135.refs_1_.refs_12_.refs_11_.refs_18_.refs_17_), channel_id=1, source_target_pairs={{0,2},{1,3},{2,0},{3,1},{4,6},{5,7},{6,4},{7,5},{8,10},{9,11},{10,... | collective-permute-start | bytes 3538952 | tf_op jit(solution)/shard_map/ppermute | solution.py:776
  83.3 22.2 %collective-permute-start.13 = (bf16[16,96,384]{2,1,0:T(8,128)(2,1)}, bf16[16,96,384]{2,1,0:T(8,128)(2,1)}, u32[]{:S(2)}, u32[]{:S(2)}) collective-permute-start(bf16[16,96,384]{2,1,0:T(8,128)(2,1)} %get-tuple-element.136.refs_2_.refs_16_.refs_15_.refs_22_.refs_21_), channel_id=1, source_target_pairs={{0,4},{1,5},{2,6},{3,7},{4,0},{5,1},{6,2},{7,3},{8,12},{9,13},{10,... | collective-permute-start | bytes 3538952 | tf_op jit(solution)/shard_map/ppermute | solution.py:776
  84.3 23.2 %collective-permute-start.6 = (bf16[16,96,384]{2,1,0:T(8,128)(2,1)}, bf16[16,96,384]{2,1,0:T(8,128)(2,1)S(1)}, u32[]{:S(2)}, u32[]{:S(2)}) collective-permute-start(bf16[16,96,384]{2,1,0:T(8,128)(2,1)} %get-tuple-element.131.refs_3_), channel_id=1, source_target_pairs={{0,1},{1,0},{2,3},{3,2},{4,5},{5,4},{6,7},{7,6},{8,9},{9,8},{10,11... | collective-permute-start | bytes 3538952 | tf_op jit(solution)/shard_map/ppermute | solution.py:776
  84.3 269.4 %reduce-scatter.5.cloned.1.call-start = ((), (), s32[]{:S(2)}) async-start(), calls=%async_computation.4 | async-start | bytes 2211840 | tf_op jit(solution)/shard_map/reduce_scatter | solution.py:920
  84.4 22.8 %collective-permute-start.7 = (bf16[8,96,384]{2,1,0:T(8,128)(2,1)}, bf16[8,96,384]{2,1,0:T(8,128)(2,1)}, u32[]{:S(2)}, u32[]{:S(2)}) collective-permute-start(bf16[8,96,384]{2,1,0:T(8,128)(2,1)} %copy-done.52), channel_id=1, source_target_pairs={{0,1},{1,0},{2,3},{3,2},{4,5},{5,4},{6,7},{7,6},{8,9},{9,8},{10,11... | collective-permute-start | bytes 1769480 | tf_op jit(solution)/shard_map/ppermute | solution.py:776
  84.9 22.5 %collective-permute-start.9 = (bf16[8,96,384]{2,1,0:T(8,128)(2,1)}, bf16[8,96,384]{2,1,0:T(8,128)(2,1)}, u32[]{:S(2)}, u32[]{:S(2)}) collective-permute-start(bf16[8,96,384]{2,1,0:T(8,128)(2,1)} %copy-done.53), channel_id=1, source_target_pairs={{0,1},{1,0},{2,3},{3,2},{4,5},{5,4},{6,7},{7,6},{8,9},{9,8},{10,11... | collective-permute-start | bytes 1769480 | tf_op jit(solution)/shard_map/ppermute | solution.py:776
  105.5 19.9 %collective-permute-start.17 = (bf16[8,96,384]{2,1,0:T(8,128)(2,1)}, bf16[8,96,384]{2,1,0:T(8,128)(2,1)}, u32[]{:S(2)}, u32[]{:S(2)}) collective-permute-start(bf16[8,96,384]{2,1,0:T(8,128)(2,1)} %get-tuple-element.138.refs_2_.refs_20_.refs_0_), channel_id=1, source_target_pairs={{0,4},{1,5},{2,6},{3,7},{4,0},{5,1},{6,2},{7,3},{8,12},{9,13},{10,... | collective-permute-start | bytes 1769480 | tf_op jit(solution)/shard_map/ppermute | solution.py:776
  129.8 22.3 %collective-permute-start.22 = (bf16[8,96,384]{2,1,0:T(8,128)(2,1)}, bf16[8,96,384]{2,1,0:T(8,128)(2,1)S(1)}, u32[]{:S(2)}, u32[]{:S(2)}) collective-permute-start(bf16[8,96,384]{2,1,0:T(8,128)(2,1)} %get-tuple-element.146.refs_6_), channel_id=1, source_target_pairs={{0,1},{1,0},{2,3},{3,2},{4,5},{5,4},{6,7},{7,6},{8,9},{9,8},{10,11... | collective-permute-start | bytes 1769480 | tf_op jit(solution)/shard_map/ppermute | solution.py:776
  132.8 32.4 %collective-permute-start.25 = (bf16[12,96,384]{2,1,0:T(8,128)(2,1)}, bf16[12,96,384]{2,1,0:T(8,128)(2,1)S(1)}, u32[]{:S(2)}, u32[]{:S(2)}) collective-permute-start(bf16[12,96,384]{2,1,0:T(8,128)(2,1)} %get-tuple-element.147.refs_19_.refs_1_.refs_10_), channel_id=1, source_target_pairs={{0,2},{1,3},{2,0},{3,1},{4,6},{5,7},{6,4},{7,5},{8,10},{9,11},{10,... | collective-permute-start | bytes 2654216 | tf_op jit(solution)/shard_map/ppermute | solution.py:776
  137.5 27.7 %collective-permute-start.26 = (bf16[12,96,384]{2,1,0:T(8,128)(2,1)S(1)}, bf16[12,96,384]{2,1,0:T(8,128)(2,1)S(1)}, u32[]{:S(2)}, u32[]{:S(2)}) collective-permute-start(bf16[12,96,384]{2,1,0:T(8,128)(2,1)S(1)} %copy-done.66), channel_id=1, source_target_pairs={{0,4},{1,5},{2,6},{3,7},{4,0},{5,1},{6,2},{7,3},{8,12},{9,13},{10,... | collective-permute-start | bytes 2654216 | tf_op jit(solution)/shard_map/ppermute | solution.py:776
  138.4 34.1 %collective-permute-start.27 = (bf16[24,96,384]{2,1,0:T(8,128)(2,1)}, bf16[24,96,384]{2,1,0:T(8,128)(2,1)}, u32[]{:S(2)}, u32[]{:S(2)}) collective-permute-start(bf16[24,96,384]{2,1,0:T(8,128)(2,1)} %get-tuple-element.149.refs_21_), channel_id=1, source_target_pairs={{0,1},{1,0},{2,3},{3,2},{4,5},{5,4},{6,7},{7,6},{8,9},{9,8},{10,11... | collective-permute-start | bytes 5308424 | tf_op jit(solution)/shard_map/ppermute | solution.py:776
  170.9 27.4 %collective-permute-start.30 = (bf16[12,96,384]{2,1,0:T(8,128)(2,1)S(1)}, bf16[12,96,384]{2,1,0:T(8,128)(2,1)S(1)}, u32[]{:S(2)}, u32[]{:S(2)}) collective-permute-start(bf16[12,96,384]{2,1,0:T(8,128)(2,1)S(1)} %rounded.1.refs_18_.refs_10_), channel_id=1, source_target_pairs={{0,2},{1,3},{2,0},{3,1},{4,6},{5,7},{6,4},{7,5},{8,10},{9,11},{10,... | collective-permute-start | bytes 2654216 | tf_op jit(solution)/shard_map/ppermute | solution.py:776
  205.2 31.3 %collective-permute-start.36 = (bf16[18,96,384]{2,1,0:T(8,128)(2,1)S(1)}, bf16[18,96,384]{2,1,0:T(8,128)(2,1)}, u32[]{:S(2)}, u32[]{:S(2)}) collective-permute-start(bf16[18,96,384]{2,1,0:T(8,128)(2,1)S(1)} %get-tuple-element.171.refs_21_), channel_id=1, source_target_pairs={{0,4},{1,5},{2,6},{3,7},{4,0},{5,1},{6,2},{7,3},{8,12},{9,13},{10,... | collective-permute-start | bytes 3981320 | tf_op jit(solution)/shard_map/ppermute | solution.py:776
  209.0 31.2 %collective-permute-start.33 = (bf16[18,96,384]{2,1,0:T(8,128)(2,1)S(1)}, bf16[18,96,384]{2,1,0:T(8,128)(2,1)S(1)}, u32[]{:S(2)}, u32[]{:S(2)}) collective-permute-start(bf16[18,96,384]{2,1,0:T(8,128)(2,1)S(1)} %get-tuple-element.168.refs_20_), channel_id=1, source_target_pairs={{0,2},{1,3},{2,0},{3,1},{4,6},{5,7},{6,4},{7,5},{8,10},{9,11},{10,... | collective-permute-start | bytes 3981320 | tf_op jit(solution)/shard_map/ppermute | solution.py:776
  239.1 27.1 %collective-permute-start.40 = (bf16[9,96,384]{2,1,0:T(8,128)(2,1)S(1)}, bf16[9,96,384]{2,1,0:T(8,128)(2,1)S(1)}, u32[]{:S(2)}, u32[]{:S(2)}) collective-permute-start(bf16[9,96,384]{2,1,0:T(8,128)(2,1)S(1)} %get-tuple-element.186.refs_27_), channel_id=1, source_target_pairs={{0,2},{1,3},{2,0},{3,1},{4,6},{5,7},{6,4},{7,5},{8,10},{9,11},{10,... | collective-permute-start | bytes 1990664 | tf_op jit(solution)/shard_map/ppermute | solution.py:776
  240.6 25.7 %collective-permute-start.39 = (bf16[9,96,384]{2,1,0:T(8,128)(2,1)S(1)}, bf16[9,96,384]{2,1,0:T(8,128)(2,1)S(1)}, u32[]{:S(2)}, u32[]{:S(2)}) collective-permute-start(bf16[9,96,384]{2,1,0:T(8,128)(2,1)S(1)} %get-tuple-element.184.refs_26_), channel_id=1, source_target_pairs={{0,4},{1,5},{2,6},{3,7},{4,0},{5,1},{6,2},{7,3},{8,12},{9,13},{10,... | collective-permute-start | bytes 1990664 | tf_op jit(solution)/shard_map/ppermute | solution.py:776
  242.2 24.1 %collective-permute-start.38 = (bf16[6,96,384]{2,1,0:T(8,128)(2,1)S(1)}, bf16[6,96,384]{2,1,0:T(8,128)(2,1)S(1)}, u32[]{:S(2)}, u32[]{:S(2)}) collective-permute-start(bf16[6,96,384]{2,1,0:T(8,128)(2,1)S(1)} %get-tuple-element.183.refs_3_.refs_29_), channel_id=1, source_target_pairs={{0,4},{1,5},{2,6},{3,7},{4,0},{5,1},{6,2},{7,3},{8,12},{9,13},{10,... | collective-permute-start | bytes 1327112 | tf_op jit(solution)/shard_map/ppermute | solution.py:776
  242.7 23.6 %collective-permute-start.37 = (bf16[6,96,384]{2,1,0:T(8,128)(2,1)S(1)}, bf16[6,96,384]{2,1,0:T(8,128)(2,1)S(1)}, u32[]{:S(2)}, u32[]{:S(2)}) collective-permute-start(bf16[6,96,384]{2,1,0:T(8,128)(2,1)S(1)} %get-tuple-element.180.refs_2_.refs_28_), channel_id=1, source_target_pairs={{0,2},{1,3},{2,0},{3,1},{4,6},{5,7},{6,4},{7,5},{8,10},{9,11},{10,... | collective-permute-start | bytes 1327112 | tf_op jit(solution)/shard_map/ppermute | solution.py:776
  283.4 29.7 %collective-permute-start.47 = (bf16[18,96,384]{2,1,0:T(8,128)(2,1)}, bf16[18,96,384]{2,1,0:T(8,128)(2,1)}, u32[]{:S(2)}, u32[]{:S(2)}) collective-permute-start(bf16[18,96,384]{2,1,0:T(8,128)(2,1)} %get-tuple-element.204.refs_26_), channel_id=1, source_target_pairs={{0,4},{1,5},{2,6},{3,7},{4,0},{5,1},{6,2},{7,3},{8,12},{9,13},{10,... | collective-permute-start | bytes 3981320 | tf_op jit(solution)/shard_map/ppermute | solution.py:776
  286.7 29.6 %collective-permute-start.46 = (bf16[18,96,384]{2,1,0:T(8,128)(2,1)}, bf16[18,96,384]{2,1,0:T(8,128)(2,1)}, u32[]{:S(2)}, u32[]{:S(2)}) collective-permute-start(bf16[18,96,384]{2,1,0:T(8,128)(2,1)} %get-tuple-element.201.refs_25_), channel_id=1, source_target_pairs={{0,2},{1,3},{2,0},{3,1},{4,6},{5,7},{6,4},{7,5},{8,10},{9,11},{10,... | collective-permute-start | bytes 3981320 | tf_op jit(solution)/shard_map/ppermute | solution.py:776
  311.8 77.9 %reduce-scatter.3.cloned.1.call-start = ((), (), s32[]{:S(2)}) async-start(), calls=%async_computation.3 | async-start | bytes 2211840 | tf_op jit(solution)/shard_map/reduce_scatter | solution.py:920
  322.9 24.8 %collective-permute-start.54 = (bf16[9,96,384]{2,1,0:T(8,128)(2,1)S(1)}, bf16[9,96,384]{2,1,0:T(8,128)(2,1)S(1)}, u32[]{:S(2)}, u32[]{:S(2)}) collective-permute-start(bf16[9,96,384]{2,1,0:T(8,128)(2,1)S(1)} %get-tuple-element.220.refs_3_), channel_id=1, source_target_pairs={{0,2},{1,3},{2,0},{3,1},{4,6},{5,7},{6,4},{7,5},{8,10},{9,11},{10,... | collective-permute-start | bytes 1990664 | tf_op jit(solution)/shard_map/ppermute | solution.py:776
  325.6 22.0 %collective-permute-start.53 = (bf16[9,96,384]{2,1,0:T(8,128)(2,1)S(1)}, bf16[9,96,384]{2,1,0:T(8,128)(2,1)S(1)}, u32[]{:S(2)}, u32[]{:S(2)}) collective-permute-start(bf16[9,96,384]{2,1,0:T(8,128)(2,1)S(1)} %get-tuple-element.218.refs_2_), channel_id=1, source_target_pairs={{0,4},{1,5},{2,6},{3,7},{4,0},{5,1},{6,2},{7,3},{8,12},{9,13},{10,... | collective-permute-start | bytes 1990664 | tf_op jit(solution)/shard_map/ppermute | solution.py:776
  353.2 26.2 %collective-permute-start.61 = (bf16[12,96,384]{2,1,0:T(8,128)(2,1)S(1)}, bf16[12,96,384]{2,1,0:T(8,128)(2,1)S(1)}, u32[]{:S(2)}, u32[]{:S(2)}) collective-permute-start(bf16[12,96,384]{2,1,0:T(8,128)(2,1)S(1)} %copy-done.1), channel_id=1, source_target_pairs={{0,1},{1,0},{2,3},{3,2},{4,5},{5,4},{6,7},{7,6},{8,9},{9,8},{10,11... | collective-permute-start | bytes 2654216 | tf_op jit(solution)/shard_map/ppermute | solution.py:776
  353.5 25.9 %collective-permute-start.62 = (bf16[12,96,384]{2,1,0:T(8,128)(2,1)S(1)}, bf16[12,96,384]{2,1,0:T(8,128)(2,1)S(1)}, u32[]{:S(2)}, u32[]{:S(2)}) collective-permute-start(bf16[12,96,384]{2,1,0:T(8,128)(2,1)S(1)} %copy-done.55), channel_id=1, source_target_pairs={{0,1},{1,0},{2,3},{3,2},{4,5},{5,4},{6,7},{7,6},{8,9},{9,8},{10,11... | collective-permute-start | bytes 2654216 | tf_op jit(solution)/shard_map/ppermute | solution.py:776
  355.0 25.3 %collective-permute-start.59 = (bf16[6,96,384]{2,1,0:T(8,128)(2,1)}, bf16[6,96,384]{2,1,0:T(8,128)(2,1)}, u32[]{:S(2)}, u32[]{:S(2)}) collective-permute-start(bf16[6,96,384]{2,1,0:T(8,128)(2,1)} %get-tuple-element.230.refs_1_.refs_6_), channel_id=1, source_target_pairs={{0,1},{1,0},{2,3},{3,2},{4,5},{5,4},{6,7},{7,6},{8,9},{9,8},{10,11... | collective-permute-start | bytes 1327112 | tf_op jit(solution)/shard_map/ppermute | solution.py:776
  (118 other events, 662.4 us)
Sparse Core Ops, SparseCore 0:
  9.8 38.7 all-gather.8
  50.7 30.8 all-gather.10
  84.4 50.0 all-gather.6
  311.9 37.4 reduce-scatter.4
  352.2 37.4 reduce-scatter.2
